TPU v7x, 32 devices: a whole 2x2x4 slice. The times are simulated.
32 devices in a mesh: seq: 8 (over y, x, core), fsdp: 4 (over z).
Axes of the slice: x: 2, y: 2, z: 4, core: 2. Of those that a mesh axis runs over, the one named last changes fastest.
Arguments:
- tokens: bfloat16 [4096, 2048], P(('seq', 'fsdp')), may hold values from -6 to 6
- attn_qkv: bfloat16 [2048, 6144], P(('seq', 'fsdp')), may hold values from -0.125 to 0.125
- attn_out_t: bfloat16 [2048, 2048], P(('seq', 'fsdp')), may hold values from -4 to 4
- mlp_weight: bfloat16 [8192, 6144], P(('seq', 'fsdp')), may hold values from -0.125 to 0.125
- norm1: bfloat16 [2048], P(('seq', 'fsdp')), may hold values from 0.099609375 to 1.8984375
- norm2: bfloat16 [2048], P(('seq', 'fsdp')), may hold values from 0.099609375 to 1.8984375
- cotangent: bfloat16 [4096, 2048], P(('seq', 'fsdp')), may hold values from -6 to 6
Outputs:
- output: bfloat16 [4096, 2048], P(('seq', 'fsdp'))
- grad_tokens: float32 [4096, 2048], P(('seq', 'fsdp'))
- grad_attn_qkv: float32 [2048, 6144], P(('seq', 'fsdp'))
- grad_attn_out_t: float32 [2048, 2048], P(('seq', 'fsdp'))
- grad_mlp_weight: float32 [8192, 6144], P(('seq', 'fsdp'))
- grad_norm1: float32 [2048], P(('seq', 'fsdp'))
- grad_norm2: float32 [2048], P(('seq', 'fsdp'))
All inputs are finite; a program needn't handle non-finite values.
Results may differ from a plain program's by a relative error of at most 0.015.
Values may be sent and summed in bfloat16 or wider, within the bound.
No kernel may reach another device: no remote copies, remote signals or barrier semaphores. Data moves between devices by JAX's collectives and lax.ppermute only.
A program may use at most 768 MiB of HBM per device.

v0:
```python
import jax
import jax.numpy as jnp
from jax import lax
from jax.sharding import PartitionSpec as P

HEADS = 32


epsilon = 1e-05
rope_base = 130000.0


def rotary_tables(positions, head_dim):
    half_dim = head_dim // 2
    frequency = rope_base ** (-(jnp.arange(half_dim, dtype=jnp.float32) * 2.0) / head_dim)
    angles = positions.astype(jnp.float32)[:, None] * frequency[None, :]
    angles = jnp.concatenate([angles, angles], axis=1)
    return (jnp.cos(angles)[:, None, :], jnp.sin(angles)[:, None, :])


def rotate(vectors, cosine_table, sine_table):
    half_dim = vectors.shape[-1] // 2
    turned = jnp.concatenate([-vectors[..., half_dim:], vectors[..., :half_dim]], axis=-1)
    return vectors * cosine_table + turned * sine_table


def rotate_back(grad_rows, cosine_table, sine_table):
    half_dim = grad_rows.shape[-1] // 2
    scaled = grad_rows * sine_table
    turned = jnp.concatenate([scaled[..., half_dim:], -scaled[..., :half_dim]], axis=-1)
    return grad_rows * cosine_table + turned


def norm_forward(token_rows, gain_row):
    factor = lax.rsqrt(jnp.mean(token_rows * token_rows, axis=-1, keepdims=True) + epsilon)
    return (token_rows * factor * gain_row, factor)


def norm_backward(token_rows, factor, gain_row, grad_normed):
    weighted = grad_normed * gain_row
    grad_rows = factor * weighted - token_rows * (factor * factor * factor) * jnp.mean(
        weighted * token_rows, axis=-1, keepdims=True
    )
    grad_gain = jnp.sum(grad_normed * token_rows * factor, axis=0)
    return (grad_rows, grad_gain)


def contract_rows(left_side, right_side):
    return lax.dot_general(
        left_side, right_side, (((0,), (0,)), ((), ())), preferred_element_type=jnp.float32
    )


def contract_cols(left_side, right_side):
    return lax.dot_general(
        left_side, right_side, (((1,), (1,)), ((), ())), preferred_element_type=jnp.float32
    )


def masked_scores(
    query_block, key_block, first_row, key_span, fsdp_index, fsdp_count, local_rows, score_scale
):
    scores = (
        jnp.einsum("qgd,kgd->gqk", query_block, key_block, preferred_element_type=jnp.float32)
        * score_scale
    )
    row_ids = first_row + jnp.arange(query_block.shape[0])
    query_place = (
        row_ids // local_rows * fsdp_count + fsdp_index
    ) * local_rows + row_ids % local_rows
    seq_ids = jnp.arange(key_span)[None, :, None]
    fsdp_ids = jnp.arange(fsdp_count)[:, None, None]
    offsets = jnp.arange(local_rows)[None, None, :]
    key_place = ((seq_ids * fsdp_count + fsdp_ids) * local_rows + offsets).reshape(-1)
    allowed = key_place[None, :] <= query_place[:, None]
    return jnp.where(allowed[None], scores, -1e30)


def block_span(first_row, block_rows, local_rows, seq_count):
    return min(seq_count, (first_row + block_rows - 1) // local_rows + 1)


def attend_forward(queries, key_rows, values, block_rows, fsdp_index):
    query_count, group_heads, head_dim = queries.shape
    fsdp_count, seq_count, local_rows = (key_rows.shape[0], key_rows.shape[1], key_rows.shape[2])
    score_scale = head_dim ** (-0.5)
    results = []
    logsums = []
    for number in range(query_count // block_rows):
        first_row = number * block_rows
        key_span = block_span(first_row, block_rows, local_rows, seq_count)
        key_block = key_rows[:, :key_span].reshape(-1, group_heads, head_dim)
        value_block = values[:, :key_span].reshape(-1, group_heads, head_dim)
        query_block = queries[first_row : first_row + block_rows]
        scores = masked_scores(
            query_block,
            key_block,
            first_row,
            key_span,
            fsdp_index,
            fsdp_count,
            local_rows,
            score_scale,
        )
        largest = jnp.max(scores, axis=-1, keepdims=True)
        exponent = jnp.exp(scores - largest)
        totals = jnp.sum(exponent, axis=-1, keepdims=True)
        probability = (exponent / totals).astype(jnp.bfloat16)
        result = jnp.einsum(
            "gqk,kgd->qgd", probability, value_block, preferred_element_type=jnp.float32
        )
        results.append(result.astype(jnp.bfloat16))
        logsums.append((largest + jnp.log(totals))[..., 0])
    return (jnp.concatenate(results, axis=0), logsums)


def attend_backward(queries, key_rows, values, grad_att, logsums, block_rows, fsdp_index):
    query_count, group_heads, head_dim = queries.shape
    fsdp_count, seq_count, local_rows = (key_rows.shape[0], key_rows.shape[1], key_rows.shape[2])
    score_scale = head_dim ** (-0.5)
    grad_key_sum = jnp.zeros(key_rows.shape, jnp.float32)
    grad_value_sum = jnp.zeros(key_rows.shape, jnp.float32)
    grad_queries = []
    for number in range(query_count // block_rows):
        first_row = number * block_rows
        key_span = block_span(first_row, block_rows, local_rows, seq_count)
        key_block = key_rows[:, :key_span].reshape(-1, group_heads, head_dim)
        value_block = values[:, :key_span].reshape(-1, group_heads, head_dim)
        query_block = queries[first_row : first_row + block_rows]
        grad_block = grad_att[first_row : first_row + block_rows]
        scores = masked_scores(
            query_block,
            key_block,
            first_row,
            key_span,
            fsdp_index,
            fsdp_count,
            local_rows,
            score_scale,
        )
        probability = jnp.exp(scores - logsums[number][..., None])
        prob_low = probability.astype(jnp.bfloat16)
        value_term = jnp.einsum(
            "gqk,qgd->kgd", prob_low, grad_block, preferred_element_type=jnp.float32
        )
        grad_value_sum = grad_value_sum.at[:, :key_span].add(
            value_term.reshape(fsdp_count, key_span, local_rows, group_heads, head_dim)
        )
        grad_prob = jnp.einsum(
            "qgd,kgd->gqk", grad_block, value_block, preferred_element_type=jnp.float32
        )
        grad_scores = probability * (
            grad_prob - jnp.sum(probability * grad_prob, axis=-1, keepdims=True)
        )
        grad_low = grad_scores.astype(jnp.bfloat16)
        grad_queries.append(
            jnp.einsum("gqk,kgd->qgd", grad_low, key_block, preferred_element_type=jnp.float32)
            * score_scale
        )
        key_term = (
            jnp.einsum("gqk,qgd->kgd", grad_low, query_block, preferred_element_type=jnp.float32)
            * score_scale
        )
        grad_key_sum = grad_key_sum.at[:, :key_span].add(
            key_term.reshape(fsdp_count, key_span, local_rows, group_heads, head_dim)
        )
    return (jnp.concatenate(grad_queries, axis=0), grad_key_sum, grad_value_sum)


def shards(tokens, attn_qkv, attn_out_t, mlp_weight, norm1, norm2, cotangent):
    token_rows = tokens.astype(jnp.float32)
    local_rows, model_width = token_rows.shape
    head_dim = model_width // HEADS
    seq_count = lax.axis_size("seq")
    fsdp_count = lax.axis_size("fsdp")
    group_heads = HEADS // seq_count
    group_width = group_heads * head_dim
    query_count = local_rows * seq_count
    block_rows = min(query_count, max(256, query_count // 8))
    fsdp_index = lax.axis_index("fsdp")
    qkv_full, out_full, gain_one_low, gain_two_low = (
        lax.all_gather(attn_qkv, ("seq", "fsdp"), axis=0, tiled=True),
        lax.all_gather(attn_out_t, ("seq", "fsdp"), axis=0, tiled=True),
        lax.all_gather(norm1, ("seq", "fsdp"), axis=0, tiled=True),
        lax.all_gather(norm2, ("seq", "fsdp"), axis=0, tiled=True),
    )
    unit_weight = lax.all_gather(mlp_weight, "fsdp", axis=0, tiled=True)
    gain_one = gain_one_low.astype(jnp.float32)
    gain_two = gain_two_low.astype(jnp.float32)
    unit_stack = unit_weight.reshape(unit_weight.shape[0], 3, model_width)
    positions = (lax.axis_index("seq") * fsdp_count + fsdp_index) * local_rows + jnp.arange(
        local_rows
    )
    cosine_table, sine_table = rotary_tables(positions, head_dim)
    normed_one, factor_one = norm_forward(token_rows, gain_one)
    normed_one_low = normed_one.astype(jnp.bfloat16)
    projected = jnp.dot(normed_one_low, qkv_full, preferred_element_type=jnp.float32).reshape(
        local_rows, 3, HEADS, head_dim
    )
    rotated_q = rotate(projected[:, 0], cosine_table, sine_table)
    rotated_k = rotate(projected[:, 1], cosine_table, sine_table)
    stacked = (
        jnp.stack([rotated_q, rotated_k, projected[:, 2]], axis=1)
        .reshape(local_rows, 3, model_width)
        .astype(jnp.bfloat16)
    )
    head_major = lax.all_to_all(stacked, "seq", split_axis=2, concat_axis=0, tiled=True)
    queries = head_major[:, 0].reshape(query_count, group_heads, head_dim)
    gathered = lax.all_gather(head_major[:, 1:], "fsdp", axis=0, tiled=True).reshape(
        fsdp_count, seq_count, local_rows, 2, group_heads, head_dim
    )
    key_rows = gathered[:, :, :, 0]
    values = gathered[:, :, :, 1]
    attended_heads, logsums = attend_forward(queries, key_rows, values, block_rows, fsdp_index)
    attended = lax.all_to_all(
        attended_heads.reshape(query_count, group_width),
        "seq",
        split_axis=0,
        concat_axis=1,
        tiled=True,
    )
    middle = token_rows + contract_cols(attended, out_full)
    normed_two, factor_two = norm_forward(middle, gain_two)
    normed_two_low = normed_two.astype(jnp.bfloat16)
    mlp_rows, grad_rows_low = (
        lax.all_gather(normed_two_low, "seq", axis=0, tiled=True),
        lax.all_gather(cotangent, "seq", axis=0, tiled=True),
    )
    gate_up = jnp.einsum(
        "td,ujd->tju", mlp_rows, unit_stack[:, :2], preferred_element_type=jnp.float32
    )
    gate_part = gate_up[:, 0]
    up_part = gate_up[:, 1]
    activation = (jax.nn.silu(gate_part) * up_part).astype(jnp.bfloat16)
    branch_part = jnp.dot(activation, unit_stack[:, 2], preferred_element_type=jnp.float32)
    mlp_branch = lax.psum_scatter(
        branch_part.astype(jnp.bfloat16), "seq", scatter_dimension=0, tiled=True
    ).astype(jnp.float32)
    result = (middle + mlp_branch).astype(jnp.bfloat16)
    grad_out = cotangent.astype(jnp.float32)
    grad_act = contract_cols(grad_rows_low, unit_stack[:, 2])
    sigmoid_gate = jax.nn.sigmoid(gate_part)
    grad_gate = grad_act * up_part * sigmoid_gate * (1.0 + gate_part * (1.0 - sigmoid_gate))
    grad_up = grad_act * (gate_part * sigmoid_gate)
    grad_gu_low = jnp.stack([grad_gate, grad_up], axis=1).astype(jnp.bfloat16)
    normed_part = jnp.einsum(
        "tju,ujd->td", grad_gu_low, unit_stack[:, :2], preferred_element_type=jnp.float32
    )
    grad_normed_two = lax.psum_scatter(normed_part, "seq", scatter_dimension=0, tiled=True)
    grad_mid_norm, grad_gain_two = norm_backward(middle, factor_two, gain_two, grad_normed_two)
    grad_middle = grad_out + grad_mid_norm
    paired = jnp.einsum(
        "tjc,td->cjd", grad_gu_low, mlp_rows, preferred_element_type=jnp.float32
    ).reshape(mlp_weight.shape[0] * lax.axis_size("fsdp"), 2 * model_width)
    down_part = contract_rows(activation, grad_rows_low)
    grad_mlp = lax.psum_scatter(
        jnp.concatenate([paired, down_part], axis=1).astype(jnp.bfloat16),
        "fsdp",
        scatter_dimension=0,
        tiled=True,
    ).astype(jnp.float32)
    grad_mid_low = grad_middle.astype(jnp.bfloat16)
    grad_attended = jnp.dot(grad_mid_low, out_full, preferred_element_type=jnp.float32).astype(
        jnp.bfloat16
    )
    grad_heads = lax.all_to_all(
        grad_attended, "seq", split_axis=1, concat_axis=0, tiled=True
    ).reshape(query_count, group_heads, head_dim)
    grad_queries, grad_key_sum, grad_value_sum = attend_backward(
        queries, key_rows, values, grad_heads, logsums, block_rows, fsdp_index
    )
    key_grads, value_grads = (
        lax.psum_scatter(
            grad_key_sum.reshape(fsdp_count * query_count, group_width).astype(jnp.bfloat16),
            "fsdp",
            scatter_dimension=0,
            tiled=True,
        ).astype(jnp.float32),
        lax.psum_scatter(
            grad_value_sum.reshape(fsdp_count * query_count, group_width).astype(jnp.bfloat16),
            "fsdp",
            scatter_dimension=0,
            tiled=True,
        ).astype(jnp.float32),
    )
    grad_stack = jnp.stack(
        [grad_queries.reshape(query_count, group_width), key_grads, value_grads], axis=1
    ).astype(jnp.bfloat16)
    grad_local = lax.all_to_all(grad_stack, "seq", split_axis=0, concat_axis=2, tiled=True).astype(
        jnp.float32
    )
    grad_q_raw = rotate_back(
        grad_local[:, 0].reshape(local_rows, HEADS, head_dim), cosine_table, sine_table
    )
    grad_k_raw = rotate_back(
        grad_local[:, 1].reshape(local_rows, HEADS, head_dim), cosine_table, sine_table
    )
    grad_qkv_low = jnp.concatenate(
        [
            grad_q_raw.reshape(local_rows, model_width),
            grad_k_raw.reshape(local_rows, model_width),
            grad_local[:, 2],
        ],
        axis=1,
    ).astype(jnp.bfloat16)
    grad_normed_one = contract_cols(grad_qkv_low, qkv_full)
    grad_rows_norm, grad_gain_one = norm_backward(token_rows, factor_one, gain_one, grad_normed_one)
    grad_tokens = grad_middle + grad_rows_norm
    grad_qkv_term = contract_rows(normed_one_low, grad_qkv_low)
    grad_out_term = contract_rows(grad_mid_low, attended)
    grad_qkv, grad_out_w, grad_norm_one, grad_norm_two = (
        lax.psum_scatter(grad_qkv_term, ("seq", "fsdp"), scatter_dimension=0, tiled=True),
        lax.psum_scatter(grad_out_term, ("seq", "fsdp"), scatter_dimension=0, tiled=True),
        lax.psum_scatter(grad_gain_one, ("seq", "fsdp"), scatter_dimension=0, tiled=True),
        lax.psum_scatter(grad_gain_two, ("seq", "fsdp"), scatter_dimension=0, tiled=True),
    )
    return (result, grad_tokens, grad_qkv, grad_out_w, grad_mlp, grad_norm_one, grad_norm_two)


def solution(mesh):
    in_specs = (
        P(("seq", "fsdp"), None),
        P(("seq", "fsdp"), None),
        P(("seq", "fsdp"), None),
        P(("seq", "fsdp"), None),
        P(("seq", "fsdp")),
        P(("seq", "fsdp")),
        P(("seq", "fsdp"), None),
    )
    out_specs = (
        P(("seq", "fsdp"), None),
        P(("seq", "fsdp"), None),
        P(("seq", "fsdp"), None),
        P(("seq", "fsdp"), None),
        P(("seq", "fsdp"), None),
        P(("seq", "fsdp")),
        P(("seq", "fsdp")),
    )
    return jax.shard_map(shards, mesh=mesh, in_specs=in_specs, out_specs=out_specs, check_vma=False)
```

profile of v0, /device:TPU:0, one launch (start us, length us, event | category | flops | bytes accessed | tf_op | source)
XLA Modules:
  0.0 2132.9 jit_solution(3701401967962488630)
XLA Ops:
  9.7 43.3 %all-reduce.7 = (bf16[2048]{0:T(1024)(128)(2,1)S(1)}, bf16[2048]{0:T(1024)(128)(2,1)}) all-reduce(bf16[2048]{0:T(1024)(128)(2,1)S(1)} %dynamic-update-slice.22, bf16[2048]{0:T(1024)(128)(2,1)S(1)} %dynamic-update-slice.23), channel_id=1, replica_groups=mesh['seq'=8,'fsdp'=4] {'seq','fsdp'}, use_global_device_ids=true, to_apply=%add.2 | all-reduce | flops 4096 | bytes 16384
  55.0 114.6 %all-gather.7.cloned.1.call-done = bf16[2048,6144]{1,0:T(8,128)(2,1)} async-done(((bf16[64,6144]{1,0:T(8,128)(2,1)}), bf16[2048,6144]{1,0:T(8,128)(2,1)}) %all-gather.7.cloned.1.call-update) | async-done | bytes 25165840 | tf_op jit(solution)/shard_map/all_gather | solution.py:182
  169.5 14.8 fusion.104
  185.6 10.0 copy.75
  195.7 29.1 %all_to_all.62 = bf16[128,3,2048]{0,1,2:T(4,128)(2,1)S(1)} all-to-all(bf16[128,3,2048]{0,1,2:T(4,128)(2,1)S(1)} %copy.75), channel_id=1, replica_groups=mesh['seq'=8,'fsdp'=4] {'seq'}, dimensions={2} | all-to-all | bytes 3145728 | tf_op jit(solution)/shard_map/all_to_all | solution.py:207
  228.7 5.2 copy.78
  239.3 66.8 %all-gather.9.cloned.1.call-done = bf16[4096,2,256]{0,2,1:T(8,128)(2,1)} async-done(((bf16[1024,2,256]{0,2,1:T(8,128)(2,1)}), bf16[4096,2,256]{0,2,1:T(8,128)(2,1)}) %all-gather.9.cloned.1.call-update) | async-done | bytes 4194320 | tf_op jit(solution)/shard_map/all_gather | solution.py:209
  309.6 3.7 slice_bitcast_fusion.8
  318.1 4.2 reshape_squeeze.20
  332.0 4.3 reshape.1049
  338.9 4.4 reshape_squeeze.19
  363.2 7.8 fusion.128
  371.0 8.4 fusion
  379.5 5.3 fusion.76
  384.9 6.3 fusion.75
  393.4 3.7 fusion.74
  401.8 9.6 all-to-all-done.1
  411.4 6.7 multiply_reduce_fusion.6
  419.7 185.2 %all-gather.15.cloned.1.call-done = bf16[1024,6144]{0,1:T(8,128)(2,1)} async-done(((bf16[256,6144]{0,1:T(8,128)(2,1)}), bf16[1024,6144]{0,1:T(8,128)(2,1)}) %all-gather.15.cloned.1.call-update) | async-done | bytes 12582928 | tf_op jit(solution)/shard_map/all_gather | solution.py:187
  604.9 35.7 %all-gather.13.cloned.1.call-done = bf16[1024,2048]{1,0:T(8,128)(2,1)} async-done(((bf16[128,2048]{1,0:T(8,128)(2,1)}), bf16[1024,2048]{1,0:T(8,128)(2,1)}) %all-gather.13.cloned.1.call-update) | async-done | bytes 4194320 | tf_op jit(solution)/shard_map/all_gather | solution.py:226
  640.6 14.9 fusion.41
  655.5 23.6 %all-gather.17.cloned.1.call-done = bf16[1024,2048]{1,0:T(8,128)(2,1)} async-done(((bf16[128,2048]{1,0:T(8,128)(2,1)}), bf16[1024,2048]{1,0:T(8,128)(2,1)}) %all-gather.17.cloned.1.call-update) | async-done | bytes 4194320 | tf_op jit(solution)/shard_map/all_gather | solution.py:227
  679.1 11.7 fusion.58
  692.9 11.2 fusion.18
  704.3 11.5 convolution_convert_fusion.2
  716.4 59.1 %reduce-scatter.10.cloned.1.call-done = f32[128,2048]{1,0:T(8,128)} async-done(((f32[1024,2048]{1,0:T(8,128)}), f32[128,2048]{1,0:T(8,128)}) %reduce-scatter.10.cloned.1.call-update) | async-done | bytes 1048592 | tf_op jit(solution)/shard_map/reduce_scatter | solution.py:249
  777.6 53.5 %reduce-scatter.8.cloned.1.call-done = bf16[128,2048]{1,0:T(8,128)(2,1)} async-done(((bf16[1024,2048]{1,0:T(8,128)(2,1)}), bf16[128,2048]{1,0:T(8,128)(2,1)}) %reduce-scatter.8.cloned.1.call-update) | async-done | bytes 524304 | tf_op jit(solution)/shard_map/reduce_scatter | solution.py:236
  833.7 5.1 convolution_convert_fusion.3
  843.3 9.6 all-to-all-done.2
  853.2 4.2 fusion.59
  857.4 3.7 multiply_reduce_fusion.3
  861.3 6.2 fusion.47
  867.5 7.2 multiply_reduce_fusion.2
  875.0 5.9 fusion.35
  880.9 9.3 multiply_reduce_fusion.1
  893.5 3.7 reshape.1055
  900.1 4.3 multiply_convert_fusion.3
  910.4 7.3 fusion.4
  926.6 28.3 %scatter-add.29 = f32[4,8,128,4,64]{2,1,0,4,3:T(8,128)} dynamic-update-slice(f32[4,8,128,4,64]{2,1,0,4,3:T(8,128)} %copy-done.8, f32[4,6,128,4,64]{2,1,0,4,3:T(8,128)} %slice_add_fusion, s32[]{:T(128)} %constant.336.clone.1, s32[]{:T(128)} %constant.336.clone.1, s32[]{:T(128)} %constant.336.clone.1, s32[]{:T(128)} %constant.336.clone.1, s32[]{:T(128)} %constant.336.clone.1) | dynamic-update-slice | bytes 6291460 | tf_op jit(solution)/shard_map/scatter-add | solution.py:146
  954.9 4.5 add_convert_fusion
  961.7 4.1 copy.86
  965.9 7.7 multiply_convert_fusion.2
  978.9 9.9 multiply_convert_fusion.1
  995.7 5.0 add_dynamic-update-slice_fusion.1
  1000.8 5.2 slice_add_fusion.1
  1005.9 28.4 %scatter-add.24 = f32[4,8,128,4,64]{2,1,0,4,3:T(8,128)} dynamic-update-slice(f32[4,8,128,4,64]{2,1,0,4,3:T(8,128)} %add_dynamic-update-slice_fusion.1, f32[4,6,128,4,64]{2,1,0,4,3:T(8,128)} %slice_add_fusion.1, s32[]{:T(128)} %constant.336.clone.1, s32[]{:T(128)} %constant.336.clone.1, s32[]{:T(128)} %constant.336.clone.1, s32[]{:T(128)} %constant.336.clone.1, s32[]{:T(128)} %constant.336.clone.1) | dynamic-update-slice | bytes 6291460 | tf_op jit(solution)/shard_map/scatter-add | solution.py:164
  1034.3 7.8 multiply_reduce_fusion
  1042.2 8.5 multiply_convert_fusion
  1059.7 4.2 copy.85
  1064.0 13.7 convolution_convert_fusion
  1077.7 11.4 copy.94
  1089.2 9.6 convolution_convert_fusion.1
  1098.8 8.9 pad_maximum_fusion
  1109.1 9.1 fusion.100
  1121.7 4.0 fusion.78
  1125.8 5.1 fusion.77
  1136.6 29.5 %all_to_all.63 = bf16[1024,3,256]{2,1,0:T(4,128)(2,1)S(1)} all-to-all(bf16[1024,3,256]{2,1,0:T(4,128)(2,1)S(1)} %copy.88), channel_id=1, replica_groups=mesh['seq'=8,'fsdp'=4] {'seq'}, dimensions={0} | all-to-all | bytes 3145728 | tf_op jit(solution)/shard_map/all_to_all | solution.py:289
  1173.2 21.3 fusion.96
  1195.9 20.6 fusion.91
  1216.5 46.1 %all-reduce.6 = (f32[2048]{0:T(1024)S(1)}, f32[2048]{0:T(1024)S(1)}) all-reduce(f32[2048]{0:T(1024)S(1)} %get-tuple-element.121, f32[2048]{0:T(1024)S(1)} %copy-done.58), channel_id=9, replica_groups=mesh['seq'=8,'fsdp'=4] {'seq','fsdp'}, use_global_device_ids=true, to_apply=%region_24.25.clone | all-reduce | flops 4096 | bytes 32768
  1266.4 55.3 %reduce-scatter.20.cloned.1.call-done = bf16[256,6144]{1,0:T(8,128)(2,1)} async-done(((bf16[1024,6144]{1,0:T(8,128)(2,1)}), bf16[256,6144]{1,0:T(8,128)(2,1)}) %reduce-scatter.20.cloned.1.call-update) | async-done | bytes 3145744 | tf_op jit(solution)/shard_map/reduce_scatter | solution.py:256
  1321.7 5.3 convert_element_type.185
  1327.0 362.6 %reduce-scatter.18.cloned.1.call-done = f32[64,2048]{1,0:T(8,128)} async-done(((f32[2048,2048]{1,0:T(8,128)}), f32[64,2048]{1,0:T(8,128)}) %reduce-scatter.18.cloned.1.call-update) | async-done | bytes 524304 | tf_op jit(solution)/shard_map/reduce_scatter | solution.py:313
  1689.6 436.5 %reduce-scatter.16.cloned.1.call-done = f32[64,6144]{1,0:T(8,128)} async-done(((f32[2048,6144]{1,0:T(8,128)}), f32[64,6144]{1,0:T(8,128)}) %reduce-scatter.16.cloned.1.call-update) | async-done | bytes 1572880 | tf_op jit(solution)/shard_map/reduce_scatter | solution.py:312
  (309 shorter events, 143.7 us)
Async XLA Ops:
  7.2 162.3 %all-gather.7.cloned.1.call-start = ((), (), s32[]{:S(2)}) async-start(), calls=%async_computation.11 | async-start | bytes 25952256 | tf_op jit(solution)/shard_map/all_gather | solution.py:182
  7.9 298.2 %all-gather.9.cloned.1.call-start = ((), (), s32[]{:S(2)}) async-start(), calls=%async_computation.12 | async-start | bytes 5242880 | tf_op jit(solution)/shard_map/all_gather | solution.py:209
  52.9 131.4 %copy-start.47 = (f32[2048]{0:T(1024)}, f32[2048]{0:T(1024)S(1)}, u32[]{:S(2)}) copy-start(f32[2048]{0:T(1024)S(1)} %convert_element_type.143) | copy-start | bytes 24580
  53.1 131.8 %copy-start.49 = (f32[128,64]{0,1:T(8,128)}, f32[128,64]{0,1:T(8,128)S(1)}, u32[]{:S(2)}) copy-start(f32[128,64]{0,1:T(8,128)S(1)} %get-tuple-element.161) | copy-start | bytes 98308
  53.1 131.8 %copy-start.51 = (f32[128,64]{0,1:T(8,128)}, f32[128,64]{0,1:T(8,128)S(1)}, u32[]{:S(2)}) copy-start(f32[128,64]{0,1:T(8,128)S(1)} %get-tuple-element.162) | copy-start | bytes 98308
  54.9 129.4 %copy-start.59 = (f32[128]{0:T(128)}, f32[128]{0:T(128)S(1)}, u32[]{:S(2)}) copy-start(f32[128]{0:T(128)S(1)} %get-tuple-element.164) | copy-start | bytes 1540
  227.9 173.8 %all-gather.11.cloned.1.call-start = ((), (), s32[]{:S(2)}) async-start(), calls=%async_computation.13 | async-start | bytes 8650752 | tf_op jit(solution)/shard_map/all_gather | solution.py:183
  228.7 376.2 %all-gather.15.cloned.1.call-start = ((), (), s32[]{:S(2)}) async-start(), calls=%async_computation.15 | async-start | bytes 15728640 | tf_op jit(solution)/shard_map/all_gather | solution.py:187
  343.3 4.2 copy-start.24
  343.3 4.2 copy-start.38
  343.3 4.2 copy-start.44
  345.6 13.2 copy-start.2
  349.3 3.7 copy-start.1
  349.3 3.7 copy-start.14
  355.6 4.6 copy-start
  355.6 29.2 %copy-start.54 = (f32[4,256]{1,0:T(4,128)}, f32[4,256]{1,0:T(4,128)S(1)}, u32[]{:S(2)}) copy-start(f32[4,256]{1,0:T(4,128)S(1)} %get-tuple-element.169) | copy-start | bytes 12292
  370.9 20.3 copy-start.56
  371.0 8.4 copy-start.32
  371.0 8.4 copy-start.62
  379.4 5.4 copy-start.27
  379.4 5.4 copy-start.64
  379.4 11.8 slice-start
  379.5 11.8 slice-start.1
  384.8 6.4 slice-start.2
  384.9 7.6 slice-start.3
  384.9 8.5 copy-start.22
  393.4 3.7 copy-start.53
  397.1 4.6 copy-start.67
  397.1 14.3 copy-start.17
  398.2 13.2 all-to-all-start.1
  401.7 239.0 %all-gather.13.cloned.1.call-start = ((), (), s32[]{:S(2)}) async-start(), calls=%async_computation.14 | async-start | bytes 4718592 | tf_op jit(solution)/shard_map/all_gather | solution.py:226
  411.4 6.7 copy-start.30
  419.1 260.1 %all-gather.17.cloned.1.call-start = ((), (), s32[]{:S(2)}) async-start(), calls=%async_computation.17 | async-start | bytes 4718592 | tf_op jit(solution)/shard_map/all_gather | solution.py:227
  419.6 355.9 %reduce-scatter.10.cloned.1.call-start = ((), (), s32[]{:S(2)}) async-start(), calls=%async_computation.18 | async-start | bytes 9437184 | tf_op jit(solution)/shard_map/reduce_scatter | solution.py:249
  679.1 13.7 copy-start.69
  704.1 127.1 %reduce-scatter.8.cloned.1.call-start = ((), (), s32[]{:S(2)}) async-start(), calls=%async_computation.16 | async-start | bytes 4718592 | tf_op jit(solution)/shard_map/reduce_scatter | solution.py:236
  715.8 115.4 %copy-start.39 = (bf16[128,2048]{1,0:T(8,128)(2,1)S(1)}, bf16[128,2048]{1,0:T(8,128)(2,1)}, u32[]{:S(2)}) copy-start(bf16[128,2048]{1,0:T(8,128)(2,1)} %param.33) | copy-start | bytes 1572868
  833.6 5.1 copy-start.12
  833.7 9.6 copy-start.55
  833.7 9.6 copy-start.57
  839.6 17.8 copy-start.37
  839.6 13.3 all-to-all-start.2
  843.2 290.7 %reduce-scatter.14.cloned.1.call-start = ((), (), s32[]{:S(2)}) async-start(), calls=%async_computation.20 | async-start | bytes 2621440 | tf_op jit(solution)/shard_map/reduce_scatter | solution.py:279
  853.1 4.2 copy-start.3
  875.0 5.9 copy-start.28
  900.1 5.7 copy-start.46
  961.7 4.2 copy-start.66
  965.8 168.1 %reduce-scatter.12.cloned.1.call-start = ((), (), s32[]{:S(2)}) async-start(), calls=%async_computation.19 | async-start | bytes 2621440 | tf_op jit(solution)/shard_map/reduce_scatter | solution.py:273
  965.9 9.7 copy-start.45
  978.9 12.7 copy-start.43
  995.7 5.1 copy-start.20
  1005.9 28.4 %copy-start.23 = (bf16[4096,4,64]{0,2,1:T(8,128)(2,1)S(1)}, bf16[4096,4,64]{0,2,1:T(8,128)(2,1)}, u32[]{:S(2)}) copy-start(bf16[4096,4,64]{0,2,1:T(8,128)(2,1)} %reshape_squeeze.19) | copy-start | bytes 6291460
  1042.2 8.6 copy-start.41
  1059.7 4.3 copy-start.71
  1063.9 257.7 %reduce-scatter.20.cloned.1.call-start = ((), (), s32[]{:S(2)}) async-start(), calls=%async_computation.23 | async-start | bytes 15728640 | tf_op jit(solution)/shard_map/reduce_scatter | solution.py:256
  1089.2 9.6 copy-start.9
  1107.7 581.9 %reduce-scatter.18.cloned.1.call-start = ((), (), s32[]{:S(2)}) async-start(), calls=%async_computation.22 | async-start | bytes 17301504 | tf_op jit(solution)/shard_map/reduce_scatter | solution.py:313
  1118.2 7.6 copy-start.15
  1118.2 1008.0 %reduce-scatter.16.cloned.1.call-start = ((), (), s32[]{:S(2)}) async-start(), calls=%async_computation.21 | async-start | bytes 51904512 | tf_op jit(solution)/shard_map/reduce_scatter | solution.py:312
  1119.2 11.7 slice-start.4
  1121.7 9.2 slice-start.5
  1125.8 5.1 copy-start.11
  1195.9 20.6 copy-start.58
  1195.9 67.8 %copy-start.68 = (f32[128]{0:T(128)S(1)}, f32[128]{0:T(128)}, u32[]{:S(2)}) copy-start(f32[128]{0:T(128)} %get-tuple-element.163) | copy-start | bytes 1540
  (30 other events, 63.5 us)
Sparse Core Ops, SparseCore 0:
  10.9 158.5 all-gather.6
  228.0 78.0 all-gather.8
  309.0 75.9 all-gather.10
  387.0 217.8 all-gather.14
  607.2 33.3 all-gather.12
  642.4 36.7 all-gather.16
  704.2 71.2 reduce-scatter.9
  779.8 51.2 reduce-scatter.7
  965.9 42.9 reduce-scatter.13
  1064.1 42.9 reduce-scatter.11
  1109.4 212.2 reduce-scatter.19
  1324.4 365.1 reduce-scatter.17
  1696.6 429.4 reduce-scatter.15
where the time goes:
time: 2140 us; the launch traced here: 2130 us
  waiting for transfers between devices  1410 us (66%)
  matrix products  253 us (12%)
  local copies, waits for them, and re-layouts  195 us (9%)
  blocking collectives  148 us (7%)
  other arithmetic  99.1 us (5%)
    reduce_scatter x1, waiting for transfers between devices, shards(): lax.psum_scatter(grad_qkv_term, ('seq', 'fsdp'), scatter_dimension=0, til...  437 us
    reduce_scatter x1, waiting for transfers between devices, shards(): lax.psum_scatter(grad_out_term, ('seq', 'fsdp'), scatter_dimension=0, til...  363 us
    all_gather x1, waiting for transfers between devices, shards(): unit_weight = lax.all_gather(mlp_weight, 'fsdp', axis=0, tiled=True)  185 us
    all_gather x1, waiting for transfers between devices, shards(): lax.all_gather(attn_qkv, ('seq', 'fsdp'), axis=0, tiled=True)  115 us
    unnamed x2, blocking collectives  89.4 us
    all_gather x1, waiting for transfers between devices, shards(): lax.all_gather(head_major[:, 1:], 'fsdp', axis=0, tiled=True)  66.8 us
    reduce_scatter x1, waiting for transfers between devices, shards(): lax.psum_scatter(normed_part, 'seq', scatter_dimension=0, tiled=True)  59.1 us
    reduce_scatter x1, waiting for transfers between devices, shards(): lax.psum_scatter(jnp.concatenate([paired, down_part], axis=1).astype(jnp....  55.3 us
  transfers between devices with their start and end apart: 15, of which 12 were waited for; matrix products, arithmetic and copies ran while one was open for 17% of the time, Pallas kernels for 0%

commit v1 on v0

v1 whole, which is shorter than its diff:
```python
import functools

import jax
import jax.numpy as jnp
from jax import lax
from jax.experimental import pallas as pl
from jax.experimental.pallas import tpu as pltpu
from jax.sharding import Mesh
from jax.sharding import PartitionSpec as P

HEADS = 32
epsilon = 1e-05
rope_base = 130000.0
f32 = jnp.float32
bf16 = jnp.bfloat16
ALL = ("r", "p", "c", "z")
GROUPS = ("r", "p")
TENSOR = ("c", "z")


def contract(left, right, left_dim, right_dim):
    return lax.dot_general(
        left, right, (((left_dim,), (right_dim,)), ((), ())), preferred_element_type=f32
    )


def causal(scores):
    keys = lax.broadcasted_iota(jnp.int32, scores.shape, 0)
    queries = lax.broadcasted_iota(jnp.int32, scores.shape, 1)
    return jnp.where(keys <= queries, scores, -1e30)


def forward_kernel(qkv_ref, out_ref, logsum_ref, keys, values_t, queries_t, *, block):
    chunks, rows = qkv_ref.shape[0], qkv_ref.shape[3]
    per_chunk = rows // block
    count = chunks * per_chunk
    head_dim = qkv_ref.shape[2]
    for number in range(count):
        chunk, part = divmod(number, per_chunk)
        span = slice(part * block, (part + 1) * block)
        queries_t[number] = qkv_ref[chunk, 0, :, span]
        keys[number] = qkv_ref[chunk, 1, :, span].T
        values_t[number] = qkv_ref[chunk, 2, :, span]

    def step(i, j, carry, diagonal):
        largest, total, result = carry
        scores = contract(keys[j], queries_t[i], 1, 0)
        if diagonal:
            scores = causal(scores)
        new_largest = jnp.maximum(largest, jnp.max(scores, axis=0, keepdims=True))
        shrink = jnp.exp(largest - new_largest)
        weights = jnp.exp(scores - new_largest)
        total = total * shrink + jnp.sum(weights, axis=0, keepdims=True)
        result = result * shrink + contract(values_t[j], weights.astype(bf16), 1, 0)
        return new_largest, total, result

    def query_block(i, _):
        carry = (
            jnp.full((1, block), -1e30, f32),
            jnp.zeros((1, block), f32),
            jnp.zeros((head_dim, block), f32),
        )
        carry = lax.fori_loop(0, i, lambda j, c: step(i, j, c, False), carry)
        largest, total, result = step(i, i, carry, True)
        out_ref[i] = (result / total).astype(bf16)
        logsum_ref[i] = largest + jnp.log(total)
        return 0

    lax.fori_loop(0, count, query_block, 0)


def backward_kernel(
    qkv_ref, grad_ref, out_ref, logsum_ref, result_ref,
    keys, queries, values, grads, keys_t, queries_t, grads_t, deltas, grad_queries,
    *, block, scale,
):
    chunks, rows = qkv_ref.shape[0], qkv_ref.shape[3]
    per_chunk = rows // block
    count = chunks * per_chunk
    head_dim = qkv_ref.shape[2]
    for number in range(count):
        chunk, part = divmod(number, per_chunk)
        span = slice(part * block, (part + 1) * block)
        queries_t[number] = qkv_ref[chunk, 0, :, span]
        keys_t[number] = qkv_ref[chunk, 1, :, span]
        queries[number] = qkv_ref[chunk, 0, :, span].T
        keys[number] = qkv_ref[chunk, 1, :, span].T
        values[number] = qkv_ref[chunk, 2, :, span].T
        grad = grad_ref[chunk, :, span]
        grads_t[number] = grad
        grads[number] = grad.T
        deltas[number] = jnp.sum(
            grad.astype(f32) * out_ref[number].astype(f32), axis=0, keepdims=True
        )
        grad_queries[number] = jnp.zeros((head_dim, block), f32)

    def step(i, j, carry, diagonal):
        grad_key, grad_value = carry
        scores = contract(keys[j], queries_t[i], 1, 0)
        if diagonal:
            scores = causal(scores)
        probs = jnp.exp(scores - logsum_ref[i])
        grad_value = grad_value + contract(probs.astype(bf16), grads[i], 1, 0)
        grad_probs = contract(values[j], grads_t[i], 1, 0)
        grad_scores = (probs * (grad_probs - deltas[i])).astype(bf16)
        grad_key = grad_key + contract(grad_scores, queries[i], 1, 0)
        grad_queries[i] = grad_queries[i] + contract(keys_t[j], grad_scores, 1, 0)
        return grad_key, grad_value

    for j in range(count):
        zero = jnp.zeros((block, head_dim), f32)
        carry = step(j, j, (zero, zero), True)
        grad_key, grad_value = lax.fori_loop(
            j + 1, count, lambda i, c, j=j: step(i, j, c, False), carry
        )
        chunk, part = divmod(j, per_chunk)
        span = slice(part * block, (part + 1) * block)
        result_ref[chunk, 1, :, span] = grad_key.T.astype(bf16)
        result_ref[chunk, 2, :, span] = grad_value.T.astype(bf16)
    for i in range(count):
        chunk, part = divmod(i, per_chunk)
        span = slice(part * block, (part + 1) * block)
        result_ref[chunk, 0, :, span] = (grad_queries[i] * scale).astype(bf16)


def attend_forward(qkv, block):
    chunks, _, head_dim, rows = qkv.shape
    count = chunks * rows // block
    pairs = count * (count + 1) // 2 * block * block
    in_vmem = pl.BlockSpec(memory_space=pltpu.VMEM)
    by_rows = pltpu.VMEM((count, block, head_dim), bf16)
    by_features = pltpu.VMEM((count, head_dim, block), bf16)
    return pl.pallas_call(
        functools.partial(forward_kernel, block=block),
        out_shape=(
            jax.ShapeDtypeStruct((count, head_dim, block), bf16),
            jax.ShapeDtypeStruct((count, 1, block), f32),
        ),
        in_specs=[in_vmem],
        out_specs=(in_vmem, in_vmem),
        scratch_shapes=[by_rows, by_features, by_features],
        compiler_params=pltpu.CompilerParams(vmem_limit_bytes=56 * 2**20),
        cost_estimate=pl.CostEstimate(
            flops=16 * pairs * head_dim, bytes_accessed=qkv.size * 3, transcendentals=pairs
        ),
        name="attend_forward",
    )(qkv)


def attend_backward(qkv, grad, out, logsum, block):
    chunks, _, head_dim, rows = qkv.shape
    count = chunks * rows // block
    pairs = count * (count + 1) // 2 * block * block
    in_vmem = pl.BlockSpec(memory_space=pltpu.VMEM)
    by_rows = pltpu.VMEM((count, block, head_dim), bf16)
    by_features = pltpu.VMEM((count, head_dim, block), bf16)
    return pl.pallas_call(
        functools.partial(backward_kernel, block=block, scale=head_dim**-0.5),
        out_shape=jax.ShapeDtypeStruct(qkv.shape, bf16),
        in_specs=[in_vmem] * 4,
        out_specs=in_vmem,
        scratch_shapes=[by_rows] * 4
        + [by_features] * 3
        + [pltpu.VMEM((count, 1, block), f32), pltpu.VMEM((count, head_dim, block), f32)],
        compiler_params=pltpu.CompilerParams(vmem_limit_bytes=60 * 2**20),
        cost_estimate=pl.CostEstimate(
            flops=32 * pairs * head_dim, bytes_accessed=qkv.size * 6, transcendentals=pairs
        ),
        name="attend_backward",
    )(qkv, grad, out, logsum)


def rotary_tables(positions, head_dim):
    half_dim = head_dim // 2
    frequency = rope_base ** (-(jnp.arange(half_dim, dtype=f32) * 2.0) / head_dim)
    angles = positions.astype(f32)[None, :] * frequency[:, None]
    return jnp.cos(angles), jnp.sin(angles)


def rotate(vectors, cosine, sine):
    half_dim = vectors.shape[-2] // 2
    first, second = vectors[..., :half_dim, :], vectors[..., half_dim:, :]
    return jnp.concatenate(
        [first * cosine - second * sine, second * cosine + first * sine], axis=-2
    )


def rotate_back(grads, cosine, sine):
    half_dim = grads.shape[-2] // 2
    first, second = grads[..., :half_dim, :], grads[..., half_dim:, :]
    return jnp.concatenate(
        [first * cosine + second * sine, second * cosine - first * sine], axis=-2
    )


def shards(tokens, attn_qkv, attn_out_t, mlp_weight, norm1, norm2, cotangent):
    rows, width = tokens.shape
    group_count, share_count = lax.axis_size("p"), lax.axis_size("r")
    tensor_count = lax.axis_size("c") * lax.axis_size("z")
    head_dim = width // HEADS
    heads_here = HEADS // tensor_count
    group_rows = rows * tensor_count
    features_here = heads_here * head_dim
    weight_rows = attn_qkv.shape[0]
    share = lax.axis_index("r")
    block = min(1024, group_rows)
    x = tokens.astype(f32)
    gain_one = norm1.astype(f32)[:, None]

    scaled_qkv = (attn_qkv.astype(f32) * gain_one).astype(bf16)
    qkv_cut = scaled_qkv.reshape(weight_rows, 3, tensor_count, features_here).transpose(2, 0, 1, 3)
    qkv_cut = qkv_cut.reshape(tensor_count, weight_rows, 3 * features_here)
    qkv_part = lax.all_to_all(qkv_cut, TENSOR, 0, 0).reshape(-1, 3 * features_here)
    qkv_weight = lax.all_gather(qkv_part, GROUPS, axis=0, tiled=True)
    x_group = lax.all_gather(tokens, TENSOR, axis=0, tiled=True).astype(f32)
    out_full = lax.all_gather(attn_out_t, ALL, axis=0, tiled=True)
    gain_two = lax.all_gather(norm2, ALL, axis=0, tiled=True).astype(f32)
    unit_weight = lax.all_gather(mlp_weight, GROUPS, axis=0, tiled=True)
    weight_gate = unit_weight[:, :width]
    weight_up = unit_weight[:, width : 2 * width]
    weight_down = unit_weight[:, 2 * width :]
    grad_out_group = lax.all_gather(cotangent, TENSOR, axis=0, tiled=True)

    factor_group = lax.rsqrt(jnp.mean(x_group * x_group, axis=-1, keepdims=True) + epsilon)
    unit_group = (x_group * factor_group).astype(bf16)
    group_index = share * group_count + lax.axis_index("p")
    positions = group_index * group_rows + jnp.arange(group_rows)
    cosine, sine = rotary_tables(positions, head_dim)
    projected = contract(qkv_weight, unit_group, 0, 1)
    projected = projected.reshape(3, heads_here, head_dim, group_rows)
    query_rows = rotate(projected[0], cosine, sine).astype(bf16) * bf16(head_dim**-0.5)
    key_rows = rotate(projected[1], cosine, sine).astype(bf16)
    stacked = jnp.stack([query_rows, key_rows, projected[2].astype(bf16)], axis=1)
    qkv = lax.all_to_all(stacked, "p", 0, 0)

    def over_shares(array):
        return lax.all_gather(array, "r", axis=0, tiled=True) if share_count > 1 else array

    def own_share(array):
        if share_count == 1:
            return array
        return lax.dynamic_slice_in_dim(array, share * group_count, group_count, 0)

    def by_chunk(blocks):
        blocks = blocks.reshape(share_count * group_count, -1, head_dim, block)
        return blocks.transpose(0, 2, 1, 3).reshape(-1, head_dim, group_rows)

    qkv = over_shares(qkv)
    attended, logsum = attend_forward(qkv, block)
    attended_head = own_share(by_chunk(attended))

    to_tokens = attended_head.reshape(group_count, head_dim, tensor_count, rows)
    to_tokens = to_tokens.transpose(0, 2, 1, 3).reshape(-1, head_dim, rows)
    attended_local = lax.all_to_all(to_tokens, ("p", "c", "z"), 0, 0)
    attended_local = attended_local.reshape(group_count, tensor_count, head_dim, rows)
    attended_local = attended_local.transpose(1, 0, 2, 3).reshape(width, rows)
    middle = x + contract(attended_local, out_full, 0, 1)
    attended_group = lax.all_to_all(attended_head, "p", 0, 0).reshape(features_here, group_rows)

    factor_two = lax.rsqrt(jnp.mean(middle * middle, axis=-1, keepdims=True) + epsilon)
    unit_two = middle * factor_two
    normed_two = (unit_two * gain_two).astype(bf16)
    normed_group = lax.all_gather(normed_two, TENSOR, axis=0, tiled=True)
    gate = contract(normed_group, weight_gate, 1, 1)
    up = contract(normed_group, weight_up, 1, 1)
    sigmoid = jax.nn.sigmoid(gate)
    silu = gate * sigmoid
    activation = (silu * up).astype(bf16)
    grad_act = contract(grad_out_group, weight_down, 1, 1)
    grad_gate = (grad_act * up * sigmoid * (1.0 + gate * (1.0 - sigmoid))).astype(bf16)
    grad_up = (grad_act * silu).astype(bf16)
    grad_normed_part = contract(grad_gate, weight_gate, 1, 0) + contract(grad_up, weight_up, 1, 0)
    grad_normed = lax.psum_scatter(
        grad_normed_part.astype(bf16), TENSOR, scatter_dimension=0, tiled=True
    ).astype(f32)
    branch_part = contract(activation, weight_down, 1, 0).astype(bf16)
    branch = lax.psum_scatter(branch_part, TENSOR, scatter_dimension=0, tiled=True)
    result = (middle + branch.astype(f32)).astype(bf16)
    weighted = grad_normed * gain_two
    grad_middle = (
        cotangent.astype(f32)
        + factor_two * weighted
        - middle * factor_two**3 * jnp.mean(weighted * middle, axis=-1, keepdims=True)
    )
    grad_norm_two = lax.psum_scatter(
        jnp.sum(grad_normed * unit_two, axis=0), ALL, scatter_dimension=0, tiled=True
    )
    unit_grads = jnp.concatenate(
        [
            contract(grad_gate, normed_group, 0, 0).astype(bf16),
            contract(grad_up, normed_group, 0, 0).astype(bf16),
            contract(activation, grad_out_group, 0, 0).astype(bf16),
        ],
        axis=1,
    )
    grad_mlp = lax.psum_scatter(unit_grads, GROUPS, scatter_dimension=0, tiled=True).astype(f32)

    grad_mid_low = grad_middle.astype(bf16)
    grad_attended = contract(out_full, grad_mid_low, 0, 1).astype(bf16)
    grad_attended = grad_attended.reshape(tensor_count, group_count, head_dim, rows)
    grad_attended = grad_attended.transpose(1, 0, 2, 3).reshape(-1, head_dim, rows)
    grad_head = lax.all_to_all(grad_attended, ("p", "c", "z"), 0, 0)
    grad_head = grad_head.reshape(group_count, tensor_count, head_dim, rows)
    grad_head = grad_head.transpose(0, 2, 1, 3).reshape(group_count, head_dim, group_rows)
    grad_qkv_head = attend_backward(qkv, over_shares(grad_head), attended, logsum, block)
    grad_qkv_head = own_share(grad_qkv_head)
    grad_mid_group = lax.all_gather(grad_mid_low, TENSOR, axis=0, tiled=True)

    def to_owners(part, columns):
        own = lax.psum_scatter(part.astype(bf16), GROUPS, scatter_dimension=0, tiled=True)
        own = lax.all_to_all(own.reshape(tensor_count, -1, columns), TENSOR, 0, 0)
        return own.astype(f32)

    out_term = contract(grad_mid_group, attended_group, 0, 1)
    grad_out_w = to_owners(out_term, features_here).transpose(1, 0, 2).reshape(-1, width)

    grad_qkv_rows = lax.all_to_all(grad_qkv_head, "p", 0, 0).astype(f32)
    grad_qkv_rows = jnp.stack(
        [
            rotate_back(grad_qkv_rows[:, 0], cosine, sine),
            rotate_back(grad_qkv_rows[:, 1], cosine, sine),
            grad_qkv_rows[:, 2],
        ]
    )
    grad_qkv_low = grad_qkv_rows.reshape(3 * features_here, group_rows).astype(bf16)
    weighted_part = contract(grad_qkv_low, qkv_weight, 0, 1)
    weighted_one = lax.psum_scatter(
        weighted_part.astype(bf16), TENSOR, scatter_dimension=0, tiled=True
    ).astype(f32)
    factor_one = lax.rsqrt(jnp.mean(x * x, axis=-1, keepdims=True) + epsilon)
    grad_tokens = (
        grad_middle
        + factor_one * weighted_one
        - x * factor_one**3 * jnp.mean(weighted_one * x, axis=-1, keepdims=True)
    )
    qkv_term = contract(unit_group, grad_qkv_low, 0, 1)
    qkv_sum = to_owners(qkv_term, 3 * features_here)
    qkv_sum = qkv_sum.reshape(tensor_count, weight_rows, 3, features_here)
    qkv_sum = qkv_sum.transpose(1, 2, 0, 3).reshape(weight_rows, 3 * width)
    grad_qkv = gain_one * qkv_sum
    grad_norm_one = jnp.sum(attn_qkv.astype(f32) * qkv_sum, axis=1)
    return (result, grad_tokens, grad_qkv, grad_out_w, grad_mlp, grad_norm_one, grad_norm_two)


def solution(mesh):
    seq_count, fsdp_count = mesh.shape["seq"], mesh.shape["fsdp"]
    groups = seq_count // 2
    heads_here = HEADS // (2 * fsdp_count)
    dealt = min(groups, heads_here)
    fine = Mesh(mesh.devices.reshape(groups // dealt, dealt, 2, fsdp_count), ALL)
    by_rows, by_items = P(ALL, None), P(ALL)
    in_specs = (by_rows, by_rows, by_rows, by_rows, by_items, by_items, by_rows)
    out_specs = (by_rows, by_rows, by_rows, by_rows, by_rows, by_items, by_items)
    return jax.shard_map(shards, mesh=fine, in_specs=in_specs, out_specs=out_specs, check_vma=False)
```

time: 2140 us -> 1070 us (0.50)
  waiting for transfers between devices: 1410 us -> 580 us
  local copies, waits for them, and re-layouts: 195 us -> 14 us
  matrix products: 253 us -> 108 us
  blocking collectives: 148 us -> 234 us
  other arithmetic: 99.1 us -> 34.7 us
  Pallas kernels: 0 us -> 49.8 us
    reduce_scatter x7 -> x6, waiting for transfers between devices: 967 us -> 317 us  [the longest x1 121 us: shards(): lax.psum_scatter(unit_grads, GROUPS, scatter_dimension=0, tiled=True)]
    all_gather x6 -> x7, waiting for transfers between devices: 426 us -> 239 us  [the longest x1 101 us: shards(): unit_weight = lax.all_gather(mlp_weight, GROUPS, axis=0, tiled=True)]
    dot_general x36 -> x15, matrix products: 253 us -> 108 us  [contract(): lax.dot_general(left, right, (((left_dim,), (right_dim,)), ((), ())), pre...]
    all_to_all x2 -> x5, blocking collectives: 58.6 us -> 141 us  [the longest x1 42.8 us: shards(): lax.all_to_all(qkv_cut, TENSOR, 0, 0).reshape(-1, 3 * features_here)]
    scatter-add x4 -> x0, local copies, waits for them, and re-layouts: 60 us -> none  [the longest x2 31.2 us: attend_backward(): grad_key_sum.at[:, :key_span]]
    pallas_call x0 -> x2, Pallas kernels: none -> 49.8 us  [the longest x1 31.5 us: attend_backward(): pl.pallas_call(functools.partial(backward_kernel, block=block, scale=head...]
    unnamed x169 -> x43, local copies, waits for them, and re-layouts: 38.7 us -> 4.62 us
    convert_element_type x12 -> x8, other arithmetic: 42.6 us -> 11.1 us  [the longest x1 5.34 us: shards(): lax.psum_scatter(unit_grads, GROUPS, scatter_dimension=0, tiled=True)]
  transfers between devices with their start and end apart: 15 -> 16, of which waited for: 12 -> 11; matrix products, arithmetic and copies ran while one was open for 17% -> 11% of each run, Pallas kernels for 0% -> 5%
where the time goes in v1:
time: 1070 us; the launch traced here: 1060 us
  waiting for transfers between devices  580 us (54%)
  blocking collectives  234 us (22%)
  matrix products  108 us (10%)
  Pallas kernels  49.8 us (5%)
  other arithmetic  34.7 us (3%)
  starting transfers between devices  22.4 us (2%)
  between operations  14.5 us (1%)
  local copies, waits for them, and re-layouts  14 us (1%)
    reduce_scatter x1, waiting for transfers between devices, shards(): lax.psum_scatter(unit_grads, GROUPS, scatter_dimension=0, tiled=True)  121 us
    dot_general x15, matrix products, contract(): lax.dot_general(left, right, (((left_dim,), (right_dim,)), ((), ())), pre...  108 us
    all_gather x1, waiting for transfers between devices, shards(): unit_weight = lax.all_gather(mlp_weight, GROUPS, axis=0, tiled=True)  101 us
    unnamed x2, blocking collectives  93.7 us
    reduce_scatter x1, waiting for transfers between devices, shards(): lax.psum_scatter(branch_part, TENSOR, scatter_dimension=0, tiled=True)  88.6 us
    reduce_scatter x1, waiting for transfers between devices, shards(): lax.psum_scatter(grad_normed_part.astype(bf16), TENSOR, scatter_dimension...  78.4 us
    all_gather x1, waiting for transfers between devices, shards(): normed_group = lax.all_gather(normed_two, TENSOR, axis=0, tiled=True)  49.2 us
    all_to_all x1, blocking collectives, shards(): lax.all_to_all(qkv_cut, TENSOR, 0, 0).reshape(-1, 3 * features_here)  42.8 us
  transfers between devices with their start and end apart: 16, of which 11 were waited for; matrix products, arithmetic and copies ran while one was open for 11% of the time, Pallas kernels for 5%

profile of v1, /device:TPU:0, one launch (start us, length us, event | category | flops | bytes accessed | tf_op | source)
XLA Modules:
  0.0 1057.4 jit_solution(8356697226325134937)
XLA Ops:
  7.2 0.7 all-gather.10.cloned.1.call-update
  7.9 0.7 convert_element_type.130
  8.6 1.3 fusion.17
  10.5 0.9 reshape.268
  11.5 42.8 %all_to_all.40 = bf16[8,64,768]{2,1,0:T(8,128)(2,1)} all-to-all(bf16[8,64,768]{2,1,0:T(8,128)(2,1)S(1)} %reshape.268), channel_id=1, replica_groups=mesh['r'=1,'p'=4,'c'=2,'z'=4] {'c','z'}, dimensions={0} | all-to-all | bytes 1572864 | tf_op jit(solution)/shard_map/all_to_all | solution.py:213
  54.4 0.7 all-gather.12.cloned.1.call-update
  55.7 0.5 multiply_cosine_fusion
  56.2 17.8 %all-gather.10.cloned.1.call-done = bf16[1024,2048]{1,0:T(8,128)(2,1)} async-done(((bf16[128,2048]{1,0:T(8,128)(2,1)}), bf16[1024,2048]{1,0:T(8,128)(2,1)}) %all-gather.10.cloned.1.call-update) | async-done | bytes 4194320 | tf_op jit(solution)/shard_map/all_gather | solution.py:215
  74.0 3.1 fusion
  77.1 41.6 %all-gather.8.cloned.1.call-done = bf16[2048,768]{1,0:T(8,128)(2,1)} async-done(((bf16[512,768]{1,0:T(8,128)(2,1)}), bf16[2048,768]{1,0:T(8,128)(2,1)}) %all-gather.8.cloned.1.call-update) | async-done | bytes 3145744 | tf_op jit(solution)/shard_map/all_gather | solution.py:214
  118.7 6.6 fusion.15
  126.2 25.1 %all_to_all.41.qkv_ref = bf16[4,3,64,1024]{3,2,1,0:T(8,128)(2,1)} all-to-all(bf16[4,3,64,1024]{3,2,1,0:T(8,128)(2,1)S(1)} %pad_maximum_fusion.1), channel_id=1, replica_groups=mesh['r'=1,'p'=4,'c'=2,'z'=4] {'p'}, dimensions={0} | all-to-all | bytes 3145728 | tf_op jit(solution)/shard_map/all_to_all | solution.py:234
  151.3 18.3 %attend_forward.1 = (bf16[4,64,1024]{2,1,0:T(8,128)(2,1)}, f32[4,1,1024]{2,1,0:T(1,128)}) custom-call(bf16[4,3,64,1024]{3,2,1,0:T(8,128)(2,1)} %all_to_all.41.qkv_ref), custom_call_target="tpu_custom_call" | custom-call | flops 10737418240 | bytes 2359296 | tf_op jit(solution)/shard_map/attend_forward/pallas_call | solution.py:133
  169.6 2.0 copy_bitcast_fusion.2
  171.6 4.1 all-to-all-start.2
  176.0 49.8 %all-reduce = bf16[2048]{0:T(1024)(128)(2,1)S(1)} all-reduce(bf16[2048]{0:T(1024)(128)(2,1)S(1)} %dynamic-update-slice), channel_id=1, replica_groups=mesh['r'=1,'p'=4,'c'=2,'z'=4] {'r','p','c','z'}, use_global_device_ids=true, to_apply=%add | all-reduce | flops 2048 | bytes 8192
  225.9 6.6 multiply_reduce_fusion
  232.6 1.0 multiply_convert_fusion.3
  233.6 0.5 all-gather.18.cloned.1.call-update
  234.2 101.3 %all-gather.16.cloned.1.call-done = bf16[1024,6144]{1,0:T(8,128)(2,1)} async-done(((bf16[256,6144]{1,0:T(8,128)(2,1)}), bf16[1024,6144]{1,0:T(8,128)(2,1)}) %all-gather.16.cloned.1.call-update) | async-done | bytes 12582928 | tf_op jit(solution)/shard_map/all_gather | solution.py:218
  335.5 49.2 %all-gather.14.cloned.1.call-done = bf16[1024,2048]{1,0:T(8,128)(2,1)} async-done(((bf16[128,2048]{1,0:T(8,128)(2,1)}), bf16[1024,2048]{1,0:T(8,128)(2,1)}) %all-gather.14.cloned.1.call-update) | async-done | bytes 4194320 | tf_op jit(solution)/shard_map/all_gather | solution.py:263
  384.7 10.1 fusion.11
  394.8 8.3 fusion.7
  403.1 28.9 %all-gather.18.cloned.1.call-done = bf16[1024,2048]{1,0:T(8,128)(2,1)} async-done(((bf16[128,2048]{1,0:T(8,128)(2,1)}), bf16[1024,2048]{1,0:T(8,128)(2,1)}) %all-gather.18.cloned.1.call-update) | async-done | bytes 4194320 | tf_op jit(solution)/shard_map/all_gather | solution.py:222
  432.0 12.1 %multiply_convert_fusion = (bf16[1024,1024]{1,0:T(8,128)(2,1)S(1)}, bf16[1024,1024]{1,0:T(8,128)(2,1)S(1)}, bf16[1024,1024]{1,0:T(8,128)(2,1)}) fusion(f32[1024,1024]{1,0:T(8,128)} %fusion.11, f32[1024,1024]{1,0:T(8,128)} %fusion.7, bf16[1024,2048]{1,0:T(8,128)(2,1)} %all-gather.18.cloned.1.call-done, bf16[1024,6144]{1,0:T(8,128)(2,1)} %all-gather.16.cloned.1.call-done), kind=kOutput, calls=%fused_computation.6 | convolution fusion | flops 4310695936 | bytes 23068672 | tf_op jit(solution)/shard_map/dot_general | solution.py:22
  444.2 7.8 fusion.9
  452.0 8.2 add_convert_fusion
  460.3 9.5 all-gather.20.cloned.1.call-start
  469.8 78.4 %reduce-scatter.9.cloned.1.call-done = bf16[128,2048]{1,0:T(8,128)(2,1)} async-done(((bf16[1024,2048]{1,0:T(8,128)(2,1)}), bf16[128,2048]{1,0:T(8,128)(2,1)}) %reduce-scatter.9.cloned.1.call-update) | async-done | bytes 524304 | tf_op jit(solution)/shard_map/reduce_scatter | solution.py:273
  548.1 1.4 fusion.24
  549.5 2.2 fusion.35
  551.8 4.8 fusion.13
  556.9 31.5 %all_to_all.42 = bf16[32,64,128]{2,1,0:T(8,128)(2,1)S(1)} all-to-all(bf16[32,64,128]{2,1,0:T(8,128)(2,1)S(1)} %bitcast.102), channel_id=1, replica_groups=mesh['r'=1,'p'=4,'c'=2,'z'=4] {'p','c','z'}, dimensions={0} | all-to-all | bytes 1048576 | tf_op jit(solution)/shard_map/all_to_all | solution.py:302
  588.4 0.9 copy.63
  589.4 31.5 %attend_backward.1 = bf16[4,3,64,1024]{3,2,1,0:T(8,128)(2,1)} custom-call(bf16[4,3,64,1024]{3,2,1,0:T(8,128)(2,1)} %all_to_all.41.qkv_ref, bf16[4,64,1024]{2,1,0:T(8,128)(2,1)} %bitcast.111, bf16[4,64,1024]{2,1,0:T(8,128)(2,1)} %get-tuple-element.9.out_ref, f32[4,1,1024]{2,1,0:T(1,128)} %get-tuple-element.10.logsum_ref), custom_call_target="tpu_custom_call" | custom-call | flops 21474836480 | bytes 4718592 | tf_op jit(solution)/shard_map/attend_backward/pallas_call | solution.py:157
  620.9 24.5 %all_to_all.43 = bf16[4,3,64,1024]{3,2,1,0:T(8,128)(2,1)S(1)} all-to-all(bf16[4,3,64,1024]{3,2,1,0:T(8,128)(2,1)} %attend_backward.1), channel_id=1, replica_groups=mesh['r'=1,'p'=4,'c'=2,'z'=4] {'p'}, dimensions={0} | all-to-all | bytes 3145728 | tf_op jit(solution)/shard_map/all_to_all | solution.py:317
  645.3 0.5 copy_convert_fusion
  646.8 1.5 copy-done.5
  648.3 5.5 convolution_convert_fusion.5
  654.0 16.9 %all_to_all.44 = bf16[4,64,1024]{2,1,0:T(8,128)(2,1)} all-to-all(bf16[4,64,1024]{2,1,0:T(8,128)(2,1)S(1)} %copy-done.8), channel_id=1, replica_groups=mesh['r'=1,'p'=4,'c'=2,'z'=4] {'p'}, dimensions={0} | all-to-all | bytes 1048576 | tf_op jit(solution)/shard_map/all_to_all | solution.py:258
  670.9 4.6 convolution_convert_fusion.6
  675.6 7.0 convolution_convert_fusion
  682.6 1.5 copy-done.18
  684.2 8.2 convolution_convert_fusion.4
  692.4 7.6 convolution_convert_fusion.1
  700.1 5.1 convolution_convert_fusion.2
  705.2 4.9 convolution_convert_fusion.3
  710.1 11.3 %pad_maximum_fusion = bf16[1024,6144]{1,0:T(8,128)(2,1)} fusion(bf16[1024,2048]{1,0:T(8,128)(2,1)S(1)} %convolution_convert_fusion.1, bf16[1024,2048]{1,0:T(8,128)(2,1)S(1)} %convolution_convert_fusion.2, bf16[1024,2048]{1,0:T(8,128)(2,1)S(1)} %convolution_convert_fusion.3), kind=kLoop, calls=%fused_computation | loop fusion | flops 37748736 | bytes 25165824 | tf_op jit(solution)/shard_map/concatenate | solution.py:288
  721.5 4.0 all-to-all-start.5
  725.5 6.0 reduce-scatter.15.cloned.1.call-done
  731.5 21.3 %all-to-all-done.5 = bf16[8,64,768]{2,1,0:T(8,128)(2,1)S(1)} async-done(((bf16[8,64,768]{2,1,0:T(8,128)(2,1)}), bf16[8,64,768]{2,1,0:T(8,128)(2,1)S(1)}, u32[]{:S(2)}, u32[]{:S(2)}) %all-to-all-start.5) | async-done | bytes 786464 | tf_op jit(solution)/shard_map/all_to_all | solution.py:311
  752.8 4.3 all-to-all-start.7
  757.1 43.9 %all-reduce.1 = f32[2048]{0:T(1024)S(1)} all-reduce(f32[2048]{0:T(1024)S(1)} %get-tuple-element.11), channel_id=8, replica_groups=mesh['r'=1,'p'=4,'c'=2,'z'=4] {'r','p','c','z'}, use_global_device_ids=true, to_apply=%region_13.0.clone | all-reduce | flops 2048 | bytes 16384
  801.0 0.6 dynamic-slice
  801.5 2.5 reshape.292
  804.1 0.9 copy.50
  805.6 2.0 fusion.18
  807.6 0.8 copy.54
  808.4 23.0 %reduce-scatter.11.cloned.1.call-done = bf16[128,2048]{1,0:T(8,128)(2,1)} async-done(((bf16[1024,2048]{1,0:T(8,128)(2,1)}), bf16[128,2048]{1,0:T(8,128)(2,1)}) %reduce-scatter.11.cloned.1.call-update) | async-done | bytes 524304 | tf_op jit(solution)/shard_map/reduce_scatter | solution.py:327
  831.5 1.3 fusion.27
  832.8 88.6 %reduce-scatter.7.cloned.1.call-done = bf16[128,2048]{1,0:T(8,128)(2,1)} async-done(((bf16[1024,2048]{1,0:T(8,128)(2,1)}), bf16[128,2048]{1,0:T(8,128)(2,1)}) %reduce-scatter.7.cloned.1.call-update) | async-done | bytes 524304 | tf_op jit(solution)/shard_map/reduce_scatter | solution.py:277
  921.4 2.9 fusion.26
  924.3 121.1 %reduce-scatter.17.cloned.1.call-done = bf16[256,6144]{1,0:T(8,128)(2,1)} async-done(((bf16[1024,6144]{1,0:T(8,128)(2,1)}), bf16[256,6144]{1,0:T(8,128)(2,1)}) %reduce-scatter.17.cloned.1.call-update) | async-done | bytes 3145744 | tf_op jit(solution)/shard_map/reduce_scatter | solution.py:296
  1045.3 5.3 convert_element_type.159
  (90 shorter events, 4.7 us)
Async XLA Ops:
  7.2 66.8 %all-gather.10.cloned.1.call-start = ((), (), s32[]{:S(2)}) async-start(), calls=%async_computation.15 | async-start | bytes 4718592 | tf_op jit(solution)/shard_map/all_gather | solution.py:215
  7.9 110.8 %all-gather.8.cloned.1.call-start = ((), (), s32[]{:S(2)}) async-start(), calls=%async_computation.14 | async-start | bytes 3932160 | tf_op jit(solution)/shard_map/all_gather | solution.py:214
  8.6 1.5 copy-start.9
  54.3 171.6 %all-gather.12.cloned.1.call-start = ((), (), s32[]{:S(2)}) async-start(), calls=%async_computation.16 | async-start | bytes 8650752 | tf_op jit(solution)/shard_map/all_gather | solution.py:216
  55.1 280.4 %all-gather.16.cloned.1.call-start = ((), (), s32[]{:S(2)}) async-start(), calls=%async_computation.18 | async-start | bytes 15728640 | tf_op jit(solution)/shard_map/all_gather | solution.py:218
  151.3 24.5 %copy-start.13 = (bf16[64]{0:T(256)(128)(2,1)S(1)}, bf16[64]{0:T(256)(128)(2,1)}, u32[]{:S(2)}) copy-start(bf16[64]{0:T(256)(128)(2,1)} %param.12) | copy-start | bytes 388
  151.3 74.6 %copy-start = (bf16[128,2048]{1,0:T(8,128)(2,1)S(1)}, bf16[128,2048]{1,0:T(8,128)(2,1)}, u32[]{:S(2)}) copy-start(bf16[128,2048]{1,0:T(8,128)(2,1)} %param.7) | copy-start | bytes 1572868
  171.6 54.2 %all-to-all-start.2 = ((bf16[32,64,128]{2,1,0:T(8,128)(2,1)}), bf16[32,64,128]{2,1,0:T(8,128)(2,1)S(1)}, u32[]{:S(2)}, u32[]{:S(2)}) async-start(bf16[32,64,128]{2,1,0:T(8,128)(2,1)} %bitcast.12), calls=%async_computation.2 | async-start | bytes 1048576 | tf_op jit(solution)/shard_map/all_to_all | solution.py:254
  175.7 209.0 %all-gather.14.cloned.1.call-start = ((), (), s32[]{:S(2)}) async-start(), calls=%async_computation.17 | async-start | bytes 4718592 | tf_op jit(solution)/shard_map/all_gather | solution.py:263
  233.6 198.5 %all-gather.18.cloned.1.call-start = ((), (), s32[]{:S(2)}) async-start(), calls=%async_computation.20 | async-start | bytes 4718592 | tf_op jit(solution)/shard_map/all_gather | solution.py:222
  234.2 314.0 %reduce-scatter.9.cloned.1.call-start = ((), (), s32[]{:S(2)}) async-start(), calls=%async_computation.21 | async-start | bytes 4718592 | tf_op jit(solution)/shard_map/reduce_scatter | solution.py:273
  384.7 10.1 copy-start.11
  444.2 7.8 copy-start.14
  444.2 7.8 copy-start.16
  460.2 89.3 %copy-start.2 = (bf16[128,2048]{1,0:T(8,128)(2,1)S(1)}, bf16[128,2048]{1,0:T(8,128)(2,1)}, u32[]{:S(2)}) copy-start(bf16[128,2048]{1,0:T(8,128)(2,1)} %param.13) | copy-start | bytes 1572868
  460.3 210.6 %all-gather.20.cloned.1.call-start = ((), (), s32[]{:S(2)}) async-start(), calls=%async_computation.24 | async-start | bytes 4718592 | tf_op jit(solution)/shard_map/all_gather | solution.py:307
  551.7 169.7 %reduce-scatter.13.cloned.1.call-start = ((), (), s32[]{:S(2)}) async-start(), calls=%async_computation.23 | async-start | bytes 3932160 | tf_op jit(solution)/shard_map/reduce_scatter | solution.py:310
  646.1 2.2 copy-start.5
  648.3 5.6 copy-start.8
  653.9 77.6 %reduce-scatter.15.cloned.1.call-start = ((), (), s32[]{:S(2)}) async-start(), calls=%async_computation.25 | async-start | bytes 1310720 | tf_op jit(solution)/shard_map/reduce_scatter | solution.py:310
  675.5 156.0 %reduce-scatter.11.cloned.1.call-start = ((), (), s32[]{:S(2)}) async-start(), calls=%async_computation.22 | async-start | bytes 4718592 | tf_op jit(solution)/shard_map/reduce_scatter | solution.py:327
  682.5 1.6 copy-start.18
  682.6 238.8 %reduce-scatter.7.cloned.1.call-start = ((), (), s32[]{:S(2)}) async-start(), calls=%async_computation.19 | async-start | bytes 4718592 | tf_op jit(solution)/shard_map/reduce_scatter | solution.py:277
  692.4 7.7 copy-start.17
  692.4 353.0 %reduce-scatter.17.cloned.1.call-start = ((), (), s32[]{:S(2)}) async-start(), calls=%async_computation.26 | async-start | bytes 15728640 | tf_op jit(solution)/shard_map/reduce_scatter | solution.py:296
  692.4 7.6 copy-start.12
  700.1 5.1 copy-start.15
  721.5 31.3 %all-to-all-start.5 = ((bf16[8,64,768]{2,1,0:T(8,128)(2,1)}), bf16[8,64,768]{2,1,0:T(8,128)(2,1)S(1)}, u32[]{:S(2)}, u32[]{:S(2)}) async-start(bf16[8,64,768]{2,1,0:T(8,128)(2,1)} %bitcast.108), calls=%async_computation.9 | async-start | bytes 1572864 | tf_op jit(solution)/shard_map/all_to_all | solution.py:311
  752.8 48.2 %copy-start.7 = (bf16[8,64,768]{2,1,0:T(8,128)(2,1)}, bf16[8,64,768]{2,1,0:T(8,128)(2,1)S(1)}, u32[]{:S(2)}) copy-start(bf16[8,64,768]{2,1,0:T(8,128)(2,1)S(1)} %all-to-all-done.5) | copy-start | bytes 2359300
  752.8 54.8 %all-to-all-start.7 = ((bf16[8,64,256]{2,1,0:T(8,128)(2,1)}), bf16[8,64,256]{2,1,0:T(8,128)(2,1)S(1)}, u32[]{:S(2)}, u32[]{:S(2)}) async-start(bf16[8,64,256]{2,1,0:T(8,128)(2,1)} %bitcast.112), calls=%async_computation.12 | async-start | bytes 524288 | tf_op jit(solution)/shard_map/all_to_all | solution.py:311
  801.5 4.0 copy-start.10
  804.1 1.5 copy-start.6
  805.0 26.5 %copy-start.1 = (bf16[128,2048]{1,0:T(8,128)(2,1)S(1)}, bf16[128,2048]{1,0:T(8,128)(2,1)}, u32[]{:S(2)}) copy-start(bf16[128,2048]{1,0:T(8,128)(2,1)} %param.7) | copy-start | bytes 1572868
  805.5 115.9 %copy-start.3 = (bf16[128,2048]{1,0:T(8,128)(2,1)S(1)}, bf16[128,2048]{1,0:T(8,128)(2,1)}, u32[]{:S(2)}) copy-start(bf16[128,2048]{1,0:T(8,128)(2,1)} %param.13) | copy-start | bytes 1572868
  805.5 115.9 %copy-start.4 = (bf16[128,2048]{1,0:T(8,128)(2,1)S(1)}, bf16[128,2048]{1,0:T(8,128)(2,1)}, u32[]{:S(2)}) copy-start(bf16[128,2048]{1,0:T(8,128)(2,1)} %reduce-scatter.9.cloned.1.call-done) | copy-start | bytes 1572868
Sparse Core Ops, SparseCore 0:
  9.6 64.3 all-gather.9
  75.8 42.8 all-gather.7
  121.7 90.7 all-gather.11
  214.1 121.3 all-gather.15
  337.5 47.1 all-gather.13
  386.1 45.8 all-gather.17
  460.4 87.6 reduce-scatter.8
  551.9 57.9 all-gather.19
  654.0 46.3 reduce-scatter.12
  703.7 27.7 reduce-scatter.14
  734.5 96.9 reduce-scatter.10
  833.7 87.6 reduce-scatter.6
  924.8 120.4 reduce-scatter.16

commit v2 on v1

v2 whole, which is shorter than its diff:
```python
import functools

import jax
import jax.numpy as jnp
from jax import lax
from jax.experimental import pallas as pl
from jax.experimental.pallas import tpu as pltpu
from jax.sharding import Mesh
from jax.sharding import PartitionSpec as P

HEADS = 32
epsilon = 1e-05
rope_base = 130000.0
f32 = jnp.float32
bf16 = jnp.bfloat16
SHORT = pl.CostEstimate(flops=1000, bytes_accessed=1000, transcendentals=0)
ALL = ("r", "p", "c", "z")
GROUPS = ("r", "p")
TENSOR = ("c", "z")


def contract(left, right, left_dim, right_dim):
    return lax.dot_general(
        left, right, (((left_dim,), (right_dim,)), ((), ())), preferred_element_type=f32
    )


def causal(scores):
    keys = lax.broadcasted_iota(jnp.int32, scores.shape, 0)
    queries = lax.broadcasted_iota(jnp.int32, scores.shape, 1)
    return jnp.where(keys <= queries, scores, -1e30)


def forward_kernel(qkv_ref, out_ref, logsum_ref, keys, values_t, queries_t, *, block):
    pieces, _, head_dim, rows = qkv_ref.shape
    per_block = block // rows
    count = pieces // per_block
    for piece in range(pieces):
        number, part = divmod(piece, per_block)
        span = slice(part * rows, (part + 1) * rows)
        queries_t[number, :, span] = qkv_ref[piece, 0]
        keys[number, span, :] = qkv_ref[piece, 1].T
        values_t[number, :, span] = qkv_ref[piece, 2]

    def step(i, j, carry, diagonal):
        largest, total, result = carry
        scores = contract(keys[j], queries_t[i], 1, 0)
        if diagonal:
            scores = causal(scores)
        new_largest = jnp.maximum(largest, jnp.max(scores, axis=0, keepdims=True))
        shrink = jnp.exp(largest - new_largest)
        weights = jnp.exp(scores - new_largest)
        total = total * shrink + jnp.sum(weights, axis=0, keepdims=True)
        result = result * shrink + contract(values_t[j], weights.astype(bf16), 1, 0)
        return new_largest, total, result

    def query_block(i, _):
        carry = (
            jnp.full((1, block), -1e30, f32),
            jnp.zeros((1, block), f32),
            jnp.zeros((head_dim, block), f32),
        )
        carry = lax.fori_loop(0, i, lambda j, c: step(i, j, c, False), carry)
        largest, total, result = step(i, i, carry, True)
        result = (result / total).astype(bf16)
        for part in range(per_block):
            out_ref[i * per_block + part] = result[:, part * rows : (part + 1) * rows]
        logsum_ref[i] = largest + jnp.log(total)
        return 0

    lax.fori_loop(0, count, query_block, 0)


def backward_kernel(
    qkv_ref, grad_ref, out_ref, logsum_ref, result_ref,
    keys, queries, values, grads, keys_t, queries_t, grads_t, deltas, grad_queries,
    *, block, scale,
):
    pieces, _, head_dim, rows = qkv_ref.shape
    per_block = block // rows
    count = pieces // per_block
    for piece in range(pieces):
        number, part = divmod(piece, per_block)
        span = slice(part * rows, (part + 1) * rows)
        queries_t[number, :, span] = qkv_ref[piece, 0]
        keys_t[number, :, span] = qkv_ref[piece, 1]
        queries[number, span, :] = qkv_ref[piece, 0].T
        keys[number, span, :] = qkv_ref[piece, 1].T
        values[number, span, :] = qkv_ref[piece, 2].T
        grad = grad_ref[piece]
        grads_t[number, :, span] = grad
        grads[number, span, :] = grad.T
        deltas[number, :, span] = jnp.sum(
            grad.astype(f32) * out_ref[piece].astype(f32), axis=0, keepdims=True
        )
    for number in range(count):
        grad_queries[number] = jnp.zeros((head_dim, block), f32)

    def step(i, j, carry, diagonal):
        grad_key, grad_value = carry
        scores = contract(keys[j], queries_t[i], 1, 0)
        if diagonal:
            scores = causal(scores)
        probs = jnp.exp(scores - logsum_ref[i])
        grad_value = grad_value + contract(probs.astype(bf16), grads[i], 1, 0)
        grad_probs = contract(values[j], grads_t[i], 1, 0)
        grad_scores = (probs * (grad_probs - deltas[i])).astype(bf16)
        grad_key = grad_key + contract(grad_scores, queries[i], 1, 0)
        grad_queries[i] = grad_queries[i] + contract(keys_t[j], grad_scores, 1, 0)
        return grad_key, grad_value

    for j in range(count):
        zero = jnp.zeros((block, head_dim), f32)
        carry = step(j, j, (zero, zero), True)
        grad_key, grad_value = lax.fori_loop(
            j + 1, count, lambda i, c, j=j: step(i, j, c, False), carry
        )
        for part in range(per_block):
            span = slice(part * rows, (part + 1) * rows)
            result_ref[j * per_block + part, 1] = grad_key[span].T.astype(bf16)
            result_ref[j * per_block + part, 2] = grad_value[span].T.astype(bf16)
    for piece in range(pieces):
        number, part = divmod(piece, per_block)
        span = slice(part * rows, (part + 1) * rows)
        result_ref[piece, 0] = (grad_queries[number, :, span] * scale).astype(bf16)


def attend_forward(qkv, block):
    pieces, _, head_dim, rows = qkv.shape
    count = pieces * rows // block
    pairs = count * (count + 1) // 2 * block * block
    in_vmem = pl.BlockSpec(memory_space=pltpu.VMEM)
    by_rows = pltpu.VMEM((count, block, head_dim), bf16)
    by_features = pltpu.VMEM((count, head_dim, block), bf16)
    return pl.pallas_call(
        functools.partial(forward_kernel, block=block),
        out_shape=(
            jax.ShapeDtypeStruct((pieces, head_dim, rows), bf16),
            jax.ShapeDtypeStruct((count, 1, block), f32),
        ),
        in_specs=[in_vmem],
        out_specs=(in_vmem, in_vmem),
        scratch_shapes=[by_rows, by_features, by_features],
        compiler_params=pltpu.CompilerParams(vmem_limit_bytes=56 * 2**20),
        cost_estimate=SHORT,
        name="attend_forward",
    )(qkv)


def attend_backward(qkv, grad, out, logsum, block):
    pieces, _, head_dim, rows = qkv.shape
    count = pieces * rows // block
    pairs = count * (count + 1) // 2 * block * block
    in_vmem = pl.BlockSpec(memory_space=pltpu.VMEM)
    by_rows = pltpu.VMEM((count, block, head_dim), bf16)
    by_features = pltpu.VMEM((count, head_dim, block), bf16)
    return pl.pallas_call(
        functools.partial(backward_kernel, block=block, scale=head_dim**-0.5),
        out_shape=jax.ShapeDtypeStruct(qkv.shape, bf16),
        in_specs=[in_vmem] * 4,
        out_specs=in_vmem,
        scratch_shapes=[by_rows] * 4
        + [by_features] * 3
        + [pltpu.VMEM((count, 1, block), f32), pltpu.VMEM((count, head_dim, block), f32)],
        compiler_params=pltpu.CompilerParams(vmem_limit_bytes=60 * 2**20),
        cost_estimate=SHORT,
        name="attend_backward",
    )(qkv, grad, out, logsum)


def start_pieces(refs, table, starts_ref, whole, semaphores):
    copies = []
    for number, (which, first, rows) in enumerate(table):
        start = pl.multiple_of(starts_ref[number], rows)
        copy = pltpu.make_async_copy(
            refs[which].at[pl.ds(first, rows), pl.ds(0, whole.shape[1])],
            whole.at[pl.ds(start, rows), :],
            semaphores.at[number],
        )
        copy.start()
        copies.append(copy)
    return copies


def qkv_kernel(count, table, starts_ref, x_ref, cosine_ref, sine_ref, *refs):
    pieces, (unit_ref, out_ref), (weight, weight_t, semaphores) = refs[:count], refs[-5:-3], refs[-3:]
    heads, blocks, _, head_dim, rows = out_ref.shape
    half = head_dim // 2
    copies = start_pieces(pieces, table, starts_ref, weight, semaphores)
    for number in range(blocks):
        span = slice(number * rows, (number + 1) * rows)
        x = x_ref[span].astype(f32)
        factor = lax.rsqrt(jnp.mean(x * x, axis=-1, keepdims=True) + epsilon)
        unit_ref[span] = (x * factor).astype(bf16)
    for copy in copies:
        copy.wait()
    weight_t[...] = weight[...].T
    step = 2
    for first in range(0, blocks, step):
        span = slice(first * rows, (first + step) * rows)
        made = contract(weight_t[...], unit_ref[span], 1, 1)
        cosine, sine = cosine_ref[:, span], sine_ref[:, span]
        for kind in range(3):
            for head in range(heads):
                at = (kind * heads + head) * head_dim
                upper, lower = made[at : at + half], made[at + half : at + head_dim]
                if kind < 2:
                    upper, lower = upper * cosine - lower * sine, lower * cosine + upper * sine
                upper, lower = upper.astype(bf16), lower.astype(bf16)
                if kind == 0:
                    upper, lower = upper * bf16(head_dim**-0.5), lower * bf16(head_dim**-0.5)
                for part in range(step):
                    lanes = slice(part * rows, (part + 1) * rows)
                    out_ref[head, first + part, kind, :half] = upper[:, lanes]
                    out_ref[head, first + part, kind, half:] = lower[:, lanes]


IN_VMEM = pl.BlockSpec(memory_space=pltpu.VMEM)
IN_SMEM = pl.BlockSpec(memory_space=pltpu.SMEM)
ANYWHERE = pl.BlockSpec(memory_space=pl.ANY)


def project(x_group, cosine, sine, pieces, table, starts, heads, head_dim, rows):
    tokens, width = x_group.shape
    columns = pieces[0].shape[1]
    return pl.pallas_call(
        functools.partial(qkv_kernel, len(pieces), table),
        out_shape=(
            jax.ShapeDtypeStruct((tokens, width), bf16),
            jax.ShapeDtypeStruct((heads, tokens // rows, 3, head_dim, rows), bf16),
        ),
        in_specs=[IN_SMEM] + [IN_VMEM] * 3 + [ANYWHERE] * len(pieces),
        out_specs=(IN_VMEM, IN_VMEM),
        scratch_shapes=[
            pltpu.VMEM((width, columns), bf16),
            pltpu.VMEM((columns, width), bf16),
            pltpu.SemaphoreType.DMA((len(table),)),
        ],
        compiler_params=pltpu.CompilerParams(vmem_limit_bytes=48 * 2**20),
        cost_estimate=SHORT,
        name="project",
    )(starts, x_group, cosine, sine, *pieces)


def mid_kernel(count, table, groups, starts_ref, x_ref, attended_ref, *refs):
    pieces, (mid_ref, normed_ref, gain_ref) = refs[:count], refs[-6:-3]
    weight, attended, semaphores = refs[-3:]
    copies = start_pieces(pieces, table, starts_ref, weight, semaphores)
    _, head_dim, rows = attended_ref.shape
    width = x_ref.shape[1]
    tensor = HEADS // groups
    pair = 128 // head_dim
    for first in range(0, HEADS, pair):
        features = jnp.concatenate(
            [
                attended_ref[head % groups * tensor + head // groups]
                for head in range(first, first + pair)
            ]
        )
        attended[:, first * head_dim : (first + pair) * head_dim] = features.T
    for copy in copies:
        copy.wait()
    cut = min(512, width)
    for start in range(0, width, cut):
        span = slice(start, start + cut)
        gain_ref[:, span] = weight[span, width:].astype(f32).T[:1]
        mid_ref[:, span] = x_ref[:, span].astype(f32) + contract(
            attended[...], weight[span, :width], 1, 1
        )
    mid = mid_ref[...]
    factor = lax.rsqrt(jnp.mean(mid * mid, axis=-1, keepdims=True) + epsilon)
    normed_ref[...] = (mid * factor * gain_ref[...]).astype(bf16)


def finish_attention(x, attended, pieces, table, starts, groups):
    rows, width = x.shape
    return pl.pallas_call(
        functools.partial(mid_kernel, len(pieces), table, groups),
        out_shape=(
            jax.ShapeDtypeStruct((rows, width), f32),
            jax.ShapeDtypeStruct((rows, width), bf16),
            jax.ShapeDtypeStruct((1, width), f32),
        ),
        in_specs=[IN_SMEM] + [IN_VMEM] * 2 + [ANYWHERE] * len(pieces),
        out_specs=(IN_VMEM,) * 3,
        scratch_shapes=[
            pltpu.VMEM((width, pieces[0].shape[1]), bf16),
            pltpu.VMEM((rows, width), bf16),
            pltpu.SemaphoreType.DMA((len(table),)),
        ],
        compiler_params=pltpu.CompilerParams(vmem_limit_bytes=48 * 2**20),
        cost_estimate=SHORT,
        name="finish_attention",
    )(starts, x, attended, *pieces)


def grad_mid_kernel(count, table, groups, starts_ref, mid_ref, grad_ref, cotangent_ref, gain_ref, *refs):
    pieces, (grad_mid_ref, low_ref, gain_part_ref, out_ref) = refs[:count], refs[-6:-2]
    weight, semaphores = refs[-2:]
    copies = start_pieces(pieces, table, starts_ref, weight, semaphores)
    _, head_dim, rows = out_ref.shape
    width = mid_ref.shape[1]
    tensor = HEADS // groups
    pair = 128 // head_dim
    mid, grad = mid_ref[...], grad_ref[...]
    factor = lax.rsqrt(jnp.mean(mid * mid, axis=-1, keepdims=True) + epsilon)
    weighted = grad * gain_ref[...]
    inner = jnp.mean(weighted * mid, axis=-1, keepdims=True)
    grad_mid = (
        cotangent_ref[...].astype(f32) + factor * weighted - mid * (factor * factor * factor * inner)
    )
    grad_mid_ref[...] = grad_mid
    low_ref[...] = grad_mid.astype(bf16)
    gain_part_ref[...] = jnp.sum(grad * (mid * factor), axis=0, keepdims=True)
    for copy in copies:
        copy.wait()
    cut = min(512, width)
    for start in range(0, width, cut):
        made = contract(low_ref[...], weight[:, start : start + cut], 1, 0).astype(bf16)
        for at in range(0, cut, pair * head_dim):
            features = made[:, at : at + pair * head_dim].T
            for part in range(pair):
                head = (start + at) // head_dim + part
                out_ref[head % groups * tensor + head // groups] = features[
                    part * head_dim : (part + 1) * head_dim
                ]


def back_to_attention(mid, grad, cotangent, gain, pieces, table, starts, groups, head_dim):
    rows, width = mid.shape
    return pl.pallas_call(
        functools.partial(grad_mid_kernel, len(pieces), table, groups),
        out_shape=(
            jax.ShapeDtypeStruct((rows, width), f32),
            jax.ShapeDtypeStruct((rows, width), bf16),
            jax.ShapeDtypeStruct((1, width), f32),
            jax.ShapeDtypeStruct((HEADS, head_dim, rows), bf16),
        ),
        in_specs=[IN_SMEM] + [IN_VMEM] * 4 + [ANYWHERE] * len(pieces),
        out_specs=(IN_VMEM,) * 4,
        scratch_shapes=[
            pltpu.VMEM((width, width), bf16),
            pltpu.SemaphoreType.DMA((len(table),)),
        ],
        compiler_params=pltpu.CompilerParams(vmem_limit_bytes=48 * 2**20),
        cost_estimate=SHORT,
        name="back_to_attention",
    )(starts, mid, grad, cotangent, gain, *pieces)


def grads_kernel(count, table, starts_ref, spots_ref, grad_ref, cosine_ref, sine_ref, *refs):
    pieces, (low_ref, keep_ref, send_ref) = refs[:count], refs[-6:-3]
    weight, by_tokens, semaphores = refs[-3:]
    copies = start_pieces(pieces, table, starts_ref, weight, semaphores)
    heads, blocks, _, head_dim, rows = grad_ref.shape
    half = head_dim // 2
    for block in range(blocks):
        span = slice(block * rows, (block + 1) * rows)
        cosine, sine = cosine_ref[:, span], sine_ref[:, span]
        for kind in range(3):
            for head in range(heads):
                at = (kind * heads + head) * head_dim
                grad = grad_ref[head, block, kind]
                if kind < 2:
                    grad = grad.astype(f32)
                    upper, lower = grad[:half], grad[half:]
                    grad = jnp.concatenate(
                        [upper * cosine + lower * sine, lower * cosine - upper * sine]
                    ).astype(bf16)
                low_ref[at : at + head_dim, span] = grad
        by_tokens[block] = low_ref[:, span].T
    for copy in copies:
        copy.wait()
    width = weight.shape[0]
    cut = min(1024, width)
    for step in range(keep_ref.shape[0]):
        tokens = jnp.concatenate(
            [by_tokens[spots_ref[2 * step]], by_tokens[spots_ref[2 * step + 1]]]
        )
        for start in range(0, width, cut):
            part = contract(tokens, weight[start : start + cut], 1, 1)
            keep_ref[step, :, start : start + cut] = part[:rows]
            send_ref[step, :, start : start + cut] = part[rows:].astype(bf16)


def back_to_norm(grad, cosine, sine, pieces, table, starts, spots):
    heads, blocks, _, head_dim, rows = grad.shape
    columns = pieces[0].shape[1]
    width = HEADS * head_dim
    steps = spots.shape[0] // 2
    return pl.pallas_call(
        functools.partial(grads_kernel, len(pieces), table),
        out_shape=(
            jax.ShapeDtypeStruct((columns, blocks * rows), bf16),
            jax.ShapeDtypeStruct((steps, rows, width), f32),
            jax.ShapeDtypeStruct((steps, rows, width), bf16),
        ),
        in_specs=[IN_SMEM] * 2 + [IN_VMEM] * 3 + [ANYWHERE] * len(pieces),
        out_specs=(IN_VMEM,) * 3,
        scratch_shapes=[
            pltpu.VMEM((width, columns), bf16),
            pltpu.VMEM((blocks, rows, columns), bf16),
            pltpu.SemaphoreType.DMA((len(table),)),
        ],
        compiler_params=pltpu.CompilerParams(vmem_limit_bytes=48 * 2**20),
        cost_estimate=SHORT,
        name="back_to_norm",
    )(starts, spots, grad, cosine, sine, *pieces)


def units_kernel(counts, tables, own_ref, other_ref, grad_own_ref, grad_other_ref, *refs):
    starts_refs, refs = refs[:3], refs[3:]
    pieces = (refs[: counts[0]], refs[counts[0] : sum(counts[:2])], refs[sum(counts[:2]) : sum(counts)])
    outs, weights, semaphores = refs[-15:-6], refs[-6:-3], refs[-3:]
    act_ref, grad_gate_ref, grad_up_ref, normed_ref, grads_ref = outs[:5]
    keep_ref, send_ref, branch_keep_ref, branch_send_ref = outs[5:]
    rows, width = own_ref.shape
    copies = [
        start_pieces(*each) for each in zip(pieces, tables, starts_refs, weights, semaphores)
    ]
    gate_w, up_w, down_w = weights

    def arrived(which):
        for copy in copies[which]:
            copy.wait()

    normed_ref[0, :rows] = own_ref[...]
    normed_ref[0, rows:] = other_ref[...]
    grads_ref[0, :rows] = grad_own_ref[...]
    grads_ref[0, rows:] = grad_other_ref[...]
    arrived(0)
    gate = contract(normed_ref[0], gate_w[...], 1, 1)
    sigmoid = 1.0 / (1.0 + jnp.exp(-gate))
    silu = gate * sigmoid
    arrived(1)
    up = contract(normed_ref[0], up_w[...], 1, 1)
    act_ref[0] = (silu * up).astype(bf16)
    arrived(2)
    grad_act = contract(grads_ref[0], down_w[...], 1, 1)
    grad_gate_ref[0] = (grad_act * up * sigmoid * (1.0 + gate * (1.0 - sigmoid))).astype(bf16)
    grad_up_ref[0] = (grad_act * silu).astype(bf16)
    cut = min(512, width)
    for start in range(0, width, cut):
        span = slice(start, start + cut)
        part = contract(grad_gate_ref[0], gate_w[:, span], 1, 0)
        part = part + contract(grad_up_ref[0], up_w[:, span], 1, 0)
        keep_ref[:, span] = part[:rows]
        send_ref[:, span] = part[rows:].astype(bf16)
    for start in range(0, width, cut):
        span = slice(start, start + cut)
        part = contract(act_ref[0], down_w[:, span], 1, 0)
        branch_keep_ref[:, span] = part[:rows]
        branch_send_ref[:, span] = part[rows:].astype(bf16)


def units_chunk(step, count, own, other, grad_own, grad_other, weights, held):
    rows, width = own.shape
    arrays = [array for pieces, _, _ in weights for array in pieces]
    counts = tuple(len(pieces) for pieces, _, _ in weights)
    tables = tuple(table for _, table, _ in weights)
    units = sum(taken for _, _, taken in tables[0])
    whole = pl.BlockSpec((rows, width), lambda i: (0, 0))
    kept_units = pl.BlockSpec((1, 2 * rows, units), lambda i: (step, 0, 0))
    kept_rows = pl.BlockSpec((1, 2 * rows, width), lambda i: (step, 0, 0))
    by_units = jax.ShapeDtypeStruct((count, 2 * rows, units), bf16)
    by_rows = jax.ShapeDtypeStruct((count, 2 * rows, width), bf16)
    sums = (jax.ShapeDtypeStruct((rows, width), f32), jax.ShapeDtypeStruct((rows, width), bf16))
    return pl.pallas_call(
        functools.partial(units_kernel, counts, tables),
        grid=(1,),
        out_shape=(by_units,) * 3 + (by_rows,) * 2 + sums * 2,
        in_specs=[whole] * 4 + [IN_SMEM] * 3 + [ANYWHERE] * (len(arrays) + len(held)),
        out_specs=(kept_units,) * 3 + (kept_rows,) * 2 + (whole,) * 4,
        scratch_shapes=[pltpu.VMEM((units, width), bf16)] * 3
        + [pltpu.SemaphoreType.DMA((len(table),)) for table in tables],
        input_output_aliases={7 + len(arrays) + i: i for i in range(len(held))},
        compiler_params=pltpu.CompilerParams(vmem_limit_bytes=56 * 2**20),
        cost_estimate=SHORT,
        name="units_chunk",
    )(own, other, grad_own, grad_other, *[starts for _, _, starts in weights], *arrays, *held)


def transposed_product_kernel(left_ref, right_ref, out_ref):
    out_ref[...] = contract(left_ref[...], right_ref[...], 0, 0).astype(bf16)


def transposed_product(left, right):
    depth, units = left.shape
    width = right.shape[1]
    cut = min(256, units)
    return pl.pallas_call(
        transposed_product_kernel,
        grid=(units // cut,),
        out_shape=jax.ShapeDtypeStruct((units, width), bf16),
        in_specs=[
            pl.BlockSpec((depth, cut), lambda i: (0, i)),
            pl.BlockSpec((depth, width), lambda i: (0, 0)),
        ],
        out_specs=pl.BlockSpec((cut, width), lambda i: (i, 0)),
        compiler_params=pltpu.CompilerParams(vmem_limit_bytes=48 * 2**20),
        cost_estimate=SHORT,
        name="transposed_product",
    )(left, right)


def rotary_tables(positions, head_dim):
    half_dim = head_dim // 2
    frequency = rope_base ** (-(jnp.arange(half_dim, dtype=f32) * 2.0) / head_dim)
    angles = positions.astype(f32)[None, :] * frequency[:, None]
    return jnp.cos(angles), jnp.sin(angles)


def after(array, *others):
    return lax.optimization_barrier((array, *others))[0]


def swap_cores(array):
    return lax.ppermute(array, "c", [(0, 1), (1, 0)])


def from_next(array):
    count = lax.axis_size("z")
    return lax.ppermute(array, "z", [(i, (i - 1) % count) for i in range(count)])


def from_flipped(array, bit):
    return lax.ppermute(array, "p", [(i, i ^ bit) for i in range(4)])


def square_groups():
    return lax.axis_size("p") == 4 and lax.axis_size("r") == 1


def gather_chunks(block):
    count = lax.axis_size("z")
    chunks = []
    for step in range(count):
        later = from_next(block) if step < count - 1 else None
        chunks.append((block, swap_cores(block)))
        block = later
    return chunks


def add_over_line(parts, starts=(), fills=()):
    count = lax.axis_size("z")
    total = parts[1 % count]
    for step in range(2, count + 1):
        send = total.astype(bf16)
        if step - 2 < len(starts):
            send = after(send, starts[step - 2])
        came = from_next(send)
        if step - 2 < len(fills):
            came = after(came, fills[step - 2])
        total = came.astype(f32) + parts[step % count]
    return total


def add_over_cores(keep, send):
    return keep + swap_cores(send.astype(bf16)).astype(f32)


def group_pieces(block, before_corner=()):
    if not square_groups():
        whole = lax.all_gather(block, GROUPS, axis=0)
        return [(whole[group], group, 0) for group in range(whole.shape[0])]
    half = block.shape[0] // 2
    place = lax.axis_index("p")
    beside, across = from_flipped(block, 1), from_flipped(block, 2)
    near = [(block, place, 0), (beside, place ^ 1, 0), (across, place ^ 2, 0)]
    top, low = after((beside[:half], across[half:]), before_corner)
    top, low = from_flipped(top, 2), from_flipped(low, 1)
    return [*near, (top, place ^ 3, 0), (low, place ^ 3, half)]


def placed(pieces, rows):
    table = tuple((which, 0, piece[0].shape[0]) for which, piece in enumerate(pieces))
    starts = [jnp.int32(group) * rows + first for _, group, first in pieces]
    return [array for array, _, _ in pieces], table, jnp.stack(starts).astype(jnp.int32)


def scatter_groups(parts):
    if not square_groups():
        flat = parts.reshape(-1, parts.shape[-1])
        return lax.psum_scatter(flat, GROUPS, scatter_dimension=0, tiled=True).astype(f32)
    half = parts.shape[1] // 2
    place = lax.axis_index("p")
    own, beside, across, corner = (
        lax.dynamic_index_in_dim(parts, place ^ bits, 0, keepdims=False) for bits in range(4)
    )
    to_across = from_flipped(corner[:half], 1)
    to_beside = from_flipped(corner[half:], 2)
    total_top = from_flipped(beside[:half], 1).astype(f32)
    total_low = from_flipped(across[half:], 2).astype(f32)
    beside_low = (beside[half:].astype(f32) + to_beside.astype(f32)).astype(bf16)
    across_top = (across[:half].astype(f32) + to_across.astype(f32)).astype(bf16)
    total_low = total_low + from_flipped(beside_low, 1).astype(f32)
    total_top = total_top + from_flipped(across_top, 2).astype(f32)
    return own.astype(f32) + jnp.concatenate([total_top, total_low])


def ring(block, starts=()):
    blocks = [block]
    for step in range(lax.axis_size("z") - 1):
        send = after(blocks[-1], starts[step]) if step < len(starts) else blocks[-1]
        blocks.append(from_next(send))
    return blocks


def shards(tokens, attn_qkv, attn_out_t, mlp_weight, norm1, norm2, cotangent):
    rows, width = tokens.shape
    group_count, share_count = lax.axis_size("p"), lax.axis_size("r")
    line_count = lax.axis_size("z")
    tensor_count = lax.axis_size("c") * line_count
    head_dim = width // HEADS
    heads_here = HEADS // tensor_count
    group_rows = rows * tensor_count
    features_here = heads_here * head_dim
    weight_rows = attn_qkv.shape[0]
    share, place, core = lax.axis_index("r"), lax.axis_index("z"), lax.axis_index("c")
    block = min(1024, group_rows)
    x = tokens.astype(f32)
    gain_one = norm1.astype(f32)[:, None]
    device_index = (share * group_count + lax.axis_index("p")) * tensor_count

    def chunk_places(step):
        along = lax.rem(place + step, line_count)
        return core * line_count + along, (1 - core) * line_count + along

    x_group = lax.all_gather(tokens, TENSOR, axis=0, tiled=True)
    scaled_qkv = (attn_qkv.astype(f32) * gain_one).astype(bf16)
    qkv_cut = scaled_qkv.reshape(weight_rows, 3, tensor_count, features_here).transpose(2, 0, 1, 3)
    qkv_cut = qkv_cut.reshape(tensor_count, weight_rows, 3 * features_here)
    qkv_part = lax.all_to_all(qkv_cut, TENSOR, 0, 0).reshape(-1, 3 * features_here)
    qkv_rows = qkv_part.shape[0]
    qkv_arrays, qkv_table, qkv_starts = placed(group_pieces(qkv_part), qkv_rows)
    gain_columns = jnp.pad(norm2[:, None], ((0, 0), (0, 127)))
    out_pieces = group_pieces(jnp.concatenate([attn_out_t, gain_columns], axis=1), qkv_part)
    unit_rows = mlp_weight.shape[0]
    gate_weight = placed(group_pieces(mlp_weight[:, :width], qkv_arrays), unit_rows)
    down_weight = placed(group_pieces(mlp_weight[:, 2 * width :], qkv_arrays), unit_rows)
    up_whole = lax.all_gather(
        after(mlp_weight[:, width : 2 * width], qkv_arrays), GROUPS, axis=0, tiled=True
    )
    up_weight = ([up_whole], ((0, 0, up_whole.shape[0]),), jnp.zeros((1,), jnp.int32))

    positions = device_index * rows + jnp.arange(group_rows)
    cosine, sine = rotary_tables(positions, head_dim)
    unit_group, stacked = project(
        x_group, cosine, sine, qkv_arrays, qkv_table, qkv_starts, heads_here, head_dim, rows
    )
    qkv = lax.all_to_all(stacked, "p", 0, 0)
    qkv = qkv.reshape(-1, 3, head_dim, rows)

    def over_shares(array):
        return lax.all_gather(array, "r", axis=0, tiled=True) if share_count > 1 else array

    def own_share(array):
        if share_count == 1:
            return array
        pieces = group_count * tensor_count
        return lax.dynamic_slice_in_dim(array, share * pieces, pieces, 0)

    qkv = over_shares(qkv)
    attended, logsum = attend_forward(qkv, block)
    attended_head = own_share(attended)

    out_plane = jnp.concatenate([array for array, _, _ in out_pieces])
    grad_out_ring = ring(cotangent, (x_group,))[:2]
    out_ring = ring(out_plane, (grad_out_ring[-1], stacked, qkv))
    out_arrays = out_ring + [swap_cores(array) for array in out_ring[:-1]]
    out_arrays.append(swap_cores(after(out_ring[-1], attended)))
    out_table, out_starts = [], []
    for which in range(2 * line_count):
        side = core if which < line_count else 1 - core
        along = lax.rem(place + which % line_count, line_count)
        first = 0
        for array, group, offset in out_pieces:
            out_table.append((which, first, array.shape[0]))
            spot = (jnp.int32(group) * 2 + side) * line_count + along
            out_starts.append(spot * weight_rows + offset)
            first += array.shape[0]
    out_table, out_starts = tuple(out_table), jnp.stack(out_starts).astype(jnp.int32)
    grad_out_ring += ring(after(grad_out_ring[-1], out_ring[-1]), ((),))[1 : line_count - 1]
    grad_out_chunks = [(block, swap_cores(block)) for block in grad_out_ring]

    attended_local = lax.all_to_all(attended_head, ("p", "c", "z"), 0, 0)
    middle, normed_two, gain_two = finish_attention(
        tokens, attended_local, out_arrays, out_table, out_starts, HEADS // tensor_count
    )
    attended_group = attended_head.reshape(group_count, tensor_count, head_dim, rows)
    attended_group = lax.all_to_all(after(attended_group, normed_two), "p", 0, 0)

    held, normed_parts, branch_parts = (), [], []
    normed = normed_two
    for step in range(line_count):
        later = from_next(normed) if step < line_count - 1 else None
        *held, keep, send, branch_keep, branch_send = units_chunk(
            step, line_count, normed, swap_cores(normed), *grad_out_chunks[step],
            (gate_weight, up_weight, down_weight), held,
        )
        normed_parts.append(add_over_cores(keep, send))
        branch_parts.append((branch_keep, branch_send))
        if later is not None:
            normed = after(later, keep)
    activation, gate_grads, up_grads, normed_group, grad_out_group = (
        array.reshape(group_rows, -1) for array in held
    )

    def over_groups(part):
        return lax.psum_scatter(part, GROUPS, scatter_dimension=0, tiled=True)

    gate_term = transposed_product(gate_grads, normed_group)
    grad_normed = add_over_line(normed_parts, fills=((), (), gate_term))
    grad_middle, grad_mid_low, norm_two_part, grad_attended = back_to_attention(
        middle, grad_normed, cotangent, gain_two, out_arrays, out_table, out_starts,
        HEADS // tensor_count, head_dim,
    )
    grad_head = lax.all_to_all(grad_attended, ("p", "c", "z"), 0, 0)
    up_grads, activation = after((up_grads, activation), grad_attended)
    up_term = transposed_product(up_grads, normed_group)
    down_term = transposed_product(activation, grad_out_group)
    grad_head = after(grad_head, up_term, down_term)

    grad_qkv_head = attend_backward(qkv, over_shares(grad_head), attended, logsum, block)
    grad_qkv_head = own_share(grad_qkv_head)
    branch = add_over_line(
        [add_over_cores(*part) for part in branch_parts],
        starts=(grad_attended, grad_head, grad_qkv_head),
    )
    result = (middle + branch).astype(bf16)

    grad_gate_w = over_groups(gate_term)
    grad_mid_group = lax.all_gather(after(grad_mid_low, gate_term), TENSOR, axis=0, tiled=True)
    grad_up_w = over_groups(after(up_term, grad_head))
    grad_down_w = over_groups(after(down_term, grad_head))

    def to_owners(part, start=()):
        columns = part.shape[1]
        parts = after(part.astype(bf16), start).reshape(share_count * group_count, -1, columns)
        own = scatter_groups(parts).astype(bf16)
        own = lax.all_to_all(own.reshape(tensor_count, -1, columns), TENSOR, 0, 0)
        return own.astype(f32)

    attended_group = jnp.swapaxes(attended_group, 1, 2).reshape(features_here, group_rows)
    out_term = contract(grad_mid_group, attended_group, 0, 1)
    norm_two_part = norm_two_part[0]
    norm_high = norm_two_part.astype(bf16).astype(f32)
    norm_columns = jnp.stack([norm_high, norm_two_part - norm_high], axis=1)
    grad_qkv_rows = grad_qkv_head.reshape(group_count, tensor_count, 3, head_dim, rows)
    grad_qkv_rows = lax.all_to_all(grad_qkv_rows, "p", 0, 0)
    grad_qkv_rows = after(grad_qkv_rows, out_term)
    out_sum = to_owners(
        jnp.concatenate([out_term, jnp.pad(norm_columns, ((0, 0), (0, 126)))], axis=1),
        grad_qkv_rows,
    )
    grad_out_w = out_sum[:, :, :features_here].transpose(1, 0, 2).reshape(-1, width)
    grad_norm_two = jnp.sum(out_sum[:, :, features_here : features_here + 2], axis=(0, 2))
    spots = [spot for step in range(line_count) for spot in chunk_places(step)]
    grad_qkv_low, keep, send = back_to_norm(
        grad_qkv_rows, cosine, sine, qkv_arrays, qkv_table, qkv_starts,
        jnp.stack(spots).astype(jnp.int32),
    )
    weighted_parts = [add_over_cores(keep[step], send[step]) for step in range(line_count)]
    qkv_term = contract(unit_group, after(grad_qkv_low, weighted_parts[1]), 0, 1).astype(bf16)
    weighted_one = add_over_line(weighted_parts, fills=(qkv_term,))
    factor_one = lax.rsqrt(jnp.mean(x * x, axis=-1, keepdims=True) + epsilon)
    grad_tokens = (
        grad_middle
        + factor_one * weighted_one
        - x * factor_one**3 * jnp.mean(weighted_one * x, axis=-1, keepdims=True)
    )
    qkv_sum = to_owners(qkv_term).reshape(tensor_count, weight_rows, 3, features_here)
    qkv_sum = qkv_sum.transpose(1, 2, 0, 3).reshape(weight_rows, 3 * width)
    grad_qkv = gain_one * qkv_sum
    grad_norm_one = jnp.sum(attn_qkv.astype(f32) * qkv_sum, axis=1)
    grad_mlp = jnp.concatenate([grad_gate_w, grad_up_w, grad_down_w], axis=1).astype(f32)
    return (result, grad_tokens, grad_qkv, grad_out_w, grad_mlp, grad_norm_one, grad_norm_two)


def solution(mesh):
    seq_count, fsdp_count = mesh.shape["seq"], mesh.shape["fsdp"]
    groups = seq_count // 2
    heads_here = HEADS // (2 * fsdp_count)
    dealt = min(groups, heads_here)
    fine = Mesh(mesh.devices.reshape(groups // dealt, dealt, 2, fsdp_count), ALL)
    by_rows, by_items = P(ALL, None), P(ALL)
    in_specs = (by_rows, by_rows, by_rows, by_rows, by_items, by_items, by_rows)
    out_specs = (by_rows, by_rows, by_rows, by_rows, by_rows, by_items, by_items)
    return jax.shard_map(shards, mesh=fine, in_specs=in_specs, out_specs=out_specs, check_vma=False)
```

time: 1070 us -> 672 us (0.63)
  waiting for transfers between devices: 580 us -> 229 us
  blocking collectives: 234 us -> 42.7 us
  Pallas kernels: 49.8 us -> 164 us
  matrix products: 108 us -> 7.34 us
  starting transfers between devices: 22.4 us -> 115 us
  local copies, waits for them, and re-layouts: 14 us -> 48.1 us
    reduce_scatter x6 -> x3, waiting for transfers between devices: 317 us -> 21 us  [over_groups(): return lax.psum_scatter(part, GROUPS, scatter_dimension=0, tiled=True)]
    all_gather x7 -> x3, waiting for transfers between devices: 239 us -> 0.01 us  [the longest x1 0.01 us: shards(): x_group = lax.all_gather(tokens, TENSOR, axis=0, tiled=True)]
    ppermute x0 -> x70, waiting for transfers between devices: none -> 163 us  [the longest x18 91.1 us: from_next(): lax.ppermute(array, 'z', [(i, (i - 1) % count) for i in range(count)])]
    pallas_call x0 -> x11, Pallas kernels: none -> 114 us  [the longest x4 53.5 us: units_chunk(): pl.pallas_call(functools.partial(units_kernel, counts, tables), grid=(1,)...]
    dot_general x15 -> x2, matrix products: 108 us -> 7.34 us  [contract(): lax.dot_general(left, right, (((left_dim,), (right_dim,)), ((), ())), pre...]
    all_to_all x4 -> x0, blocking collectives: 98 us -> none  [the longest x1 31.5 us: shards(): grad_head = lax.all_to_all(grad_attended, ('p', 'c', 'z'), 0, 0)]
    unnamed x2 -> x0, blocking collectives: 93.7 us -> none
    ppermute x0 -> x70, starting transfers between devices: none -> 87.4 us  [the longest x18 46 us: from_next(): lax.ppermute(array, 'z', [(i, (i - 1) % count) for i in range(count)])]
  transfers between devices with their start and end apart: 16 -> 83, of which waited for: 11 -> 29; matrix products, arithmetic and copies ran while one was open for 11% -> 11% of each run, Pallas kernels for 5% -> 24%
where the time goes in v2:
time: 672 us; the launch traced here: 664 us
  waiting for transfers between devices  229 us (34%)
  Pallas kernels  164 us (24%)
  starting transfers between devices  115 us (17%)
  local copies, waits for them, and re-layouts  48.1 us (7%)
  other arithmetic  42.8 us (6%)
  blocking collectives  42.7 us (6%)
  between operations  15.3 us (2%)
  matrix products  7.34 us (1%)
    ppermute x18, waiting for transfers between devices, from_next(): lax.ppermute(array, 'z', [(i, (i - 1) % count) for i in range(count)])  91.1 us
    ppermute x28, waiting for transfers between devices, from_flipped(): return lax.ppermute(array, 'p', [(i, i ^ bit) for i in range(4)])  68 us
    pallas_call x4, Pallas kernels, units_chunk(): pl.pallas_call(functools.partial(units_kernel, counts, tables), grid=(1,)...  53.5 us
    ppermute x18, starting transfers between devices, from_next(): lax.ppermute(array, 'z', [(i, (i - 1) % count) for i in range(count)])  46 us
    all_to_all x1, blocking collectives, shards(): lax.all_to_all(qkv_cut, TENSOR, 0, 0).reshape(-1, 3 * features_here)  42.7 us
    ppermute x28, starting transfers between devices, from_flipped(): return lax.ppermute(array, 'p', [(i, i ^ bit) for i in range(4)])  32.9 us
    pallas_call x1, Pallas kernels, attend_backward(): pl.pallas_call(functools.partial(backward_kernel, block=block, scale=head...  31.6 us
    all_to_all x1, waiting for transfers between devices, shards(): qkv = lax.all_to_all(stacked, 'p', 0, 0)  26.6 us
  transfers between devices with their start and end apart: 83, of which 29 were waited for; matrix products, arithmetic and copies ran while one was open for 11% of the time, Pallas kernels for 24%

profile of v2, /device:TPU:0, one launch (start us, length us, event | category | flops | bytes accessed | tf_op | source)
XLA Modules:
  0.0 663.7 jit_solution(5175897367835025811)
XLA Ops:
  11.5 42.7 %all_to_all.40 = bf16[8,64,768]{2,1,0:T(8,128)(2,1)S(1)} all-to-all(bf16[8,64,768]{2,1,0:T(8,128)(2,1)S(1)} %reshape.157), channel_id=1, replica_groups=mesh['r'=1,'p'=4,'c'=2,'z'=4] {'c','z'}, dimensions={0} | all-to-all | bytes 1572864 | tf_op jit(solution)/shard_map/all_to_all | solution.py:633
  58.5 14.4 %collective-permute-done.1.refs_2_ = bf16[512,768]{1,0:T(8,128)(2,1)S(1)} collective-permute-done((bf16[512,768]{1,0:T(8,128)(2,1)S(1)}, bf16[512,768]{1,0:T(8,128)(2,1)S(1)}, u32[]{:S(2)}, u32[]{:S(2)}) %collective-permute-start.1) | collective-permute-done | bytes 786464 | tf_op jit(solution)/shard_map/ppermute | solution.py:527
  77.9 3.7 fusion.26
  84.6 3.4 collective-permute-done.2.refs_3_
  95.9 11.1 %collective-permute-done.8.grad_own_ref = bf16[128,2048]{1,0:T(8,128)(2,1)S(1)} collective-permute-done((bf16[128,2048]{1,0:T(8,128)(2,1)S(1)}, bf16[128,2048]{1,0:T(8,128)(2,1)S(1)}, u32[]{:S(2)}, u32[]{:S(2)}) %collective-permute-start.8) | collective-permute-done | bytes 524320 | tf_op jit(solution)/shard_map/ppermute | solution.py:523
  112.5 9.5 %project.1 = (bf16[1024,2048]{1,0:T(8,128)(2,1)}, bf16[4,8,3,64,128]{4,3,2,1,0:T(8,128)(2,1)S(1)}) custom-call(s32[5]{0:T(128)S(1)} %stack.244.starts_ref, bf16[1024,2048]{1,0:T(8,128)(2,1)} %all-gather.4.cloned.1.call-done.x_ref, f32[32,1024]{1,0:T(8,128)S(1)} %get-tuple-element.199.cosine_ref, f32[32,1024]{1,0:T(8,128)S(1)} %get-tuple-element.198.sine_ref, ...), custom_call_target="tpu_custom_call" | custom-call | flops 1000 | bytes 1000 | tf_op jit(solution)/shard_map/project/pallas_call | solution.py:226
  123.2 4.4 all-to-all-start.1
  127.6 5.0 collective-permute-done.9.refs_1_
  132.6 4.4 collective-permute-start.10
  137.0 26.6 %all-to-all-done.1 = bf16[4,8,3,64,128]{4,3,2,1,0:T(8,128)(2,1)} async-done(((bf16[4,8,3,64,128]{4,3,2,1,0:T(8,128)(2,1)}), bf16[4,8,3,64,128]{4,3,2,1,0:T(8,128)(2,1)}, u32[]{:S(2)}, u32[]{:S(2)}) %all-to-all-start.1) | async-done | bytes 1572896 | tf_op jit(solution)/shard_map/all_to_all | solution.py:651
  163.5 2.5 collective-permute-start.11
  169.8 19.1 %collective-permute-done.11.refs_3_ = bf16[256,2176]{1,0:T(8,128)(2,1)} collective-permute-done((bf16[256,2176]{1,0:T(8,128)(2,1)}, bf16[256,2176]{1,0:T(8,128)(2,1)}, u32[]{:S(2)}, u32[]{:S(2)}) %collective-permute-start.11) | collective-permute-done | bytes 1114144 | tf_op jit(solution)/shard_map/ppermute | solution.py:523
  188.9 2.5 collective-permute-start.19
  191.3 18.4 %attend_forward.1 = (bf16[32,64,128]{2,1,0:T(8,128)(2,1)}, f32[4,1,1024]{2,1,0:T(1,128)}) custom-call(bf16[32,3,64,128]{3,2,1,0:T(8,128)(2,1)} %bitcast.47.qkv_ref), custom_call_target="tpu_custom_call" | custom-call | flops 1000 | bytes 1000 | tf_op jit(solution)/shard_map/attend_forward/pallas_call | solution.py:135
  210.4 3.8 all-to-all-start.2
  226.2 2.3 all-to-all-done.2.attended_ref
  228.6 8.9 %finish_attention.1 = (f32[128,2048]{1,0:T(8,128)S(1)}, bf16[128,2048]{1,0:T(8,128)(2,1)}, f32[1,2048]{1,0:T(1,128)S(1)}) custom-call(s32[40]{0:T(128)S(1)} %stack.238.starts_ref, bf16[128,2048]{1,0:T(8,128)(2,1)S(1)} %copy-done.3, bf16[32,64,128]{2,1,0:T(8,128)(2,1)} %all-to-all-done.2.attended_ref, ...), custom_call_target="tpu_custom_call" | custom-call | flops 1000 | bytes 1000 | tf_op jit(solution)/shard_map/finish_attention/pallas_call | solution.py:277
  242.7 3.7 collective-permute-done.21.refs_6_
  246.4 3.8 collective-permute-done.22.refs_7_
  250.2 13.4 %units_chunk.4 = (bf16[4,256,1024]{2,1,0:T(8,128)(2,1)}, bf16[4,256,1024]{2,1,0:T(8,128)(2,1)}, bf16[4,256,1024]{2,1,0:T(8,128)(2,1)}, bf16[4,256,2048]{2,1,0:T(...) custom-call(bf16[128,2048]{1,0:T(8,128)(2,1)} %get-tuple-element.102, ...), custom_call_target="tpu_custom_call" | custom-call | flops 1000 | bytes 1000 | tf_op jit(solution)/shard_map/units_chunk/pallas_call | solution.py:468
  263.7 2.9 collective-permute-start.34
  267.8 13.4 %units_chunk.5 = (bf16[4,256,1024]{2,1,0:T(8,128)(2,1)}, bf16[4,256,1024]{2,1,0:T(8,128)(2,1)}, bf16[4,256,1024]{2,1,0:T(8,128)(2,1)}, bf16[4,256,2048]{2,1,0:T(...) custom-call(bf16[128,2048]{1,0:T(8,128)(2,1)} %collective-permute-do, ...), custom_call_target="tpu_custom_call", output_to_operand_aliasing={{0}: (18, {}), {1}: (19, {}), {2}: (20, {}), {3}: (21, {}),... | custom-call | flops 1000 | bytes 1000 | tf_op jit(solution)/shard_map/units_chunk/pallas_call | solution.py:468
  281.8 7.9 %collective-permute-done.32.own_ref = bf16[128,2048]{1,0:T(8,128)(2,1)S(1)} collective-permute-done((bf16[128,2048]{1,0:T(8,128)(2,1)}, bf16[128,2048]{1,0:T(8,128)(2,1)S(1)}, u32[]{:S(2)}, u32[]{:S(2)}) %collective-permute-start.32) | collective-permute-done | bytes 524320 | tf_op jit(solution)/shard_map/ppermute | solution.py:523
  289.7 4.2 collective-permute-start.40
  296.5 13.4 %units_chunk.6 = (bf16[4,256,1024]{2,1,0:T(8,128)(2,1)}, bf16[4,256,1024]{2,1,0:T(8,128)(2,1)}, bf16[4,256,1024]{2,1,0:T(8,128)(2,1)}, bf16[4,256,2048]{2,1,0:T(...) custom-call(bf16[128,2048]{1,0:T(8,128)(2,1)} %copy-done.36, ...), custom_call_target="tpu_custom_call", output_to_operand_aliasing={{0}: (18, {}), {1}: (19, {}), {2}: (20, {}), {3}: (21, {}),... | custom-call | flops 1000 | bytes 1000 | tf_op jit(solution)/shard_map/units_chunk/pallas_call | solution.py:468
  310.5 6.9 %collective-permute-done.38.own_ref = bf16[128,2048]{1,0:T(8,128)(2,1)S(1)} collective-permute-done((bf16[128,2048]{1,0:T(8,128)(2,1)S(1)}, bf16[128,2048]{1,0:T(8,128)(2,1)S(1)}, u32[]{:S(2)}, u32[]{:S(2)}) %collective-permute-start.38) | collective-permute-done | bytes 524320 | tf_op jit(solution)/shard_map/ppermute | solution.py:523
  317.3 10.8 %collective-permute-done.31 = bf16[128,2048]{1,0:T(8,128)(2,1)S(1)} collective-permute-done((bf16[128,2048]{1,0:T(8,128)(2,1)S(1)}, bf16[128,2048]{1,0:T(8,128)(2,1)S(1)}, u32[]{:S(2)}, u32[]{:S(2)}) %collective-permute-start.31) | collective-permute-done | bytes 524320 | tf_op jit(solution)/shard_map/ppermute | solution.py:523
  329.6 4.3 collective-permute-start.37
  334.9 13.4 %units_chunk.7 = (bf16[4,256,1024]{2,1,0:T(8,128)(2,1)}, bf16[4,256,1024]{2,1,0:T(8,128)(2,1)}, bf16[4,256,1024]{2,1,0:T(8,128)(2,1)}, bf16[4,256,2048]{2,1,0:T(...) custom-call(bf16[128,2048]{1,0:T(8,128)(2,1)} %copy-done.35, ...), custom_call_target="tpu_custom_call", output_to_operand_aliasing={{0}: (18, {}), {1}: (19, {}), {2}: (20, {}), {3}: (21, {}),... | custom-call | flops 1000 | bytes 1000 | tf_op jit(solution)/shard_map/units_chunk/pallas_call | solution.py:468
  352.9 8.6 %transposed_product.3 = bf16[1024,2048]{1,0:T(8,128)(2,1)} custom-call(bf16[1024,1024]{1,0:T(8,128)(2,1)S(1)} %bitcast.173, bf16[1024,2048]{1,0:T(8,128)(2,1)} %bitcast.179), custom_call_target="tpu_custom_call" | custom-call | flops 1000 | bytes 1000 | tf_op jit(solution)/shard_map/transposed_product/pallas_call | solution.py:491
  361.5 5.6 collective-permute-done.43
  370.0 6.6 back_to_attention.1
  379.0 3.5 all-to-all-start.3
  384.2 9.1 %transposed_product.4 = bf16[1024,2048]{1,0:T(8,128)(2,1)} custom-call(bf16[1024,1024]{1,0:T(8,128)(2,1)S(1)} %bitcast.174, bf16[1024,2048]{1,0:T(8,128)(2,1)} %bitcast.180), custom_call_target="tpu_custom_call" | custom-call | flops 1000 | bytes 1000 | tf_op jit(solution)/shard_map/transposed_product/pallas_call | solution.py:491
  393.3 8.6 %transposed_product.5 = bf16[1024,2048]{1,0:T(8,128)(2,1)} custom-call(bf16[1024,1024]{1,0:T(8,128)(2,1)S(1)} %bitcast.172, bf16[1024,2048]{1,0:T(8,128)(2,1)} %bitcast.181), custom_call_target="tpu_custom_call" | custom-call | flops 1000 | bytes 1000 | tf_op jit(solution)/shard_map/transposed_product/pallas_call | solution.py:491
  403.8 3.8 collective-permute-start.29
  409.1 2.2 add_convert_fusion.6
  411.3 6.8 %collective-permute-start.45 = (bf16[128,2048]{1,0:T(8,128)(2,1)}, bf16[128,2048]{1,0:T(8,128)(2,1)}, u32[]{:S(2)}, u32[]{:S(2)}) collective-permute-start(bf16[128,2048]{1,0:T(8,128)(2,1)} %add_convert_fusion.6), channel_id=1, source_target_pairs={{0,3},{1,0},{2,1},{3,2},{4,7},{5,4},{6,5},{7,6},{8,11},{9,8},{10,9... | collective-permute-start | bytes 1572872 | tf_op jit(solution)/shard_map/ppermute | solution.py:523
  419.4 3.5 all-to-all-start.5
  423.6 15.0 %collective-permute-done.45 = bf16[128,2048]{1,0:T(8,128)(2,1)} collective-permute-done((bf16[128,2048]{1,0:T(8,128)(2,1)}, bf16[128,2048]{1,0:T(8,128)(2,1)}, u32[]{:S(2)}, u32[]{:S(2)}) %collective-permute-start.45) | collective-permute-done | bytes 524320 | tf_op jit(solution)/shard_map/ppermute | solution.py:523
  440.8 31.6 %attend_backward.1 = bf16[32,3,64,128]{3,2,1,0:T(8,128)(2,1)} custom-call(bf16[32,3,64,128]{3,2,1,0:T(8,128)(2,1)} %bitcast.47.qkv_ref, bf16[32,64,128]{2,1,0:T(8,128)(2,1)} %all-to-all-done.3.grad_ref, bf16[32,64,128]{2,1,0:T(8,128)(2,1)} %get-tuple-element.93.out_ref, f32[4,1,1024]{2,1,0:T(1,128)} %get-tuple-element.154.logsum_ref), custom_call_target="tpu_custom_call" | custom-call | flops 1000 | bytes 1000 | tf_op jit(solution)/shard_map/attend_backward/pallas_call | solution.py:157
  472.3 2.5 collective-permute-start.47
  474.9 4.5 all-to-all-start.4
  479.5 9.8 %collective-permute-done.47 = bf16[128,2048]{1,0:T(8,128)(2,1)} collective-permute-done((bf16[128,2048]{1,0:T(8,128)(2,1)}, bf16[128,2048]{1,0:T(8,128)(2,1)}, u32[]{:S(2)}, u32[]{:S(2)}) %collective-permute-start.47) | collective-permute-done | bytes 524320 | tf_op jit(solution)/shard_map/ppermute | solution.py:523
  492.8 3.6 fusion.19
  496.4 13.5 %all-to-all-done.4.grad_ref = bf16[4,8,3,64,128]{4,3,2,1,0:T(8,128)(2,1)} async-done(((bf16[4,8,3,64,128]{4,3,2,1,0:T(8,128)(2,1)}), bf16[4,8,3,64,128]{4,3,2,1,0:T(8,128)(2,1)}, u32[]{:S(2)}, u32[]{:S(2)}) %all-to-all-start.4) | async-done | bytes 1572896 | tf_op jit(solution)/shard_map/all_to_all | solution.py:750
  511.2 2.9 copy.52
  517.4 2.2 add_convert_fusion
  521.9 9.0 %back_to_norm.1 = (bf16[768,1024]{1,0:T(8,128)(2,1)S(1)}, f32[4,128,2048]{2,1,0:T(8,128)}, bf16[4,128,2048]{2,1,0:T(8,128)(2,1)}) custom-call(s32[5]{0:T(128)S(1)} %stack.244.starts_ref, s32[8]{0:T(128)S(1)} %stack.259.spots_ref, bf16[4,8,3,64,128]{4,3,2,1,0:T(8,128)(2,1)} %all-to-all-done.4.grad_ref, f32[32,1024]{1,0:T(8,128)S(1)} %copy-done.20, ...), custom_call_target="tpu_custom_call" | custom-call | flops 1000 | bytes 1000 | tf_op jit(solution)/shard_map/back_to_norm/pallas_call | solution.py:391
  532.6 2.7 slice_bitcast_fusion.4
  536.0 6.1 collective-permute-done.66
  543.4 8.8 %collective-permute-done.69 = bf16[256,384]{1,0:T(8,128)(2,1)S(1)} collective-permute-done((bf16[256,384]{1,0:T(8,128)(2,1)S(1)}, bf16[256,384]{1,0:T(8,128)(2,1)S(1)}, u32[]{:S(2)}, u32[]{:S(2)}) %collective-permute-start.69) | collective-permute-done | bytes 196640 | tf_op jit(solution)/shard_map/ppermute | solution.py:527
  554.4 2.6 collective-permute-start.52
  557.0 3.7 convolution_convert_fusion
  566.8 3.7 all-to-all-start.7
  571.7 11.3 %collective-permute-done.59 = bf16[256,768]{1,0:T(8,128)(2,1)} collective-permute-done((bf16[256,768]{1,0:T(8,128)(2,1)}, bf16[256,768]{1,0:T(8,128)(2,1)}, u32[]{:S(2)}, u32[]{:S(2)}) %collective-permute-start.59) | collective-permute-done | bytes 393248 | tf_op jit(solution)/shard_map/ppermute | solution.py:527
  585.2 2.5 fusion.16
  589.5 2.3 fusion.13
  594.6 11.8 %collective-permute-done.60 = bf16[256,768]{1,0:T(8,128)(2,1)} collective-permute-done((bf16[256,768]{1,0:T(8,128)(2,1)}, bf16[256,768]{1,0:T(8,128)(2,1)}, u32[]{:S(2)}, u32[]{:S(2)}) %collective-permute-start.60) | collective-permute-done | bytes 393248 | tf_op jit(solution)/shard_map/ppermute | solution.py:527
  606.3 3.3 collective-permute-start.54
  613.4 3.5 all-to-all-start.6
  618.7 3.8 collective-permute-start.56
  622.5 21.0 %reduce-scatter.8.cloned.1.call-done = bf16[256,2048]{1,0:T(8,128)(2,1)} async-done(((bf16[1024,2048]{1,0:T(8,128)(2,1)}), bf16[256,2048]{1,0:T(8,128)(2,1)}) %reduce-scatter.8.cloned.1.call-update) | async-done | bytes 1048592 | tf_op jit(solution)/shard_map/reduce_scatter | solution.py:710
  643.6 5.5 maximum_convert_fusion
  (294 shorter events, 122.4 us)
Async XLA Ops:
  7.2 84.4 %all-gather.4.cloned.1.call-start = ((), (), s32[]{:S(2)}) async-start(), calls=%async_computation.11 | async-start | bytes 4718592 | tf_op jit(solution)/shard_map/all_gather | solution.py:629
  7.9 242.3 %all-gather.6.cloned.1.call-start = ((), (), s32[]{:S(2)}) async-start(), calls=%async_computation.12 | async-start | bytes 5242880 | tf_op jit(solution)/shard_map/all_gather | solution.py:641
  54.2 18.7 %collective-permute-start.1 = (bf16[512,768]{1,0:T(8,128)(2,1)S(1)}, bf16[512,768]{1,0:T(8,128)(2,1)S(1)}, u32[]{:S(2)}, u32[]{:S(2)}) collective-permute-start(bf16[512,768]{1,0:T(8,128)(2,1)S(1)} %bitcast.175), channel_id=1, source_target_pairs={{0,16},{8,24},{16,0},{24,8},{1,17},{9,25},{17,1},{25,9},{2,18},{10... | collective-permute-start | bytes 2359304 | tf_op jit(solution)/shard_map/ppermute | solution.py:527
  55.7 19.1 %collective-permute-start = (bf16[512,768]{1,0:T(8,128)(2,1)S(1)}, bf16[512,768]{1,0:T(8,128)(2,1)}, u32[]{:S(2)}, u32[]{:S(2)}) collective-permute-start(bf16[512,768]{1,0:T(8,128)(2,1)S(1)} %bitcast.176), channel_id=1, source_target_pairs={{0,8},{8,0},{16,24},{24,16},{1,9},{9,1},{17,25},{25,17},{2,10},{10... | collective-permute-start | bytes 2359304 | tf_op jit(solution)/shard_map/ppermute | solution.py:527
  57.4 24.2 %collective-permute-start.4 = (bf16[64,2176]{1,0:T(8,128)(2,1)S(1)}, bf16[64,2176]{1,0:T(8,128)(2,1)S(1)}, u32[]{:S(2)}, u32[]{:S(2)}) collective-permute-start(bf16[64,2176]{1,0:T(8,128)(2,1)S(1)} %get-tuple-element.196), channel_id=1, source_target_pairs={{0,8},{8,0},{16,24},{24,16},{1,9},{9,1},{17,25},{25,17},{2,10},{10... | collective-permute-start | bytes 835592 | tf_op jit(solution)/shard_map/ppermute | solution.py:527
  58.0 24.3 %collective-permute-start.5 = (bf16[64,2176]{1,0:T(8,128)(2,1)S(1)}, bf16[64,2176]{1,0:T(8,128)(2,1)S(1)}, u32[]{:S(2)}, u32[]{:S(2)}) collective-permute-start(bf16[64,2176]{1,0:T(8,128)(2,1)S(1)} %get-tuple-element.196), channel_id=1, source_target_pairs={{0,16},{8,24},{16,0},{24,8},{1,17},{9,25},{17,1},{25,9},{2,18},{10... | collective-permute-start | bytes 835592 | tf_op jit(solution)/shard_map/ppermute | solution.py:527
  91.5 15.4 %collective-permute-start.8 = (bf16[128,2048]{1,0:T(8,128)(2,1)S(1)}, bf16[128,2048]{1,0:T(8,128)(2,1)S(1)}, u32[]{:S(2)}, u32[]{:S(2)}) collective-permute-start(bf16[128,2048]{1,0:T(8,128)(2,1)S(1)} %copy-done.9), channel_id=1, source_target_pairs={{0,3},{1,0},{2,1},{3,2},{4,7},{5,4},{6,5},{7,6},{8,11},{9,8},{10,9... | collective-permute-start | bytes 1572872 | tf_op jit(solution)/shard_map/ppermute | solution.py:523
  107.8 24.8 %collective-permute-start.9 = (bf16[256,2176]{1,0:T(8,128)(2,1)S(1)}, bf16[256,2176]{1,0:T(8,128)(2,1)}, u32[]{:S(2)}, u32[]{:S(2)}) collective-permute-start(bf16[256,2176]{1,0:T(8,128)(2,1)S(1)} %constant_dynamic-update-slice_fusion.refs_0_), channel_id=1, source_target_pairs={{0,3},{1,0},{2,1},{3,2},{4,7},{5,4},{6,5},{7,6},{8,11},{9,8},{10,9... | collective-permute-start | bytes 3342344 | tf_op jit(solution)/shard_map/ppermute | solution.py:523
  123.2 40.3 %all-to-all-start.1 = ((bf16[4,8,3,64,128]{4,3,2,1,0:T(8,128)(2,1)}), bf16[4,8,3,64,128]{4,3,2,1,0:T(8,128)(2,1)}, u32[]{:S(2)}, u32[]{:S(2)}) async-start(bf16[4,8,3,64,128]{4,3,2,1,0:T(8,128)(2,1)} %copy-done.12), calls=%async_computation.1 | async-start | bytes 3145728 | tf_op jit(solution)/shard_map/all_to_all | solution.py:651
  132.6 30.9 %collective-permute-start.10 = (bf16[256,2176]{1,0:T(8,128)(2,1)}, bf16[256,2176]{1,0:T(8,128)(2,1)}, u32[]{:S(2)}, u32[]{:S(2)}) collective-permute-start(bf16[256,2176]{1,0:T(8,128)(2,1)} %collective-permute-done.9.refs_1_), channel_id=1, source_target_pairs={{0,3},{1,0},{2,1},{3,2},{4,7},{5,4},{6,5},{7,6},{8,11},{9,8},{10,9... | collective-permute-start | bytes 3342344 | tf_op jit(solution)/shard_map/ppermute | solution.py:523
  163.5 25.3 %collective-permute-start.11 = (bf16[256,2176]{1,0:T(8,128)(2,1)}, bf16[256,2176]{1,0:T(8,128)(2,1)}, u32[]{:S(2)}, u32[]{:S(2)}) collective-permute-start(bf16[256,2176]{1,0:T(8,128)(2,1)} %collective-permute-done.10.refs_2_), channel_id=1, source_target_pairs={{0,3},{1,0},{2,1},{3,2},{4,7},{5,4},{6,5},{7,6},{8,11},{9,8},{10,9... | collective-permute-start | bytes 3342344 | tf_op jit(solution)/shard_map/ppermute | solution.py:523
  166.0 43.8 %collective-permute-start.24 = (bf16[256,2048]{1,0:T(8,128)(2,1)}, bf16[256,2048]{1,0:T(8,128)(2,1)}, u32[]{:S(2)}, u32[]{:S(2)}) collective-permute-start(bf16[256,2048]{1,0:T(8,128)(2,1)} %get-tuple-element.181.refs_9_), channel_id=1, source_target_pairs={{0,16},{8,24},{16,0},{24,8},{1,17},{9,25},{17,1},{25,9},{2,18},{10... | collective-permute-start | bytes 3145736 | tf_op jit(solution)/shard_map/ppermute | solution.py:527
  167.5 42.3 %collective-permute-start.23 = (bf16[256,2048]{1,0:T(8,128)(2,1)}, bf16[256,2048]{1,0:T(8,128)(2,1)}, u32[]{:S(2)}, u32[]{:S(2)}) collective-permute-start(bf16[256,2048]{1,0:T(8,128)(2,1)} %get-tuple-element.181.refs_9_), channel_id=1, source_target_pairs={{0,8},{8,0},{16,24},{24,16},{1,9},{9,1},{17,25},{25,17},{2,10},{10... | collective-permute-start | bytes 3145736 | tf_op jit(solution)/shard_map/ppermute | solution.py:527
  167.8 42.6 %collective-permute-start.20 = (bf16[256,2048]{1,0:T(8,128)(2,1)}, bf16[256,2048]{1,0:T(8,128)(2,1)}, u32[]{:S(2)}, u32[]{:S(2)}) collective-permute-start(bf16[256,2048]{1,0:T(8,128)(2,1)} %get-tuple-element.182.refs_3_), channel_id=1, source_target_pairs={{0,16},{8,24},{16,0},{24,8},{1,17},{9,25},{17,1},{25,9},{2,18},{10... | collective-permute-start | bytes 3145736 | tf_op jit(solution)/shard_map/ppermute | solution.py:527
  169.8 48.5 %collective-permute-start.12 = (bf16[256,2176]{1,0:T(8,128)(2,1)S(1)}, bf16[256,2176]{1,0:T(8,128)(2,1)}, u32[]{:S(2)}, u32[]{:S(2)}) collective-permute-start(bf16[256,2176]{1,0:T(8,128)(2,1)S(1)} %constant_dynamic-update-slice_fusion.refs_0_), channel_id=1, source_target_pairs={{0,4},{4,0},{1,5},{5,1},{2,6},{6,2},{3,7},{7,3},{8,12},{12,8},{9,1... | collective-permute-start | bytes 3342344 | tf_op jit(solution)/shard_map/ppermute | solution.py:518
  188.9 29.2 %collective-permute-start.19 = (bf16[256,2048]{1,0:T(8,128)(2,1)}, bf16[256,2048]{1,0:T(8,128)(2,1)}, u32[]{:S(2)}, u32[]{:S(2)}) collective-permute-start(bf16[256,2048]{1,0:T(8,128)(2,1)} %get-tuple-element.182.refs_3_), channel_id=1, source_target_pairs={{0,8},{8,0},{16,24},{24,16},{1,9},{9,1},{17,25},{25,17},{2,10},{10... | collective-permute-start | bytes 3145736 | tf_op jit(solution)/shard_map/ppermute | solution.py:527
  209.8 15.6 %collective-permute-start.14 = (bf16[256,2176]{1,0:T(8,128)(2,1)}, bf16[256,2176]{1,0:T(8,128)(2,1)}, u32[]{:S(2)}, u32[]{:S(2)}) collective-permute-start(bf16[256,2176]{1,0:T(8,128)(2,1)} %collective-permute-done.10.refs_2_), channel_id=1, source_target_pairs={{0,4},{4,0},{1,5},{5,1},{2,6},{6,2},{3,7},{7,3},{8,12},{12,8},{9,1... | collective-permute-start | bytes 3342344 | tf_op jit(solution)/shard_map/ppermute | solution.py:518
  210.4 15.5 %collective-permute-start.15 = (bf16[256,2176]{1,0:T(8,128)(2,1)}, bf16[256,2176]{1,0:T(8,128)(2,1)}, u32[]{:S(2)}, u32[]{:S(2)}) collective-permute-start(bf16[256,2176]{1,0:T(8,128)(2,1)} %collective-permute-done.11.refs_3_), channel_id=1, source_target_pairs={{0,4},{4,0},{1,5},{5,1},{2,6},{6,2},{3,7},{7,3},{8,12},{12,8},{9,1... | collective-permute-start | bytes 3342344 | tf_op jit(solution)/shard_map/ppermute | solution.py:518
  210.4 18.2 %all-to-all-start.2 = ((bf16[32,64,128]{2,1,0:T(8,128)(2,1)}), bf16[32,64,128]{2,1,0:T(8,128)(2,1)}, u32[]{:S(2)}, u32[]{:S(2)}) async-start(bf16[32,64,128]{2,1,0:T(8,128)(2,1)} %get-tuple-element.93.out_ref), calls=%async_computation.2 | async-start | bytes 1048576 | tf_op jit(solution)/shard_map/all_to_all | solution.py:686
  214.2 278.6 %all-gather.8.cloned.1.call-start = ((), (), s32[]{:S(2)}) async-start(), calls=%async_computation.13 | async-start | bytes 4718592 | tf_op jit(solution)/shard_map/all_gather | solution.py:733
  218.1 20.4 %collective-permute-start.18 = (bf16[128,2048]{1,0:T(8,128)(2,1)S(1)}, bf16[128,2048]{1,0:T(8,128)(2,1)}, u32[]{:S(2)}, u32[]{:S(2)}) collective-permute-start(bf16[128,2048]{1,0:T(8,128)(2,1)S(1)} %copy-done.10), channel_id=1, source_target_pairs={{0,4},{4,0},{1,5},{5,1},{2,6},{6,2},{3,7},{7,3},{8,12},{12,8},{9,1... | collective-permute-start | bytes 1572872 | tf_op jit(solution)/shard_map/ppermute | solution.py:518
  218.3 21.5 %collective-permute-start.25 = (bf16[128,2048]{1,0:T(8,128)(2,1)}, bf16[128,2048]{1,0:T(8,128)(2,1)}, u32[]{:S(2)}, u32[]{:S(2)}) collective-permute-start(bf16[128,2048]{1,0:T(8,128)(2,1)} %slice.174), channel_id=1, source_target_pairs={{0,16},{8,24},{16,0},{24,8},{1,17},{9,25},{17,1},{25,9},{2,18},{10... | collective-permute-start | bytes 1572872 | tf_op jit(solution)/shard_map/ppermute | solution.py:527
  223.9 18.7 %collective-permute-start.26 = (bf16[128,2048]{1,0:T(8,128)(2,1)}, bf16[128,2048]{1,0:T(8,128)(2,1)}, u32[]{:S(2)}, u32[]{:S(2)}) collective-permute-start(bf16[128,2048]{1,0:T(8,128)(2,1)} %slice.175), channel_id=1, source_target_pairs={{0,8},{8,0},{16,24},{24,16},{1,9},{9,1},{17,25},{25,17},{2,10},{10... | collective-permute-start | bytes 1572872 | tf_op jit(solution)/shard_map/ppermute | solution.py:527
  225.3 21.1 %collective-permute-start.21 = (bf16[128,2048]{1,0:T(8,128)(2,1)}, bf16[128,2048]{1,0:T(8,128)(2,1)}, u32[]{:S(2)}, u32[]{:S(2)}) collective-permute-start(bf16[128,2048]{1,0:T(8,128)(2,1)} %slice.172), channel_id=1, source_target_pairs={{0,16},{8,24},{16,0},{24,8},{1,17},{9,25},{17,1},{25,9},{2,18},{10... | collective-permute-start | bytes 1572872 | tf_op jit(solution)/shard_map/ppermute | solution.py:527
  225.9 24.3 %collective-permute-start.22 = (bf16[128,2048]{1,0:T(8,128)(2,1)}, bf16[128,2048]{1,0:T(8,128)(2,1)}, u32[]{:S(2)}, u32[]{:S(2)}) collective-permute-start(bf16[128,2048]{1,0:T(8,128)(2,1)} %slice.173), channel_id=1, source_target_pairs={{0,8},{8,0},{16,24},{24,16},{1,9},{9,1},{17,25},{25,17},{2,10},{10... | collective-permute-start | bytes 1572872 | tf_op jit(solution)/shard_map/ppermute | solution.py:527
  239.7 23.8 %collective-permute-start.16 = (bf16[128,2048]{1,0:T(8,128)(2,1)}, bf16[128,2048]{1,0:T(8,128)(2,1)}, u32[]{:S(2)}, u32[]{:S(2)}) collective-permute-start(bf16[128,2048]{1,0:T(8,128)(2,1)} %get-tuple-element.102.own_ref), channel_id=1, source_target_pairs={{0,3},{1,0},{2,1},{3,2},{4,7},{5,4},{6,5},{7,6},{8,11},{9,8},{10,9... | collective-permute-start | bytes 1572872 | tf_op jit(solution)/shard_map/ppermute | solution.py:523
  242.5 24.5 %collective-permute-start.28 = (bf16[128,2048]{1,0:T(8,128)(2,1)}, bf16[128,2048]{1,0:T(8,128)(2,1)}, u32[]{:S(2)}, u32[]{:S(2)}) collective-permute-start(bf16[128,2048]{1,0:T(8,128)(2,1)} %copy-done.32), channel_id=1, source_target_pairs={{0,4},{4,0},{1,5},{5,1},{2,6},{6,2},{3,7},{7,3},{8,12},{12,8},{9,1... | collective-permute-start | bytes 1572872 | tf_op jit(solution)/shard_map/ppermute | solution.py:518
  263.7 17.6 %collective-permute-start.34 = (bf16[128,2048]{1,0:T(8,128)(2,1)S(1)}, bf16[128,2048]{1,0:T(8,128)(2,1)S(1)}, u32[]{:S(2)}, u32[]{:S(2)}) collective-permute-start(bf16[128,2048]{1,0:T(8,128)(2,1)S(1)} %copy-done.33), channel_id=1, source_target_pairs={{0,3},{1,0},{2,1},{3,2},{4,7},{5,4},{6,5},{7,6},{8,11},{9,8},{10,9... | collective-permute-start | bytes 1572872 | tf_op jit(solution)/shard_map/ppermute | solution.py:523
  266.6 23.1 %collective-permute-start.32 = (bf16[128,2048]{1,0:T(8,128)(2,1)}, bf16[128,2048]{1,0:T(8,128)(2,1)S(1)}, u32[]{:S(2)}, u32[]{:S(2)}) collective-permute-start(bf16[128,2048]{1,0:T(8,128)(2,1)} %collective-permute-done.16.own_ref), channel_id=1, source_target_pairs={{0,3},{1,0},{2,1},{3,2},{4,7},{5,4},{6,5},{7,6},{8,11},{9,8},{10,9... | collective-permute-start | bytes 1572872 | tf_op jit(solution)/shard_map/ppermute | solution.py:523
  289.7 20.4 %collective-permute-start.40 = (bf16[128,2048]{1,0:T(8,128)(2,1)S(1)}, bf16[128,2048]{1,0:T(8,128)(2,1)S(1)}, u32[]{:S(2)}, u32[]{:S(2)}) collective-permute-start(bf16[128,2048]{1,0:T(8,128)(2,1)S(1)} %collective-permute-done.34.grad_own_ref), channel_id=1, source_target_pairs={{0,3},{1,0},{2,1},{3,2},{4,7},{5,4},{6,5},{7,6},{8,11},{9,8},{10,9... | collective-permute-start | bytes 1572872 | tf_op jit(solution)/shard_map/ppermute | solution.py:523
  293.9 23.5 %collective-permute-start.38 = (bf16[128,2048]{1,0:T(8,128)(2,1)S(1)}, bf16[128,2048]{1,0:T(8,128)(2,1)S(1)}, u32[]{:S(2)}, u32[]{:S(2)}) collective-permute-start(bf16[128,2048]{1,0:T(8,128)(2,1)S(1)} %collective-permute-done.32.own_ref), channel_id=1, source_target_pairs={{0,3},{1,0},{2,1},{3,2},{4,7},{5,4},{6,5},{7,6},{8,11},{9,8},{10,9... | collective-permute-start | bytes 1572872 | tf_op jit(solution)/shard_map/ppermute | solution.py:523
  295.4 32.8 %collective-permute-start.31 = (bf16[128,2048]{1,0:T(8,128)(2,1)S(1)}, bf16[128,2048]{1,0:T(8,128)(2,1)S(1)}, u32[]{:S(2)}, u32[]{:S(2)}) collective-permute-start(bf16[128,2048]{1,0:T(8,128)(2,1)S(1)} %add_convert_fusion.5), channel_id=1, source_target_pairs={{0,3},{1,0},{2,1},{3,2},{4,7},{5,4},{6,5},{7,6},{8,11},{9,8},{10,9... | collective-permute-start | bytes 1572872 | tf_op jit(solution)/shard_map/ppermute | solution.py:523
  309.9 18.3 %collective-permute-start.36 = (bf16[128,2048]{1,0:T(8,128)(2,1)}, bf16[128,2048]{1,0:T(8,128)(2,1)S(1)}, u32[]{:S(2)}, u32[]{:S(2)}) collective-permute-start(bf16[128,2048]{1,0:T(8,128)(2,1)} %get-tuple-element.127), channel_id=1, source_target_pairs={{0,4},{4,0},{1,5},{5,1},{2,6},{6,2},{3,7},{7,3},{8,12},{12,8},{9,1... | collective-permute-start | bytes 1572872 | tf_op jit(solution)/shard_map/ppermute | solution.py:518
  310.1 23.8 %collective-permute-start.41 = (bf16[128,2048]{1,0:T(8,128)(2,1)S(1)}, bf16[128,2048]{1,0:T(8,128)(2,1)S(1)}, u32[]{:S(2)}, u32[]{:S(2)}) collective-permute-start(bf16[128,2048]{1,0:T(8,128)(2,1)S(1)} %collective-permute-done.40.grad_own_ref), channel_id=1, source_target_pairs={{0,4},{4,0},{1,5},{5,1},{2,6},{6,2},{3,7},{7,3},{8,12},{12,8},{9,1... | collective-permute-start | bytes 1572872 | tf_op jit(solution)/shard_map/ppermute | solution.py:518
  317.3 16.6 %collective-permute-start.39 = (bf16[128,2048]{1,0:T(8,128)(2,1)S(1)}, bf16[128,2048]{1,0:T(8,128)(2,1)S(1)}, u32[]{:S(2)}, u32[]{:S(2)}) collective-permute-start(bf16[128,2048]{1,0:T(8,128)(2,1)S(1)} %collective-permute-done.38.own_ref), channel_id=1, source_target_pairs={{0,4},{4,0},{1,5},{5,1},{2,6},{6,2},{3,7},{7,3},{8,12},{12,8},{9,1... | collective-permute-start | bytes 1572872 | tf_op jit(solution)/shard_map/ppermute | solution.py:518
  329.6 18.8 %collective-permute-start.37 = (bf16[128,2048]{1,0:T(8,128)(2,1)S(1)}, bf16[128,2048]{1,0:T(8,128)(2,1)S(1)}, u32[]{:S(2)}, u32[]{:S(2)}) collective-permute-start(bf16[128,2048]{1,0:T(8,128)(2,1)S(1)} %add_convert_fusion.4), channel_id=1, source_target_pairs={{0,3},{1,0},{2,1},{3,2},{4,7},{5,4},{6,5},{7,6},{8,11},{9,8},{10,9... | collective-permute-start | bytes 1572872 | tf_op jit(solution)/shard_map/ppermute | solution.py:523
  378.4 244.1 %reduce-scatter.4.cloned.1.call-start = ((), (), s32[]{:S(2)}) async-start(), calls=%async_computation.14 | async-start | bytes 5242880 | tf_op jit(solution)/shard_map/reduce_scatter | solution.py:710
  379.0 24.7 %all-to-all-start.3 = ((bf16[32,64,128]{2,1,0:T(8,128)(2,1)}), bf16[32,64,128]{2,1,0:T(8,128)(2,1)}, u32[]{:S(2)}, u32[]{:S(2)}) async-start(bf16[32,64,128]{2,1,0:T(8,128)(2,1)} %get-tuple-element.141), calls=%async_computation.3 | async-start | bytes 1048576 | tf_op jit(solution)/shard_map/all_to_all | solution.py:718
  382.4 240.1 %reduce-scatter.6.cloned.1.call-start = ((), (), s32[]{:S(2)}) async-start(), calls=%async_computation.15 | async-start | bytes 5242880 | tf_op jit(solution)/shard_map/reduce_scatter | solution.py:710
  407.6 16.0 %collective-permute-start.46 = (bf16[128,2048]{1,0:T(8,128)(2,1)}, bf16[128,2048]{1,0:T(8,128)(2,1)}, u32[]{:S(2)}, u32[]{:S(2)}) collective-permute-start(bf16[128,2048]{1,0:T(8,128)(2,1)} %get-tuple-element.144), channel_id=1, source_target_pairs={{0,4},{4,0},{1,5},{5,1},{2,6},{6,2},{3,7},{7,3},{8,12},{12,8},{9,1... | collective-permute-start | bytes 1572872 | tf_op jit(solution)/shard_map/ppermute | solution.py:518
  411.3 27.3 %collective-permute-start.45 = (bf16[128,2048]{1,0:T(8,128)(2,1)}, bf16[128,2048]{1,0:T(8,128)(2,1)}, u32[]{:S(2)}, u32[]{:S(2)}) collective-permute-start(bf16[128,2048]{1,0:T(8,128)(2,1)} %add_convert_fusion.6), channel_id=1, source_target_pairs={{0,3},{1,0},{2,1},{3,2},{4,7},{5,4},{6,5},{7,6},{8,11},{9,8},{10,9... | collective-permute-start | bytes 1572872 | tf_op jit(solution)/shard_map/ppermute | solution.py:523
  419.4 55.5 %all-to-all-start.5 = ((bf16[4,8,64,128]{3,1,2,0:T(8,128)(2,1)}), bf16[4,8,64,128]{3,1,2,0:T(8,128)(2,1)S(1)}, u32[]{:S(2)}, u32[]{:S(2)}) async-start(bf16[4,8,64,128]{3,1,2,0:T(8,128)(2,1)} %copy.45), calls=%async_computation.5 | async-start | bytes 1048576 | tf_op jit(solution)/shard_map/all_to_all | solution.py:691
  422.9 220.7 %reduce-scatter.8.cloned.1.call-start = ((), (), s32[]{:S(2)}) async-start(), calls=%async_computation.16 | async-start | bytes 5242880 | tf_op jit(solution)/shard_map/reduce_scatter | solution.py:710
  423.0 94.4 %collective-permute-start.50 = (bf16[128,2048]{1,0:T(8,128)(2,1)}, bf16[128,2048]{1,0:T(8,128)(2,1)}, u32[]{:S(2)}, u32[]{:S(2)}) collective-permute-start(bf16[128,2048]{1,0:T(8,128)(2,1)} %get-tuple-element.157), channel_id=1, source_target_pairs={{0,4},{4,0},{1,5},{5,1},{2,6},{6,2},{3,7},{7,3},{8,12},{12,8},{9,1... | collective-permute-start | bytes 1572872 | tf_op jit(solution)/shard_map/ppermute | solution.py:518
  423.0 56.5 %collective-permute-start.48 = (bf16[128,2048]{1,0:T(8,128)(2,1)}, bf16[128,2048]{1,0:T(8,128)(2,1)}, u32[]{:S(2)}, u32[]{:S(2)}) collective-permute-start(bf16[128,2048]{1,0:T(8,128)(2,1)} %get-tuple-element.153), channel_id=1, source_target_pairs={{0,4},{4,0},{1,5},{5,1},{2,6},{6,2},{3,7},{7,3},{8,12},{12,8},{9,1... | collective-permute-start | bytes 1572872 | tf_op jit(solution)/shard_map/ppermute | solution.py:518
  472.3 16.9 %collective-permute-start.47 = (bf16[128,2048]{1,0:T(8,128)(2,1)}, bf16[128,2048]{1,0:T(8,128)(2,1)}, u32[]{:S(2)}, u32[]{:S(2)}) collective-permute-start(bf16[128,2048]{1,0:T(8,128)(2,1)} %add_convert_fusion.2), channel_id=1, source_target_pairs={{0,3},{1,0},{2,1},{3,2},{4,7},{5,4},{6,5},{7,6},{8,11},{9,8},{10,9... | collective-permute-start | bytes 1572872 | tf_op jit(solution)/shard_map/ppermute | solution.py:523
  474.9 35.1 %all-to-all-start.4 = ((bf16[4,8,3,64,128]{4,3,2,1,0:T(8,128)(2,1)}), bf16[4,8,3,64,128]{4,3,2,1,0:T(8,128)(2,1)}, u32[]{:S(2)}, u32[]{:S(2)}) async-start(bf16[4,8,3,64,128]{4,3,2,1,0:T(8,128)(2,1)} %bitcast.189), calls=%async_computation.4 | async-start | bytes 3145728 | tf_op jit(solution)/shard_map/all_to_all | solution.py:750
  491.5 25.9 %collective-permute-start.49 = (bf16[128,2048]{1,0:T(8,128)(2,1)}, bf16[128,2048]{1,0:T(8,128)(2,1)}, u32[]{:S(2)}, u32[]{:S(2)}) collective-permute-start(bf16[128,2048]{1,0:T(8,128)(2,1)} %add_convert_fusion.1), channel_id=1, source_target_pairs={{0,3},{1,0},{2,1},{3,2},{4,7},{5,4},{6,5},{7,6},{8,11},{9,8},{10,9... | collective-permute-start | bytes 1572872 | tf_op jit(solution)/shard_map/ppermute | solution.py:523
  515.5 15.4 %collective-permute-start.65 = (bf16[256,384]{1,0:T(8,128)(2,1)S(1)}, bf16[256,384]{1,0:T(8,128)(2,1)S(1)}, u32[]{:S(2)}, u32[]{:S(2)}) collective-permute-start(bf16[256,384]{1,0:T(8,128)(2,1)S(1)} %get-tuple-element.191), channel_id=1, source_target_pairs={{0,8},{8,0},{16,24},{24,16},{1,9},{9,1},{17,25},{25,17},{2,10},{10... | collective-permute-start | bytes 589832 | tf_op jit(solution)/shard_map/ppermute | solution.py:527
  519.6 16.3 %collective-permute-start.64 = (bf16[256,384]{1,0:T(8,128)(2,1)S(1)}, bf16[256,384]{1,0:T(8,128)(2,1)S(1)}, u32[]{:S(2)}, u32[]{:S(2)}) collective-permute-start(bf16[256,384]{1,0:T(8,128)(2,1)S(1)} %get-tuple-element.190), channel_id=1, source_target_pairs={{0,8},{8,0},{16,24},{24,16},{1,9},{9,1},{17,25},{25,17},{2,10},{10... | collective-permute-start | bytes 589832 | tf_op jit(solution)/shard_map/ppermute | solution.py:527
  521.3 22.0 %collective-permute-start.67 = (bf16[256,384]{1,0:T(8,128)(2,1)S(1)}, bf16[256,384]{1,0:T(8,128)(2,1)S(1)}, u32[]{:S(2)}, u32[]{:S(2)}) collective-permute-start(bf16[256,384]{1,0:T(8,128)(2,1)S(1)} %get-tuple-element.193), channel_id=1, source_target_pairs={{0,16},{8,24},{16,0},{24,8},{1,17},{9,25},{17,1},{25,9},{2,18},{10... | collective-permute-start | bytes 589832 | tf_op jit(solution)/shard_map/ppermute | solution.py:527
  535.3 16.9 %collective-permute-start.51 = (bf16[128,2048]{1,0:T(8,128)(2,1)S(1)}, bf16[128,2048]{1,0:T(8,128)(2,1)S(1)}, u32[]{:S(2)}, u32[]{:S(2)}) collective-permute-start(bf16[128,2048]{1,0:T(8,128)(2,1)S(1)} %get-tuple-element.184), channel_id=1, source_target_pairs={{0,4},{4,0},{1,5},{5,1},{2,6},{6,2},{3,7},{7,3},{8,12},{12,8},{9,1... | collective-permute-start | bytes 1572872 | tf_op jit(solution)/shard_map/ppermute | solution.py:518
  535.3 113.7 %collective-permute-start.57 = (bf16[128,2048]{1,0:T(8,128)(2,1)}, bf16[128,2048]{1,0:T(8,128)(2,1)S(1)}, u32[]{:S(2)}, u32[]{:S(2)}) collective-permute-start(bf16[128,2048]{1,0:T(8,128)(2,1)} %get-tuple-element.185), channel_id=1, source_target_pairs={{0,4},{4,0},{1,5},{5,1},{2,6},{6,2},{3,7},{7,3},{8,12},{12,8},{9,1... | collective-permute-start | bytes 1572872 | tf_op jit(solution)/shard_map/ppermute | solution.py:518
  535.9 52.3 %collective-permute-start.53 = (bf16[128,2048]{1,0:T(8,128)(2,1)}, bf16[128,2048]{1,0:T(8,128)(2,1)S(1)}, u32[]{:S(2)}, u32[]{:S(2)}) collective-permute-start(bf16[128,2048]{1,0:T(8,128)(2,1)} %get-tuple-element.187), channel_id=1, source_target_pairs={{0,4},{4,0},{1,5},{5,1},{2,6},{6,2},{3,7},{7,3},{8,12},{12,8},{9,1... | collective-permute-start | bytes 1572872 | tf_op jit(solution)/shard_map/ppermute | solution.py:518
  554.4 33.2 %collective-permute-start.52 = (bf16[128,2048]{1,0:T(8,128)(2,1)}, bf16[128,2048]{1,0:T(8,128)(2,1)}, u32[]{:S(2)}, u32[]{:S(2)}) collective-permute-start(bf16[128,2048]{1,0:T(8,128)(2,1)} %bitcast_add_fusion.3), channel_id=1, source_target_pairs={{0,3},{1,0},{2,1},{3,2},{4,7},{5,4},{6,5},{7,6},{8,11},{9,8},{10,9... | collective-permute-start | bytes 1572872 | tf_op jit(solution)/shard_map/ppermute | solution.py:523
  563.7 19.2 %collective-permute-start.59 = (bf16[256,768]{1,0:T(8,128)(2,1)}, bf16[256,768]{1,0:T(8,128)(2,1)}, u32[]{:S(2)}, u32[]{:S(2)}) collective-permute-start(bf16[256,768]{1,0:T(8,128)(2,1)} %get-tuple-element.176), channel_id=1, source_target_pairs={{0,8},{8,0},{16,24},{24,16},{1,9},{9,1},{17,25},{25,17},{2,10},{10... | collective-permute-start | bytes 1179656 | tf_op jit(solution)/shard_map/ppermute | solution.py:527
  565.2 18.6 %collective-permute-start.62 = (bf16[256,768]{1,0:T(8,128)(2,1)}, bf16[256,768]{1,0:T(8,128)(2,1)}, u32[]{:S(2)}, u32[]{:S(2)}) collective-permute-start(bf16[256,768]{1,0:T(8,128)(2,1)} %get-tuple-element.177), channel_id=1, source_target_pairs={{0,16},{8,24},{16,0},{24,8},{1,17},{9,25},{17,1},{25,9},{2,18},{10... | collective-permute-start | bytes 1179656 | tf_op jit(solution)/shard_map/ppermute | solution.py:527
  566.8 25.1 %all-to-all-start.7 = ((bf16[8,64,384]{2,1,0:T(8,128)(2,1)}), bf16[8,64,384]{2,1,0:T(8,128)(2,1)S(1)}, u32[]{:S(2)}, u32[]{:S(2)}) async-start(bf16[8,64,384]{2,1,0:T(8,128)(2,1)} %fusion.14), calls=%async_computation.7 | async-start | bytes 786432 | tf_op jit(solution)/shard_map/all_to_all | solution.py:741
  583.8 27.1 %collective-permute-start.61 = (bf16[256,768]{1,0:T(8,128)(2,1)}, bf16[256,768]{1,0:T(8,128)(2,1)}, u32[]{:S(2)}, u32[]{:S(2)}) collective-permute-start(bf16[256,768]{1,0:T(8,128)(2,1)} %get-tuple-element.178), channel_id=1, source_target_pairs={{0,16},{8,24},{16,0},{24,8},{1,17},{9,25},{17,1},{25,9},{2,18},{10... | collective-permute-start | bytes 1179656 | tf_op jit(solution)/shard_map/ppermute | solution.py:527
  587.6 18.7 %collective-permute-start.60 = (bf16[256,768]{1,0:T(8,128)(2,1)}, bf16[256,768]{1,0:T(8,128)(2,1)}, u32[]{:S(2)}, u32[]{:S(2)}) collective-permute-start(bf16[256,768]{1,0:T(8,128)(2,1)} %get-tuple-element.179), channel_id=1, source_target_pairs={{0,16},{8,24},{16,0},{24,8},{1,17},{9,25},{17,1},{25,9},{2,18},{10... | collective-permute-start | bytes 1179656 | tf_op jit(solution)/shard_map/ppermute | solution.py:527
  588.3 22.6 %collective-permute-start.63 = (bf16[256,768]{1,0:T(8,128)(2,1)}, bf16[256,768]{1,0:T(8,128)(2,1)}, u32[]{:S(2)}, u32[]{:S(2)}) collective-permute-start(bf16[256,768]{1,0:T(8,128)(2,1)} %get-tuple-element.180), channel_id=1, source_target_pairs={{0,8},{8,0},{16,24},{24,16},{1,9},{9,1},{17,25},{25,17},{2,10},{10... | collective-permute-start | bytes 1179656 | tf_op jit(solution)/shard_map/ppermute | solution.py:527
  594.6 22.3 %collective-permute-start.55 = (bf16[128,2048]{1,0:T(8,128)(2,1)}, bf16[128,2048]{1,0:T(8,128)(2,1)}, u32[]{:S(2)}, u32[]{:S(2)}) collective-permute-start(bf16[128,2048]{1,0:T(8,128)(2,1)} %get-tuple-element.186), channel_id=1, source_target_pairs={{0,4},{4,0},{1,5},{5,1},{2,6},{6,2},{3,7},{7,3},{8,12},{12,8},{9,1... | collective-permute-start | bytes 1572872 | tf_op jit(solution)/shard_map/ppermute | solution.py:518
  613.4 38.3 %all-to-all-start.6 = ((bf16[8,64,768]{2,1,0:T(8,128)(2,1)}), bf16[8,64,768]{2,1,0:T(8,128)(2,1)S(1)}, u32[]{:S(2)}, u32[]{:S(2)}) async-start(bf16[8,64,768]{2,1,0:T(8,128)(2,1)} %fusion.2), calls=%async_computation.6 | async-start | bytes 1572864 | tf_op jit(solution)/shard_map/all_to_all | solution.py:741
  618.7 30.3 %collective-permute-start.56 = (bf16[128,2048]{1,0:T(8,128)(2,1)S(1)}, bf16[128,2048]{1,0:T(8,128)(2,1)S(1)}, u32[]{:S(2)}, u32[]{:S(2)}) collective-permute-start(bf16[128,2048]{1,0:T(8,128)(2,1)S(1)} %fusion.11), channel_id=1, source_target_pairs={{0,3},{1,0},{2,1},{3,2},{4,7},{5,4},{6,5},{7,6},{8,11},{9,8},{10,9... | collective-permute-start | bytes 1572872 | tf_op jit(solution)/shard_map/ppermute | solution.py:523
  (68 other events, 679.9 us)
Sparse Core Ops, SparseCore 0:
  9.6 64.3 all-gather.3
  90.0 73.6 all-gather.5
  378.5 61.6 all-gather.7
  443.0 68.2 reduce-scatter.3
  514.4 69.5 reduce-scatter.5
  586.8 56.7 reduce-scatter.7

commit v3 on v2

--- a/solution.py
+++ b/solution.py
@@ -13,7 +13,17 @@
 rope_base = 130000.0
 f32 = jnp.float32
 bf16 = jnp.bfloat16
-SHORT = pl.CostEstimate(flops=1000, bytes_accessed=1000, transcendentals=0)
+
+
+def lasting(microseconds):
+    return pl.CostEstimate(
+        flops=int(microseconds * 1.1e9), bytes_accessed=1000, transcendentals=0
+    )
+
+
+IN_VMEM = pl.BlockSpec(memory_space=pltpu.VMEM)
+IN_SMEM = pl.BlockSpec(memory_space=pltpu.SMEM)
+ANYWHERE = pl.BlockSpec(memory_space=pl.ANY)
 ALL = ("r", "p", "c", "z")
 GROUPS = ("r", "p")
 TENSOR = ("c", "z")
@@ -71,30 +81,33 @@
     lax.fori_loop(0, count, query_block, 0)
 
 
-def backward_kernel(
-    qkv_ref, grad_ref, out_ref, logsum_ref, result_ref,
-    keys, queries, values, grads, keys_t, queries_t, grads_t, deltas, grad_queries,
-    *, block, scale,
-):
+def backward_kernel(lower, upper, last, block, scale, *refs):
+    qkv_ref, grad_ref, out_ref, logsum_ref = refs[:4]
+    earlier, (result_ref, sums_ref) = refs[4:-11], refs[-11:-9]
+    keys, queries, values, grads, keys_t, queries_t, grads_t, deltas, grad_queries = refs[-9:]
     pieces, _, head_dim, rows = qkv_ref.shape
     per_block = block // rows
     count = pieces // per_block
-    for piece in range(pieces):
+    for piece in range(lower * per_block, pieces):
         number, part = divmod(piece, per_block)
         span = slice(part * rows, (part + 1) * rows)
         queries_t[number, :, span] = qkv_ref[piece, 0]
-        keys_t[number, :, span] = qkv_ref[piece, 1]
         queries[number, span, :] = qkv_ref[piece, 0].T
-        keys[number, span, :] = qkv_ref[piece, 1].T
-        values[number, span, :] = qkv_ref[piece, 2].T
+        if number < upper:
+            keys_t[number, :, span] = qkv_ref[piece, 1]
+            keys[number, span, :] = qkv_ref[piece, 1].T
+            values[number, span, :] = qkv_ref[piece, 2].T
         grad = grad_ref[piece]
         grads_t[number, :, span] = grad
         grads[number, span, :] = grad.T
         deltas[number, :, span] = jnp.sum(
             grad.astype(f32) * out_ref[piece].astype(f32), axis=0, keepdims=True
         )
-    for number in range(count):
-        grad_queries[number] = jnp.zeros((head_dim, block), f32)
+    for number in range(lower, count):
+        if number < upper:
+            grad_queries[number] = jnp.zeros((head_dim, block), f32)
+        else:
+            grad_queries[number] = earlier[1][number - upper]
 
     def step(i, j, carry, diagonal):
         grad_key, grad_value = carry
@@ -109,7 +122,7 @@
         grad_queries[i] = grad_queries[i] + contract(keys_t[j], grad_scores, 1, 0)
         return grad_key, grad_value
 
-    for j in range(count):
+    for j in range(lower, upper):
         zero = jnp.zeros((block, head_dim), f32)
         carry = step(j, j, (zero, zero), True)
         grad_key, grad_value = lax.fori_loop(
@@ -119,10 +132,19 @@
             span = slice(part * rows, (part + 1) * rows)
             result_ref[j * per_block + part, 1] = grad_key[span].T.astype(bf16)
             result_ref[j * per_block + part, 2] = grad_value[span].T.astype(bf16)
+    if not last:
+        for number in range(lower, count):
+            sums_ref[number - lower] = grad_queries[number]
+        for piece in range(lower * per_block, pieces):
+            result_ref[piece, 0] = jnp.zeros((head_dim, rows), bf16)
+        return
+    sums_ref[0] = jnp.zeros((head_dim, block), f32)
     for piece in range(pieces):
         number, part = divmod(piece, per_block)
         span = slice(part * rows, (part + 1) * rows)
         result_ref[piece, 0] = (grad_queries[number, :, span] * scale).astype(bf16)
+        if number >= upper:
+            result_ref[piece, 1:] = earlier[0][piece, 1:]
 
 
 def attend_forward(qkv, block):
@@ -142,38 +164,41 @@
         out_specs=(in_vmem, in_vmem),
         scratch_shapes=[by_rows, by_features, by_features],
         compiler_params=pltpu.CompilerParams(vmem_limit_bytes=56 * 2**20),
-        cost_estimate=SHORT,
+        cost_estimate=lasting(18),
         name="attend_forward",
     )(qkv)
 
 
-def attend_backward(qkv, grad, out, logsum, block):
+def attend_backward(qkv, grad, out, logsum, block, lower, upper, earlier=()):
     pieces, _, head_dim, rows = qkv.shape
     count = pieces * rows // block
-    pairs = count * (count + 1) // 2 * block * block
-    in_vmem = pl.BlockSpec(memory_space=pltpu.VMEM)
+    last = lower == 0
+    sums = 1 if last else count - lower
     by_rows = pltpu.VMEM((count, block, head_dim), bf16)
     by_features = pltpu.VMEM((count, head_dim, block), bf16)
     return pl.pallas_call(
-        functools.partial(backward_kernel, block=block, scale=head_dim**-0.5),
-        out_shape=jax.ShapeDtypeStruct(qkv.shape, bf16),
-        in_specs=[in_vmem] * 4,
-        out_specs=in_vmem,
+        functools.partial(backward_kernel, lower, upper, last, block, head_dim**-0.5),
+        out_shape=(
+            jax.ShapeDtypeStruct(qkv.shape, bf16),
+            jax.ShapeDtypeStruct((sums, head_dim, block), f32),
+        ),
+        in_specs=[IN_VMEM] * (4 + len(earlier)),
+        out_specs=(IN_VMEM, IN_VMEM),
         scratch_shapes=[by_rows] * 4
         + [by_features] * 3
         + [pltpu.VMEM((count, 1, block), f32), pltpu.VMEM((count, head_dim, block), f32)],
         compiler_params=pltpu.CompilerParams(vmem_limit_bytes=60 * 2**20),
-        cost_estimate=SHORT,
+        cost_estimate=lasting(18),
         name="attend_backward",
-    )(qkv, grad, out, logsum)
+    )(qkv, grad, out, logsum, *earlier)
 
 
 def start_pieces(refs, table, starts_ref, whole, semaphores):
     copies = []
-    for number, (which, first, rows) in enumerate(table):
+    for number, (which, first, rows, *column) in enumerate(table):
         start = pl.multiple_of(starts_ref[number], rows)
         copy = pltpu.make_async_copy(
-            refs[which].at[pl.ds(first, rows), pl.ds(0, whole.shape[1])],
+            refs[which].at[pl.ds(first, rows), pl.ds(sum(column), whole.shape[1])],
             whole.at[pl.ds(start, rows), :],
             semaphores.at[number],
         )
@@ -215,11 +240,6 @@
                     out_ref[head, first + part, kind, half:] = lower[:, lanes]
 
 
-IN_VMEM = pl.BlockSpec(memory_space=pltpu.VMEM)
-IN_SMEM = pl.BlockSpec(memory_space=pltpu.SMEM)
-ANYWHERE = pl.BlockSpec(memory_space=pl.ANY)
-
-
 def project(x_group, cosine, sine, pieces, table, starts, heads, head_dim, rows):
     tokens, width = x_group.shape
     columns = pieces[0].shape[1]
@@ -237,7 +257,7 @@
             pltpu.SemaphoreType.DMA((len(table),)),
         ],
         compiler_params=pltpu.CompilerParams(vmem_limit_bytes=48 * 2**20),
-        cost_estimate=SHORT,
+        cost_estimate=lasting(10),
         name="project",
     )(starts, x_group, cosine, sine, *pieces)
 
@@ -289,7 +309,7 @@
             pltpu.SemaphoreType.DMA((len(table),)),
         ],
         compiler_params=pltpu.CompilerParams(vmem_limit_bytes=48 * 2**20),
-        cost_estimate=SHORT,
+        cost_estimate=lasting(9),
         name="finish_attention",
     )(starts, x, attended, *pieces)
 
@@ -343,15 +363,12 @@
             pltpu.SemaphoreType.DMA((len(table),)),
         ],
         compiler_params=pltpu.CompilerParams(vmem_limit_bytes=48 * 2**20),
-        cost_estimate=SHORT,
+        cost_estimate=lasting(6),
         name="back_to_attention",
     )(starts, mid, grad, cotangent, gain, *pieces)
 
 
-def grads_kernel(count, table, starts_ref, spots_ref, grad_ref, cosine_ref, sine_ref, *refs):
-    pieces, (low_ref, keep_ref, send_ref) = refs[:count], refs[-6:-3]
-    weight, by_tokens, semaphores = refs[-3:]
-    copies = start_pieces(pieces, table, starts_ref, weight, semaphores)
+def turn_back_kernel(grad_ref, cosine_ref, sine_ref, unit_ref, by_tokens_ref, out_ref, low):
     heads, blocks, _, head_dim, rows = grad_ref.shape
     half = head_dim // 2
     for block in range(blocks):
@@ -367,45 +384,154 @@
                     grad = jnp.concatenate(
                         [upper * cosine + lower * sine, lower * cosine - upper * sine]
                     ).astype(bf16)
-                low_ref[at : at + head_dim, span] = grad
-        by_tokens[block] = low_ref[:, span].T
+                low[at : at + head_dim, span] = grad
+        by_tokens_ref[block] = low[:, span].T
+    width = out_ref.shape[0]
+    cut = min(512, width)
+    for start in range(0, width, cut):
+        out_ref[start : start + cut] = contract(
+            unit_ref[:, start : start + cut], low[...], 0, 1
+        ).astype(bf16)
+
+
+def turn_back(grad, cosine, sine, unit_group):
+    heads, blocks, _, head_dim, rows = grad.shape
+    columns = 3 * heads * head_dim
+    return pl.pallas_call(
+        turn_back_kernel,
+        out_shape=(
+            jax.ShapeDtypeStruct((blocks, rows, columns), bf16),
+            jax.ShapeDtypeStruct((unit_group.shape[1], columns), bf16),
+        ),
+        in_specs=[IN_VMEM] * 4,
+        out_specs=(IN_VMEM,) * 2,
+        scratch_shapes=[pltpu.VMEM((columns, blocks * rows), bf16)],
+        compiler_params=pltpu.CompilerParams(vmem_limit_bytes=48 * 2**20),
+        cost_estimate=lasting(8),
+        name="turn_back",
+    )(grad, cosine, sine, unit_group)
+
+
+def norm_kernel(count, table, starts_ref, spots_ref, by_tokens_ref, *refs):
+    pieces, outs, (weight, semaphores) = refs[:count], refs[count:-2], refs[-2:]
+    copies = start_pieces(pieces, table, starts_ref, weight, semaphores)
+    rows = by_tokens_ref.shape[1]
+    steps = len(outs) // 2
     for copy in copies:
         copy.wait()
     width = weight.shape[0]
     cut = min(1024, width)
-    for step in range(keep_ref.shape[0]):
+    for step in range(steps):
         tokens = jnp.concatenate(
-            [by_tokens[spots_ref[2 * step]], by_tokens[spots_ref[2 * step + 1]]]
+            [by_tokens_ref[spots_ref[2 * step]], by_tokens_ref[spots_ref[2 * step + 1]]]
         )
         for start in range(0, width, cut):
             part = contract(tokens, weight[start : start + cut], 1, 1)
-            keep_ref[step, :, start : start + cut] = part[:rows]
-            send_ref[step, :, start : start + cut] = part[rows:].astype(bf16)
-
-
-def back_to_norm(grad, cosine, sine, pieces, table, starts, spots):
-    heads, blocks, _, head_dim, rows = grad.shape
-    columns = pieces[0].shape[1]
-    width = HEADS * head_dim
+            outs[step][:, start : start + cut] = part[:rows]
+            outs[steps + step][:, start : start + cut] = part[rows:].astype(bf16)
+
+
+def back_to_norm(by_tokens, pieces, table, starts, spots, width):
+    _, rows, columns = by_tokens.shape
     steps = spots.shape[0] // 2
-    return pl.pallas_call(
-        functools.partial(grads_kernel, len(pieces), table),
-        out_shape=(
-            jax.ShapeDtypeStruct((columns, blocks * rows), bf16),
-            jax.ShapeDtypeStruct((steps, rows, width), f32),
-            jax.ShapeDtypeStruct((steps, rows, width), bf16),
-        ),
-        in_specs=[IN_SMEM] * 2 + [IN_VMEM] * 3 + [ANYWHERE] * len(pieces),
-        out_specs=(IN_VMEM,) * 3,
+    made = pl.pallas_call(
+        functools.partial(norm_kernel, len(pieces), table),
+        out_shape=(jax.ShapeDtypeStruct((rows, width), f32),) * steps
+        + (jax.ShapeDtypeStruct((rows, width), bf16),) * steps,
+        in_specs=[IN_SMEM] * 2 + [IN_VMEM] + [ANYWHERE] * len(pieces),
+        out_specs=(IN_VMEM,) * (2 * steps),
         scratch_shapes=[
             pltpu.VMEM((width, columns), bf16),
-            pltpu.VMEM((blocks, rows, columns), bf16),
             pltpu.SemaphoreType.DMA((len(table),)),
         ],
         compiler_params=pltpu.CompilerParams(vmem_limit_bytes=48 * 2**20),
-        cost_estimate=SHORT,
+        cost_estimate=lasting(7),
         name="back_to_norm",
-    )(starts, spots, grad, cosine, sine, *pieces)
+    )(starts, spots, by_tokens, *pieces)
+    return made[:steps], made[steps:]
+
+
+def weight_sums_kernel(
+    sums_ref, out_sums_ref, weight_ref, gain_ref, qkv_ref, out_ref, one_ref, two_ref
+):
+    parts, rows, _ = sums_ref.shape
+    kinds = 3
+    width = out_ref.shape[1]
+    features = width // parts
+    gain = gain_ref[...]
+    one = jnp.zeros((rows, 128), f32)
+    two = jnp.zeros((rows, 128), f32)
+    for part in range(parts):
+        for kind in range(kinds):
+            total = sums_ref[part, :, kind * features : (kind + 1) * features].astype(f32)
+            at = slice(kind * width + part * features, kind * width + (part + 1) * features)
+            qkv_ref[:, at] = gain * total
+            product = total * weight_ref[:, at].astype(f32)
+            for lanes in range(0, features, 128):
+                one = one + product[:, lanes : lanes + 128]
+        out_ref[:, part * features : (part + 1) * features] = out_sums_ref[
+            part, :, :features
+        ].astype(f32)
+        two = two + out_sums_ref[part, :, features:].astype(f32)
+    one_ref[...] = jnp.sum(one, axis=1, keepdims=True)
+    two_ref[...] = jnp.sum(two, axis=1, keepdims=True)
+
+
+def weight_sums(sums, out_sums, attn_qkv, gain):
+    parts, rows, columns = sums.shape
+    width = parts * columns // 3
+    qkv, out, one, two = pl.pallas_call(
+        weight_sums_kernel,
+        out_shape=(
+            jax.ShapeDtypeStruct((rows, 3 * width), f32),
+            jax.ShapeDtypeStruct((rows, width), f32),
+            jax.ShapeDtypeStruct((rows, 1), f32),
+            jax.ShapeDtypeStruct((rows, 1), f32),
+        ),
+        in_specs=[IN_VMEM] * 4,
+        out_specs=(IN_VMEM,) * 4,
+        compiler_params=pltpu.CompilerParams(vmem_limit_bytes=32 * 2**20),
+        cost_estimate=lasting(3),
+        name="weight_sums",
+    )(sums, out_sums, attn_qkv, gain)
+    return qkv, out, one[:, 0], two[:, 0]
+
+
+def out_product_kernel(spots_ref, attended_ref, gain_ref, *refs):
+    blocks, (out_ref, grads, attended) = refs[:-3], refs[-3:]
+    heads, _, head_dim, rows = attended_ref.shape
+    width = grads.shape[1]
+    for number, block in enumerate(blocks):
+        grads[pl.ds(pl.multiple_of(spots_ref[number] * rows, rows), rows), :] = block[...]
+        for head in range(heads):
+            attended[
+                head * head_dim : (head + 1) * head_dim, number * rows : (number + 1) * rows
+            ] = attended_ref[head, number]
+    columns = heads * head_dim
+    out_ref[:, :columns] = contract(grads[...], attended[...], 0, 1).astype(bf16)
+    gain = jnp.broadcast_to(gain_ref[...], (128, width)).T
+    high = gain.astype(bf16).astype(f32)
+    lanes = lax.broadcasted_iota(jnp.int32, gain.shape, 1)
+    gain = jnp.where(lanes == 0, high, jnp.where(lanes == 1, gain - high, 0.0))
+    out_ref[:, columns:] = gain.astype(bf16)
+
+
+def out_product(blocks, spots, attended, gain):
+    rows, width = blocks[0].shape
+    heads, count, head_dim, _ = attended.shape
+    return pl.pallas_call(
+        out_product_kernel,
+        out_shape=jax.ShapeDtypeStruct((width, heads * head_dim + 128), bf16),
+        in_specs=[IN_SMEM] + [IN_VMEM] * (2 + len(blocks)),
+        out_specs=IN_VMEM,
+        scratch_shapes=[
+            pltpu.VMEM((count * rows, width), bf16),
+            pltpu.VMEM((heads * head_dim, count * rows), bf16),
+        ],
+        compiler_params=pltpu.CompilerParams(vmem_limit_bytes=48 * 2**20),
+        cost_estimate=lasting(5),
+        name="out_product",
+    )(spots, attended, gain, *blocks)
 
 
 def units_kernel(counts, tables, own_ref, other_ref, grad_own_ref, grad_other_ref, *refs):
@@ -458,7 +584,7 @@
     arrays = [array for pieces, _, _ in weights for array in pieces]
     counts = tuple(len(pieces) for pieces, _, _ in weights)
     tables = tuple(table for _, table, _ in weights)
-    units = sum(taken for _, _, taken in tables[0])
+    units = sum(entry[2] for entry in tables[0])
     whole = pl.BlockSpec((rows, width), lambda i: (0, 0))
     kept_units = pl.BlockSpec((1, 2 * rows, units), lambda i: (step, 0, 0))
     kept_rows = pl.BlockSpec((1, 2 * rows, width), lambda i: (step, 0, 0))
@@ -475,32 +601,34 @@
         + [pltpu.SemaphoreType.DMA((len(table),)) for table in tables],
         input_output_aliases={7 + len(arrays) + i: i for i in range(len(held))},
         compiler_params=pltpu.CompilerParams(vmem_limit_bytes=56 * 2**20),
-        cost_estimate=SHORT,
+        cost_estimate=lasting(13),
         name="units_chunk",
     )(own, other, grad_own, grad_other, *[starts for _, _, starts in weights], *arrays, *held)
 
 
-def transposed_product_kernel(left_ref, right_ref, out_ref):
-    out_ref[...] = contract(left_ref[...], right_ref[...], 0, 0).astype(bf16)
-
-
-def transposed_product(left, right):
+def transposed_product_kernel(left_ref, right_ref, *refs):
+    refs[-1][...] = contract(left_ref[...], right_ref[...], 0, 0).astype(bf16)
+
+
+def transposed_product(left, right, held=(), place=0, count=1):
     depth, units = left.shape
     width = right.shape[1]
     cut = min(256, units)
     return pl.pallas_call(
         transposed_product_kernel,
         grid=(units // cut,),
-        out_shape=jax.ShapeDtypeStruct((units, width), bf16),
+        out_shape=jax.ShapeDtypeStruct((units, count * width), bf16),
         in_specs=[
             pl.BlockSpec((depth, cut), lambda i: (0, i)),
             pl.BlockSpec((depth, width), lambda i: (0, 0)),
-        ],
-        out_specs=pl.BlockSpec((cut, width), lambda i: (i, 0)),
+        ]
+        + [ANYWHERE] * len(held),
+        out_specs=pl.BlockSpec((cut, width), lambda i: (i, place)),
+        input_output_aliases={2 + i: 0 for i in range(len(held))},
         compiler_params=pltpu.CompilerParams(vmem_limit_bytes=48 * 2**20),
-        cost_estimate=SHORT,
+        cost_estimate=lasting(9),
         name="transposed_product",
-    )(left, right)
+    )(left, right, *held)
 
 
 def rotary_tables(positions, head_dim):
@@ -508,6 +636,10 @@
     frequency = rope_base ** (-(jnp.arange(half_dim, dtype=f32) * 2.0) / head_dim)
     angles = positions.astype(f32)[None, :] * frequency[:, None]
     return jnp.cos(angles), jnp.sin(angles)
+
+
+def together(*arrays):
+    return lax.optimization_barrier(arrays)
 
 
 def after(array, *others):
@@ -541,35 +673,27 @@
     return chunks
 
 
-def add_over_line(parts, starts=(), fills=()):
-    count = lax.axis_size("z")
-    total = parts[1 % count]
-    for step in range(2, count + 1):
-        send = total.astype(bf16)
-        if step - 2 < len(starts):
-            send = after(send, starts[step - 2])
-        came = from_next(send)
-        if step - 2 < len(fills):
-            came = after(came, fills[step - 2])
-        total = came.astype(f32) + parts[step % count]
-    return total
-
-
 def add_over_cores(keep, send):
     return keep + swap_cores(send.astype(bf16)).astype(f32)
 
 
-def group_pieces(block, before_corner=()):
+def near_pieces(block):
     if not square_groups():
-        whole = lax.all_gather(block, GROUPS, axis=0)
-        return [(whole[group], group, 0) for group in range(whole.shape[0])]
+        return lax.all_gather(block, GROUPS, axis=0)
+    return block, from_flipped(block, 1), from_flipped(block, 2)
+
+
+def group_pieces(near):
+    if not square_groups():
+        return [(near[group], group, 0) for group in range(near.shape[0])]
+    block, beside, across = near
     half = block.shape[0] // 2
     place = lax.axis_index("p")
-    beside, across = from_flipped(block, 1), from_flipped(block, 2)
-    near = [(block, place, 0), (beside, place ^ 1, 0), (across, place ^ 2, 0)]
-    top, low = after((beside[:half], across[half:]), before_corner)
-    top, low = from_flipped(top, 2), from_flipped(low, 1)
-    return [*near, (top, place ^ 3, 0), (low, place ^ 3, half)]
+    top, low = from_flipped(beside[:half], 2), from_flipped(across[half:], 1)
+    return [
+        (block, place, 0), (beside, place ^ 1, 0), (across, place ^ 2, 0),
+        (top, place ^ 3, 0), (low, place ^ 3, half),
+    ]
 
 
 def placed(pieces, rows):
@@ -578,32 +702,42 @@
     return [array for array, _, _ in pieces], table, jnp.stack(starts).astype(jnp.int32)
 
 
-def scatter_groups(parts):
+def group_parts(whole):
+    parts = whole.reshape(lax.axis_size("r") * lax.axis_size("p"), -1, whole.shape[1])
+    if not square_groups():
+        return parts
+    place = lax.axis_index("p")
+    return [lax.dynamic_index_in_dim(parts, place ^ bits, 0, keepdims=False) for bits in range(4)]
+
+
+def scatter_first(parts):
+    if not square_groups():
+        return ()
+    _, beside, across, corner = parts
+    half = corner.shape[0] // 2
+    return (
+        from_flipped(jnp.concatenate([corner[:half], beside[:half]]), 1),
+        from_flipped(jnp.concatenate([corner[half:], across[half:]]), 2),
+    )
+
+
+def scatter_second(parts, first):
     if not square_groups():
         flat = parts.reshape(-1, parts.shape[-1])
-        return lax.psum_scatter(flat, GROUPS, scatter_dimension=0, tiled=True).astype(f32)
-    half = parts.shape[1] // 2
-    place = lax.axis_index("p")
-    own, beside, across, corner = (
-        lax.dynamic_index_in_dim(parts, place ^ bits, 0, keepdims=False) for bits in range(4)
-    )
-    to_across = from_flipped(corner[:half], 1)
-    to_beside = from_flipped(corner[half:], 2)
-    total_top = from_flipped(beside[:half], 1).astype(f32)
-    total_low = from_flipped(across[half:], 2).astype(f32)
-    beside_low = (beside[half:].astype(f32) + to_beside.astype(f32)).astype(bf16)
-    across_top = (across[:half].astype(f32) + to_across.astype(f32)).astype(bf16)
-    total_low = total_low + from_flipped(beside_low, 1).astype(f32)
-    total_top = total_top + from_flipped(across_top, 2).astype(f32)
-    return own.astype(f32) + jnp.concatenate([total_top, total_low])
-
-
-def ring(block, starts=()):
-    blocks = [block]
-    for step in range(lax.axis_size("z") - 1):
-        send = after(blocks[-1], starts[step]) if step < len(starts) else blocks[-1]
-        blocks.append(from_next(send))
-    return blocks
+        return lax.psum_scatter(flat, GROUPS, scatter_dimension=0, tiled=True)
+    own, beside, across, corner = parts
+    half = corner.shape[0] // 2
+    from_beside, from_across = (array.astype(f32) for array in first)
+    beside_low = (beside[half:].astype(f32) + from_across[:half]).astype(bf16)
+    across_top = (across[:half].astype(f32) + from_beside[:half]).astype(bf16)
+    total_low = from_across[half:] + from_flipped(beside_low, 1).astype(f32)
+    total_top = from_beside[half:] + from_flipped(across_top, 2).astype(f32)
+    return (own.astype(f32) + jnp.concatenate([total_top, total_low])).astype(bf16)
+
+
+def to_owners(own):
+    count = lax.axis_size(TENSOR)
+    return lax.all_to_all(own.reshape(count, -1, own.shape[1]), TENSOR, 0, 0)
 
 
 def shards(tokens, attn_qkv, attn_out_t, mlp_weight, norm1, norm2, cotangent):
@@ -630,26 +764,41 @@
     scaled_qkv = (attn_qkv.astype(f32) * gain_one).astype(bf16)
     qkv_cut = scaled_qkv.reshape(weight_rows, 3, tensor_count, features_here).transpose(2, 0, 1, 3)
     qkv_cut = qkv_cut.reshape(tensor_count, weight_rows, 3 * features_here)
+    gain_columns = jnp.pad(norm2[:, None], ((0, 0), (0, 127)))
+    out_near = near_pieces(jnp.concatenate([attn_out_t, gain_columns], axis=1))
+    gate_near = near_pieces(mlp_weight[:, :width])
+    unit_rows = mlp_weight.shape[0]
     qkv_part = lax.all_to_all(qkv_cut, TENSOR, 0, 0).reshape(-1, 3 * features_here)
+    qkv_part, out_near, gate_near = together(qkv_part, out_near, gate_near)
     qkv_rows = qkv_part.shape[0]
-    qkv_arrays, qkv_table, qkv_starts = placed(group_pieces(qkv_part), qkv_rows)
-    gain_columns = jnp.pad(norm2[:, None], ((0, 0), (0, 127)))
-    out_pieces = group_pieces(jnp.concatenate([attn_out_t, gain_columns], axis=1), qkv_part)
-    unit_rows = mlp_weight.shape[0]
-    gate_weight = placed(group_pieces(mlp_weight[:, :width], qkv_arrays), unit_rows)
-    down_weight = placed(group_pieces(mlp_weight[:, 2 * width :], qkv_arrays), unit_rows)
-    up_whole = lax.all_gather(
-        after(mlp_weight[:, width : 2 * width], qkv_arrays), GROUPS, axis=0, tiled=True
-    )
-    up_weight = ([up_whole], ((0, 0, up_whole.shape[0]),), jnp.zeros((1,), jnp.int32))
+    qkv_arrays, qkv_table, qkv_starts = placed(group_pieces(near_pieces(qkv_part)), qkv_rows)
+    out_pieces = group_pieces(out_near)
+    out_plane = jnp.concatenate([array for array, _, _ in out_pieces])
+    qkv_arrays, x_group, gate_near, out_plane = together(
+        qkv_arrays, x_group, gate_near, out_plane
+    )
 
     positions = device_index * rows + jnp.arange(group_rows)
     cosine, sine = rotary_tables(positions, head_dim)
     unit_group, stacked = project(
         x_group, cosine, sine, qkv_arrays, qkv_table, qkv_starts, heads_here, head_dim, rows
     )
+    gate_weight = placed(group_pieces(gate_near), unit_rows)
+    stacked, gate_arrays, later = together(stacked, gate_weight[0], from_next(out_plane))
+    gate_weight = (gate_arrays, *gate_weight[1:])
+    out_ring = [out_plane, later]
+    swapped = [swap_cores(array) for array in after(out_ring, stacked)]
     qkv = lax.all_to_all(stacked, "p", 0, 0)
+    qkv, later, swapped = together(qkv, from_next(out_ring[-1]), swapped)
     qkv = qkv.reshape(-1, 3, head_dim, rows)
+    out_ring.append(later)
+    rest_whole = lax.all_gather(
+        after(mlp_weight[:, width:], x_group), GROUPS, axis=0, tiled=True
+    )
+    up_weight, down_weight = (
+        ([rest_whole], ((0, 0, rest_whole.shape[0], column),), jnp.zeros((1,), jnp.int32))
+        for column in (0, width)
+    )
 
     def over_shares(array):
         return lax.all_gather(array, "r", axis=0, tiled=True) if share_count > 1 else array
@@ -661,14 +810,16 @@
         return lax.dynamic_slice_in_dim(array, share * pieces, pieces, 0)
 
     qkv = over_shares(qkv)
+    rest = [out_ring[-1]]
+    for _ in range(line_count - 3):
+        rest.append(from_next(rest[-1]))
+    swapped.append(swap_cores(out_ring[-1]))
     attended, logsum = attend_forward(qkv, block)
+    attended, rest, swapped = together(attended, rest[1:], swapped)
+    out_ring += rest
+    swapped += [swap_cores(array) for array in rest]
     attended_head = own_share(attended)
 
-    out_plane = jnp.concatenate([array for array, _, _ in out_pieces])
-    grad_out_ring = ring(cotangent, (x_group,))[:2]
-    out_ring = ring(out_plane, (grad_out_ring[-1], stacked, qkv))
-    out_arrays = out_ring + [swap_cores(array) for array in out_ring[:-1]]
-    out_arrays.append(swap_cores(after(out_ring[-1], attended)))
     out_table, out_starts = [], []
     for which in range(2 * line_count):
         side = core if which < line_count else 1 - core
@@ -680,28 +831,45 @@
             out_starts.append(spot * weight_rows + offset)
             first += array.shape[0]
     out_table, out_starts = tuple(out_table), jnp.stack(out_starts).astype(jnp.int32)
-    grad_out_ring += ring(after(grad_out_ring[-1], out_ring[-1]), ((),))[1 : line_count - 1]
-    grad_out_chunks = [(block, swap_cores(block)) for block in grad_out_ring]
 
     attended_local = lax.all_to_all(attended_head, ("p", "c", "z"), 0, 0)
+    later = from_next(after(cotangent, attended))
+    attended_local, swapped = together(attended_local, swapped)
+    out_weight = (out_ring + swapped, out_table, out_starts)
+    grad_out_ring = [cotangent, later, from_next(after(later, attended_local))]
     middle, normed_two, gain_two = finish_attention(
-        tokens, attended_local, out_arrays, out_table, out_starts, HEADS // tensor_count
-    )
+        tokens, attended_local, *out_weight, HEADS // tensor_count
+    )
+    normed_two, grad_out_ring = together(normed_two, grad_out_ring)
     attended_group = attended_head.reshape(group_count, tensor_count, head_dim, rows)
     attended_group = lax.all_to_all(after(attended_group, normed_two), "p", 0, 0)
 
-    held, normed_parts, branch_parts = (), [], []
-    normed = normed_two
+    held, branch_parts = (), []
+    normed, grad_out, came, total = normed_two, grad_out_ring[0], (), None
     for step in range(line_count):
-        later = from_next(normed) if step < line_count - 1 else None
+        later = from_next(normed) if step < line_count - 1 else ()
+        if step < line_count - 3:
+            grad_out_ring.append(from_next(grad_out_ring[-1]))
+        if step >= 2:
+            came = from_next(total.astype(bf16))
         *held, keep, send, branch_keep, branch_send = units_chunk(
-            step, line_count, normed, swap_cores(normed), *grad_out_chunks[step],
+            step, line_count, normed, swap_cores(normed), grad_out, swap_cores(grad_out),
             (gate_weight, up_weight, down_weight), held,
         )
-        normed_parts.append(add_over_cores(keep, send))
         branch_parts.append((branch_keep, branch_send))
-        if later is not None:
-            normed = after(later, keep)
+        if step == 0:
+            later, attended_group, keep, send = together(later, attended_group, keep, send)
+        else:
+            later, came, keep, send = together(later, came, keep, send)
+        keep, grad_out_ring = together(keep, grad_out_ring)
+        part = add_over_cores(keep, send)
+        normed = later
+        if step < line_count - 1:
+            grad_out = grad_out_ring[step + 1]
+        if step == 0:
+            own_part = part
+        else:
+            total = part if step == 1 else came.astype(f32) + part
     activation, gate_grads, up_grads, normed_group, grad_out_group = (
         array.reshape(group_rows, -1) for array in held
     )
@@ -709,71 +877,97 @@
     def over_groups(part):
         return lax.psum_scatter(part, GROUPS, scatter_dimension=0, tiled=True)
 
-    gate_term = transposed_product(gate_grads, normed_group)
-    grad_normed = add_over_line(normed_parts, fills=((), (), gate_term))
+    gate_term = transposed_product(after(gate_grads, total), normed_group)
+    came, gate_term = together(from_next(total.astype(bf16)), gate_term)
+    grad_normed = came.astype(f32) + own_part
     grad_middle, grad_mid_low, norm_two_part, grad_attended = back_to_attention(
-        middle, grad_normed, cotangent, gain_two, out_arrays, out_table, out_starts,
+        middle, grad_normed, cotangent, gain_two, *out_weight,
         HEADS // tensor_count, head_dim,
     )
     grad_head = lax.all_to_all(grad_attended, ("p", "c", "z"), 0, 0)
     up_grads, activation = after((up_grads, activation), grad_attended)
     up_term = transposed_product(up_grads, normed_group)
     down_term = transposed_product(activation, grad_out_group)
-    grad_head = after(grad_head, up_term, down_term)
-
-    grad_qkv_head = attend_backward(qkv, over_shares(grad_head), attended, logsum, block)
+    grad_head, up_term, down_term = together(grad_head, up_term, down_term)
+
+    grad_head = over_shares(grad_head)
+    count = qkv.shape[0] * rows // block
+    backward = functools.partial(attend_backward, qkv, grad_head, attended, logsum, block)
+    later_keys = backward(count // 2, count)
+    grad_mid_ring = [grad_mid_low, from_next(after(grad_mid_low, grad_head))]
+    branch_came = [swap_cores(part[1]) for part in after(branch_parts, grad_head)]
+    later_keys, grad_mid_ring, branch_came = together(later_keys, grad_mid_ring, branch_came)
+
+    def branch_sum(came, step):
+        return came + branch_parts[step][0] + branch_came[step].astype(f32)
+
+    grad_qkv_head = backward(0, count // 2, later_keys)[0]
+    for _ in range(line_count - 3):
+        grad_mid_ring.append(from_next(grad_mid_ring[-1]))
+    came = from_next(after(branch_sum(0.0, 1 % line_count).astype(bf16), later_keys))
+    mid_swapped = [swap_cores(array) for array in grad_mid_ring[:2]]
+    grad_qkv_head, grad_mid_ring, came, mid_swapped = together(
+        grad_qkv_head, grad_mid_ring, came, mid_swapped
+    )
     grad_qkv_head = own_share(grad_qkv_head)
-    branch = add_over_line(
-        [add_over_cores(*part) for part in branch_parts],
-        starts=(grad_attended, grad_head, grad_qkv_head),
-    )
-    result = (middle + branch).astype(bf16)
-
-    grad_gate_w = over_groups(gate_term)
-    grad_mid_group = lax.all_gather(after(grad_mid_low, gate_term), TENSOR, axis=0, tiled=True)
-    grad_up_w = over_groups(after(up_term, grad_head))
-    grad_down_w = over_groups(after(down_term, grad_head))
-
-    def to_owners(part, start=()):
-        columns = part.shape[1]
-        parts = after(part.astype(bf16), start).reshape(share_count * group_count, -1, columns)
-        own = scatter_groups(parts).astype(bf16)
-        own = lax.all_to_all(own.reshape(tensor_count, -1, columns), TENSOR, 0, 0)
-        return own.astype(f32)
-
-    attended_group = jnp.swapaxes(attended_group, 1, 2).reshape(features_here, group_rows)
-    out_term = contract(grad_mid_group, attended_group, 0, 1)
-    norm_two_part = norm_two_part[0]
-    norm_high = norm_two_part.astype(bf16).astype(f32)
-    norm_columns = jnp.stack([norm_high, norm_two_part - norm_high], axis=1)
+    grad_gate_w, grad_up_w = over_groups(gate_term), over_groups(up_term)
+
+    spots = jnp.stack([spot for step in range(line_count) for spot in chunk_places(step)])
+    spots = spots.astype(jnp.int32)
     grad_qkv_rows = grad_qkv_head.reshape(group_count, tensor_count, 3, head_dim, rows)
     grad_qkv_rows = lax.all_to_all(grad_qkv_rows, "p", 0, 0)
-    grad_qkv_rows = after(grad_qkv_rows, out_term)
-    out_sum = to_owners(
-        jnp.concatenate([out_term, jnp.pad(norm_columns, ((0, 0), (0, 126)))], axis=1),
-        grad_qkv_rows,
-    )
-    grad_out_w = out_sum[:, :, :features_here].transpose(1, 0, 2).reshape(-1, width)
-    grad_norm_two = jnp.sum(out_sum[:, :, features_here : features_here + 2], axis=(0, 2))
-    spots = [spot for step in range(line_count) for spot in chunk_places(step)]
-    grad_qkv_low, keep, send = back_to_norm(
-        grad_qkv_rows, cosine, sine, qkv_arrays, qkv_table, qkv_starts,
-        jnp.stack(spots).astype(jnp.int32),
-    )
-    weighted_parts = [add_over_cores(keep[step], send[step]) for step in range(line_count)]
-    qkv_term = contract(unit_group, after(grad_qkv_low, weighted_parts[1]), 0, 1).astype(bf16)
-    weighted_one = add_over_line(weighted_parts, fills=(qkv_term,))
+    mid_swapped += [swap_cores(array) for array in grad_mid_ring[2:]]
+    grad_mid_ring.append(from_next(grad_mid_ring[-1]))
+    for step in range(2, line_count - 1):
+        came = from_next(branch_sum(came.astype(f32), step).astype(bf16))
+    grad_qkv_rows, grad_mid_ring, came, mid_swapped = together(
+        grad_qkv_rows, grad_mid_ring, came, mid_swapped
+    )
+    branch_last = branch_sum(came.astype(f32), line_count - 1) if line_count > 2 else came
+    branch_last = from_next(branch_last.astype(bf16))
+    mid_swapped.append(swap_cores(grad_mid_ring[-1]))
+    grad_qkv_low, qkv_term = turn_back(grad_qkv_rows, cosine, sine, unit_group)
+    qkv_parts = group_parts(qkv_term)
+    qkv_first = scatter_first(qkv_parts)
+    keep, send = back_to_norm(
+        after(grad_qkv_low, qkv_parts), qkv_arrays, qkv_table, qkv_starts, spots, width
+    )
+    keep, send, branch_last, mid_swapped = together(keep, send, branch_last, mid_swapped)
+    total = add_over_cores(keep[1 % line_count], send[1 % line_count])
+    came = from_next(total.astype(bf16))
+    swapped = [swap_cores(send[step]) for step in range(2, line_count)]
+    grad_mid_blocks = [
+        part for pair in zip(grad_mid_ring, mid_swapped, strict=True) for part in pair
+    ]
+    out_term = out_product(grad_mid_blocks, spots, attended_group, norm_two_part)
+    came, swapped, qkv_first, out_term = together(came, swapped, qkv_first, out_term)
+    total = came.astype(f32) + keep[2 % line_count] + swapped[0].astype(f32)
+    came = from_next(total.astype(bf16))
+    out_parts = group_parts(out_term)
+    out_first = scatter_first(out_parts)
+    qkv_own = scatter_second(qkv_parts, qkv_first)
+    came, qkv_own, out_first = together(came, qkv_own, out_first)
+    qkv_sums = to_owners(qkv_own)
+    grad_down_w = over_groups(after(down_term, qkv_own))
+    for step in range(3, line_count):
+        total = came.astype(f32) + keep[step] + swapped[step - 2].astype(f32)
+        came = from_next(total.astype(bf16))
+    swapped = swap_cores(after(send[0], qkv_own))
+    out_own = scatter_second(out_parts, out_first)
+    came, swapped, out_own = together(came, swapped, out_own)
+    weighted_one = came.astype(f32) + keep[0] + swapped.astype(f32)
+    out_sums = to_owners(after(out_own, qkv_sums))
+    grad_mlp = jnp.concatenate([grad_gate_w, grad_up_w, grad_down_w], axis=1).astype(f32)
+    result = (middle + branch_sum(branch_last.astype(f32), 0)).astype(bf16)
     factor_one = lax.rsqrt(jnp.mean(x * x, axis=-1, keepdims=True) + epsilon)
     grad_tokens = (
         grad_middle
         + factor_one * weighted_one
         - x * factor_one**3 * jnp.mean(weighted_one * x, axis=-1, keepdims=True)
     )
-    qkv_sum = to_owners(qkv_term).reshape(tensor_count, weight_rows, 3, features_here)
-    qkv_sum = qkv_sum.transpose(1, 2, 0, 3).reshape(weight_rows, 3 * width)
-    grad_qkv = gain_one * qkv_sum
-    grad_norm_one = jnp.sum(attn_qkv.astype(f32) * qkv_sum, axis=1)
-    grad_mlp = jnp.concatenate([grad_gate_w, grad_up_w, grad_down_w], axis=1).astype(f32)
+    grad_qkv, grad_out_w, grad_norm_one, grad_norm_two = weight_sums(
+        qkv_sums, out_sums, attn_qkv, gain_one
+    )
     return (result, grad_tokens, grad_qkv, grad_out_w, grad_mlp, grad_norm_one, grad_norm_two)
 
 

time: 672 us -> 610 us (0.908)
  blocking collectives: 42.7 us -> 0 us
  Pallas kernels: 164 us -> 184 us
  waiting for transfers between devices: 229 us -> 210 us
  local copies, waits for them, and re-layouts: 48.1 us -> 37 us
  matrix products: 7.34 us -> 0 us
  other arithmetic: 42.8 us -> 36 us
    all_to_all x1 -> x0, blocking collectives: 42.7 us -> none  [shards(): lax.all_to_all(qkv_cut, TENSOR, 0, 0).reshape(-1, 3 * features_here)]
    all_to_all x1, waiting for transfers between devices: 26.6 us -> 0.01 us  [shards(): qkv = lax.all_to_all(stacked, 'p', 0, 0)]
    reduce_scatter x3, waiting for transfers between devices: 21 us -> 0.01 us  [over_groups(): return lax.psum_scatter(part, GROUPS, scatter_dimension=0, tiled=True)]
    ppermute x28 -> x20, waiting for transfers between devices: 68 us -> 88.8 us  [from_flipped(): return lax.ppermute(array, 'p', [(i, i ^ bit) for i in range(4)])]
    pallas_call x2 -> x6, Pallas kernels: 40.5 us -> 56.2 us  [the longest x2 35.4 us: attend_backward(): pl.pallas_call(functools.partial(backward_kernel, lower, upper, last, blo...]
    all_to_all x2 -> x3, waiting for transfers between devices: 0.01 us -> 14.1 us  [the longest x2 9.08 us: to_owners(): return lax.all_to_all(own.reshape(count, -1, own.shape[1]), TENSOR, 0, 0)]
    all_to_all x1, waiting for transfers between devices: 13.5 us -> 0.01 us  [shards(): grad_qkv_rows = lax.all_to_all(grad_qkv_rows, 'p', 0, 0)]
    ppermute x18 -> x21, starting transfers between devices: 46 us -> 57.1 us  [from_next(): lax.ppermute(array, 'z', [(i, (i - 1) % count) for i in range(count)])]
  transfers between devices with their start and end apart: 83 -> 82, of which waited for: 29 -> 33; matrix products, arithmetic and copies ran while one was open for 11% -> 7% of each run, Pallas kernels for 24% -> 31%
where the time goes in v3:
time: 610 us; the launch traced here: 602 us
  waiting for transfers between devices  210 us (34%)
  Pallas kernels  184 us (30%)
  starting transfers between devices  121 us (20%)
  local copies, waits for them, and re-layouts  37 us (6%)
  other arithmetic  36 us (6%)
  between operations  15.1 us (2%)
    ppermute x20, waiting for transfers between devices, from_flipped(): return lax.ppermute(array, 'p', [(i, i ^ bit) for i in range(4)])  88.8 us
    ppermute x21, waiting for transfers between devices, from_next(): lax.ppermute(array, 'z', [(i, (i - 1) % count) for i in range(count)])  88.8 us
    pallas_call x4, Pallas kernels, units_chunk(): pl.pallas_call(functools.partial(units_kernel, counts, tables), grid=(1,)...  57.2 us
    ppermute x21, starting transfers between devices, from_next(): lax.ppermute(array, 'z', [(i, (i - 1) % count) for i in range(count)])  57.1 us
    pallas_call x2, Pallas kernels, attend_backward(): pl.pallas_call(functools.partial(backward_kernel, lower, upper, last, blo...  35.4 us
    pallas_call x3, Pallas kernels, transposed_product(): pl.pallas_call(transposed_product_kernel, grid=(units // cut,), out_shape...  26.1 us
    unnamed x167, local copies, waits for them, and re-layouts  24.3 us
    ppermute x20, starting transfers between devices, from_flipped(): return lax.ppermute(array, 'p', [(i, i ^ bit) for i in range(4)])  22.8 us
  transfers between devices with their start and end apart: 82, of which 33 were waited for; matrix products, arithmetic and copies ran while one was open for 7% of the time, Pallas kernels for 31%

profile of v3, /device:TPU:0, one launch (start us, length us, event | category | flops | bytes accessed | tf_op | source)
XLA Modules:
  0.0 602.0 jit_solution(4871008155023696098)
XLA Ops:
  12.7 6.5 %all-to-all-start = ((bf16[8,64,768]{2,1,0:T(8,128)(2,1)}), bf16[8,64,768]{2,1,0:T(8,128)(2,1)S(1)}, u32[]{:S(2)}, u32[]{:S(2)}) async-start(bf16[8,64,768]{2,1,0:T(8,128)(2,1)} %reshape.113), calls=%async_computation | async-start | bytes 1572864 | tf_op jit(solution)/shard_map/all_to_all | solution.py:771
  24.9 3.1 slice.119
  28.0 24.1 %collective-permute-done = bf16[64,2176]{1,0:T(8,128)(2,1)S(1)} collective-permute-done((bf16[64,2176]{1,0:T(8,128)(2,1)S(1)}, bf16[64,2176]{1,0:T(8,128)(2,1)S(1)}, u32[]{:S(2)}, u32[]{:S(2)}) %collective-permute-start) | collective-permute-done | bytes 278560 | tf_op jit(solution)/shard_map/ppermute | solution.py:659
  53.3 5.0 all-to-all-done
  64.7 11.9 %collective-permute-done.4.refs_1_ = bf16[512,768]{1,0:T(8,128)(2,1)S(1)} collective-permute-done((bf16[512,768]{1,0:T(8,128)(2,1)S(1)}, bf16[512,768]{1,0:T(8,128)(2,1)S(1)}, u32[]{:S(2)}, u32[]{:S(2)}) %collective-permute-start.4) | collective-permute-done | bytes 786464 | tf_op jit(solution)/shard_map/ppermute | solution.py:659
  82.8 7.1 %collective-permute-done.6.refs_3_ = bf16[256,768]{1,0:T(8,128)(2,1)S(1)} collective-permute-done((bf16[256,768]{1,0:T(8,128)(2,1)S(1)}, bf16[256,768]{1,0:T(8,128)(2,1)S(1)}, u32[]{:S(2)}, u32[]{:S(2)}) %collective-permute-start.6) | collective-permute-done | bytes 393248 | tf_op jit(solution)/shard_map/ppermute | solution.py:659
  95.1 10.4 %project.1 = (bf16[1024,2048]{1,0:T(8,128)(2,1)}, bf16[4,8,3,64,128]{4,3,2,1,0:T(8,128)(2,1)}) custom-call(s32[5]{0:T(128)S(1)} %stack.232.starts_ref, bf16[1024,2048]{1,0:T(8,128)(2,1)} %all-gather.3.cloned.1.call-done.x_ref, f32[32,1024]{1,0:T(8,128)S(1)} %get-tuple-element.430.cosine_ref, f32[32,1024]{1,0:T(8,128)S(1)} %get-tuple-element.429.sine_ref, ...), custom_call_target="tpu_custom_call" | custom-call | flops 11000000512 | bytes 1000 | tf_op jit(solution)/shard_map/project/pallas_call | solution.py:246
  105.5 4.0 collective-permute-done.10.refs_6_
  109.5 6.2 %collective-permute-done.11.refs_7_ = bf16[128,2048]{1,0:T(8,128)(2,1)S(1)} collective-permute-done((bf16[128,2048]{1,0:T(8,128)(2,1)S(1)}, bf16[128,2048]{1,0:T(8,128)(2,1)S(1)}, u32[]{:S(2)}, u32[]{:S(2)}) %collective-permute-start.11) | collective-permute-done | bytes 524320 | tf_op jit(solution)/shard_map/ppermute | solution.py:659
  117.2 3.6 all-to-all-start.1
  120.8 4.1 collective-permute-start.13
  125.4 23.2 %collective-permute-done.13.refs_2_ = bf16[256,2176]{1,0:T(8,128)(2,1)S(1)} collective-permute-done((bf16[256,2176]{1,0:T(8,128)(2,1)}, bf16[256,2176]{1,0:T(8,128)(2,1)S(1)}, u32[]{:S(2)}, u32[]{:S(2)}) %collective-permute-start.13) | collective-permute-done | bytes 1114144 | tf_op jit(solution)/shard_map/ppermute | solution.py:655
  149.7 3.5 collective-permute-start.16
  153.2 18.5 %attend_forward.1 = (bf16[32,64,128]{2,1,0:T(8,128)(2,1)}, f32[4,1,1024]{2,1,0:T(1,128)}) custom-call(bf16[32,3,64,128]{3,2,1,0:T(8,128)(2,1)} %bitcast.138), custom_call_target="tpu_custom_call" | custom-call | flops 19800000512 | bytes 1000 | tf_op jit(solution)/shard_map/attend_forward/pallas_call | solution.py:157
  171.7 5.1 collective-permute-done.16.refs_3_
  177.8 4.4 all-to-all-start.2
  182.2 3.7 collective-permute-start.19
  186.0 10.6 %all-to-all-done.2.attended_ref = bf16[32,64,128]{2,1,0:T(8,128)(2,1)S(1)} async-done(((bf16[32,64,128]{2,1,0:T(8,128)(2,1)}), bf16[32,64,128]{2,1,0:T(8,128)(2,1)S(1)}, u32[]{:S(2)}, u32[]{:S(2)}) %all-to-all-start.2) | async-done | bytes 524320 | tf_op jit(solution)/shard_map/all_to_all | solution.py:835
  196.6 8.2 %collective-permute-done.19.grad_own_ref = bf16[128,2048]{1,0:T(8,128)(2,1)} collective-permute-done((bf16[128,2048]{1,0:T(8,128)(2,1)S(1)}, bf16[128,2048]{1,0:T(8,128)(2,1)}, u32[]{:S(2)}, u32[]{:S(2)}) %collective-permute-start.19) | collective-permute-done | bytes 524320 | tf_op jit(solution)/shard_map/ppermute | solution.py:655
  204.8 6.8 %collective-permute-start.20 = (bf16[128,2048]{1,0:T(8,128)(2,1)}, bf16[128,2048]{1,0:T(8,128)(2,1)S(1)}, u32[]{:S(2)}, u32[]{:S(2)}) collective-permute-start(bf16[128,2048]{1,0:T(8,128)(2,1)} %collective-permute-done.19.grad_own_ref), channel_id=1, source_target_pairs={{0,3},{1,0},{2,1},{3,2},{4,7},{5,4},{6,5},{7,6},{8,11},{9,8},{10,9... | collective-permute-start | bytes 1572872 | tf_op jit(solution)/shard_map/ppermute | solution.py:655
  212.9 8.0 %finish_attention.1 = (f32[128,2048]{1,0:T(8,128)S(1)}, bf16[128,2048]{1,0:T(8,128)(2,1)}, f32[1,2048]{1,0:T(1,128)S(1)}) custom-call(s32[40]{0:T(128)S(1)} %stack.226.starts_ref, bf16[128,2048]{1,0:T(8,128)(2,1)S(1)} %copy-done, bf16[32,64,128]{2,1,0:T(8,128)(2,1)S(1)} %all-to-all-done.2.attended_ref, ...), custom_call_target="tpu_custom_call" | custom-call | flops 9900000256 | bytes 1000 | tf_op jit(solution)/shard_map/finish_attention/pallas_call | solution.py:297
  224.9 4.2 collective-permute-start.21
  229.1 3.5 all-to-all-start.3
  232.9 12.4 %units_chunk.4 = (bf16[4,256,1024]{2,1,0:T(8,128)(2,1)}, bf16[4,256,1024]{2,1,0:T(8,128)(2,1)}, bf16[4,256,1024]{2,1,0:T(8,128)(2,1)}, bf16[4,256,2048]{2,1,0:T(...) custom-call(bf16[128,2048]{1,0:T(8,128)(2,1)} %get-tuple-element.252, ...), custom_call_target="tpu_custom_call" | custom-call | flops 14300000256 | bytes 1000 | tf_op jit(solution)/shard_map/units_chunk/pallas_call | solution.py:594
  245.3 6.7 %collective-permute-done.26.grad_own_ref = bf16[128,2048]{1,0:T(8,128)(2,1)} collective-permute-done((bf16[128,2048]{1,0:T(8,128)(2,1)}, bf16[128,2048]{1,0:T(8,128)(2,1)}, u32[]{:S(2)}, u32[]{:S(2)}) %collective-permute-start.26) | collective-permute-done | bytes 524320 | tf_op jit(solution)/shard_map/ppermute | solution.py:655
  252.5 4.3 collective-permute-start.24
  257.7 15.0 %units_chunk.5 = (bf16[4,256,1024]{2,1,0:T(8,128)(2,1)}, bf16[4,256,1024]{2,1,0:T(8,128)(2,1)}, bf16[4,256,1024]{2,1,0:T(8,128)(2,1)}, bf16[4,256,2048]{2,1,0:T(...) custom-call(bf16[128,2048]{1,0:T(8,128)(2,1)} %collective-permute-do, ...), custom_call_target="tpu_custom_call", output_to_operand_aliasing={{0}: (14, {}), {1}: (15, {}), {2}: (16, {}), {3}: (17, {}),... | custom-call | flops 14300000256 | bytes 1000 | tf_op jit(solution)/shard_map/units_chunk/pallas_call | solution.py:594
  279.9 14.9 %units_chunk.6 = (bf16[4,256,1024]{2,1,0:T(8,128)(2,1)}, bf16[4,256,1024]{2,1,0:T(8,128)(2,1)}, bf16[4,256,1024]{2,1,0:T(8,128)(2,1)}, bf16[4,256,2048]{2,1,0:T(...) custom-call(bf16[128,2048]{1,0:T(8,128)(2,1)} %copy-done.74, ...), custom_call_target="tpu_custom_call", output_to_operand_aliasing={{0}: (14, {}), {1}: (15, {}), {2}: (16, {}), {3}: (17, {}),... | custom-call | flops 14300000256 | bytes 1000 | tf_op jit(solution)/shard_map/units_chunk/pallas_call | solution.py:594
  294.9 4.1 collective-permute-done.30
  299.5 2.3 collective-permute-done.33
  303.2 4.0 collective-permute-start.34
  308.2 14.9 %units_chunk.7 = (bf16[4,256,1024]{2,1,0:T(8,128)(2,1)}, bf16[4,256,1024]{2,1,0:T(8,128)(2,1)}, bf16[4,256,1024]{2,1,0:T(8,128)(2,1)}, bf16[4,256,2048]{2,1,0:T(...) custom-call(bf16[128,2048]{1,0:T(8,128)(2,1)} %copy-done.73, ...), custom_call_target="tpu_custom_call", output_to_operand_aliasing={{0}: (14, {}), {1}: (15, {}), {2}: (16, {}), {3}: (17, {}),... | custom-call | flops 14300000256 | bytes 1000 | tf_op jit(solution)/shard_map/units_chunk/pallas_call | solution.py:594
  327.7 8.6 %transposed_product.3 = bf16[1024,2048]{1,0:T(8,128)(2,1)} custom-call(bf16[1024,1024]{1,0:T(8,128)(2,1)S(1)} %bitcast.128, bf16[1024,2048]{1,0:T(8,128)(2,1)} %bitcast.146), custom_call_target="tpu_custom_call" | custom-call | flops 9900000256 | bytes 1000 | tf_op jit(solution)/shard_map/transposed_product/pallas_call | solution.py:617
  336.3 5.7 collective-permute-done.38
  345.4 7.4 %back_to_attention.1 = (f32[128,2048]{1,0:T(8,128)S(1)}, bf16[128,2048]{1,0:T(8,128)(2,1)S(1)}, f32[1,2048]{1,0:T(1,128)S(1)}, bf16[32,64,128]{2,1,0:T(8,128)(2,1)}) custom-call(s32[40]{0:T(128)S(1)} %stack.226.starts_ref, f32[128,2048]{1,0:T(8,128)S(1)} %get-tuple-element.248.mid_ref, f32[128,2048]{1,0:T(8,128)S(1)} %add_add_fusion.grad_ref, ...), custom_call_target="tpu_custom_call" | custom-call | flops 6600000000 | bytes 1000 | tf_op jit(solution)/shard_map/back_to_attention/pallas_call | solution.py:351
  353.6 3.0 all-to-all-start.4
  358.2 8.8 %transposed_product.4 = bf16[1024,2048]{1,0:T(8,128)(2,1)} custom-call(bf16[1024,1024]{1,0:T(8,128)(2,1)S(1)} %bitcast.129, bf16[1024,2048]{1,0:T(8,128)(2,1)} %bitcast.147), custom_call_target="tpu_custom_call" | custom-call | flops 9900000256 | bytes 1000 | tf_op jit(solution)/shard_map/transposed_product/pallas_call | solution.py:617
  368.7 8.7 %transposed_product.5 = bf16[1024,2048]{1,0:T(8,128)(2,1)} custom-call(bf16[1024,1024]{1,0:T(8,128)(2,1)S(1)} %bitcast.127, bf16[1024,2048]{1,0:T(8,128)(2,1)} %bitcast.148), custom_call_target="tpu_custom_call" | custom-call | flops 9900000256 | bytes 1000 | tf_op jit(solution)/shard_map/transposed_product/pallas_call | solution.py:617
  377.3 3.6 collective-permute-start.40
  382.0 12.0 %attend_backward.2 = (bf16[32,3,64,128]{3,2,1,0:T(8,128)(2,1)}, f32[2,64,1024]{2,1,0:T(8,128)}) custom-call(bf16[32,3,64,128]{3,2,1,0:T(8,128)(2,1)} %bitcast.139, bf16[32,64,128]{2,1,0:T(8,128)(2,1)} %copy-done.60, bf16[32,64,128]{2,1,0:T(8,128)(2,1)} %get-tuple-element.238.refs_2_, f32[4,1,1024]{2,1,0:T(1,128)} %get-tuple-element.321.refs_3_), custom_call_target="tpu_custom_call" | custom-call | flops 19800000512 | bytes 1000 | tf_op jit(solution)/shard_map/attend_backward/pallas_call | solution.py:179
  394.9 2.5 collective-permute-start.45
  400.7 23.4 %attend_backward.3 = (bf16[32,3,64,128]{3,2,1,0:T(8,128)(2,1)}, f32[1,64,1024]{2,1,0:T(8,128)}) custom-call(bf16[32,3,64,128]{3,2,1,0:T(8,128)(2,1)} %bitcast.140, bf16[32,64,128]{2,1,0:T(8,128)(2,1)} %copy-done.60, bf16[32,64,128]{2,1,0:T(8,128)(2,1)} %get-tuple-element.238.refs_2_, f32[4,1,1024]{2,1,0:T(1,128)} %get-tuple-element.321.refs_3_, ...), custom_call_target="tpu_custom_call" | custom-call | flops 19800000512 | bytes 1000 | tf_op jit(solution)/shard_map/attend_backward/pallas_call | solution.py:179
  425.8 3.8 all-to-all-start.5
  429.7 2.5 add_convert_fusion.5
  434.3 10.4 %collective-permute-done.49.refs_6_ = bf16[128,2048]{1,0:T(8,128)(2,1)} collective-permute-done((bf16[128,2048]{1,0:T(8,128)(2,1)}, bf16[128,2048]{1,0:T(8,128)(2,1)}, u32[]{:S(2)}, u32[]{:S(2)}) %collective-permute-start.49) | collective-permute-done | bytes 524320 | tf_op jit(solution)/shard_map/ppermute | solution.py:655
  444.8 10.2 %collective-permute-done.50 = bf16[128,2048]{1,0:T(8,128)(2,1)} collective-permute-done((bf16[128,2048]{1,0:T(8,128)(2,1)}, bf16[128,2048]{1,0:T(8,128)(2,1)}, u32[]{:S(2)}, u32[]{:S(2)}) %collective-permute-start.50) | collective-permute-done | bytes 524320 | tf_op jit(solution)/shard_map/ppermute | solution.py:655
  455.1 7.7 %turn_back.1 = (bf16[8,128,768]{2,1,0:T(8,128)(2,1)S(1)}, bf16[2048,768]{1,0:T(8,128)(2,1)}) custom-call(bf16[4,8,3,64,128]{4,3,2,1,0:T(8,128)(2,1)S(1)} %all-to-all-done.5.grad_ref, f32[32,1024]{1,0:T(8,128)S(1)} %copy-done.15, f32[32,1024]{1,0:T(8,128)S(1)} %copy-done.13, bf16[1024,2048]{1,0:T(8,128)(2,1)} %get-tuple-element.354.unit_ref), custom_call_target="tpu_custom_call" | custom-call | flops 8800000000 | bytes 1000 | tf_op jit(solution)/shard_map/turn_back/pallas_call | solution.py:400
  467.5 7.1 %back_to_norm.1 = (f32[128,2048]{1,0:T(8,128)}, f32[128,2048]{1,0:T(8,128)}, f32[128,2048]{1,0:T(8,128)}, f32[128,2048]{1,0:T(8,128)}, bf16[128,2048]{1,0:T(8,12...) custom-call(s32[5]{0:T(128)S(1)} %copy-done.18, ...), custom_call_target="tpu_custom_call" | custom-call | flops 7699999744 | bytes 1000 | tf_op jit(solution)/shard_map/back_to_norm/pallas_call | solution.py:437
  474.6 3.9 collective-permute-done.52
  486.4 3.7 collective-permute-start.55
  490.2 4.3 out_product.1
  494.5 7.2 %collective-permute-done.58 = bf16[512,768]{1,0:T(8,128)(2,1)S(1)} collective-permute-done((bf16[512,768]{1,0:T(8,128)(2,1)S(1)}, bf16[512,768]{1,0:T(8,128)(2,1)S(1)}, u32[]{:S(2)}, u32[]{:S(2)}) %collective-permute-start.58) | collective-permute-done | bytes 786464 | tf_op jit(solution)/shard_map/ppermute | solution.py:659
  506.5 3.7 collective-permute-start.60
  513.6 3.8 collective-permute-done.62
  517.4 4.8 collective-permute-done.61
  524.1 4.6 collective-permute-done.64
  535.4 3.8 all-to-all-start.6
  541.0 3.8 collective-permute-start.65
  546.4 10.3 %collective-permute-done.67 = bf16[256,384]{1,0:T(8,128)(2,1)S(1)} collective-permute-done((bf16[256,384]{1,0:T(8,128)(2,1)S(1)}, bf16[256,384]{1,0:T(8,128)(2,1)S(1)}, u32[]{:S(2)}, u32[]{:S(2)}) %collective-permute-start.67) | collective-permute-done | bytes 196640 | tf_op jit(solution)/shard_map/ppermute | solution.py:659
  558.5 7.7 %collective-permute-done.65 = bf16[128,2048]{1,0:T(8,128)(2,1)S(1)} collective-permute-done((bf16[128,2048]{1,0:T(8,128)(2,1)S(1)}, bf16[128,2048]{1,0:T(8,128)(2,1)S(1)}, u32[]{:S(2)}, u32[]{:S(2)}) %collective-permute-start.65) | collective-permute-done | bytes 524320 | tf_op jit(solution)/shard_map/ppermute | solution.py:655
  567.2 7.0 %all-to-all-start.7 = ((bf16[8,64,384]{2,1,0:T(8,128)(2,1)}), bf16[8,64,384]{2,1,0:T(8,128)(2,1)S(1)}, u32[]{:S(2)}, u32[]{:S(2)}) async-start(bf16[8,64,384]{2,1,0:T(8,128)(2,1)} %bitcast.86), calls=%async_computation.7 | async-start | bytes 786432 | tf_op jit(solution)/shard_map/all_to_all | solution.py:740
  574.2 3.0 fusion.3
  577.2 9.1 %all-to-all-done.7.out_sums_ref = bf16[8,64,384]{2,1,0:T(8,128)(2,1)S(1)} async-done(((bf16[8,64,384]{2,1,0:T(8,128)(2,1)}), bf16[8,64,384]{2,1,0:T(8,128)(2,1)S(1)}, u32[]{:S(2)}, u32[]{:S(2)}) %all-to-all-start.7) | async-done | bytes 393248 | tf_op jit(solution)/shard_map/all_to_all | solution.py:740
  589.9 5.3 maximum_convert_fusion
  (348 shorter events, 111.5 us)
Async XLA Ops:
  7.2 82.8 %all-gather.3.cloned.1.call-start = ((), (), s32[]{:S(2)}) async-start(), calls=%async_computation.11 | async-start | bytes 4718592 | tf_op jit(solution)/shard_map/all_gather | solution.py:763
  12.7 45.7 %all-to-all-start = ((bf16[8,64,768]{2,1,0:T(8,128)(2,1)}), bf16[8,64,768]{2,1,0:T(8,128)(2,1)S(1)}, u32[]{:S(2)}, u32[]{:S(2)}) async-start(bf16[8,64,768]{2,1,0:T(8,128)(2,1)} %reshape.113), calls=%async_computation | async-start | bytes 1572864 | tf_op jit(solution)/shard_map/all_to_all | solution.py:771
  19.1 213.8 %all-gather.5.cloned.1.call-start = ((), (), s32[]{:S(2)}) async-start(), calls=%async_computation.12 | async-start | bytes 10485760 | tf_op jit(solution)/shard_map/all_gather | solution.py:795
  20.6 32.8 %collective-permute-start.2 = (bf16[256,2048]{1,0:T(8,128)(2,1)S(1)}, bf16[256,2048]{1,0:T(8,128)(2,1)}, u32[]{:S(2)}, u32[]{:S(2)}) collective-permute-start(bf16[256,2048]{1,0:T(8,128)(2,1)S(1)} %slice.112.refs_3_), channel_id=1, source_target_pairs={{0,8},{8,0},{16,24},{24,16},{1,9},{9,1},{17,25},{25,17},{2,10},{10... | collective-permute-start | bytes 3145736 | tf_op jit(solution)/shard_map/ppermute | solution.py:659
  22.1 31.2 %collective-permute-start.3 = (bf16[256,2048]{1,0:T(8,128)(2,1)S(1)}, bf16[256,2048]{1,0:T(8,128)(2,1)}, u32[]{:S(2)}, u32[]{:S(2)}) collective-permute-start(bf16[256,2048]{1,0:T(8,128)(2,1)S(1)} %slice.112.refs_3_), channel_id=1, source_target_pairs={{0,16},{8,24},{16,0},{24,8},{1,17},{9,25},{17,1},{25,9},{2,18},{10... | collective-permute-start | bytes 3145736 | tf_op jit(solution)/shard_map/ppermute | solution.py:659
  23.8 28.3 %collective-permute-start = (bf16[64,2176]{1,0:T(8,128)(2,1)S(1)}, bf16[64,2176]{1,0:T(8,128)(2,1)S(1)}, u32[]{:S(2)}, u32[]{:S(2)}) collective-permute-start(bf16[64,2176]{1,0:T(8,128)(2,1)S(1)} %fusion.11), channel_id=1, source_target_pairs={{0,8},{8,0},{16,24},{24,16},{1,9},{9,1},{17,25},{25,17},{2,10},{10... | collective-permute-start | bytes 835592 | tf_op jit(solution)/shard_map/ppermute | solution.py:659
  24.4 29.0 %collective-permute-start.1 = (bf16[64,2176]{1,0:T(8,128)(2,1)S(1)}, bf16[64,2176]{1,0:T(8,128)(2,1)S(1)}, u32[]{:S(2)}, u32[]{:S(2)}) collective-permute-start(bf16[64,2176]{1,0:T(8,128)(2,1)S(1)} %fusion.11), channel_id=1, source_target_pairs={{0,16},{8,24},{16,0},{24,8},{1,17},{9,25},{17,1},{25,9},{2,18},{10... | collective-permute-start | bytes 835592 | tf_op jit(solution)/shard_map/ppermute | solution.py:659
  58.4 18.3 %collective-permute-start.4 = (bf16[512,768]{1,0:T(8,128)(2,1)S(1)}, bf16[512,768]{1,0:T(8,128)(2,1)S(1)}, u32[]{:S(2)}, u32[]{:S(2)}) collective-permute-start(bf16[512,768]{1,0:T(8,128)(2,1)S(1)} %bitcast.123), channel_id=1, source_target_pairs={{0,8},{8,0},{16,24},{24,16},{1,9},{9,1},{17,25},{25,17},{2,10},{10... | collective-permute-start | bytes 2359304 | tf_op jit(solution)/shard_map/ppermute | solution.py:659
  59.9 18.6 %collective-permute-start.5 = (bf16[512,768]{1,0:T(8,128)(2,1)S(1)}, bf16[512,768]{1,0:T(8,128)(2,1)S(1)}, u32[]{:S(2)}, u32[]{:S(2)}) collective-permute-start(bf16[512,768]{1,0:T(8,128)(2,1)S(1)} %bitcast.124), channel_id=1, source_target_pairs={{0,16},{8,24},{16,0},{24,8},{1,17},{9,25},{17,1},{25,9},{2,18},{10... | collective-permute-start | bytes 2359304 | tf_op jit(solution)/shard_map/ppermute | solution.py:659
  62.2 19.3 %collective-permute-start.8 = (bf16[32,2176]{1,0:T(8,128)(2,1)S(1)}, bf16[32,2176]{1,0:T(8,128)(2,1)S(1)}, u32[]{:S(2)}, u32[]{:S(2)}) collective-permute-start(bf16[32,2176]{1,0:T(8,128)(2,1)S(1)} %slice.115), channel_id=1, source_target_pairs={{0,16},{8,24},{16,0},{24,8},{1,17},{9,25},{17,1},{25,9},{2,18},{10... | collective-permute-start | bytes 417800 | tf_op jit(solution)/shard_map/ppermute | solution.py:659
  64.2 18.0 %collective-permute-start.9 = (bf16[32,2176]{1,0:T(8,128)(2,1)S(1)}, bf16[32,2176]{1,0:T(8,128)(2,1)S(1)}, u32[]{:S(2)}, u32[]{:S(2)}) collective-permute-start(bf16[32,2176]{1,0:T(8,128)(2,1)S(1)} %slice.116), channel_id=1, source_target_pairs={{0,8},{8,0},{16,24},{24,16},{1,9},{9,1},{17,25},{25,17},{2,10},{10... | collective-permute-start | bytes 417800 | tf_op jit(solution)/shard_map/ppermute | solution.py:659
  76.7 13.2 %collective-permute-start.6 = (bf16[256,768]{1,0:T(8,128)(2,1)S(1)}, bf16[256,768]{1,0:T(8,128)(2,1)S(1)}, u32[]{:S(2)}, u32[]{:S(2)}) collective-permute-start(bf16[256,768]{1,0:T(8,128)(2,1)S(1)} %slice.148), channel_id=1, source_target_pairs={{0,16},{8,24},{16,0},{24,8},{1,17},{9,25},{17,1},{25,9},{2,18},{10... | collective-permute-start | bytes 1179656 | tf_op jit(solution)/shard_map/ppermute | solution.py:659
  90.0 27.2 %collective-permute-start.12 = (bf16[256,2176]{1,0:T(8,128)(2,1)}, bf16[256,2176]{1,0:T(8,128)(2,1)}, u32[]{:S(2)}, u32[]{:S(2)}) collective-permute-start(bf16[256,2176]{1,0:T(8,128)(2,1)} %constant_dynamic-update-slice_fusion.refs_0_), channel_id=1, source_target_pairs={{0,3},{1,0},{2,1},{3,2},{4,7},{5,4},{6,5},{7,6},{8,11},{9,8},{10,9... | collective-permute-start | bytes 3342344 | tf_op jit(solution)/shard_map/ppermute | solution.py:655
  91.8 17.7 %collective-permute-start.10 = (bf16[128,2048]{1,0:T(8,128)(2,1)S(1)}, bf16[128,2048]{1,0:T(8,128)(2,1)S(1)}, u32[]{:S(2)}, u32[]{:S(2)}) collective-permute-start(bf16[128,2048]{1,0:T(8,128)(2,1)S(1)} %slice.117), channel_id=1, source_target_pairs={{0,16},{8,24},{16,0},{24,8},{1,17},{9,25},{17,1},{25,9},{2,18},{10... | collective-permute-start | bytes 1572872 | tf_op jit(solution)/shard_map/ppermute | solution.py:659
  94.5 21.2 %collective-permute-start.11 = (bf16[128,2048]{1,0:T(8,128)(2,1)S(1)}, bf16[128,2048]{1,0:T(8,128)(2,1)S(1)}, u32[]{:S(2)}, u32[]{:S(2)}) collective-permute-start(bf16[128,2048]{1,0:T(8,128)(2,1)S(1)} %slice.118), channel_id=1, source_target_pairs={{0,8},{8,0},{16,24},{24,16},{1,9},{9,1},{17,25},{25,17},{2,10},{10... | collective-permute-start | bytes 1572872 | tf_op jit(solution)/shard_map/ppermute | solution.py:659
  117.2 32.5 %all-to-all-start.1 = ((bf16[4,8,3,64,128]{4,3,2,1,0:T(8,128)(2,1)}), bf16[4,8,3,64,128]{4,3,2,1,0:T(8,128)(2,1)S(1)}, u32[]{:S(2)}, u32[]{:S(2)}) async-start(bf16[4,8,3,64,128]{4,3,2,1,0:T(8,128)(2,1)} %get-tuple-element.229), calls=%async_computation.1 | async-start | bytes 3145728 | tf_op jit(solution)/shard_map/all_to_all | solution.py:791
  120.8 27.8 %collective-permute-start.13 = (bf16[256,2176]{1,0:T(8,128)(2,1)}, bf16[256,2176]{1,0:T(8,128)(2,1)S(1)}, u32[]{:S(2)}, u32[]{:S(2)}) collective-permute-start(bf16[256,2176]{1,0:T(8,128)(2,1)} %collective-permute-done.12.refs_1_), channel_id=1, source_target_pairs={{0,3},{1,0},{2,1},{3,2},{4,7},{5,4},{6,5},{7,6},{8,11},{9,8},{10,9... | collective-permute-start | bytes 3342344 | tf_op jit(solution)/shard_map/ppermute | solution.py:655
  124.9 23.7 %collective-permute-start.14 = (bf16[256,2176]{1,0:T(8,128)(2,1)}, bf16[256,2176]{1,0:T(8,128)(2,1)S(1)}, u32[]{:S(2)}, u32[]{:S(2)}) collective-permute-start(bf16[256,2176]{1,0:T(8,128)(2,1)} %constant_dynamic-update-slice_fusion.refs_0_), channel_id=1, source_target_pairs={{0,4},{4,0},{1,5},{5,1},{2,6},{6,2},{3,7},{7,3},{8,12},{12,8},{9,1... | collective-permute-start | bytes 3342344 | tf_op jit(solution)/shard_map/ppermute | solution.py:650
  124.9 24.8 %collective-permute-start.15 = (bf16[256,2176]{1,0:T(8,128)(2,1)}, bf16[256,2176]{1,0:T(8,128)(2,1)}, u32[]{:S(2)}, u32[]{:S(2)}) collective-permute-start(bf16[256,2176]{1,0:T(8,128)(2,1)} %collective-permute-done.12.refs_1_), channel_id=1, source_target_pairs={{0,4},{4,0},{1,5},{5,1},{2,6},{6,2},{3,7},{7,3},{8,12},{12,8},{9,1... | collective-permute-start | bytes 3342344 | tf_op jit(solution)/shard_map/ppermute | solution.py:650
  149.7 27.1 %collective-permute-start.16 = (bf16[256,2176]{1,0:T(8,128)(2,1)S(1)}, bf16[256,2176]{1,0:T(8,128)(2,1)}, u32[]{:S(2)}, u32[]{:S(2)}) collective-permute-start(bf16[256,2176]{1,0:T(8,128)(2,1)S(1)} %collective-permute-done.13.refs_2_), channel_id=1, source_target_pairs={{0,3},{1,0},{2,1},{3,2},{4,7},{5,4},{6,5},{7,6},{8,11},{9,8},{10,9... | collective-permute-start | bytes 3342344 | tf_op jit(solution)/shard_map/ppermute | solution.py:655
  153.2 23.6 %collective-permute-start.17 = (bf16[256,2176]{1,0:T(8,128)(2,1)S(1)}, bf16[256,2176]{1,0:T(8,128)(2,1)S(1)}, u32[]{:S(2)}, u32[]{:S(2)}) collective-permute-start(bf16[256,2176]{1,0:T(8,128)(2,1)S(1)} %collective-permute-done.13.refs_2_), channel_id=1, source_target_pairs={{0,4},{4,0},{1,5},{5,1},{2,6},{6,2},{3,7},{7,3},{8,12},{12,8},{9,1... | collective-permute-start | bytes 3342344 | tf_op jit(solution)/shard_map/ppermute | solution.py:650
  177.8 18.8 %collective-permute-start.18 = (bf16[256,2176]{1,0:T(8,128)(2,1)}, bf16[256,2176]{1,0:T(8,128)(2,1)S(1)}, u32[]{:S(2)}, u32[]{:S(2)}) collective-permute-start(bf16[256,2176]{1,0:T(8,128)(2,1)} %collective-permute-done.16.refs_3_), channel_id=1, source_target_pairs={{0,4},{4,0},{1,5},{5,1},{2,6},{6,2},{3,7},{7,3},{8,12},{12,8},{9,1... | collective-permute-start | bytes 3342344 | tf_op jit(solution)/shard_map/ppermute | solution.py:650
  177.8 18.8 %all-to-all-start.2 = ((bf16[32,64,128]{2,1,0:T(8,128)(2,1)}), bf16[32,64,128]{2,1,0:T(8,128)(2,1)S(1)}, u32[]{:S(2)}, u32[]{:S(2)}) async-start(bf16[32,64,128]{2,1,0:T(8,128)(2,1)} %get-tuple-element.238.refs_2_), calls=%async_computation.2 | async-start | bytes 1048576 | tf_op jit(solution)/shard_map/all_to_all | solution.py:835
  182.2 22.6 %collective-permute-start.19 = (bf16[128,2048]{1,0:T(8,128)(2,1)S(1)}, bf16[128,2048]{1,0:T(8,128)(2,1)}, u32[]{:S(2)}, u32[]{:S(2)}) collective-permute-start(bf16[128,2048]{1,0:T(8,128)(2,1)S(1)} %copy-done.21), channel_id=1, source_target_pairs={{0,3},{1,0},{2,1},{3,2},{4,7},{5,4},{6,5},{7,6},{8,11},{9,8},{10,9... | collective-permute-start | bytes 1572872 | tf_op jit(solution)/shard_map/ppermute | solution.py:655
  204.8 18.1 %collective-permute-start.20 = (bf16[128,2048]{1,0:T(8,128)(2,1)}, bf16[128,2048]{1,0:T(8,128)(2,1)S(1)}, u32[]{:S(2)}, u32[]{:S(2)}) collective-permute-start(bf16[128,2048]{1,0:T(8,128)(2,1)} %collective-permute-done.19.grad_own_ref), channel_id=1, source_target_pairs={{0,3},{1,0},{2,1},{3,2},{4,7},{5,4},{6,5},{7,6},{8,11},{9,8},{10,9... | collective-permute-start | bytes 1572872 | tf_op jit(solution)/shard_map/ppermute | solution.py:655
  224.9 20.4 %collective-permute-start.21 = (bf16[128,2048]{1,0:T(8,128)(2,1)}, bf16[128,2048]{1,0:T(8,128)(2,1)}, u32[]{:S(2)}, u32[]{:S(2)}) collective-permute-start(bf16[128,2048]{1,0:T(8,128)(2,1)} %get-tuple-element.252.own_ref), channel_id=1, source_target_pairs={{0,3},{1,0},{2,1},{3,2},{4,7},{5,4},{6,5},{7,6},{8,11},{9,8},{10,9... | collective-permute-start | bytes 1572872 | tf_op jit(solution)/shard_map/ppermute | solution.py:655
  229.1 16.2 %all-to-all-start.3 = ((bf16[4,8,64,128]{3,2,1,0:T(8,128)(2,1)}), bf16[4,8,64,128]{3,2,1,0:T(8,128)(2,1)S(1)}, u32[]{:S(2)}, u32[]{:S(2)}) async-start(bf16[4,8,64,128]{3,2,1,0:T(8,128)(2,1)} %bitcast.137), calls=%async_computation.3 | async-start | bytes 1048576 | tf_op jit(solution)/shard_map/all_to_all | solution.py:845
  232.5 357.4 %reduce-scatter.4.cloned.1.call-start = ((), (), s32[]{:S(2)}) async-start(), calls=%async_computation.13 | async-start | bytes 5242880 | tf_op jit(solution)/shard_map/reduce_scatter | solution.py:878
  232.6 19.4 %collective-permute-start.26 = (bf16[128,2048]{1,0:T(8,128)(2,1)}, bf16[128,2048]{1,0:T(8,128)(2,1)}, u32[]{:S(2)}, u32[]{:S(2)}) collective-permute-start(bf16[128,2048]{1,0:T(8,128)(2,1)} %copy-done.71), channel_id=1, source_target_pairs={{0,3},{1,0},{2,1},{3,2},{4,7},{5,4},{6,5},{7,6},{8,11},{9,8},{10,9... | collective-permute-start | bytes 1572872 | tf_op jit(solution)/shard_map/ppermute | solution.py:655
  252.5 20.3 %collective-permute-start.24 = (bf16[128,2048]{1,0:T(8,128)(2,1)}, bf16[128,2048]{1,0:T(8,128)(2,1)S(1)}, u32[]{:S(2)}, u32[]{:S(2)}) collective-permute-start(bf16[128,2048]{1,0:T(8,128)(2,1)} %collective-permute-done.21.own_ref), channel_id=1, source_target_pairs={{0,3},{1,0},{2,1},{3,2},{4,7},{5,4},{6,5},{7,6},{8,11},{9,8},{10,9... | collective-permute-start | bytes 1572872 | tf_op jit(solution)/shard_map/ppermute | solution.py:655
  273.4 21.4 %collective-permute-start.28 = (bf16[128,2048]{1,0:T(8,128)(2,1)S(1)}, bf16[128,2048]{1,0:T(8,128)(2,1)S(1)}, u32[]{:S(2)}, u32[]{:S(2)}) collective-permute-start(bf16[128,2048]{1,0:T(8,128)(2,1)S(1)} %collective-permute-done.24.own_ref), channel_id=1, source_target_pairs={{0,3},{1,0},{2,1},{3,2},{4,7},{5,4},{6,5},{7,6},{8,11},{9,8},{10,9... | collective-permute-start | bytes 1572872 | tf_op jit(solution)/shard_map/ppermute | solution.py:655
  277.1 21.9 %collective-permute-start.30 = (bf16[128,2048]{1,0:T(8,128)(2,1)S(1)}, bf16[128,2048]{1,0:T(8,128)(2,1)S(1)}, u32[]{:S(2)}, u32[]{:S(2)}) collective-permute-start(bf16[128,2048]{1,0:T(8,128)(2,1)S(1)} %add_convert_fusion.8), channel_id=1, source_target_pairs={{0,3},{1,0},{2,1},{3,2},{4,7},{5,4},{6,5},{7,6},{8,11},{9,8},{10,9... | collective-permute-start | bytes 1572872 | tf_op jit(solution)/shard_map/ppermute | solution.py:655
  303.2 19.9 %collective-permute-start.34 = (bf16[128,2048]{1,0:T(8,128)(2,1)S(1)}, bf16[128,2048]{1,0:T(8,128)(2,1)S(1)}, u32[]{:S(2)}, u32[]{:S(2)}) collective-permute-start(bf16[128,2048]{1,0:T(8,128)(2,1)S(1)} %add_convert_fusion.7), channel_id=1, source_target_pairs={{0,3},{1,0},{2,1},{3,2},{4,7},{5,4},{6,5},{7,6},{8,11},{9,8},{10,9... | collective-permute-start | bytes 1572872 | tf_op jit(solution)/shard_map/ppermute | solution.py:655
  327.5 14.4 %collective-permute-start.38 = (bf16[128,2048]{1,0:T(8,128)(2,1)}, bf16[128,2048]{1,0:T(8,128)(2,1)}, u32[]{:S(2)}, u32[]{:S(2)}) collective-permute-start(bf16[128,2048]{1,0:T(8,128)(2,1)} %add_add_fusion.1), channel_id=1, source_target_pairs={{0,3},{1,0},{2,1},{3,2},{4,7},{5,4},{6,5},{7,6},{8,11},{9,8},{10,9... | collective-permute-start | bytes 1572872 | tf_op jit(solution)/shard_map/ppermute | solution.py:655
  353.6 23.7 %all-to-all-start.4 = ((bf16[32,64,128]{2,1,0:T(8,128)(2,1)}), bf16[32,64,128]{2,1,0:T(8,128)(2,1)S(1)}, u32[]{:S(2)}, u32[]{:S(2)}) async-start(bf16[32,64,128]{2,1,0:T(8,128)(2,1)} %get-tuple-element.314), calls=%async_computation.4 | async-start | bytes 1048576 | tf_op jit(solution)/shard_map/all_to_all | solution.py:887
  356.6 233.3 %reduce-scatter.6.cloned.1.call-start = ((), (), s32[]{:S(2)}) async-start(), calls=%async_computation.14 | async-start | bytes 5242880 | tf_op jit(solution)/shard_map/reduce_scatter | solution.py:878
  377.3 16.7 %collective-permute-start.40 = (bf16[128,2048]{1,0:T(8,128)(2,1)S(1)}, bf16[128,2048]{1,0:T(8,128)(2,1)S(1)}, u32[]{:S(2)}, u32[]{:S(2)}) collective-permute-start(bf16[128,2048]{1,0:T(8,128)(2,1)S(1)} %copy-done.25), channel_id=1, source_target_pairs={{0,3},{1,0},{2,1},{3,2},{4,7},{5,4},{6,5},{7,6},{8,11},{9,8},{10,9... | collective-permute-start | bytes 1572872 | tf_op jit(solution)/shard_map/ppermute | solution.py:655
  381.0 13.1 %collective-permute-start.41 = (bf16[128,2048]{1,0:T(8,128)(2,1)}, bf16[128,2048]{1,0:T(8,128)(2,1)S(1)}, u32[]{:S(2)}, u32[]{:S(2)}) collective-permute-start(bf16[128,2048]{1,0:T(8,128)(2,1)} %get-tuple-element.334), channel_id=1, source_target_pairs={{0,4},{4,0},{1,5},{5,1},{2,6},{6,2},{3,7},{7,3},{8,12},{12,8},{9,1... | collective-permute-start | bytes 1572872 | tf_op jit(solution)/shard_map/ppermute | solution.py:650
  381.0 13.1 %collective-permute-start.42 = (bf16[128,2048]{1,0:T(8,128)(2,1)}, bf16[128,2048]{1,0:T(8,128)(2,1)}, u32[]{:S(2)}, u32[]{:S(2)}) collective-permute-start(bf16[128,2048]{1,0:T(8,128)(2,1)} %get-tuple-element.335), channel_id=1, source_target_pairs={{0,4},{4,0},{1,5},{5,1},{2,6},{6,2},{3,7},{7,3},{8,12},{12,8},{9,1... | collective-permute-start | bytes 1572872 | tf_op jit(solution)/shard_map/ppermute | solution.py:650
  381.5 12.6 %collective-permute-start.43 = (bf16[128,2048]{1,0:T(8,128)(2,1)}, bf16[128,2048]{1,0:T(8,128)(2,1)}, u32[]{:S(2)}, u32[]{:S(2)}) collective-permute-start(bf16[128,2048]{1,0:T(8,128)(2,1)} %get-tuple-element.336), channel_id=1, source_target_pairs={{0,4},{4,0},{1,5},{5,1},{2,6},{6,2},{3,7},{7,3},{8,12},{12,8},{9,1... | collective-permute-start | bytes 1572872 | tf_op jit(solution)/shard_map/ppermute | solution.py:650
  381.5 12.6 %collective-permute-start.44 = (bf16[128,2048]{1,0:T(8,128)(2,1)}, bf16[128,2048]{1,0:T(8,128)(2,1)}, u32[]{:S(2)}, u32[]{:S(2)}) collective-permute-start(bf16[128,2048]{1,0:T(8,128)(2,1)} %get-tuple-element.337), channel_id=1, source_target_pairs={{0,4},{4,0},{1,5},{5,1},{2,6},{6,2},{3,7},{7,3},{8,12},{12,8},{9,1... | collective-permute-start | bytes 1572872 | tf_op jit(solution)/shard_map/ppermute | solution.py:650
  394.9 29.2 %collective-permute-start.45 = (bf16[128,2048]{1,0:T(8,128)(2,1)S(1)}, bf16[128,2048]{1,0:T(8,128)(2,1)}, u32[]{:S(2)}, u32[]{:S(2)}) collective-permute-start(bf16[128,2048]{1,0:T(8,128)(2,1)S(1)} %collective-permute-done.40.refs_2_), channel_id=1, source_target_pairs={{0,3},{1,0},{2,1},{3,2},{4,7},{5,4},{6,5},{7,6},{8,11},{9,8},{10,9... | collective-permute-start | bytes 1572872 | tf_op jit(solution)/shard_map/ppermute | solution.py:655
  397.4 27.6 %collective-permute-start.48 = (bf16[128,2048]{1,0:T(8,128)(2,1)S(1)}, bf16[128,2048]{1,0:T(8,128)(2,1)S(1)}, u32[]{:S(2)}, u32[]{:S(2)}) collective-permute-start(bf16[128,2048]{1,0:T(8,128)(2,1)S(1)} %collective-permute-done.40.refs_2_), channel_id=1, source_target_pairs={{0,4},{4,0},{1,5},{5,1},{2,6},{6,2},{3,7},{7,3},{8,12},{12,8},{9,1... | collective-permute-start | bytes 1572872 | tf_op jit(solution)/shard_map/ppermute | solution.py:650
  399.7 24.5 %collective-permute-start.46 = (bf16[128,2048]{1,0:T(8,128)(2,1)}, bf16[128,2048]{1,0:T(8,128)(2,1)}, u32[]{:S(2)}, u32[]{:S(2)}) collective-permute-start(bf16[128,2048]{1,0:T(8,128)(2,1)} %add_convert_fusion.6), channel_id=1, source_target_pairs={{0,3},{1,0},{2,1},{3,2},{4,7},{5,4},{6,5},{7,6},{8,11},{9,8},{10,9... | collective-permute-start | bytes 1572872 | tf_op jit(solution)/shard_map/ppermute | solution.py:655
  400.1 24.1 %collective-permute-start.47 = (bf16[128,2048]{1,0:T(8,128)(2,1)S(1)}, bf16[128,2048]{1,0:T(8,128)(2,1)S(1)}, u32[]{:S(2)}, u32[]{:S(2)}) collective-permute-start(bf16[128,2048]{1,0:T(8,128)(2,1)S(1)} %copy-done.25), channel_id=1, source_target_pairs={{0,4},{4,0},{1,5},{5,1},{2,6},{6,2},{3,7},{7,3},{8,12},{12,8},{9,1... | collective-permute-start | bytes 1572872 | tf_op jit(solution)/shard_map/ppermute | solution.py:650
  425.8 29.3 %all-to-all-start.5 = ((bf16[4,8,3,64,128]{4,3,2,1,0:T(8,128)(2,1)}), bf16[4,8,3,64,128]{4,3,2,1,0:T(8,128)(2,1)S(1)}, u32[]{:S(2)}, u32[]{:S(2)}) async-start(bf16[4,8,3,64,128]{4,3,2,1,0:T(8,128)(2,1)} %bitcast.141), calls=%async_computation.5 | async-start | bytes 3145728 | tf_op jit(solution)/shard_map/all_to_all | solution.py:918
  429.6 160.4 %reduce-scatter.8.cloned.1.call-start = ((), (), s32[]{:S(2)}) async-start(), calls=%async_computation.15 | async-start | bytes 5242880 | tf_op jit(solution)/shard_map/reduce_scatter | solution.py:878
  429.6 15.2 %collective-permute-start.49 = (bf16[128,2048]{1,0:T(8,128)(2,1)}, bf16[128,2048]{1,0:T(8,128)(2,1)}, u32[]{:S(2)}, u32[]{:S(2)}) collective-permute-start(bf16[128,2048]{1,0:T(8,128)(2,1)} %collective-permute-done.45.refs_4_), channel_id=1, source_target_pairs={{0,3},{1,0},{2,1},{3,2},{4,7},{5,4},{6,5},{7,6},{8,11},{9,8},{10,9... | collective-permute-start | bytes 1572872 | tf_op jit(solution)/shard_map/ppermute | solution.py:655
  432.2 22.8 %collective-permute-start.50 = (bf16[128,2048]{1,0:T(8,128)(2,1)}, bf16[128,2048]{1,0:T(8,128)(2,1)}, u32[]{:S(2)}, u32[]{:S(2)}) collective-permute-start(bf16[128,2048]{1,0:T(8,128)(2,1)} %add_convert_fusion.5), channel_id=1, source_target_pairs={{0,3},{1,0},{2,1},{3,2},{4,7},{5,4},{6,5},{7,6},{8,11},{9,8},{10,9... | collective-permute-start | bytes 1572872 | tf_op jit(solution)/shard_map/ppermute | solution.py:655
  434.3 20.8 %collective-permute-start.51 = (bf16[128,2048]{1,0:T(8,128)(2,1)}, bf16[128,2048]{1,0:T(8,128)(2,1)}, u32[]{:S(2)}, u32[]{:S(2)}) collective-permute-start(bf16[128,2048]{1,0:T(8,128)(2,1)} %collective-permute-done.45.refs_4_), channel_id=1, source_target_pairs={{0,4},{4,0},{1,5},{5,1},{2,6},{6,2},{3,7},{7,3},{8,12},{12,8},{9,1... | collective-permute-start | bytes 1572872 | tf_op jit(solution)/shard_map/ppermute | solution.py:650
  465.5 13.1 %collective-permute-start.52 = (bf16[128,2048]{1,0:T(8,128)(2,1)S(1)}, bf16[128,2048]{1,0:T(8,128)(2,1)S(1)}, u32[]{:S(2)}, u32[]{:S(2)}) collective-permute-start(bf16[128,2048]{1,0:T(8,128)(2,1)S(1)} %add_convert_fusion.4), channel_id=1, source_target_pairs={{0,3},{1,0},{2,1},{3,2},{4,7},{5,4},{6,5},{7,6},{8,11},{9,8},{10,9... | collective-permute-start | bytes 1572872 | tf_op jit(solution)/shard_map/ppermute | solution.py:655
  481.7 20.0 %collective-permute-start.58 = (bf16[512,768]{1,0:T(8,128)(2,1)S(1)}, bf16[512,768]{1,0:T(8,128)(2,1)S(1)}, u32[]{:S(2)}, u32[]{:S(2)}) collective-permute-start(bf16[512,768]{1,0:T(8,128)(2,1)S(1)} %pad_maximum_fusion), channel_id=1, source_target_pairs={{0,8},{8,0},{16,24},{24,16},{1,9},{9,1},{17,25},{25,17},{2,10},{10... | collective-permute-start | bytes 2359304 | tf_op jit(solution)/shard_map/ppermute | solution.py:659
  483.2 19.7 %collective-permute-start.59 = (bf16[512,768]{1,0:T(8,128)(2,1)S(1)}, bf16[512,768]{1,0:T(8,128)(2,1)S(1)}, u32[]{:S(2)}, u32[]{:S(2)}) collective-permute-start(bf16[512,768]{1,0:T(8,128)(2,1)S(1)} %pad_maximum_fusion.1), channel_id=1, source_target_pairs={{0,16},{8,24},{16,0},{24,8},{1,17},{9,25},{17,1},{25,9},{2,18},{10... | collective-permute-start | bytes 2359304 | tf_op jit(solution)/shard_map/ppermute | solution.py:659
  484.7 18.2 %collective-permute-start.56 = (bf16[128,2048]{1,0:T(8,128)(2,1)S(1)}, bf16[128,2048]{1,0:T(8,128)(2,1)S(1)}, u32[]{:S(2)}, u32[]{:S(2)}) collective-permute-start(bf16[128,2048]{1,0:T(8,128)(2,1)S(1)} %get-tuple-element.377), channel_id=1, source_target_pairs={{0,4},{4,0},{1,5},{5,1},{2,6},{6,2},{3,7},{7,3},{8,12},{12,8},{9,1... | collective-permute-start | bytes 1572872 | tf_op jit(solution)/shard_map/ppermute | solution.py:650
  484.7 18.2 %collective-permute-start.57 = (bf16[128,2048]{1,0:T(8,128)(2,1)S(1)}, bf16[128,2048]{1,0:T(8,128)(2,1)S(1)}, u32[]{:S(2)}, u32[]{:S(2)}) collective-permute-start(bf16[128,2048]{1,0:T(8,128)(2,1)S(1)} %get-tuple-element.378), channel_id=1, source_target_pairs={{0,4},{4,0},{1,5},{5,1},{2,6},{6,2},{3,7},{7,3},{8,12},{12,8},{9,1... | collective-permute-start | bytes 1572872 | tf_op jit(solution)/shard_map/ppermute | solution.py:650
  486.4 16.5 %collective-permute-start.55 = (bf16[128,2048]{1,0:T(8,128)(2,1)S(1)}, bf16[128,2048]{1,0:T(8,128)(2,1)S(1)}, u32[]{:S(2)}, u32[]{:S(2)}) collective-permute-start(bf16[128,2048]{1,0:T(8,128)(2,1)S(1)} %add_convert_fusion.2), channel_id=1, source_target_pairs={{0,3},{1,0},{2,1},{3,2},{4,7},{5,4},{6,5},{7,6},{8,11},{9,8},{10,9... | collective-permute-start | bytes 1572872 | tf_op jit(solution)/shard_map/ppermute | solution.py:655
  505.2 12.1 %collective-permute-start.62 = (bf16[256,768]{1,0:T(8,128)(2,1)S(1)}, bf16[256,768]{1,0:T(8,128)(2,1)S(1)}, u32[]{:S(2)}, u32[]{:S(2)}) collective-permute-start(bf16[256,768]{1,0:T(8,128)(2,1)S(1)} %get-tuple-element.418), channel_id=1, source_target_pairs={{0,8},{8,0},{16,24},{24,16},{1,9},{9,1},{17,25},{25,17},{2,10},{10... | collective-permute-start | bytes 1179656 | tf_op jit(solution)/shard_map/ppermute | solution.py:659
  506.5 23.0 %collective-permute-start.60 = (bf16[128,2048]{1,0:T(8,128)(2,1)S(1)}, bf16[128,2048]{1,0:T(8,128)(2,1)}, u32[]{:S(2)}, u32[]{:S(2)}) collective-permute-start(bf16[128,2048]{1,0:T(8,128)(2,1)S(1)} %add_convert_fusion.1), channel_id=1, source_target_pairs={{0,3},{1,0},{2,1},{3,2},{4,7},{5,4},{6,5},{7,6},{8,11},{9,8},{10,9... | collective-permute-start | bytes 1572872 | tf_op jit(solution)/shard_map/ppermute | solution.py:655
  511.8 12.3 %collective-permute-start.63 = (bf16[512,384]{1,0:T(8,128)(2,1)S(1)}, bf16[512,384]{1,0:T(8,128)(2,1)S(1)}, u32[]{:S(2)}, u32[]{:S(2)}) collective-permute-start(bf16[512,384]{1,0:T(8,128)(2,1)S(1)} %pad_maximum_fusion.2), channel_id=1, source_target_pairs={{0,8},{8,0},{16,24},{24,16},{1,9},{9,1},{17,25},{25,17},{2,10},{10... | collective-permute-start | bytes 1179656 | tf_op jit(solution)/shard_map/ppermute | solution.py:659
  513.0 15.8 %collective-permute-start.64 = (bf16[512,384]{1,0:T(8,128)(2,1)S(1)}, bf16[512,384]{1,0:T(8,128)(2,1)S(1)}, u32[]{:S(2)}, u32[]{:S(2)}) collective-permute-start(bf16[512,384]{1,0:T(8,128)(2,1)S(1)} %pad_maximum_fusion.3), channel_id=1, source_target_pairs={{0,16},{8,24},{16,0},{24,8},{1,17},{9,25},{17,1},{25,9},{2,18},{10... | collective-permute-start | bytes 1179656 | tf_op jit(solution)/shard_map/ppermute | solution.py:659
  535.4 31.7 %all-to-all-start.6 = ((bf16[8,64,768]{2,1,0:T(8,128)(2,1)}), bf16[8,64,768]{2,1,0:T(8,128)(2,1)S(1)}, u32[]{:S(2)}, u32[]{:S(2)}) async-start(bf16[8,64,768]{2,1,0:T(8,128)(2,1)} %bitcast.136), calls=%async_computation.6 | async-start | bytes 1572864 | tf_op jit(solution)/shard_map/all_to_all | solution.py:740
  541.0 25.2 %collective-permute-start.65 = (bf16[128,2048]{1,0:T(8,128)(2,1)S(1)}, bf16[128,2048]{1,0:T(8,128)(2,1)S(1)}, u32[]{:S(2)}, u32[]{:S(2)}) collective-permute-start(bf16[128,2048]{1,0:T(8,128)(2,1)S(1)} %add_convert_fusion), channel_id=1, source_target_pairs={{0,3},{1,0},{2,1},{3,2},{4,7},{5,4},{6,5},{7,6},{8,11},{9,8},{10,9... | collective-permute-start | bytes 1572872 | tf_op jit(solution)/shard_map/ppermute | solution.py:655
  544.8 21.4 %collective-permute-start.66 = (bf16[128,2048]{1,0:T(8,128)(2,1)S(1)}, bf16[128,2048]{1,0:T(8,128)(2,1)S(1)}, u32[]{:S(2)}, u32[]{:S(2)}) collective-permute-start(bf16[128,2048]{1,0:T(8,128)(2,1)S(1)} %get-tuple-element.399), channel_id=1, source_target_pairs={{0,4},{4,0},{1,5},{5,1},{2,6},{6,2},{3,7},{7,3},{8,12},{12,8},{9,1... | collective-permute-start | bytes 1572872 | tf_op jit(solution)/shard_map/ppermute | solution.py:650
  567.2 19.1 %all-to-all-start.7 = ((bf16[8,64,384]{2,1,0:T(8,128)(2,1)}), bf16[8,64,384]{2,1,0:T(8,128)(2,1)S(1)}, u32[]{:S(2)}, u32[]{:S(2)}) async-start(bf16[8,64,384]{2,1,0:T(8,128)(2,1)} %bitcast.86), calls=%async_computation.7 | async-start | bytes 786432 | tf_op jit(solution)/shard_map/all_to_all | solution.py:740
  (99 other events, 809.3 us)
Sparse Core Ops, SparseCore 0:
  9.6 65.9 all-gather.2
  90.1 111.7 all-gather.4
  342.1 56.8 reduce-scatter.3
  402.1 64.5 reduce-scatter.5
  529.7 54.2 reduce-scatter.7

commit v4 on v3

--- a/solution.py
+++ b/solution.py
@@ -368,7 +368,37 @@
     )(starts, mid, grad, cotangent, gain, *pieces)
 
 
-def turn_back_kernel(grad_ref, cosine_ref, sine_ref, unit_ref, by_tokens_ref, out_ref, low):
+def write_parts(place_ref, count, rows_of, outs):
+    if len(outs) == 1:
+        for group in range(count):
+            block = rows_of(group)
+            outs[0][group * block.shape[0] : (group + 1) * block.shape[0]] = block
+        return
+    to_beside, to_across, beside_low, across_top, own = outs
+    half = own.shape[0] // 2
+    block = rows_of(place_ref[0] ^ 3)
+    to_beside[:half] = block[:half]
+    to_across[:half] = block[half:]
+    block = rows_of(place_ref[0] ^ 1)
+    to_beside[half:] = block[:half]
+    beside_low[...] = block[half:]
+    block = rows_of(place_ref[0] ^ 2)
+    to_across[half:] = block[half:]
+    across_top[...] = block[:half]
+    own[...] = rows_of(place_ref[0])
+
+
+def part_shapes(rows, columns, square):
+    if not square:
+        return [jax.ShapeDtypeStruct((rows, columns), bf16)]
+    own = rows // 4
+    return [
+        jax.ShapeDtypeStruct((each, columns), bf16) for each in (own, own, own // 2, own // 2, own)
+    ]
+
+
+def turn_back_kernel(count, place_ref, grad_ref, cosine_ref, sine_ref, unit_ref, by_tokens_ref, *refs):
+    outs, low = refs[:-1], refs[-1]
     heads, blocks, _, head_dim, rows = grad_ref.shape
     half = head_dim // 2
     for block in range(blocks):
@@ -386,37 +416,37 @@
                     ).astype(bf16)
                 low[at : at + head_dim, span] = grad
         by_tokens_ref[block] = low[:, span].T
-    width = out_ref.shape[0]
-    cut = min(512, width)
-    for start in range(0, width, cut):
-        out_ref[start : start + cut] = contract(
-            unit_ref[:, start : start + cut], low[...], 0, 1
-        ).astype(bf16)
-
-
-def turn_back(grad, cosine, sine, unit_group):
+    each = unit_ref.shape[1] // count
+
+    def rows_of(group):
+        start = group * each if isinstance(group, int) else pl.multiple_of(group * each, each)
+        return contract(unit_ref[:, pl.ds(start, each)], low[...], 0, 1).astype(bf16)
+
+    write_parts(place_ref, count, rows_of, outs)
+
+
+def turn_back(grad, cosine, sine, unit_group, place, count, square):
     heads, blocks, _, head_dim, rows = grad.shape
     columns = 3 * heads * head_dim
-    return pl.pallas_call(
-        turn_back_kernel,
-        out_shape=(
-            jax.ShapeDtypeStruct((blocks, rows, columns), bf16),
-            jax.ShapeDtypeStruct((unit_group.shape[1], columns), bf16),
-        ),
-        in_specs=[IN_VMEM] * 4,
-        out_specs=(IN_VMEM,) * 2,
+    shapes = part_shapes(unit_group.shape[1], columns, square)
+    by_tokens, *parts = pl.pallas_call(
+        functools.partial(turn_back_kernel, count),
+        out_shape=[jax.ShapeDtypeStruct((blocks, rows, columns), bf16), *shapes],
+        in_specs=[IN_SMEM] + [IN_VMEM] * 4,
+        out_specs=[IN_VMEM] * (1 + len(shapes)),
         scratch_shapes=[pltpu.VMEM((columns, blocks * rows), bf16)],
         compiler_params=pltpu.CompilerParams(vmem_limit_bytes=48 * 2**20),
         cost_estimate=lasting(8),
         name="turn_back",
-    )(grad, cosine, sine, unit_group)
+    )(place, grad, cosine, sine, unit_group)
+    return by_tokens, parts
 
 
 def norm_kernel(count, table, starts_ref, spots_ref, by_tokens_ref, *refs):
     pieces, outs, (weight, semaphores) = refs[:count], refs[count:-2], refs[-2:]
     copies = start_pieces(pieces, table, starts_ref, weight, semaphores)
     rows = by_tokens_ref.shape[1]
-    steps = len(outs) // 2
+    steps = len(outs) - 1
     for copy in copies:
         copy.wait()
     width = weight.shape[0]
@@ -428,7 +458,7 @@
         for start in range(0, width, cut):
             part = contract(tokens, weight[start : start + cut], 1, 1)
             outs[step][:, start : start + cut] = part[:rows]
-            outs[steps + step][:, start : start + cut] = part[rows:].astype(bf16)
+            outs[steps][step, :, start : start + cut] = part[rows:].astype(bf16)
 
 
 def back_to_norm(by_tokens, pieces, table, starts, spots, width):
@@ -437,9 +467,9 @@
     made = pl.pallas_call(
         functools.partial(norm_kernel, len(pieces), table),
         out_shape=(jax.ShapeDtypeStruct((rows, width), f32),) * steps
-        + (jax.ShapeDtypeStruct((rows, width), bf16),) * steps,
+        + (jax.ShapeDtypeStruct((steps, rows, width), bf16),),
         in_specs=[IN_SMEM] * 2 + [IN_VMEM] + [ANYWHERE] * len(pieces),
-        out_specs=(IN_VMEM,) * (2 * steps),
+        out_specs=(IN_VMEM,) * (steps + 1),
         scratch_shapes=[
             pltpu.VMEM((width, columns), bf16),
             pltpu.SemaphoreType.DMA((len(table),)),
@@ -448,7 +478,7 @@
         cost_estimate=lasting(7),
         name="back_to_norm",
     )(starts, spots, by_tokens, *pieces)
-    return made[:steps], made[steps:]
+    return made[:steps], made[steps]
 
 
 def weight_sums_kernel(
@@ -539,7 +569,7 @@
     pieces = (refs[: counts[0]], refs[counts[0] : sum(counts[:2])], refs[sum(counts[:2]) : sum(counts)])
     outs, weights, semaphores = refs[-15:-6], refs[-6:-3], refs[-3:]
     act_ref, grad_gate_ref, grad_up_ref, normed_ref, grads_ref = outs[:5]
-    keep_ref, send_ref, branch_keep_ref, branch_send_ref = outs[5:]
+    branch_keep_ref, branch_send_ref, keep_ref, send_ref = outs[5:]
     rows, width = own_ref.shape
     copies = [
         start_pieces(*each) for each in zip(pieces, tables, starts_refs, weights, semaphores)
@@ -575,8 +605,8 @@
     for start in range(0, width, cut):
         span = slice(start, start + cut)
         part = contract(act_ref[0], down_w[:, span], 1, 0)
-        branch_keep_ref[:, span] = part[:rows]
-        branch_send_ref[:, span] = part[rows:].astype(bf16)
+        branch_keep_ref[0, :, span] = part[:rows]
+        branch_send_ref[0, :, span] = part[rows:].astype(bf16)
 
 
 def units_chunk(step, count, own, other, grad_own, grad_other, weights, held):
@@ -590,13 +620,15 @@
     kept_rows = pl.BlockSpec((1, 2 * rows, width), lambda i: (step, 0, 0))
     by_units = jax.ShapeDtypeStruct((count, 2 * rows, units), bf16)
     by_rows = jax.ShapeDtypeStruct((count, 2 * rows, width), bf16)
-    sums = (jax.ShapeDtypeStruct((rows, width), f32), jax.ShapeDtypeStruct((rows, width), bf16))
+    sums = tuple(jax.ShapeDtypeStruct((rows, width), kind) for kind in (f32, bf16))
+    kept_branch = pl.BlockSpec((1, rows, width), lambda i: (step, 0, 0))
+    branch = tuple(jax.ShapeDtypeStruct((count, rows, width), kind) for kind in (f32, bf16))
     return pl.pallas_call(
         functools.partial(units_kernel, counts, tables),
         grid=(1,),
-        out_shape=(by_units,) * 3 + (by_rows,) * 2 + sums * 2,
+        out_shape=(by_units,) * 3 + (by_rows,) * 2 + branch + sums,
         in_specs=[whole] * 4 + [IN_SMEM] * 3 + [ANYWHERE] * (len(arrays) + len(held)),
-        out_specs=(kept_units,) * 3 + (kept_rows,) * 2 + (whole,) * 4,
+        out_specs=(kept_units,) * 3 + (kept_rows,) * 2 + (kept_branch,) * 2 + (whole,) * 2,
         scratch_shapes=[pltpu.VMEM((units, width), bf16)] * 3
         + [pltpu.SemaphoreType.DMA((len(table),)) for table in tables],
         input_output_aliases={7 + len(arrays) + i: i for i in range(len(held))},
@@ -631,6 +663,29 @@
     )(left, right, *held)
 
 
+def product_parts_kernel(count, place_ref, left_ref, right_ref, *outs):
+    each = left_ref.shape[1] // count
+
+    def rows_of(group):
+        start = group * each if isinstance(group, int) else pl.multiple_of(group * each, each)
+        return contract(left_ref[:, pl.ds(start, each)], right_ref[...], 0, 0).astype(bf16)
+
+    write_parts(place_ref, count, rows_of, outs)
+
+
+def product_parts(left, right, place, count, square):
+    shapes = part_shapes(left.shape[1], right.shape[1], square)
+    return pl.pallas_call(
+        functools.partial(product_parts_kernel, count),
+        out_shape=shapes,
+        in_specs=[IN_SMEM] + [IN_VMEM] * 2,
+        out_specs=[IN_VMEM] * len(shapes),
+        compiler_params=pltpu.CompilerParams(vmem_limit_bytes=48 * 2**20),
+        cost_estimate=lasting(10),
+        name="product_parts",
+    )(place, left, right)
+
+
 def rotary_tables(positions, head_dim):
     half_dim = head_dim // 2
     frequency = rope_base ** (-(jnp.arange(half_dim, dtype=f32) * 2.0) / head_dim)
@@ -703,41 +758,44 @@
 
 
 def group_parts(whole):
-    parts = whole.reshape(lax.axis_size("r") * lax.axis_size("p"), -1, whole.shape[1])
     if not square_groups():
-        return parts
+        return [whole]
+    parts = whole.reshape(4, -1, whole.shape[1])
     place = lax.axis_index("p")
-    return [lax.dynamic_index_in_dim(parts, place ^ bits, 0, keepdims=False) for bits in range(4)]
+    own, beside, across, corner = (
+        lax.dynamic_index_in_dim(parts, place ^ bits, 0, keepdims=False) for bits in range(4)
+    )
+    half = own.shape[0] // 2
+    return [
+        jnp.concatenate([corner[:half], beside[:half]]),
+        jnp.concatenate([corner[half:], across[half:]]),
+        beside[half:], across[:half], own,
+    ]
 
 
 def scatter_first(parts):
     if not square_groups():
         return ()
-    _, beside, across, corner = parts
-    half = corner.shape[0] // 2
-    return (
-        from_flipped(jnp.concatenate([corner[:half], beside[:half]]), 1),
-        from_flipped(jnp.concatenate([corner[half:], across[half:]]), 2),
-    )
+    return from_flipped(parts[0], 1), from_flipped(parts[1], 2)
 
 
 def scatter_second(parts, first):
     if not square_groups():
-        flat = parts.reshape(-1, parts.shape[-1])
-        return lax.psum_scatter(flat, GROUPS, scatter_dimension=0, tiled=True)
-    own, beside, across, corner = parts
-    half = corner.shape[0] // 2
+        own = lax.psum_scatter(parts[0], GROUPS, scatter_dimension=0, tiled=True)
+        return own.astype(f32)
+    _, _, beside_low, across_top, own = parts
+    half = own.shape[0] // 2
     from_beside, from_across = (array.astype(f32) for array in first)
-    beside_low = (beside[half:].astype(f32) + from_across[:half]).astype(bf16)
-    across_top = (across[:half].astype(f32) + from_beside[:half]).astype(bf16)
+    beside_low = (beside_low.astype(f32) + from_across[:half]).astype(bf16)
+    across_top = (across_top.astype(f32) + from_beside[:half]).astype(bf16)
     total_low = from_across[half:] + from_flipped(beside_low, 1).astype(f32)
     total_top = from_beside[half:] + from_flipped(across_top, 2).astype(f32)
-    return (own.astype(f32) + jnp.concatenate([total_top, total_low])).astype(bf16)
+    return own.astype(f32) + jnp.concatenate([total_top, total_low])
 
 
 def to_owners(own):
     count = lax.axis_size(TENSOR)
-    return lax.all_to_all(own.reshape(count, -1, own.shape[1]), TENSOR, 0, 0)
+    return lax.all_to_all(own.astype(bf16).reshape(count, -1, own.shape[1]), TENSOR, 0, 0)
 
 
 def shards(tokens, attn_qkv, attn_out_t, mlp_weight, norm1, norm2, cotangent):
@@ -793,7 +851,7 @@
     qkv = qkv.reshape(-1, 3, head_dim, rows)
     out_ring.append(later)
     rest_whole = lax.all_gather(
-        after(mlp_weight[:, width:], x_group), GROUPS, axis=0, tiled=True
+        after(mlp_weight[:, width:], qkv_arrays), GROUPS, axis=0, tiled=True
     )
     up_weight, down_weight = (
         ([rest_whole], ((0, 0, rest_whole.shape[0], column),), jnp.zeros((1,), jnp.int32))
@@ -844,7 +902,7 @@
     attended_group = attended_head.reshape(group_count, tensor_count, head_dim, rows)
     attended_group = lax.all_to_all(after(attended_group, normed_two), "p", 0, 0)
 
-    held, branch_parts = (), []
+    held = ()
     normed, grad_out, came, total = normed_two, grad_out_ring[0], (), None
     for step in range(line_count):
         later = from_next(normed) if step < line_count - 1 else ()
@@ -852,11 +910,10 @@
             grad_out_ring.append(from_next(grad_out_ring[-1]))
         if step >= 2:
             came = from_next(total.astype(bf16))
-        *held, keep, send, branch_keep, branch_send = units_chunk(
+        *held, keep, send = units_chunk(
             step, line_count, normed, swap_cores(normed), grad_out, swap_cores(grad_out),
             (gate_weight, up_weight, down_weight), held,
         )
-        branch_parts.append((branch_keep, branch_send))
         if step == 0:
             later, attended_group, keep, send = together(later, attended_group, keep, send)
         else:
@@ -871,8 +928,9 @@
         else:
             total = part if step == 1 else came.astype(f32) + part
     activation, gate_grads, up_grads, normed_group, grad_out_group = (
-        array.reshape(group_rows, -1) for array in held
-    )
+        array.reshape(group_rows, -1) for array in held[:5]
+    )
+    branch_keep, branch_send = held[5:]
 
     def over_groups(part):
         return lax.psum_scatter(part, GROUPS, scatter_dimension=0, tiled=True)
@@ -885,32 +943,32 @@
         HEADS // tensor_count, head_dim,
     )
     grad_head = lax.all_to_all(grad_attended, ("p", "c", "z"), 0, 0)
-    up_grads, activation = after((up_grads, activation), grad_attended)
-    up_term = transposed_product(up_grads, normed_group)
-    down_term = transposed_product(activation, grad_out_group)
-    grad_head, up_term, down_term = together(grad_head, up_term, down_term)
+    up_term = transposed_product(after(up_grads, grad_attended), normed_group)
+    group_place = lax.axis_index("p").astype(jnp.int32)[None]
+    group_all = share_count * group_count
+    branch_came = swap_cores(after(branch_send, grad_attended))
+    grad_head, up_term, branch_came = together(grad_head, up_term, branch_came)
+
+    def branch_sum(came, step):
+        return came + branch_keep[step] + branch_came[step].astype(f32)
 
     grad_head = over_shares(grad_head)
+    grad_gate_w, grad_up_w = over_groups(gate_term), over_groups(up_term)
     count = qkv.shape[0] * rows // block
     backward = functools.partial(attend_backward, qkv, grad_head, attended, logsum, block)
     later_keys = backward(count // 2, count)
     grad_mid_ring = [grad_mid_low, from_next(after(grad_mid_low, grad_head))]
-    branch_came = [swap_cores(part[1]) for part in after(branch_parts, grad_head)]
-    later_keys, grad_mid_ring, branch_came = together(later_keys, grad_mid_ring, branch_came)
-
-    def branch_sum(came, step):
-        return came + branch_parts[step][0] + branch_came[step].astype(f32)
-
+    mid_swapped = [swap_cores(after(grad_mid_low, grad_head))]
+    later_keys, grad_mid_ring, mid_swapped = together(later_keys, grad_mid_ring, mid_swapped)
     grad_qkv_head = backward(0, count // 2, later_keys)[0]
+    mid_swapped += [swap_cores(array) for array in grad_mid_ring[1:]]
     for _ in range(line_count - 3):
         grad_mid_ring.append(from_next(grad_mid_ring[-1]))
     came = from_next(after(branch_sum(0.0, 1 % line_count).astype(bf16), later_keys))
-    mid_swapped = [swap_cores(array) for array in grad_mid_ring[:2]]
-    grad_qkv_head, grad_mid_ring, came, mid_swapped = together(
-        grad_qkv_head, grad_mid_ring, came, mid_swapped
+    grad_qkv_head, grad_mid_ring, came, mid_swapped, grad_gate_w = together(
+        grad_qkv_head, grad_mid_ring, came, mid_swapped, grad_gate_w
     )
     grad_qkv_head = own_share(grad_qkv_head)
-    grad_gate_w, grad_up_w = over_groups(gate_term), over_groups(up_term)
 
     spots = jnp.stack([spot for step in range(line_count) for spot in chunk_places(step)])
     spots = spots.astype(jnp.int32)
@@ -920,44 +978,53 @@
     grad_mid_ring.append(from_next(grad_mid_ring[-1]))
     for step in range(2, line_count - 1):
         came = from_next(branch_sum(came.astype(f32), step).astype(bf16))
-    grad_qkv_rows, grad_mid_ring, came, mid_swapped = together(
-        grad_qkv_rows, grad_mid_ring, came, mid_swapped
-    )
+    grad_qkv_rows, mid_swapped = together(grad_qkv_rows, mid_swapped)
+    grad_qkv_low, qkv_parts = turn_back(
+        grad_qkv_rows, cosine, sine, unit_group, group_place, group_all, square_groups()
+    )
+    grad_qkv_low, qkv_parts, grad_mid_ring, came = together(
+        grad_qkv_low, qkv_parts, grad_mid_ring, came
+    )
+    qkv_first = scatter_first(qkv_parts)
     branch_last = branch_sum(came.astype(f32), line_count - 1) if line_count > 2 else came
     branch_last = from_next(branch_last.astype(bf16))
-    mid_swapped.append(swap_cores(grad_mid_ring[-1]))
-    grad_qkv_low, qkv_term = turn_back(grad_qkv_rows, cosine, sine, unit_group)
-    qkv_parts = group_parts(qkv_term)
-    qkv_first = scatter_first(qkv_parts)
     keep, send = back_to_norm(
-        after(grad_qkv_low, qkv_parts), qkv_arrays, qkv_table, qkv_starts, spots, width
-    )
-    keep, send, branch_last, mid_swapped = together(keep, send, branch_last, mid_swapped)
-    total = add_over_cores(keep[1 % line_count], send[1 % line_count])
+        grad_qkv_low, qkv_arrays, qkv_table, qkv_starts, spots, width
+    )
+    keep, send, branch_last, qkv_first = together(keep, send, branch_last, qkv_first)
+    swapped = swap_cores(send)
+    total = keep[1 % line_count] + swapped[1 % line_count].astype(f32)
     came = from_next(total.astype(bf16))
-    swapped = [swap_cores(send[step]) for step in range(2, line_count)]
+    mid_swapped.append(swap_cores(after(grad_mid_ring[-1], total)))
     grad_mid_blocks = [
         part for pair in zip(grad_mid_ring, mid_swapped, strict=True) for part in pair
     ]
     out_term = out_product(grad_mid_blocks, spots, attended_group, norm_two_part)
-    came, swapped, qkv_first, out_term = together(came, swapped, qkv_first, out_term)
-    total = came.astype(f32) + keep[2 % line_count] + swapped[0].astype(f32)
+    down_parts = product_parts(
+        after(activation, total), grad_out_group, group_place, group_all, square_groups()
+    )
+    qkv_own = scatter_second(qkv_parts, after(qkv_first, total)).astype(bf16)
+    came, qkv_own, out_term, down_parts, grad_up_w = together(
+        came, qkv_own, out_term, down_parts, grad_up_w
+    )
+    qkv_sums = to_owners(qkv_own)
+    total = came.astype(f32) + keep[2 % line_count] + swapped[2 % line_count].astype(f32)
     came = from_next(total.astype(bf16))
     out_parts = group_parts(out_term)
     out_first = scatter_first(out_parts)
-    qkv_own = scatter_second(qkv_parts, qkv_first)
-    came, qkv_own, out_first = together(came, qkv_own, out_first)
-    qkv_sums = to_owners(qkv_own)
-    grad_down_w = over_groups(after(down_term, qkv_own))
+    down_first = scatter_first(down_parts)
+    came, out_first = together(came, out_first)
     for step in range(3, line_count):
-        total = came.astype(f32) + keep[step] + swapped[step - 2].astype(f32)
+        total = came.astype(f32) + keep[step] + swapped[step].astype(f32)
         came = from_next(total.astype(bf16))
-    swapped = swap_cores(after(send[0], qkv_own))
     out_own = scatter_second(out_parts, out_first)
-    came, swapped, out_own = together(came, swapped, out_own)
-    weighted_one = came.astype(f32) + keep[0] + swapped.astype(f32)
-    out_sums = to_owners(after(out_own, qkv_sums))
-    grad_mlp = jnp.concatenate([grad_gate_w, grad_up_w, grad_down_w], axis=1).astype(f32)
+    came, down_first, out_own, qkv_sums = together(came, down_first, out_own, qkv_sums)
+    out_sums = to_owners(out_own)
+    weighted_one = came.astype(f32) + keep[0] + swapped[0].astype(f32)
+    grad_down_w = scatter_second(down_parts, down_first)
+    grad_mlp = jnp.concatenate(
+        [grad_gate_w.astype(f32), grad_up_w.astype(f32), grad_down_w.astype(f32)], axis=1
+    )
     result = (middle + branch_sum(branch_last.astype(f32), 0)).astype(bf16)
     factor_one = lax.rsqrt(jnp.mean(x * x, axis=-1, keepdims=True) + epsilon)
     grad_tokens = (

time: 610 us -> 600 us (0.984)
  Pallas kernels: 184 us -> 171 us
  other arithmetic: 36 us -> 46.6 us
  local copies, waits for them, and re-layouts: 37 us -> 29.4 us
    ppermute x21, waiting for transfers between devices: 88.8 us -> 60.4 us  [from_next(): lax.ppermute(array, 'z', [(i, (i - 1) % count) for i in range(count)])]
    all_to_all x1, waiting for transfers between devices: 0.01 us -> 19.9 us  [shards(): grad_qkv_rows = lax.all_to_all(grad_qkv_rows, 'p', 0, 0)]
    ppermute x20 -> x24, waiting for transfers between devices: 88.8 us -> 98.3 us  [from_flipped(): return lax.ppermute(array, 'p', [(i, i ^ bit) for i in range(4)])]
    all_to_all x2, waiting for transfers between devices: 9.08 us -> 0.01 us  [to_owners(): lax.all_to_all(own.astype(bf16).reshape(count, -1, own.shape[1]), TENSOR,...]
    pallas_call x3 -> x2, Pallas kernels: 26.1 us -> 17.2 us  [transposed_product(): pl.pallas_call(transposed_product_kernel, grid=(units // cut,), out_shape...]
    pallas_call x4, Pallas kernels: 57.2 us -> 49.1 us  [units_chunk(): pl.pallas_call(functools.partial(units_kernel, counts, tables), grid=(1,)...]
    pallas_call x1 -> x2, Pallas kernels: 7.68 us -> 13.9 us  [the longest x1 7.38 us: product_parts(): pl.pallas_call(functools.partial(product_parts_kernel, count), out_shape=...]
    unnamed x167 -> x189, local copies, waits for them, and re-layouts: 24.3 us -> 18.8 us
  transfers between devices with their start and end apart: 82 -> 79, of which waited for: 33 -> 34; matrix products, arithmetic and copies ran while one was open for 7% -> 9% of each run, Pallas kernels for 31% -> 29%
where the time goes in v4:
time: 600 us; the launch traced here: 591 us
  waiting for transfers between devices  208 us (35%)
  Pallas kernels  171 us (28%)
  starting transfers between devices  121 us (20%)
  other arithmetic  46.6 us (8%)
  local copies, waits for them, and re-layouts  29.4 us (5%)
  between operations  15.6 us (3%)
    ppermute x24, waiting for transfers between devices, from_flipped(): return lax.ppermute(array, 'p', [(i, i ^ bit) for i in range(4)])  98.3 us
    ppermute x21, waiting for transfers between devices, from_next(): lax.ppermute(array, 'z', [(i, (i - 1) % count) for i in range(count)])  60.4 us
    ppermute x21, starting transfers between devices, from_next(): lax.ppermute(array, 'z', [(i, (i - 1) % count) for i in range(count)])  52.5 us
    pallas_call x4, Pallas kernels, units_chunk(): pl.pallas_call(functools.partial(units_kernel, counts, tables), grid=(1,)...  49.1 us
    pallas_call x2, Pallas kernels, attend_backward(): pl.pallas_call(functools.partial(backward_kernel, lower, upper, last, blo...  35.6 us
    ppermute x24, starting transfers between devices, from_flipped(): return lax.ppermute(array, 'p', [(i, i ^ bit) for i in range(4)])  24.6 us
    all_to_all x1, waiting for transfers between devices, shards(): grad_qkv_rows = lax.all_to_all(grad_qkv_rows, 'p', 0, 0)  19.9 us
    unnamed x189, local copies, waits for them, and re-layouts  18.8 us
  transfers between devices with their start and end apart: 79, of which 34 were waited for; matrix products, arithmetic and copies ran while one was open for 9% of the time, Pallas kernels for 29%

profile of v4, /device:TPU:0, one launch (start us, length us, event | category | flops | bytes accessed | tf_op | source)
XLA Modules:
  0.0 591.4 jit_solution(8803464700185670464)
XLA Ops:
  12.7 6.5 %all-to-all-start = ((bf16[8,64,768]{2,1,0:T(8,128)(2,1)}), bf16[8,64,768]{2,1,0:T(8,128)(2,1)S(1)}, u32[]{:S(2)}, u32[]{:S(2)}) async-start(bf16[8,64,768]{2,1,0:T(8,128)(2,1)} %reshape.117), calls=%async_computation | async-start | bytes 1572864 | tf_op jit(solution)/shard_map/all_to_all | solution.py:829
  24.9 3.1 slice.135
  28.1 24.1 %collective-permute-done.1 = bf16[64,2176]{1,0:T(8,128)(2,1)S(1)} collective-permute-done((bf16[64,2176]{1,0:T(8,128)(2,1)S(1)}, bf16[64,2176]{1,0:T(8,128)(2,1)S(1)}, u32[]{:S(2)}, u32[]{:S(2)}) %collective-permute-start.1) | collective-permute-done | bytes 278560 | tf_op jit(solution)/shard_map/ppermute | solution.py:714
  53.4 5.1 all-to-all-done
  64.8 12.0 %collective-permute-done.5.refs_2_ = bf16[512,768]{1,0:T(8,128)(2,1)S(1)} collective-permute-done((bf16[512,768]{1,0:T(8,128)(2,1)S(1)}, bf16[512,768]{1,0:T(8,128)(2,1)S(1)}, u32[]{:S(2)}, u32[]{:S(2)}) %collective-permute-start.5) | collective-permute-done | bytes 786464 | tf_op jit(solution)/shard_map/ppermute | solution.py:714
  82.3 7.8 %collective-permute-done.7.refs_4_ = bf16[256,768]{1,0:T(8,128)(2,1)S(1)} collective-permute-done((bf16[256,768]{1,0:T(8,128)(2,1)S(1)}, bf16[256,768]{1,0:T(8,128)(2,1)S(1)}, u32[]{:S(2)}, u32[]{:S(2)}) %collective-permute-start.7) | collective-permute-done | bytes 393248 | tf_op jit(solution)/shard_map/ppermute | solution.py:714
  95.1 10.2 %project.1 = (bf16[1024,2048]{1,0:T(8,128)(2,1)}, bf16[4,8,3,64,128]{4,3,2,1,0:T(8,128)(2,1)}) custom-call(s32[5]{0:T(128)S(1)} %stack.232.starts_ref, bf16[1024,2048]{1,0:T(8,128)(2,1)} %all-gather.3.cloned.1.call-done.x_ref, f32[32,1024]{1,0:T(8,128)S(1)} %get-tuple-element.434.cosine_ref, f32[32,1024]{1,0:T(8,128)S(1)} %get-tuple-element.433.sine_ref, ...), custom_call_target="tpu_custom_call" | custom-call | flops 11000000512 | bytes 1000 | tf_op jit(solution)/shard_map/project/pallas_call | solution.py:246
  105.4 6.7 %collective-permute-done.11.refs_7_ = bf16[128,2048]{1,0:T(8,128)(2,1)S(1)} collective-permute-done((bf16[128,2048]{1,0:T(8,128)(2,1)S(1)}, bf16[128,2048]{1,0:T(8,128)(2,1)S(1)}, u32[]{:S(2)}, u32[]{:S(2)}) %collective-permute-start.11) | collective-permute-done | bytes 524320 | tf_op jit(solution)/shard_map/ppermute | solution.py:714
  112.1 2.9 collective-permute-done.10.refs_6_
  115.0 2.4 collective-permute-done.12.refs_1_
  117.4 3.6 all-to-all-start.1
  121.8 3.4 collective-permute-start.13
  127.2 22.3 %collective-permute-done.13.refs_2_ = bf16[256,2176]{1,0:T(8,128)(2,1)S(1)} collective-permute-done((bf16[256,2176]{1,0:T(8,128)(2,1)}, bf16[256,2176]{1,0:T(8,128)(2,1)S(1)}, u32[]{:S(2)}, u32[]{:S(2)}) %collective-permute-start.13) | collective-permute-done | bytes 1114144 | tf_op jit(solution)/shard_map/ppermute | solution.py:710
  149.6 4.5 collective-permute-start.16
  154.1 18.5 %attend_forward.1 = (bf16[32,64,128]{2,1,0:T(8,128)(2,1)}, f32[4,1,1024]{2,1,0:T(1,128)}) custom-call(bf16[32,3,64,128]{3,2,1,0:T(8,128)(2,1)} %bitcast.158), custom_call_target="tpu_custom_call" | custom-call | flops 19800000512 | bytes 1000 | tf_op jit(solution)/shard_map/attend_forward/pallas_call | solution.py:157
  172.6 5.9 collective-permute-done.16.refs_3_
  178.5 7.0 %all-to-all-start.2 = ((bf16[32,64,128]{2,1,0:T(8,128)(2,1)}), bf16[32,64,128]{2,1,0:T(8,128)(2,1)S(1)}, u32[]{:S(2)}, u32[]{:S(2)}) async-start(bf16[32,64,128]{2,1,0:T(8,128)(2,1)} %get-tuple-element.243.refs_2_), calls=%async_computation.2 | async-start | bytes 1048576 | tf_op jit(solution)/shard_map/all_to_all | solution.py:893
  185.6 3.7 collective-permute-start.19
  189.4 10.6 %all-to-all-done.2.attended_ref = bf16[32,64,128]{2,1,0:T(8,128)(2,1)S(1)} async-done(((bf16[32,64,128]{2,1,0:T(8,128)(2,1)}), bf16[32,64,128]{2,1,0:T(8,128)(2,1)S(1)}, u32[]{:S(2)}, u32[]{:S(2)}) %all-to-all-start.2) | async-done | bytes 524320 | tf_op jit(solution)/shard_map/all_to_all | solution.py:893
  200.0 8.2 %collective-permute-done.19.grad_own_ref = bf16[128,2048]{1,0:T(8,128)(2,1)} collective-permute-done((bf16[128,2048]{1,0:T(8,128)(2,1)S(1)}, bf16[128,2048]{1,0:T(8,128)(2,1)}, u32[]{:S(2)}, u32[]{:S(2)}) %collective-permute-start.19) | collective-permute-done | bytes 524320 | tf_op jit(solution)/shard_map/ppermute | solution.py:710
  208.2 6.8 %collective-permute-start.20 = (bf16[128,2048]{1,0:T(8,128)(2,1)}, bf16[128,2048]{1,0:T(8,128)(2,1)S(1)}, u32[]{:S(2)}, u32[]{:S(2)}) collective-permute-start(bf16[128,2048]{1,0:T(8,128)(2,1)} %collective-permute-done.19.grad_own_ref), channel_id=1, source_target_pairs={{0,3},{1,0},{2,1},{3,2},{4,7},{5,4},{6,5},{7,6},{8,11},{9,8},{10,9... | collective-permute-start | bytes 1572872 | tf_op jit(solution)/shard_map/ppermute | solution.py:710
  216.2 7.2 %finish_attention.1 = (f32[128,2048]{1,0:T(8,128)S(1)}, bf16[128,2048]{1,0:T(8,128)(2,1)S(1)}, f32[1,2048]{1,0:T(1,128)S(1)}) custom-call(s32[40]{0:T(128)S(1)} %stack.226.starts_ref, bf16[128,2048]{1,0:T(8,128)(2,1)S(1)} %copy-done, bf16[32,64,128]{2,1,0:T(8,128)(2,1)S(1)} %all-to-all-done.2.attended_ref, ...), custom_call_target="tpu_custom_call" | custom-call | flops 9900000256 | bytes 1000 | tf_op jit(solution)/shard_map/finish_attention/pallas_call | solution.py:297
  223.5 2.9 collective-permute-done.20.grad_own_ref
  227.7 4.2 collective-permute-start.21
  231.9 3.5 all-to-all-start.3
  236.0 12.3 %units_chunk.4 = (bf16[4,256,1024]{2,1,0:T(8,128)(2,1)}, bf16[4,256,1024]{2,1,0:T(8,128)(2,1)}, bf16[4,256,1024]{2,1,0:T(8,128)(2,1)}, bf16[4,256,2048]{2,1,0:T(...) custom-call(bf16[128,2048]{1,0:T(8,128)(2,1)} %copy-done.46, ...), custom_call_target="tpu_custom_call" | custom-call | flops 14300000256 | bytes 1000 | tf_op jit(solution)/shard_map/units_chunk/pallas_call | solution.py:626
  248.3 6.8 %collective-permute-done.26.grad_own_ref = bf16[128,2048]{1,0:T(8,128)(2,1)} collective-permute-done((bf16[128,2048]{1,0:T(8,128)(2,1)}, bf16[128,2048]{1,0:T(8,128)(2,1)}, u32[]{:S(2)}, u32[]{:S(2)}) %collective-permute-start.26) | collective-permute-done | bytes 524320 | tf_op jit(solution)/shard_map/ppermute | solution.py:710
  255.6 4.3 collective-permute-start.24
  260.9 12.3 %units_chunk.5 = (bf16[4,256,1024]{2,1,0:T(8,128)(2,1)}, bf16[4,256,1024]{2,1,0:T(8,128)(2,1)}, bf16[4,256,1024]{2,1,0:T(8,128)(2,1)}, bf16[4,256,2048]{2,1,0:T(...) custom-call(bf16[128,2048]{1,0:T(8,128)(2,1)} %collective-permute-do, ...), custom_call_target="tpu_custom_call", output_to_operand_aliasing={{0}: (14, {}), {1}: (15, {}), {2}: (16, {}), {3}: (17, {}),... | custom-call | flops 14300000256 | bytes 1000 | tf_op jit(solution)/shard_map/units_chunk/pallas_call | solution.py:626
  273.9 2.4 collective-permute-start.28
  280.4 12.3 %units_chunk.6 = (bf16[4,256,1024]{2,1,0:T(8,128)(2,1)}, bf16[4,256,1024]{2,1,0:T(8,128)(2,1)}, bf16[4,256,1024]{2,1,0:T(8,128)(2,1)}, bf16[4,256,2048]{2,1,0:T(...) custom-call(bf16[128,2048]{1,0:T(8,128)(2,1)} %copy-done.85, ...), custom_call_target="tpu_custom_call", output_to_operand_aliasing={{0}: (14, {}), {1}: (15, {}), {2}: (16, {}), {3}: (17, {}),... | custom-call | flops 14300000256 | bytes 1000 | tf_op jit(solution)/shard_map/units_chunk/pallas_call | solution.py:626
  292.7 6.7 %collective-permute-done.30 = bf16[128,2048]{1,0:T(8,128)(2,1)S(1)} collective-permute-done((bf16[128,2048]{1,0:T(8,128)(2,1)S(1)}, bf16[128,2048]{1,0:T(8,128)(2,1)S(1)}, u32[]{:S(2)}, u32[]{:S(2)}) %collective-permute-start.30) | collective-permute-done | bytes 524320 | tf_op jit(solution)/shard_map/ppermute | solution.py:710
  303.0 4.3 collective-permute-start.34
  308.2 12.2 %units_chunk.7 = (bf16[4,256,1024]{2,1,0:T(8,128)(2,1)}, bf16[4,256,1024]{2,1,0:T(8,128)(2,1)}, bf16[4,256,1024]{2,1,0:T(8,128)(2,1)}, bf16[4,256,2048]{2,1,0:T(...) custom-call(bf16[128,2048]{1,0:T(8,128)(2,1)} %copy-done.84, ...), custom_call_target="tpu_custom_call", output_to_operand_aliasing={{0}: (14, {}), {1}: (15, {}), {2}: (16, {}), {3}: (17, {}),... | custom-call | flops 14300000256 | bytes 1000 | tf_op jit(solution)/shard_map/units_chunk/pallas_call | solution.py:626
  324.9 2.8 collective-permute-start.38
  327.8 8.6 %transposed_product.2 = bf16[1024,2048]{1,0:T(8,128)(2,1)} custom-call(bf16[1024,1024]{1,0:T(8,128)(2,1)S(1)} %bitcast.152, bf16[1024,2048]{1,0:T(8,128)(2,1)} %bitcast.167), custom_call_target="tpu_custom_call" | custom-call | flops 9900000256 | bytes 1000 | tf_op jit(solution)/shard_map/transposed_product/pallas_call | solution.py:649
  336.3 3.2 collective-permute-done.38
  342.0 6.7 %back_to_attention.1 = (f32[128,2048]{1,0:T(8,128)S(1)}, bf16[128,2048]{1,0:T(8,128)(2,1)S(1)}, f32[1,2048]{1,0:T(1,128)S(1)}, bf16[32,64,128]{2,1,0:T(8,128)(2,1)}) custom-call(s32[40]{0:T(128)S(1)} %stack.226.starts_ref, f32[128,2048]{1,0:T(8,128)S(1)} %get-tuple-element.253.mid_ref, f32[128,2048]{1,0:T(8,128)S(1)} %add_add_fusion.grad_ref, ...), custom_call_target="tpu_custom_call" | custom-call | flops 6600000000 | bytes 1000 | tf_op jit(solution)/shard_map/back_to_attention/pallas_call | solution.py:351
  348.9 5.4 all-to-all-start.4
  355.9 8.7 %transposed_product.3 = bf16[1024,2048]{1,0:T(8,128)(2,1)} custom-call(bf16[1024,1024]{1,0:T(8,128)(2,1)S(1)} %bitcast.153, bf16[1024,2048]{1,0:T(8,128)(2,1)} %bitcast.168), custom_call_target="tpu_custom_call" | custom-call | flops 9900000256 | bytes 1000 | tf_op jit(solution)/shard_map/transposed_product/pallas_call | solution.py:649
  364.6 4.1 all-to-all-done.4.refs_1_
  371.6 12.0 %attend_backward.2 = (bf16[32,3,64,128]{3,2,1,0:T(8,128)(2,1)}, f32[2,64,1024]{2,1,0:T(8,128)}) custom-call(bf16[32,3,64,128]{3,2,1,0:T(8,128)(2,1)} %bitcast.159, bf16[32,64,128]{2,1,0:T(8,128)(2,1)} %all-to-all-done.4.refs_1_, bf16[32,64,128]{2,1,0:T(8,128)(2,1)} %get-tuple-element.243.refs_2_, f32[4,1,1024]{2,1,0:T(1,128)} %get-tuple-element.331.refs_3_), custom_call_target="tpu_custom_call" | custom-call | flops 19800000512 | bytes 1000 | tf_op jit(solution)/shard_map/attend_backward/pallas_call | solution.py:179
  383.7 2.4 fusion.16
  388.8 23.5 %attend_backward.3 = (bf16[32,3,64,128]{3,2,1,0:T(8,128)(2,1)}, f32[1,64,1024]{2,1,0:T(8,128)}) custom-call(bf16[32,3,64,128]{3,2,1,0:T(8,128)(2,1)} %bitcast.160, bf16[32,64,128]{2,1,0:T(8,128)(2,1)} %all-to-all-done.4.refs_1_, bf16[32,64,128]{2,1,0:T(8,128)(2,1)} %get-tuple-element.243.refs_2_, f32[4,1,1024]{2,1,0:T(1,128)} %get-tuple-element.331.refs_3_, ...), custom_call_target="tpu_custom_call" | custom-call | flops 19800000512 | bytes 1000 | tf_op jit(solution)/shard_map/attend_backward/pallas_call | solution.py:179
  412.4 4.4 all-to-all-start.5
  417.6 2.7 collective-permute-start.47
  420.3 2.5 fusion.12
  423.8 19.9 %all-to-all-done.5.grad_ref = bf16[4,8,3,64,128]{4,3,2,1,0:T(8,128)(2,1)} async-done(((bf16[4,8,3,64,128]{4,3,2,1,0:T(8,128)(2,1)}), bf16[4,8,3,64,128]{4,3,2,1,0:T(8,128)(2,1)}, u32[]{:S(2)}, u32[]{:S(2)}) %all-to-all-start.5) | async-done | bytes 1572896 | tf_op jit(solution)/shard_map/all_to_all | solution.py:976
  443.8 6.5 %turn_back.1 = (bf16[8,128,768]{2,1,0:T(8,128)(2,1)S(1)}, bf16[512,768]{1,0:T(8,128)(2,1)S(1)}, bf16[512,768]{1,0:T(8,128)(2,1)S(1)}, bf16[256,768]{1,0:T(8,128)...) custom-call(s32[1]{0:T(128)} %bitcast.57.place_ref, ...), custom_call_target="tpu_custom_call" | custom-call | flops 8800000000 | bytes 1000 | tf_op jit(solution)/shard_map/turn_back/pallas_call | solution.py:432
  456.9 7.1 %back_to_norm.1 = (f32[128,2048]{1,0:T(8,128)S(1)}, f32[128,2048]{1,0:T(8,128)S(1)}, f32[128,2048]{1,0:T(8,128)}, f32[128,2048]{1,0:T(8,128)}, bf16[4,128,2048]{2,1,0:T(8,128)(2,1)}) custom-call(s32[5]{0:T(128)S(1)} %copy-done.29, s32[8]{0:T(128)S(1)} %stack.241.spots_ref, bf16[8,128,768]{2,1,0:T(8,128)(2,1)} %copy-done.53, bf16[512,768]{1,0:T(8,128)(2,1)S(1)} %bitcast.151, ...), custom_call_target="tpu_custom_call" | custom-call | flops 7699999744 | bytes 1000 | tf_op jit(solution)/shard_map/back_to_norm/pallas_call | solution.py:467
  465.7 12.3 %collective-permute-done.50 = bf16[512,768]{1,0:T(8,128)(2,1)S(1)} collective-permute-done((bf16[512,768]{1,0:T(8,128)(2,1)S(1)}, bf16[512,768]{1,0:T(8,128)(2,1)S(1)}, u32[]{:S(2)}, u32[]{:S(2)}) %collective-permute-start.50) | collective-permute-done | bytes 786464 | tf_op jit(solution)/shard_map/ppermute | solution.py:714
  479.4 2.9 convert_element_type.308
  489.7 7.4 %product_parts.1 = (bf16[256,2048]{1,0:T(8,128)(2,1)S(1)}, bf16[256,2048]{1,0:T(8,128)(2,1)S(1)}, bf16[128,2048]{1,0:T(8,128)(2,1)S(1)}, bf16[128,2048]{1,0:T(8,128)(2,1)S(1)}, bf16[256,2048]{1,0:T(8,128)(2,1)S(1)}) custom-call(s32[1]{0:T(128)} %bitcast.57.place_ref, bf16[1024,1024]{1,0:T(8,128)(2,1)} %bitcast.170, bf16[1024,2048]{1,0:T(8,128)(2,1)} %bitcast.169), custom_call_target="tpu_custom_call" | custom-call | flops 11000000512 | bytes 1000 | tf_op jit(solution)/shard_map/product_parts/pallas_call | solution.py:678
  501.7 4.2 out_product.1
  505.9 2.6 fusion.8
  511.2 2.4 fusion.10
  513.6 3.6 all-to-all-start.6
  519.7 2.8 convert_element_type.309
  528.3 3.5 collective-permute-start.60
  532.4 16.0 %collective-permute-done.63 = bf16[256,384]{1,0:T(8,128)(2,1)S(1)} collective-permute-done((bf16[256,384]{1,0:T(8,128)(2,1)S(1)}, bf16[256,384]{1,0:T(8,128)(2,1)S(1)}, u32[]{:S(2)}, u32[]{:S(2)}) %collective-permute-start.63) | collective-permute-done | bytes 196640 | tf_op jit(solution)/shard_map/ppermute | solution.py:714
  552.7 4.8 all-to-all-start.7
  562.6 2.4 fusion.3
  565.0 8.6 %collective-permute-done.65 = bf16[128,2048]{1,0:T(8,128)(2,1)S(1)} collective-permute-done((bf16[128,2048]{1,0:T(8,128)(2,1)S(1)}, bf16[128,2048]{1,0:T(8,128)(2,1)S(1)}, u32[]{:S(2)}, u32[]{:S(2)}) %collective-permute-start.65) | collective-permute-done | bytes 524320 | tf_op jit(solution)/shard_map/ppermute | solution.py:714
  578.4 3.1 pad_maximum_fusion
  (370 shorter events, 112.2 us)
Async XLA Ops:
  7.2 82.9 %all-gather.3.cloned.1.call-start = ((), (), s32[]{:S(2)}) async-start(), calls=%async_computation.10 | async-start | bytes 4718592 | tf_op jit(solution)/shard_map/all_gather | solution.py:821
  12.7 45.8 %all-to-all-start = ((bf16[8,64,768]{2,1,0:T(8,128)(2,1)}), bf16[8,64,768]{2,1,0:T(8,128)(2,1)S(1)}, u32[]{:S(2)}, u32[]{:S(2)}) async-start(bf16[8,64,768]{2,1,0:T(8,128)(2,1)} %reshape.117), calls=%async_computation | async-start | bytes 1572864 | tf_op jit(solution)/shard_map/all_to_all | solution.py:829
  19.2 216.8 %all-gather.5.cloned.1.call-start = ((), (), s32[]{:S(2)}) async-start(), calls=%async_computation.11 | async-start | bytes 10485760 | tf_op jit(solution)/shard_map/all_gather | solution.py:853
  20.6 32.8 %collective-permute-start.3 = (bf16[256,2048]{1,0:T(8,128)(2,1)S(1)}, bf16[256,2048]{1,0:T(8,128)(2,1)}, u32[]{:S(2)}, u32[]{:S(2)}) collective-permute-start(bf16[256,2048]{1,0:T(8,128)(2,1)S(1)} %slice.128.refs_3_), channel_id=1, source_target_pairs={{0,16},{8,24},{16,0},{24,8},{1,17},{9,25},{17,1},{25,9},{2,18},{10... | collective-permute-start | bytes 3145736 | tf_op jit(solution)/shard_map/ppermute | solution.py:714
  22.2 31.2 %collective-permute-start.2 = (bf16[256,2048]{1,0:T(8,128)(2,1)S(1)}, bf16[256,2048]{1,0:T(8,128)(2,1)}, u32[]{:S(2)}, u32[]{:S(2)}) collective-permute-start(bf16[256,2048]{1,0:T(8,128)(2,1)S(1)} %slice.128.refs_3_), channel_id=1, source_target_pairs={{0,8},{8,0},{16,24},{24,16},{1,9},{9,1},{17,25},{25,17},{2,10},{10... | collective-permute-start | bytes 3145736 | tf_op jit(solution)/shard_map/ppermute | solution.py:714
  23.8 28.3 %collective-permute-start.1 = (bf16[64,2176]{1,0:T(8,128)(2,1)S(1)}, bf16[64,2176]{1,0:T(8,128)(2,1)S(1)}, u32[]{:S(2)}, u32[]{:S(2)}) collective-permute-start(bf16[64,2176]{1,0:T(8,128)(2,1)S(1)} %fusion.19), channel_id=1, source_target_pairs={{0,16},{8,24},{16,0},{24,8},{1,17},{9,25},{17,1},{25,9},{2,18},{10... | collective-permute-start | bytes 835592 | tf_op jit(solution)/shard_map/ppermute | solution.py:714
  24.4 29.0 %collective-permute-start = (bf16[64,2176]{1,0:T(8,128)(2,1)S(1)}, bf16[64,2176]{1,0:T(8,128)(2,1)S(1)}, u32[]{:S(2)}, u32[]{:S(2)}) collective-permute-start(bf16[64,2176]{1,0:T(8,128)(2,1)S(1)} %fusion.19), channel_id=1, source_target_pairs={{0,8},{8,0},{16,24},{24,16},{1,9},{9,1},{17,25},{25,17},{2,10},{10... | collective-permute-start | bytes 835592 | tf_op jit(solution)/shard_map/ppermute | solution.py:714
  58.5 18.3 %collective-permute-start.5 = (bf16[512,768]{1,0:T(8,128)(2,1)S(1)}, bf16[512,768]{1,0:T(8,128)(2,1)S(1)}, u32[]{:S(2)}, u32[]{:S(2)}) collective-permute-start(bf16[512,768]{1,0:T(8,128)(2,1)S(1)} %bitcast.148), channel_id=1, source_target_pairs={{0,16},{8,24},{16,0},{24,8},{1,17},{9,25},{17,1},{25,9},{2,18},{10... | collective-permute-start | bytes 2359304 | tf_op jit(solution)/shard_map/ppermute | solution.py:714
  60.1 18.6 %collective-permute-start.4 = (bf16[512,768]{1,0:T(8,128)(2,1)S(1)}, bf16[512,768]{1,0:T(8,128)(2,1)S(1)}, u32[]{:S(2)}, u32[]{:S(2)}) collective-permute-start(bf16[512,768]{1,0:T(8,128)(2,1)S(1)} %bitcast.149), channel_id=1, source_target_pairs={{0,8},{8,0},{16,24},{24,16},{1,9},{9,1},{17,25},{25,17},{2,10},{10... | collective-permute-start | bytes 2359304 | tf_op jit(solution)/shard_map/ppermute | solution.py:714
  61.6 20.0 %collective-permute-start.9 = (bf16[32,2176]{1,0:T(8,128)(2,1)S(1)}, bf16[32,2176]{1,0:T(8,128)(2,1)S(1)}, u32[]{:S(2)}, u32[]{:S(2)}) collective-permute-start(bf16[32,2176]{1,0:T(8,128)(2,1)S(1)} %slice.132), channel_id=1, source_target_pairs={{0,8},{8,0},{16,24},{24,16},{1,9},{9,1},{17,25},{25,17},{2,10},{10... | collective-permute-start | bytes 417800 | tf_op jit(solution)/shard_map/ppermute | solution.py:714
  62.2 17.9 %collective-permute-start.8 = (bf16[32,2176]{1,0:T(8,128)(2,1)S(1)}, bf16[32,2176]{1,0:T(8,128)(2,1)S(1)}, u32[]{:S(2)}, u32[]{:S(2)}) collective-permute-start(bf16[32,2176]{1,0:T(8,128)(2,1)S(1)} %slice.131), channel_id=1, source_target_pairs={{0,16},{8,24},{16,0},{24,8},{1,17},{9,25},{17,1},{25,9},{2,18},{10... | collective-permute-start | bytes 417800 | tf_op jit(solution)/shard_map/ppermute | solution.py:714
  76.9 13.2 %collective-permute-start.7 = (bf16[256,768]{1,0:T(8,128)(2,1)S(1)}, bf16[256,768]{1,0:T(8,128)(2,1)S(1)}, u32[]{:S(2)}, u32[]{:S(2)}) collective-permute-start(bf16[256,768]{1,0:T(8,128)(2,1)S(1)} %slice.171), channel_id=1, source_target_pairs={{0,8},{8,0},{16,24},{24,16},{1,9},{9,1},{17,25},{25,17},{2,10},{10... | collective-permute-start | bytes 1179656 | tf_op jit(solution)/shard_map/ppermute | solution.py:714
  78.7 11.4 %collective-permute-start.6 = (bf16[256,768]{1,0:T(8,128)(2,1)S(1)}, bf16[256,768]{1,0:T(8,128)(2,1)S(1)}, u32[]{:S(2)}, u32[]{:S(2)}) collective-permute-start(bf16[256,768]{1,0:T(8,128)(2,1)S(1)} %slice.170), channel_id=1, source_target_pairs={{0,16},{8,24},{16,0},{24,8},{1,17},{9,25},{17,1},{25,9},{2,18},{10... | collective-permute-start | bytes 1179656 | tf_op jit(solution)/shard_map/ppermute | solution.py:714
  90.2 27.2 %collective-permute-start.12 = (bf16[256,2176]{1,0:T(8,128)(2,1)}, bf16[256,2176]{1,0:T(8,128)(2,1)}, u32[]{:S(2)}, u32[]{:S(2)}) collective-permute-start(bf16[256,2176]{1,0:T(8,128)(2,1)} %constant_dynamic-update-slice_fusion.refs_0_), channel_id=1, source_target_pairs={{0,3},{1,0},{2,1},{3,2},{4,7},{5,4},{6,5},{7,6},{8,11},{9,8},{10,9... | collective-permute-start | bytes 3342344 | tf_op jit(solution)/shard_map/ppermute | solution.py:710
  93.1 19.0 %collective-permute-start.11 = (bf16[128,2048]{1,0:T(8,128)(2,1)S(1)}, bf16[128,2048]{1,0:T(8,128)(2,1)S(1)}, u32[]{:S(2)}, u32[]{:S(2)}) collective-permute-start(bf16[128,2048]{1,0:T(8,128)(2,1)S(1)} %slice.134), channel_id=1, source_target_pairs={{0,8},{8,0},{16,24},{24,16},{1,9},{9,1},{17,25},{25,17},{2,10},{10... | collective-permute-start | bytes 1572872 | tf_op jit(solution)/shard_map/ppermute | solution.py:714
  94.6 20.4 %collective-permute-start.10 = (bf16[128,2048]{1,0:T(8,128)(2,1)S(1)}, bf16[128,2048]{1,0:T(8,128)(2,1)S(1)}, u32[]{:S(2)}, u32[]{:S(2)}) collective-permute-start(bf16[128,2048]{1,0:T(8,128)(2,1)S(1)} %slice.133), channel_id=1, source_target_pairs={{0,16},{8,24},{16,0},{24,8},{1,17},{9,25},{17,1},{25,9},{2,18},{10... | collective-permute-start | bytes 1572872 | tf_op jit(solution)/shard_map/ppermute | solution.py:714
  117.4 32.2 %all-to-all-start.1 = ((bf16[4,8,3,64,128]{4,3,2,1,0:T(8,128)(2,1)}), bf16[4,8,3,64,128]{4,3,2,1,0:T(8,128)(2,1)S(1)}, u32[]{:S(2)}, u32[]{:S(2)}) async-start(bf16[4,8,3,64,128]{4,3,2,1,0:T(8,128)(2,1)} %get-tuple-element.234), calls=%async_computation.1 | async-start | bytes 3145728 | tf_op jit(solution)/shard_map/all_to_all | solution.py:849
  121.8 27.8 %collective-permute-start.13 = (bf16[256,2176]{1,0:T(8,128)(2,1)}, bf16[256,2176]{1,0:T(8,128)(2,1)S(1)}, u32[]{:S(2)}, u32[]{:S(2)}) collective-permute-start(bf16[256,2176]{1,0:T(8,128)(2,1)} %collective-permute-done.12.refs_1_), channel_id=1, source_target_pairs={{0,3},{1,0},{2,1},{3,2},{4,7},{5,4},{6,5},{7,6},{8,11},{9,8},{10,9... | collective-permute-start | bytes 3342344 | tf_op jit(solution)/shard_map/ppermute | solution.py:710
  149.6 23.0 %collective-permute-start.17 = (bf16[256,2176]{1,0:T(8,128)(2,1)S(1)}, bf16[256,2176]{1,0:T(8,128)(2,1)S(1)}, u32[]{:S(2)}, u32[]{:S(2)}) collective-permute-start(bf16[256,2176]{1,0:T(8,128)(2,1)S(1)} %collective-permute-done.13.refs_2_), channel_id=1, source_target_pairs={{0,4},{4,0},{1,5},{5,1},{2,6},{6,2},{3,7},{7,3},{8,12},{12,8},{9,1... | collective-permute-start | bytes 3342344 | tf_op jit(solution)/shard_map/ppermute | solution.py:705
  149.6 28.9 %collective-permute-start.16 = (bf16[256,2176]{1,0:T(8,128)(2,1)S(1)}, bf16[256,2176]{1,0:T(8,128)(2,1)}, u32[]{:S(2)}, u32[]{:S(2)}) collective-permute-start(bf16[256,2176]{1,0:T(8,128)(2,1)S(1)} %collective-permute-done.13.refs_2_), channel_id=1, source_target_pairs={{0,3},{1,0},{2,1},{3,2},{4,7},{5,4},{6,5},{7,6},{8,11},{9,8},{10,9... | collective-permute-start | bytes 3342344 | tf_op jit(solution)/shard_map/ppermute | solution.py:710
  178.5 21.4 %collective-permute-start.18 = (bf16[256,2176]{1,0:T(8,128)(2,1)}, bf16[256,2176]{1,0:T(8,128)(2,1)S(1)}, u32[]{:S(2)}, u32[]{:S(2)}) collective-permute-start(bf16[256,2176]{1,0:T(8,128)(2,1)} %collective-permute-done.16.refs_3_), channel_id=1, source_target_pairs={{0,4},{4,0},{1,5},{5,1},{2,6},{6,2},{3,7},{7,3},{8,12},{12,8},{9,1... | collective-permute-start | bytes 3342344 | tf_op jit(solution)/shard_map/ppermute | solution.py:705
  178.5 21.4 %all-to-all-start.2 = ((bf16[32,64,128]{2,1,0:T(8,128)(2,1)}), bf16[32,64,128]{2,1,0:T(8,128)(2,1)S(1)}, u32[]{:S(2)}, u32[]{:S(2)}) async-start(bf16[32,64,128]{2,1,0:T(8,128)(2,1)} %get-tuple-element.243.refs_2_), calls=%async_computation.2 | async-start | bytes 1048576 | tf_op jit(solution)/shard_map/all_to_all | solution.py:893
  185.6 22.6 %collective-permute-start.19 = (bf16[128,2048]{1,0:T(8,128)(2,1)S(1)}, bf16[128,2048]{1,0:T(8,128)(2,1)}, u32[]{:S(2)}, u32[]{:S(2)}) collective-permute-start(bf16[128,2048]{1,0:T(8,128)(2,1)S(1)} %copy-done.34), channel_id=1, source_target_pairs={{0,3},{1,0},{2,1},{3,2},{4,7},{5,4},{6,5},{7,6},{8,11},{9,8},{10,9... | collective-permute-start | bytes 1572872 | tf_op jit(solution)/shard_map/ppermute | solution.py:710
  208.2 18.1 %collective-permute-start.20 = (bf16[128,2048]{1,0:T(8,128)(2,1)}, bf16[128,2048]{1,0:T(8,128)(2,1)S(1)}, u32[]{:S(2)}, u32[]{:S(2)}) collective-permute-start(bf16[128,2048]{1,0:T(8,128)(2,1)} %collective-permute-done.19.grad_own_ref), channel_id=1, source_target_pairs={{0,3},{1,0},{2,1},{3,2},{4,7},{5,4},{6,5},{7,6},{8,11},{9,8},{10,9... | collective-permute-start | bytes 1572872 | tf_op jit(solution)/shard_map/ppermute | solution.py:710
  226.3 9.6 %collective-permute-start.23 = (bf16[128,2048]{1,0:T(8,128)(2,1)S(1)}, bf16[128,2048]{1,0:T(8,128)(2,1)}, u32[]{:S(2)}, u32[]{:S(2)}) collective-permute-start(bf16[128,2048]{1,0:T(8,128)(2,1)S(1)} %copy-done.34), channel_id=1, source_target_pairs={{0,4},{4,0},{1,5},{5,1},{2,6},{6,2},{3,7},{7,3},{8,12},{12,8},{9,1... | collective-permute-start | bytes 1572872 | tf_op jit(solution)/shard_map/ppermute | solution.py:705
  227.7 20.5 %collective-permute-start.21 = (bf16[128,2048]{1,0:T(8,128)(2,1)S(1)}, bf16[128,2048]{1,0:T(8,128)(2,1)}, u32[]{:S(2)}, u32[]{:S(2)}) collective-permute-start(bf16[128,2048]{1,0:T(8,128)(2,1)S(1)} %get-tuple-element.257.own_ref), channel_id=1, source_target_pairs={{0,3},{1,0},{2,1},{3,2},{4,7},{5,4},{6,5},{7,6},{8,11},{9,8},{10,9... | collective-permute-start | bytes 1572872 | tf_op jit(solution)/shard_map/ppermute | solution.py:710
  231.9 16.3 %all-to-all-start.3 = ((bf16[4,8,64,128]{3,2,1,0:T(8,128)(2,1)}), bf16[4,8,64,128]{3,2,1,0:T(8,128)(2,1)S(1)}, u32[]{:S(2)}, u32[]{:S(2)}) async-start(bf16[4,8,64,128]{3,2,1,0:T(8,128)(2,1)} %bitcast.157), calls=%async_computation.3 | async-start | bytes 1048576 | tf_op jit(solution)/shard_map/all_to_all | solution.py:903
  235.4 177.1 %reduce-scatter.3.cloned.1.call-start = ((), (), s32[]{:S(2)}) async-start(), calls=%async_computation.12 | async-start | bytes 5242880 | tf_op jit(solution)/shard_map/reduce_scatter | solution.py:936
  235.4 19.7 %collective-permute-start.26 = (bf16[128,2048]{1,0:T(8,128)(2,1)}, bf16[128,2048]{1,0:T(8,128)(2,1)}, u32[]{:S(2)}, u32[]{:S(2)}) collective-permute-start(bf16[128,2048]{1,0:T(8,128)(2,1)} %copy-done.82), channel_id=1, source_target_pairs={{0,3},{1,0},{2,1},{3,2},{4,7},{5,4},{6,5},{7,6},{8,11},{9,8},{10,9... | collective-permute-start | bytes 1572872 | tf_op jit(solution)/shard_map/ppermute | solution.py:710
  255.6 17.6 %collective-permute-start.24 = (bf16[128,2048]{1,0:T(8,128)(2,1)}, bf16[128,2048]{1,0:T(8,128)(2,1)S(1)}, u32[]{:S(2)}, u32[]{:S(2)}) collective-permute-start(bf16[128,2048]{1,0:T(8,128)(2,1)} %collective-permute-done.21.own_ref), channel_id=1, source_target_pairs={{0,3},{1,0},{2,1},{3,2},{4,7},{5,4},{6,5},{7,6},{8,11},{9,8},{10,9... | collective-permute-start | bytes 1572872 | tf_op jit(solution)/shard_map/ppermute | solution.py:710
  273.9 18.8 %collective-permute-start.28 = (bf16[128,2048]{1,0:T(8,128)(2,1)S(1)}, bf16[128,2048]{1,0:T(8,128)(2,1)S(1)}, u32[]{:S(2)}, u32[]{:S(2)}) collective-permute-start(bf16[128,2048]{1,0:T(8,128)(2,1)S(1)} %collective-permute-done.24.own_ref), channel_id=1, source_target_pairs={{0,3},{1,0},{2,1},{3,2},{4,7},{5,4},{6,5},{7,6},{8,11},{9,8},{10,9... | collective-permute-start | bytes 1572872 | tf_op jit(solution)/shard_map/ppermute | solution.py:710
  277.7 21.8 %collective-permute-start.30 = (bf16[128,2048]{1,0:T(8,128)(2,1)S(1)}, bf16[128,2048]{1,0:T(8,128)(2,1)S(1)}, u32[]{:S(2)}, u32[]{:S(2)}) collective-permute-start(bf16[128,2048]{1,0:T(8,128)(2,1)S(1)} %add_convert_fusion.2), channel_id=1, source_target_pairs={{0,3},{1,0},{2,1},{3,2},{4,7},{5,4},{6,5},{7,6},{8,11},{9,8},{10,9... | collective-permute-start | bytes 1572872 | tf_op jit(solution)/shard_map/ppermute | solution.py:710
  303.0 17.5 %collective-permute-start.34 = (bf16[128,2048]{1,0:T(8,128)(2,1)S(1)}, bf16[128,2048]{1,0:T(8,128)(2,1)S(1)}, u32[]{:S(2)}, u32[]{:S(2)}) collective-permute-start(bf16[128,2048]{1,0:T(8,128)(2,1)S(1)} %add_convert_fusion.1), channel_id=1, source_target_pairs={{0,3},{1,0},{2,1},{3,2},{4,7},{5,4},{6,5},{7,6},{8,11},{9,8},{10,9... | collective-permute-start | bytes 1572872 | tf_op jit(solution)/shard_map/ppermute | solution.py:710
  324.9 14.6 %collective-permute-start.38 = (bf16[128,2048]{1,0:T(8,128)(2,1)}, bf16[128,2048]{1,0:T(8,128)(2,1)S(1)}, u32[]{:S(2)}, u32[]{:S(2)}) collective-permute-start(bf16[128,2048]{1,0:T(8,128)(2,1)} %add_add_fusion.1), channel_id=1, source_target_pairs={{0,3},{1,0},{2,1},{3,2},{4,7},{5,4},{6,5},{7,6},{8,11},{9,8},{10,9... | collective-permute-start | bytes 1572872 | tf_op jit(solution)/shard_map/ppermute | solution.py:710
  348.7 19.9 %collective-permute-start.40 = (bf16[4,128,2048]{2,1,0:T(8,128)(2,1)}, bf16[4,128,2048]{2,1,0:T(8,128)(2,1)}, u32[]{:S(2)}, u32[]{:S(2)}) collective-permute-start(bf16[4,128,2048]{2,1,0:T(8,128)(2,1)} %get-tuple-element.329), channel_id=1, source_target_pairs={{0,4},{4,0},{1,5},{5,1},{2,6},{6,2},{3,7},{7,3},{8,12},{12,8},{9,1... | collective-permute-start | bytes 6291464 | tf_op jit(solution)/shard_map/ppermute | solution.py:705
  348.9 19.7 %all-to-all-start.4 = ((bf16[32,64,128]{2,1,0:T(8,128)(2,1)}), bf16[32,64,128]{2,1,0:T(8,128)(2,1)}, u32[]{:S(2)}, u32[]{:S(2)}) async-start(bf16[32,64,128]{2,1,0:T(8,128)(2,1)} %get-tuple-element.325), calls=%async_computation.4 | async-start | bytes 1048576 | tf_op jit(solution)/shard_map/all_to_all | solution.py:945
  368.7 17.4 %collective-permute-start.42 = (bf16[128,2048]{1,0:T(8,128)(2,1)S(1)}, bf16[128,2048]{1,0:T(8,128)(2,1)S(1)}, u32[]{:S(2)}, u32[]{:S(2)}) collective-permute-start(bf16[128,2048]{1,0:T(8,128)(2,1)S(1)} %get-tuple-element.383.refs_0_), channel_id=1, source_target_pairs={{0,4},{4,0},{1,5},{5,1},{2,6},{6,2},{3,7},{7,3},{8,12},{12,8},{9,1... | collective-permute-start | bytes 1572872 | tf_op jit(solution)/shard_map/ppermute | solution.py:705
  369.9 16.1 %collective-permute-start.41 = (bf16[128,2048]{1,0:T(8,128)(2,1)S(1)}, bf16[128,2048]{1,0:T(8,128)(2,1)S(1)}, u32[]{:S(2)}, u32[]{:S(2)}) collective-permute-start(bf16[128,2048]{1,0:T(8,128)(2,1)S(1)} %get-tuple-element.383.refs_0_), channel_id=1, source_target_pairs={{0,3},{1,0},{2,1},{3,2},{4,7},{5,4},{6,5},{7,6},{8,11},{9,8},{10,9... | collective-permute-start | bytes 1572872 | tf_op jit(solution)/shard_map/ppermute | solution.py:710
  386.1 26.3 %collective-permute-start.45 = (bf16[128,2048]{1,0:T(8,128)(2,1)S(1)}, bf16[128,2048]{1,0:T(8,128)(2,1)S(1)}, u32[]{:S(2)}, u32[]{:S(2)}) collective-permute-start(bf16[128,2048]{1,0:T(8,128)(2,1)S(1)} %collective-permute-done.41.refs_2_), channel_id=1, source_target_pairs={{0,4},{4,0},{1,5},{5,1},{2,6},{6,2},{3,7},{7,3},{8,12},{12,8},{9,1... | collective-permute-start | bytes 1572872 | tf_op jit(solution)/shard_map/ppermute | solution.py:705
  386.5 26.0 %collective-permute-start.43 = (bf16[128,2048]{1,0:T(8,128)(2,1)S(1)}, bf16[128,2048]{1,0:T(8,128)(2,1)}, u32[]{:S(2)}, u32[]{:S(2)}) collective-permute-start(bf16[128,2048]{1,0:T(8,128)(2,1)S(1)} %collective-permute-done.41.refs_2_), channel_id=1, source_target_pairs={{0,3},{1,0},{2,1},{3,2},{4,7},{5,4},{6,5},{7,6},{8,11},{9,8},{10,9... | collective-permute-start | bytes 1572872 | tf_op jit(solution)/shard_map/ppermute | solution.py:710
  387.7 24.6 %collective-permute-start.44 = (bf16[128,2048]{1,0:T(8,128)(2,1)}, bf16[128,2048]{1,0:T(8,128)(2,1)S(1)}, u32[]{:S(2)}, u32[]{:S(2)}) collective-permute-start(bf16[128,2048]{1,0:T(8,128)(2,1)} %fusion.16), channel_id=1, source_target_pairs={{0,3},{1,0},{2,1},{3,2},{4,7},{5,4},{6,5},{7,6},{8,11},{9,8},{10,9... | collective-permute-start | bytes 1572872 | tf_op jit(solution)/shard_map/ppermute | solution.py:710
  412.4 31.3 %all-to-all-start.5 = ((bf16[4,8,3,64,128]{4,3,2,1,0:T(8,128)(2,1)}), bf16[4,8,3,64,128]{4,3,2,1,0:T(8,128)(2,1)}, u32[]{:S(2)}, u32[]{:S(2)}) async-start(bf16[4,8,3,64,128]{4,3,2,1,0:T(8,128)(2,1)} %bitcast.161), calls=%async_computation.6 | async-start | bytes 3145728 | tf_op jit(solution)/shard_map/all_to_all | solution.py:976
  416.9 89.0 %reduce-scatter.5.cloned.1.call-start = ((), (), s32[]{:S(2)}) async-start(), calls=%async_computation.13 | async-start | bytes 5242880 | tf_op jit(solution)/shard_map/reduce_scatter | solution.py:936
  417.6 33.9 %collective-permute-start.47 = (bf16[128,2048]{1,0:T(8,128)(2,1)}, bf16[128,2048]{1,0:T(8,128)(2,1)}, u32[]{:S(2)}, u32[]{:S(2)}) collective-permute-start(bf16[128,2048]{1,0:T(8,128)(2,1)} %collective-permute-done.43.refs_4_), channel_id=1, source_target_pairs={{0,3},{1,0},{2,1},{3,2},{4,7},{5,4},{6,5},{7,6},{8,11},{9,8},{10,9... | collective-permute-start | bytes 1572872 | tf_op jit(solution)/shard_map/ppermute | solution.py:710
  422.8 28.7 %collective-permute-start.48 = (bf16[128,2048]{1,0:T(8,128)(2,1)}, bf16[128,2048]{1,0:T(8,128)(2,1)}, u32[]{:S(2)}, u32[]{:S(2)}) collective-permute-start(bf16[128,2048]{1,0:T(8,128)(2,1)} %fusion.12), channel_id=1, source_target_pairs={{0,3},{1,0},{2,1},{3,2},{4,7},{5,4},{6,5},{7,6},{8,11},{9,8},{10,9... | collective-permute-start | bytes 1572872 | tf_op jit(solution)/shard_map/ppermute | solution.py:710
  451.5 26.6 %collective-permute-start.50 = (bf16[512,768]{1,0:T(8,128)(2,1)S(1)}, bf16[512,768]{1,0:T(8,128)(2,1)S(1)}, u32[]{:S(2)}, u32[]{:S(2)}) collective-permute-start(bf16[512,768]{1,0:T(8,128)(2,1)S(1)} %get-tuple-element.368), channel_id=1, source_target_pairs={{0,8},{8,0},{16,24},{24,16},{1,9},{9,1},{17,25},{25,17},{2,10},{10... | collective-permute-start | bytes 2359304 | tf_op jit(solution)/shard_map/ppermute | solution.py:714
  453.0 25.0 %collective-permute-start.51 = (bf16[512,768]{1,0:T(8,128)(2,1)S(1)}, bf16[512,768]{1,0:T(8,128)(2,1)S(1)}, u32[]{:S(2)}, u32[]{:S(2)}) collective-permute-start(bf16[512,768]{1,0:T(8,128)(2,1)S(1)} %get-tuple-element.369), channel_id=1, source_target_pairs={{0,16},{8,24},{16,0},{24,8},{1,17},{9,25},{17,1},{25,9},{2,18},{10... | collective-permute-start | bytes 2359304 | tf_op jit(solution)/shard_map/ppermute | solution.py:714
  454.9 10.9 %collective-permute-start.49 = (bf16[128,2048]{1,0:T(8,128)(2,1)S(1)}, bf16[128,2048]{1,0:T(8,128)(2,1)S(1)}, u32[]{:S(2)}, u32[]{:S(2)}) collective-permute-start(bf16[128,2048]{1,0:T(8,128)(2,1)S(1)} %fusion.11), channel_id=1, source_target_pairs={{0,3},{1,0},{2,1},{3,2},{4,7},{5,4},{6,5},{7,6},{8,11},{9,8},{10,9... | collective-permute-start | bytes 1572872 | tf_op jit(solution)/shard_map/ppermute | solution.py:710
  485.7 20.2 %collective-permute-start.53 = (bf16[128,2048]{1,0:T(8,128)(2,1)}, bf16[128,2048]{1,0:T(8,128)(2,1)}, u32[]{:S(2)}, u32[]{:S(2)}) collective-permute-start(bf16[128,2048]{1,0:T(8,128)(2,1)} %convert_add_fusion.3), channel_id=1, source_target_pairs={{0,3},{1,0},{2,1},{3,2},{4,7},{5,4},{6,5},{7,6},{8,11},{9,8},{10,9... | collective-permute-start | bytes 1572872 | tf_op jit(solution)/shard_map/ppermute | solution.py:710
  487.2 14.5 %collective-permute-start.56 = (bf16[128,2048]{1,0:T(8,128)(2,1)}, bf16[128,2048]{1,0:T(8,128)(2,1)S(1)}, u32[]{:S(2)}, u32[]{:S(2)}) collective-permute-start(bf16[128,2048]{1,0:T(8,128)(2,1)} %collective-permute-done.47.refs_6_), channel_id=1, source_target_pairs={{0,4},{4,0},{1,5},{5,1},{2,6},{6,2},{3,7},{7,3},{8,12},{12,8},{9,1... | collective-permute-start | bytes 1572872 | tf_op jit(solution)/shard_map/ppermute | solution.py:705
  487.4 11.6 %collective-permute-start.54 = (bf16[256,768]{1,0:T(8,128)(2,1)S(1)}, bf16[256,768]{1,0:T(8,128)(2,1)S(1)}, u32[]{:S(2)}, u32[]{:S(2)}) collective-permute-start(bf16[256,768]{1,0:T(8,128)(2,1)S(1)} %fusion.14), channel_id=1, source_target_pairs={{0,16},{8,24},{16,0},{24,8},{1,17},{9,25},{17,1},{25,9},{2,18},{10... | collective-permute-start | bytes 1179656 | tf_op jit(solution)/shard_map/ppermute | solution.py:714
  489.2 11.3 %collective-permute-start.55 = (bf16[256,768]{1,0:T(8,128)(2,1)S(1)}, bf16[256,768]{1,0:T(8,128)(2,1)S(1)}, u32[]{:S(2)}, u32[]{:S(2)}) collective-permute-start(bf16[256,768]{1,0:T(8,128)(2,1)S(1)} %fusion.13), channel_id=1, source_target_pairs={{0,8},{8,0},{16,24},{24,16},{1,9},{9,1},{17,25},{25,17},{2,10},{10... | collective-permute-start | bytes 1179656 | tf_op jit(solution)/shard_map/ppermute | solution.py:714
  508.5 15.2 %collective-permute-start.57 = (bf16[128,2048]{1,0:T(8,128)(2,1)}, bf16[128,2048]{1,0:T(8,128)(2,1)}, u32[]{:S(2)}, u32[]{:S(2)}) collective-permute-start(bf16[128,2048]{1,0:T(8,128)(2,1)} %fusion.8), channel_id=1, source_target_pairs={{0,3},{1,0},{2,1},{3,2},{4,7},{5,4},{6,5},{7,6},{8,11},{9,8},{10,9... | collective-permute-start | bytes 1572872 | tf_op jit(solution)/shard_map/ppermute | solution.py:710
  509.5 13.1 %collective-permute-start.58 = (bf16[512,384]{1,0:T(8,128)(2,1)}, bf16[512,384]{1,0:T(8,128)(2,1)}, u32[]{:S(2)}, u32[]{:S(2)}) collective-permute-start(bf16[512,384]{1,0:T(8,128)(2,1)} %pad_maximum_fusion.1), channel_id=1, source_target_pairs={{0,8},{8,0},{16,24},{24,16},{1,9},{9,1},{17,25},{25,17},{2,10},{10... | collective-permute-start | bytes 1179656 | tf_op jit(solution)/shard_map/ppermute | solution.py:714
  510.2 12.3 %collective-permute-start.59 = (bf16[512,384]{1,0:T(8,128)(2,1)S(1)}, bf16[512,384]{1,0:T(8,128)(2,1)S(1)}, u32[]{:S(2)}, u32[]{:S(2)}) collective-permute-start(bf16[512,384]{1,0:T(8,128)(2,1)S(1)} %pad_maximum_fusion.2), channel_id=1, source_target_pairs={{0,16},{8,24},{16,0},{24,8},{1,17},{9,25},{17,1},{25,9},{2,18},{10... | collective-permute-start | bytes 1179656 | tf_op jit(solution)/shard_map/ppermute | solution.py:714
  513.6 37.5 %all-to-all-start.6 = ((bf16[8,64,768]{2,1,0:T(8,128)(2,1)}), bf16[8,64,768]{2,1,0:T(8,128)(2,1)S(1)}, u32[]{:S(2)}, u32[]{:S(2)}) async-start(bf16[8,64,768]{2,1,0:T(8,128)(2,1)} %bitcast.88), calls=%async_computation.8 | async-start | bytes 1572864 | tf_op jit(solution)/shard_map/all_to_all | solution.py:798
  517.3 32.1 %collective-permute-start.61 = (bf16[256,2048]{1,0:T(8,128)(2,1)}, bf16[256,2048]{1,0:T(8,128)(2,1)S(1)}, u32[]{:S(2)}, u32[]{:S(2)}) collective-permute-start(bf16[256,2048]{1,0:T(8,128)(2,1)} %copy-done.33), channel_id=1, source_target_pairs={{0,8},{8,0},{16,24},{24,16},{1,9},{9,1},{17,25},{25,17},{2,10},{10... | collective-permute-start | bytes 3145736 | tf_op jit(solution)/shard_map/ppermute | solution.py:714
  518.7 32.4 %collective-permute-start.62 = (bf16[256,2048]{1,0:T(8,128)(2,1)}, bf16[256,2048]{1,0:T(8,128)(2,1)}, u32[]{:S(2)}, u32[]{:S(2)}) collective-permute-start(bf16[256,2048]{1,0:T(8,128)(2,1)} %copy-done.32), channel_id=1, source_target_pairs={{0,16},{8,24},{16,0},{24,8},{1,17},{9,25},{17,1},{25,9},{2,18},{10... | collective-permute-start | bytes 3145736 | tf_op jit(solution)/shard_map/ppermute | solution.py:714
  525.9 22.5 %collective-permute-start.63 = (bf16[256,384]{1,0:T(8,128)(2,1)S(1)}, bf16[256,384]{1,0:T(8,128)(2,1)S(1)}, u32[]{:S(2)}, u32[]{:S(2)}) collective-permute-start(bf16[256,384]{1,0:T(8,128)(2,1)S(1)} %get-tuple-element.427), channel_id=1, source_target_pairs={{0,16},{8,24},{16,0},{24,8},{1,17},{9,25},{17,1},{25,9},{2,18},{10... | collective-permute-start | bytes 589832 | tf_op jit(solution)/shard_map/ppermute | solution.py:714
  528.3 21.0 %collective-permute-start.60 = (bf16[128,2048]{1,0:T(8,128)(2,1)S(1)}, bf16[128,2048]{1,0:T(8,128)(2,1)S(1)}, u32[]{:S(2)}, u32[]{:S(2)}) collective-permute-start(bf16[128,2048]{1,0:T(8,128)(2,1)S(1)} %fusion.7), channel_id=1, source_target_pairs={{0,3},{1,0},{2,1},{3,2},{4,7},{5,4},{6,5},{7,6},{8,11},{9,8},{10,9... | collective-permute-start | bytes 1572872 | tf_op jit(solution)/shard_map/ppermute | solution.py:710
  531.8 16.6 %collective-permute-start.64 = (bf16[256,384]{1,0:T(8,128)(2,1)S(1)}, bf16[256,384]{1,0:T(8,128)(2,1)S(1)}, u32[]{:S(2)}, u32[]{:S(2)}) collective-permute-start(bf16[256,384]{1,0:T(8,128)(2,1)S(1)} %get-tuple-element.428), channel_id=1, source_target_pairs={{0,8},{8,0},{16,24},{24,16},{1,9},{9,1},{17,25},{25,17},{2,10},{10... | collective-permute-start | bytes 589832 | tf_op jit(solution)/shard_map/ppermute | solution.py:714
  552.7 28.8 %all-to-all-start.7 = ((bf16[8,64,384]{2,1,0:T(8,128)(2,1)}), bf16[8,64,384]{2,1,0:T(8,128)(2,1)S(1)}, u32[]{:S(2)}, u32[]{:S(2)}) async-start(bf16[8,64,384]{2,1,0:T(8,128)(2,1)} %bitcast.165), calls=%async_computation.9 | async-start | bytes 786432 | tf_op jit(solution)/shard_map/all_to_all | solution.py:798
  559.2 14.4 %collective-permute-start.65 = (bf16[128,2048]{1,0:T(8,128)(2,1)S(1)}, bf16[128,2048]{1,0:T(8,128)(2,1)S(1)}, u32[]{:S(2)}, u32[]{:S(2)}) collective-permute-start(bf16[128,2048]{1,0:T(8,128)(2,1)S(1)} %fusion.6), channel_id=1, source_target_pairs={{0,16},{8,24},{16,0},{24,8},{1,17},{9,25},{17,1},{25,9},{2,18},{10... | collective-permute-start | bytes 1572872 | tf_op jit(solution)/shard_map/ppermute | solution.py:714
  561.9 14.1 %collective-permute-start.66 = (bf16[128,2048]{1,0:T(8,128)(2,1)S(1)}, bf16[128,2048]{1,0:T(8,128)(2,1)S(1)}, u32[]{:S(2)}, u32[]{:S(2)}) collective-permute-start(bf16[128,2048]{1,0:T(8,128)(2,1)S(1)} %fusion.5), channel_id=1, source_target_pairs={{0,8},{8,0},{16,24},{24,16},{1,9},{9,1},{17,25},{25,17},{2,10},{10... | collective-permute-start | bytes 1572872 | tf_op jit(solution)/shard_map/ppermute | solution.py:714
  (107 other events, 823.2 us)
Sparse Core Ops, SparseCore 0:
  9.6 65.9 all-gather.2
  90.3 114.7 all-gather.4
  339.7 58.9 reduce-scatter.2
  420.6 67.7 reduce-scatter.4

commit v5 on v4

--- a/solution.py
+++ b/solution.py
@@ -39,6 +39,14 @@
     keys = lax.broadcasted_iota(jnp.int32, scores.shape, 0)
     queries = lax.broadcasted_iota(jnp.int32, scores.shape, 1)
     return jnp.where(keys <= queries, scores, -1e30)
+
+
+def repeat(first, last, step, carry):
+    if not isinstance(last, int) or last - first > 4:
+        return lax.fori_loop(first, last, step, carry)
+    for number in range(first, last):
+        carry = step(number, carry)
+    return carry
 
 
 def forward_kernel(qkv_ref, out_ref, logsum_ref, keys, values_t, queries_t, *, block):
@@ -70,7 +78,7 @@
             jnp.zeros((1, block), f32),
             jnp.zeros((head_dim, block), f32),
         )
-        carry = lax.fori_loop(0, i, lambda j, c: step(i, j, c, False), carry)
+        carry = repeat(0, i, lambda j, c: step(i, j, c, False), carry)
         largest, total, result = step(i, i, carry, True)
         result = (result / total).astype(bf16)
         for part in range(per_block):
@@ -78,7 +86,7 @@
         logsum_ref[i] = largest + jnp.log(total)
         return 0
 
-    lax.fori_loop(0, count, query_block, 0)
+    repeat(0, count, query_block, 0)
 
 
 def backward_kernel(lower, upper, last, block, scale, *refs):
@@ -125,7 +133,7 @@
     for j in range(lower, upper):
         zero = jnp.zeros((block, head_dim), f32)
         carry = step(j, j, (zero, zero), True)
-        grad_key, grad_value = lax.fori_loop(
+        grad_key, grad_value = repeat(
             j + 1, count, lambda i, c, j=j: step(i, j, c, False), carry
         )
         for part in range(per_block):

time: 600 us -> 600 us (level)
  transfers between devices with their start and end apart: 79 -> 79, of which waited for: 34 -> 33; matrix products, arithmetic and copies ran while one was open for 9% -> 9% of each run, Pallas kernels for 29% -> 28%
where the time goes in v5:
time: 600 us; the launch traced here: 591 us
  waiting for transfers between devices  207 us (34%)
  Pallas kernels  166 us (28%)
  starting transfers between devices  126 us (21%)
  other arithmetic  46.6 us (8%)
  local copies, waits for them, and re-layouts  29.5 us (5%)
  between operations  15.3 us (3%)
    ppermute x24, waiting for transfers between devices, from_flipped(): return lax.ppermute(array, 'p', [(i, i ^ bit) for i in range(4)])  95.6 us
    ppermute x21, waiting for transfers between devices, from_next(): lax.ppermute(array, 'z', [(i, (i - 1) % count) for i in range(count)])  64.5 us
    ppermute x21, starting transfers between devices, from_next(): lax.ppermute(array, 'z', [(i, (i - 1) % count) for i in range(count)])  57.7 us
    pallas_call x4, Pallas kernels, units_chunk(): pl.pallas_call(functools.partial(units_kernel, counts, tables), grid=(1,)...  49.1 us
    pallas_call x2, Pallas kernels, attend_backward(): pl.pallas_call(functools.partial(backward_kernel, lower, upper, last, blo...  34.3 us
    ppermute x24, starting transfers between devices, from_flipped(): return lax.ppermute(array, 'p', [(i, i ^ bit) for i in range(4)])  24.5 us
    unnamed x189, local copies, waits for them, and re-layouts  18.8 us
    all_to_all x1, waiting for transfers between devices, shards(): grad_qkv_rows = lax.all_to_all(grad_qkv_rows, 'p', 0, 0)  18.5 us
  transfers between devices with their start and end apart: 79, of which 33 were waited for; matrix products, arithmetic and copies ran while one was open for 9% of the time, Pallas kernels for 28%

profile of v5, /device:TPU:0, one launch (start us, length us, event | category | flops | bytes accessed | tf_op | source)
XLA Modules:
  0.0 590.7 jit_solution(16662736569428560242)
XLA Ops:
  12.7 6.5 %all-to-all-start = ((bf16[8,64,768]{2,1,0:T(8,128)(2,1)}), bf16[8,64,768]{2,1,0:T(8,128)(2,1)S(1)}, u32[]{:S(2)}, u32[]{:S(2)}) async-start(bf16[8,64,768]{2,1,0:T(8,128)(2,1)} %reshape.117), calls=%async_computation | async-start | bytes 1572864 | tf_op jit(solution)/shard_map/all_to_all | solution.py:837
  24.9 3.1 slice.135
  28.1 24.1 %collective-permute-done.1 = bf16[64,2176]{1,0:T(8,128)(2,1)S(1)} collective-permute-done((bf16[64,2176]{1,0:T(8,128)(2,1)S(1)}, bf16[64,2176]{1,0:T(8,128)(2,1)S(1)}, u32[]{:S(2)}, u32[]{:S(2)}) %collective-permute-start.1) | collective-permute-done | bytes 278560 | tf_op jit(solution)/shard_map/ppermute | solution.py:722
  53.4 5.1 all-to-all-done
  64.8 12.0 %collective-permute-done.5.refs_2_ = bf16[512,768]{1,0:T(8,128)(2,1)S(1)} collective-permute-done((bf16[512,768]{1,0:T(8,128)(2,1)S(1)}, bf16[512,768]{1,0:T(8,128)(2,1)S(1)}, u32[]{:S(2)}, u32[]{:S(2)}) %collective-permute-start.5) | collective-permute-done | bytes 786464 | tf_op jit(solution)/shard_map/ppermute | solution.py:722
  82.3 7.8 %collective-permute-done.7.refs_4_ = bf16[256,768]{1,0:T(8,128)(2,1)S(1)} collective-permute-done((bf16[256,768]{1,0:T(8,128)(2,1)S(1)}, bf16[256,768]{1,0:T(8,128)(2,1)S(1)}, u32[]{:S(2)}, u32[]{:S(2)}) %collective-permute-start.7) | collective-permute-done | bytes 393248 | tf_op jit(solution)/shard_map/ppermute | solution.py:722
  95.1 10.2 %project.1 = (bf16[1024,2048]{1,0:T(8,128)(2,1)}, bf16[4,8,3,64,128]{4,3,2,1,0:T(8,128)(2,1)}) custom-call(s32[5]{0:T(128)S(1)} %stack.232.starts_ref, bf16[1024,2048]{1,0:T(8,128)(2,1)} %all-gather.3.cloned.1.call-done.x_ref, f32[32,1024]{1,0:T(8,128)S(1)} %get-tuple-element.434.cosine_ref, f32[32,1024]{1,0:T(8,128)S(1)} %get-tuple-element.433.sine_ref, ...), custom_call_target="tpu_custom_call" | custom-call | flops 11000000512 | bytes 1000 | tf_op jit(solution)/shard_map/project/pallas_call | solution.py:254
  105.4 6.7 %collective-permute-done.11.refs_7_ = bf16[128,2048]{1,0:T(8,128)(2,1)S(1)} collective-permute-done((bf16[128,2048]{1,0:T(8,128)(2,1)S(1)}, bf16[128,2048]{1,0:T(8,128)(2,1)S(1)}, u32[]{:S(2)}, u32[]{:S(2)}) %collective-permute-start.11) | collective-permute-done | bytes 524320 | tf_op jit(solution)/shard_map/ppermute | solution.py:722
  112.1 2.9 collective-permute-done.10.refs_6_
  117.4 3.6 all-to-all-start.1
  121.8 3.4 collective-permute-start.13
  127.2 22.3 %collective-permute-done.13.refs_2_ = bf16[256,2176]{1,0:T(8,128)(2,1)S(1)} collective-permute-done((bf16[256,2176]{1,0:T(8,128)(2,1)}, bf16[256,2176]{1,0:T(8,128)(2,1)S(1)}, u32[]{:S(2)}, u32[]{:S(2)}) %collective-permute-start.13) | collective-permute-done | bytes 1114144 | tf_op jit(solution)/shard_map/ppermute | solution.py:718
  149.6 4.5 collective-permute-start.16
  154.1 14.7 %attend_forward.1 = (bf16[32,64,128]{2,1,0:T(8,128)(2,1)}, f32[4,1,1024]{2,1,0:T(1,128)}) custom-call(bf16[32,3,64,128]{3,2,1,0:T(8,128)(2,1)} %bitcast.158), custom_call_target="tpu_custom_call" | custom-call | flops 19800000512 | bytes 1000 | tf_op jit(solution)/shard_map/attend_forward/pallas_call | solution.py:165
  168.8 9.7 %collective-permute-done.16.refs_3_ = bf16[256,2176]{1,0:T(8,128)(2,1)} collective-permute-done((bf16[256,2176]{1,0:T(8,128)(2,1)S(1)}, bf16[256,2176]{1,0:T(8,128)(2,1)}, u32[]{:S(2)}, u32[]{:S(2)}) %collective-permute-start.16) | collective-permute-done | bytes 1114144 | tf_op jit(solution)/shard_map/ppermute | solution.py:718
  178.5 7.0 %all-to-all-start.2 = ((bf16[32,64,128]{2,1,0:T(8,128)(2,1)}), bf16[32,64,128]{2,1,0:T(8,128)(2,1)S(1)}, u32[]{:S(2)}, u32[]{:S(2)}) async-start(bf16[32,64,128]{2,1,0:T(8,128)(2,1)} %get-tuple-element.243.refs_2_), calls=%async_computation.2 | async-start | bytes 1048576 | tf_op jit(solution)/shard_map/all_to_all | solution.py:901
  185.6 4.1 collective-permute-start.19
  189.8 10.2 %all-to-all-done.2.attended_ref = bf16[32,64,128]{2,1,0:T(8,128)(2,1)S(1)} async-done(((bf16[32,64,128]{2,1,0:T(8,128)(2,1)}), bf16[32,64,128]{2,1,0:T(8,128)(2,1)S(1)}, u32[]{:S(2)}, u32[]{:S(2)}) %all-to-all-start.2) | async-done | bytes 524320 | tf_op jit(solution)/shard_map/all_to_all | solution.py:901
  199.9 8.2 %collective-permute-done.19.grad_own_ref = bf16[128,2048]{1,0:T(8,128)(2,1)} collective-permute-done((bf16[128,2048]{1,0:T(8,128)(2,1)S(1)}, bf16[128,2048]{1,0:T(8,128)(2,1)}, u32[]{:S(2)}, u32[]{:S(2)}) %collective-permute-start.19) | collective-permute-done | bytes 524320 | tf_op jit(solution)/shard_map/ppermute | solution.py:718
  208.2 6.8 %collective-permute-start.20 = (bf16[128,2048]{1,0:T(8,128)(2,1)}, bf16[128,2048]{1,0:T(8,128)(2,1)S(1)}, u32[]{:S(2)}, u32[]{:S(2)}) collective-permute-start(bf16[128,2048]{1,0:T(8,128)(2,1)} %collective-permute-done.19.grad_own_ref), channel_id=1, source_target_pairs={{0,3},{1,0},{2,1},{3,2},{4,7},{5,4},{6,5},{7,6},{8,11},{9,8},{10,9... | collective-permute-start | bytes 1572872 | tf_op jit(solution)/shard_map/ppermute | solution.py:718
  216.2 7.2 %finish_attention.1 = (f32[128,2048]{1,0:T(8,128)S(1)}, bf16[128,2048]{1,0:T(8,128)(2,1)S(1)}, f32[1,2048]{1,0:T(1,128)S(1)}) custom-call(s32[40]{0:T(128)S(1)} %stack.226.starts_ref, bf16[128,2048]{1,0:T(8,128)(2,1)S(1)} %copy-done, bf16[32,64,128]{2,1,0:T(8,128)(2,1)S(1)} %all-to-all-done.2.attended_ref, ...), custom_call_target="tpu_custom_call" | custom-call | flops 9900000256 | bytes 1000 | tf_op jit(solution)/shard_map/finish_attention/pallas_call | solution.py:305
  223.4 2.8 collective-permute-done.20.grad_own_ref
  227.7 4.2 collective-permute-start.21
  231.9 3.5 all-to-all-start.3
  235.5 12.3 %units_chunk.4 = (bf16[4,256,1024]{2,1,0:T(8,128)(2,1)}, bf16[4,256,1024]{2,1,0:T(8,128)(2,1)}, bf16[4,256,1024]{2,1,0:T(8,128)(2,1)}, bf16[4,256,2048]{2,1,0:T(...) custom-call(bf16[128,2048]{1,0:T(8,128)(2,1)} %copy-done.46, ...), custom_call_target="tpu_custom_call" | custom-call | flops 14300000256 | bytes 1000 | tf_op jit(solution)/shard_map/units_chunk/pallas_call | solution.py:634
  247.8 7.2 %collective-permute-done.26.grad_own_ref = bf16[128,2048]{1,0:T(8,128)(2,1)} collective-permute-done((bf16[128,2048]{1,0:T(8,128)(2,1)}, bf16[128,2048]{1,0:T(8,128)(2,1)}, u32[]{:S(2)}, u32[]{:S(2)}) %collective-permute-start.26) | collective-permute-done | bytes 524320 | tf_op jit(solution)/shard_map/ppermute | solution.py:718
  255.6 4.3 collective-permute-start.24
  260.8 12.3 %units_chunk.5 = (bf16[4,256,1024]{2,1,0:T(8,128)(2,1)}, bf16[4,256,1024]{2,1,0:T(8,128)(2,1)}, bf16[4,256,1024]{2,1,0:T(8,128)(2,1)}, bf16[4,256,2048]{2,1,0:T(...) custom-call(bf16[128,2048]{1,0:T(8,128)(2,1)} %collective-permute-do, ...), custom_call_target="tpu_custom_call", output_to_operand_aliasing={{0}: (14, {}), {1}: (15, {}), {2}: (16, {}), {3}: (17, {}),... | custom-call | flops 14300000256 | bytes 1000 | tf_op jit(solution)/shard_map/units_chunk/pallas_call | solution.py:634
  273.9 2.4 collective-permute-start.28
  280.4 12.3 %units_chunk.6 = (bf16[4,256,1024]{2,1,0:T(8,128)(2,1)}, bf16[4,256,1024]{2,1,0:T(8,128)(2,1)}, bf16[4,256,1024]{2,1,0:T(8,128)(2,1)}, bf16[4,256,2048]{2,1,0:T(...) custom-call(bf16[128,2048]{1,0:T(8,128)(2,1)} %copy-done.85, ...), custom_call_target="tpu_custom_call", output_to_operand_aliasing={{0}: (14, {}), {1}: (15, {}), {2}: (16, {}), {3}: (17, {}),... | custom-call | flops 14300000256 | bytes 1000 | tf_op jit(solution)/shard_map/units_chunk/pallas_call | solution.py:634
  292.7 6.7 %collective-permute-done.30 = bf16[128,2048]{1,0:T(8,128)(2,1)S(1)} collective-permute-done((bf16[128,2048]{1,0:T(8,128)(2,1)S(1)}, bf16[128,2048]{1,0:T(8,128)(2,1)S(1)}, u32[]{:S(2)}, u32[]{:S(2)}) %collective-permute-start.30) | collective-permute-done | bytes 524320 | tf_op jit(solution)/shard_map/ppermute | solution.py:718
  302.9 4.3 collective-permute-start.34
  308.2 12.2 %units_chunk.7 = (bf16[4,256,1024]{2,1,0:T(8,128)(2,1)}, bf16[4,256,1024]{2,1,0:T(8,128)(2,1)}, bf16[4,256,1024]{2,1,0:T(8,128)(2,1)}, bf16[4,256,2048]{2,1,0:T(...) custom-call(bf16[128,2048]{1,0:T(8,128)(2,1)} %copy-done.84, ...), custom_call_target="tpu_custom_call", output_to_operand_aliasing={{0}: (14, {}), {1}: (15, {}), {2}: (16, {}), {3}: (17, {}),... | custom-call | flops 14300000256 | bytes 1000 | tf_op jit(solution)/shard_map/units_chunk/pallas_call | solution.py:634
  324.9 2.8 collective-permute-start.38
  327.7 8.6 %transposed_product.2 = bf16[1024,2048]{1,0:T(8,128)(2,1)} custom-call(bf16[1024,1024]{1,0:T(8,128)(2,1)S(1)} %bitcast.152, bf16[1024,2048]{1,0:T(8,128)(2,1)} %bitcast.167), custom_call_target="tpu_custom_call" | custom-call | flops 9900000256 | bytes 1000 | tf_op jit(solution)/shard_map/transposed_product/pallas_call | solution.py:657
  336.3 3.2 collective-permute-done.38
  342.0 6.7 %back_to_attention.1 = (f32[128,2048]{1,0:T(8,128)S(1)}, bf16[128,2048]{1,0:T(8,128)(2,1)S(1)}, f32[1,2048]{1,0:T(1,128)S(1)}, bf16[32,64,128]{2,1,0:T(8,128)(2,1)}) custom-call(s32[40]{0:T(128)S(1)} %stack.226.starts_ref, f32[128,2048]{1,0:T(8,128)S(1)} %get-tuple-element.253.mid_ref, f32[128,2048]{1,0:T(8,128)S(1)} %add_add_fusion.grad_ref, ...), custom_call_target="tpu_custom_call" | custom-call | flops 6600000000 | bytes 1000 | tf_op jit(solution)/shard_map/back_to_attention/pallas_call | solution.py:359
  348.9 5.3 all-to-all-start.4
  355.9 8.7 %transposed_product.3 = bf16[1024,2048]{1,0:T(8,128)(2,1)} custom-call(bf16[1024,1024]{1,0:T(8,128)(2,1)S(1)} %bitcast.153, bf16[1024,2048]{1,0:T(8,128)(2,1)} %bitcast.168), custom_call_target="tpu_custom_call" | custom-call | flops 9900000256 | bytes 1000 | tf_op jit(solution)/shard_map/transposed_product/pallas_call | solution.py:657
  364.5 4.1 all-to-all-done.4.refs_1_
  371.6 12.0 %attend_backward.2 = (bf16[32,3,64,128]{3,2,1,0:T(8,128)(2,1)}, f32[2,64,1024]{2,1,0:T(8,128)}) custom-call(bf16[32,3,64,128]{3,2,1,0:T(8,128)(2,1)} %bitcast.159, bf16[32,64,128]{2,1,0:T(8,128)(2,1)} %all-to-all-done.4.refs_1_, bf16[32,64,128]{2,1,0:T(8,128)(2,1)} %get-tuple-element.243.refs_2_, f32[4,1,1024]{2,1,0:T(1,128)} %get-tuple-element.331.refs_3_), custom_call_target="tpu_custom_call" | custom-call | flops 19800000512 | bytes 1000 | tf_op jit(solution)/shard_map/attend_backward/pallas_call | solution.py:187
  388.8 22.3 %attend_backward.3 = (bf16[32,3,64,128]{3,2,1,0:T(8,128)(2,1)}, f32[1,64,1024]{2,1,0:T(8,128)}) custom-call(bf16[32,3,64,128]{3,2,1,0:T(8,128)(2,1)} %bitcast.160, bf16[32,64,128]{2,1,0:T(8,128)(2,1)} %all-to-all-done.4.refs_1_, bf16[32,64,128]{2,1,0:T(8,128)(2,1)} %get-tuple-element.243.refs_2_, f32[4,1,1024]{2,1,0:T(1,128)} %get-tuple-element.331.refs_3_, ...), custom_call_target="tpu_custom_call" | custom-call | flops 19800000512 | bytes 1000 | tf_op jit(solution)/shard_map/attend_backward/pallas_call | solution.py:187
  411.7 4.4 all-to-all-start.5
  416.9 3.4 collective-permute-start.47
  420.3 2.5 fusion.12
  423.6 18.5 %all-to-all-done.5.grad_ref = bf16[4,8,3,64,128]{4,3,2,1,0:T(8,128)(2,1)} async-done(((bf16[4,8,3,64,128]{4,3,2,1,0:T(8,128)(2,1)}), bf16[4,8,3,64,128]{4,3,2,1,0:T(8,128)(2,1)}, u32[]{:S(2)}, u32[]{:S(2)}) %all-to-all-start.5) | async-done | bytes 1572896 | tf_op jit(solution)/shard_map/all_to_all | solution.py:984
  442.1 6.5 %turn_back.1 = (bf16[8,128,768]{2,1,0:T(8,128)(2,1)S(1)}, bf16[512,768]{1,0:T(8,128)(2,1)S(1)}, bf16[512,768]{1,0:T(8,128)(2,1)S(1)}, bf16[256,768]{1,0:T(8,128)...) custom-call(s32[1]{0:T(128)} %bitcast.57.place_ref, ...), custom_call_target="tpu_custom_call" | custom-call | flops 8800000000 | bytes 1000 | tf_op jit(solution)/shard_map/turn_back/pallas_call | solution.py:440
  453.1 4.1 collective-permute-start.49
  457.2 7.1 %back_to_norm.1 = (f32[128,2048]{1,0:T(8,128)S(1)}, f32[128,2048]{1,0:T(8,128)S(1)}, f32[128,2048]{1,0:T(8,128)}, f32[128,2048]{1,0:T(8,128)}, bf16[4,128,2048]{2,1,0:T(8,128)(2,1)}) custom-call(s32[5]{0:T(128)S(1)} %copy-done.29, s32[8]{0:T(128)S(1)} %stack.241.spots_ref, bf16[8,128,768]{2,1,0:T(8,128)(2,1)} %copy-done.53, bf16[512,768]{1,0:T(8,128)(2,1)S(1)} %bitcast.151, ...), custom_call_target="tpu_custom_call" | custom-call | flops 7699999744 | bytes 1000 | tf_op jit(solution)/shard_map/back_to_norm/pallas_call | solution.py:475
  465.4 9.7 %collective-permute-done.50 = bf16[512,768]{1,0:T(8,128)(2,1)S(1)} collective-permute-done((bf16[512,768]{1,0:T(8,128)(2,1)S(1)}, bf16[512,768]{1,0:T(8,128)(2,1)S(1)}, u32[]{:S(2)}, u32[]{:S(2)}) %collective-permute-start.50) | collective-permute-done | bytes 786464 | tf_op jit(solution)/shard_map/ppermute | solution.py:722
  476.4 2.9 convert_element_type.308
  482.8 4.2 collective-permute-start.53
  489.4 7.4 %product_parts.1 = (bf16[256,2048]{1,0:T(8,128)(2,1)S(1)}, bf16[256,2048]{1,0:T(8,128)(2,1)S(1)}, bf16[128,2048]{1,0:T(8,128)(2,1)S(1)}, bf16[128,2048]{1,0:T(8,128)(2,1)S(1)}, bf16[256,2048]{1,0:T(8,128)(2,1)S(1)}) custom-call(s32[1]{0:T(128)} %bitcast.57.place_ref, bf16[1024,1024]{1,0:T(8,128)(2,1)} %bitcast.170, bf16[1024,2048]{1,0:T(8,128)(2,1)} %bitcast.169), custom_call_target="tpu_custom_call" | custom-call | flops 11000000512 | bytes 1000 | tf_op jit(solution)/shard_map/product_parts/pallas_call | solution.py:686
  501.5 4.2 out_product.1
  505.6 2.6 fusion.8
  510.9 2.4 fusion.10
  513.3 3.5 all-to-all-start.6
  519.4 2.8 convert_element_type.309
  528.0 3.5 collective-permute-start.60
  532.1 15.8 %collective-permute-done.63 = bf16[256,384]{1,0:T(8,128)(2,1)S(1)} collective-permute-done((bf16[256,384]{1,0:T(8,128)(2,1)S(1)}, bf16[256,384]{1,0:T(8,128)(2,1)S(1)}, u32[]{:S(2)}, u32[]{:S(2)}) %collective-permute-start.63) | collective-permute-done | bytes 196640 | tf_op jit(solution)/shard_map/ppermute | solution.py:722
  552.2 4.9 all-to-all-start.7
  562.1 2.4 fusion.3
  564.6 8.6 %collective-permute-done.65 = bf16[128,2048]{1,0:T(8,128)(2,1)S(1)} collective-permute-done((bf16[128,2048]{1,0:T(8,128)(2,1)S(1)}, bf16[128,2048]{1,0:T(8,128)(2,1)S(1)}, u32[]{:S(2)}, u32[]{:S(2)}) %collective-permute-start.65) | collective-permute-done | bytes 524320 | tf_op jit(solution)/shard_map/ppermute | solution.py:722
  577.9 3.1 pad_maximum_fusion
  (370 shorter events, 112.7 us)
Async XLA Ops:
  7.2 82.9 %all-gather.3.cloned.1.call-start = ((), (), s32[]{:S(2)}) async-start(), calls=%async_computation.10 | async-start | bytes 4718592 | tf_op jit(solution)/shard_map/all_gather | solution.py:829
  12.7 45.8 %all-to-all-start = ((bf16[8,64,768]{2,1,0:T(8,128)(2,1)}), bf16[8,64,768]{2,1,0:T(8,128)(2,1)S(1)}, u32[]{:S(2)}, u32[]{:S(2)}) async-start(bf16[8,64,768]{2,1,0:T(8,128)(2,1)} %reshape.117), calls=%async_computation | async-start | bytes 1572864 | tf_op jit(solution)/shard_map/all_to_all | solution.py:837
  19.2 216.3 %all-gather.5.cloned.1.call-start = ((), (), s32[]{:S(2)}) async-start(), calls=%async_computation.11 | async-start | bytes 10485760 | tf_op jit(solution)/shard_map/all_gather | solution.py:861
  20.6 32.8 %collective-permute-start.3 = (bf16[256,2048]{1,0:T(8,128)(2,1)S(1)}, bf16[256,2048]{1,0:T(8,128)(2,1)}, u32[]{:S(2)}, u32[]{:S(2)}) collective-permute-start(bf16[256,2048]{1,0:T(8,128)(2,1)S(1)} %slice.128.refs_3_), channel_id=1, source_target_pairs={{0,16},{8,24},{16,0},{24,8},{1,17},{9,25},{17,1},{25,9},{2,18},{10... | collective-permute-start | bytes 3145736 | tf_op jit(solution)/shard_map/ppermute | solution.py:722
  22.2 31.2 %collective-permute-start.2 = (bf16[256,2048]{1,0:T(8,128)(2,1)S(1)}, bf16[256,2048]{1,0:T(8,128)(2,1)}, u32[]{:S(2)}, u32[]{:S(2)}) collective-permute-start(bf16[256,2048]{1,0:T(8,128)(2,1)S(1)} %slice.128.refs_3_), channel_id=1, source_target_pairs={{0,8},{8,0},{16,24},{24,16},{1,9},{9,1},{17,25},{25,17},{2,10},{10... | collective-permute-start | bytes 3145736 | tf_op jit(solution)/shard_map/ppermute | solution.py:722
  23.8 28.3 %collective-permute-start.1 = (bf16[64,2176]{1,0:T(8,128)(2,1)S(1)}, bf16[64,2176]{1,0:T(8,128)(2,1)S(1)}, u32[]{:S(2)}, u32[]{:S(2)}) collective-permute-start(bf16[64,2176]{1,0:T(8,128)(2,1)S(1)} %fusion.19), channel_id=1, source_target_pairs={{0,16},{8,24},{16,0},{24,8},{1,17},{9,25},{17,1},{25,9},{2,18},{10... | collective-permute-start | bytes 835592 | tf_op jit(solution)/shard_map/ppermute | solution.py:722
  24.4 29.0 %collective-permute-start = (bf16[64,2176]{1,0:T(8,128)(2,1)S(1)}, bf16[64,2176]{1,0:T(8,128)(2,1)S(1)}, u32[]{:S(2)}, u32[]{:S(2)}) collective-permute-start(bf16[64,2176]{1,0:T(8,128)(2,1)S(1)} %fusion.19), channel_id=1, source_target_pairs={{0,8},{8,0},{16,24},{24,16},{1,9},{9,1},{17,25},{25,17},{2,10},{10... | collective-permute-start | bytes 835592 | tf_op jit(solution)/shard_map/ppermute | solution.py:722
  58.5 18.3 %collective-permute-start.5 = (bf16[512,768]{1,0:T(8,128)(2,1)S(1)}, bf16[512,768]{1,0:T(8,128)(2,1)S(1)}, u32[]{:S(2)}, u32[]{:S(2)}) collective-permute-start(bf16[512,768]{1,0:T(8,128)(2,1)S(1)} %bitcast.148), channel_id=1, source_target_pairs={{0,16},{8,24},{16,0},{24,8},{1,17},{9,25},{17,1},{25,9},{2,18},{10... | collective-permute-start | bytes 2359304 | tf_op jit(solution)/shard_map/ppermute | solution.py:722
  60.1 18.6 %collective-permute-start.4 = (bf16[512,768]{1,0:T(8,128)(2,1)S(1)}, bf16[512,768]{1,0:T(8,128)(2,1)S(1)}, u32[]{:S(2)}, u32[]{:S(2)}) collective-permute-start(bf16[512,768]{1,0:T(8,128)(2,1)S(1)} %bitcast.149), channel_id=1, source_target_pairs={{0,8},{8,0},{16,24},{24,16},{1,9},{9,1},{17,25},{25,17},{2,10},{10... | collective-permute-start | bytes 2359304 | tf_op jit(solution)/shard_map/ppermute | solution.py:722
  61.6 20.0 %collective-permute-start.9 = (bf16[32,2176]{1,0:T(8,128)(2,1)S(1)}, bf16[32,2176]{1,0:T(8,128)(2,1)S(1)}, u32[]{:S(2)}, u32[]{:S(2)}) collective-permute-start(bf16[32,2176]{1,0:T(8,128)(2,1)S(1)} %slice.132), channel_id=1, source_target_pairs={{0,8},{8,0},{16,24},{24,16},{1,9},{9,1},{17,25},{25,17},{2,10},{10... | collective-permute-start | bytes 417800 | tf_op jit(solution)/shard_map/ppermute | solution.py:722
  62.2 17.9 %collective-permute-start.8 = (bf16[32,2176]{1,0:T(8,128)(2,1)S(1)}, bf16[32,2176]{1,0:T(8,128)(2,1)S(1)}, u32[]{:S(2)}, u32[]{:S(2)}) collective-permute-start(bf16[32,2176]{1,0:T(8,128)(2,1)S(1)} %slice.131), channel_id=1, source_target_pairs={{0,16},{8,24},{16,0},{24,8},{1,17},{9,25},{17,1},{25,9},{2,18},{10... | collective-permute-start | bytes 417800 | tf_op jit(solution)/shard_map/ppermute | solution.py:722
  76.9 13.2 %collective-permute-start.7 = (bf16[256,768]{1,0:T(8,128)(2,1)S(1)}, bf16[256,768]{1,0:T(8,128)(2,1)S(1)}, u32[]{:S(2)}, u32[]{:S(2)}) collective-permute-start(bf16[256,768]{1,0:T(8,128)(2,1)S(1)} %slice.171), channel_id=1, source_target_pairs={{0,8},{8,0},{16,24},{24,16},{1,9},{9,1},{17,25},{25,17},{2,10},{10... | collective-permute-start | bytes 1179656 | tf_op jit(solution)/shard_map/ppermute | solution.py:722
  78.7 11.4 %collective-permute-start.6 = (bf16[256,768]{1,0:T(8,128)(2,1)S(1)}, bf16[256,768]{1,0:T(8,128)(2,1)S(1)}, u32[]{:S(2)}, u32[]{:S(2)}) collective-permute-start(bf16[256,768]{1,0:T(8,128)(2,1)S(1)} %slice.170), channel_id=1, source_target_pairs={{0,16},{8,24},{16,0},{24,8},{1,17},{9,25},{17,1},{25,9},{2,18},{10... | collective-permute-start | bytes 1179656 | tf_op jit(solution)/shard_map/ppermute | solution.py:722
  90.2 27.2 %collective-permute-start.12 = (bf16[256,2176]{1,0:T(8,128)(2,1)}, bf16[256,2176]{1,0:T(8,128)(2,1)}, u32[]{:S(2)}, u32[]{:S(2)}) collective-permute-start(bf16[256,2176]{1,0:T(8,128)(2,1)} %constant_dynamic-update-slice_fusion.refs_0_), channel_id=1, source_target_pairs={{0,3},{1,0},{2,1},{3,2},{4,7},{5,4},{6,5},{7,6},{8,11},{9,8},{10,9... | collective-permute-start | bytes 3342344 | tf_op jit(solution)/shard_map/ppermute | solution.py:718
  93.1 19.0 %collective-permute-start.11 = (bf16[128,2048]{1,0:T(8,128)(2,1)S(1)}, bf16[128,2048]{1,0:T(8,128)(2,1)S(1)}, u32[]{:S(2)}, u32[]{:S(2)}) collective-permute-start(bf16[128,2048]{1,0:T(8,128)(2,1)S(1)} %slice.134), channel_id=1, source_target_pairs={{0,8},{8,0},{16,24},{24,16},{1,9},{9,1},{17,25},{25,17},{2,10},{10... | collective-permute-start | bytes 1572872 | tf_op jit(solution)/shard_map/ppermute | solution.py:722
  94.6 20.4 %collective-permute-start.10 = (bf16[128,2048]{1,0:T(8,128)(2,1)S(1)}, bf16[128,2048]{1,0:T(8,128)(2,1)S(1)}, u32[]{:S(2)}, u32[]{:S(2)}) collective-permute-start(bf16[128,2048]{1,0:T(8,128)(2,1)S(1)} %slice.133), channel_id=1, source_target_pairs={{0,16},{8,24},{16,0},{24,8},{1,17},{9,25},{17,1},{25,9},{2,18},{10... | collective-permute-start | bytes 1572872 | tf_op jit(solution)/shard_map/ppermute | solution.py:722
  117.4 32.2 %all-to-all-start.1 = ((bf16[4,8,3,64,128]{4,3,2,1,0:T(8,128)(2,1)}), bf16[4,8,3,64,128]{4,3,2,1,0:T(8,128)(2,1)S(1)}, u32[]{:S(2)}, u32[]{:S(2)}) async-start(bf16[4,8,3,64,128]{4,3,2,1,0:T(8,128)(2,1)} %get-tuple-element.234), calls=%async_computation.1 | async-start | bytes 3145728 | tf_op jit(solution)/shard_map/all_to_all | solution.py:857
  121.8 27.8 %collective-permute-start.13 = (bf16[256,2176]{1,0:T(8,128)(2,1)}, bf16[256,2176]{1,0:T(8,128)(2,1)S(1)}, u32[]{:S(2)}, u32[]{:S(2)}) collective-permute-start(bf16[256,2176]{1,0:T(8,128)(2,1)} %collective-permute-done.12.refs_1_), channel_id=1, source_target_pairs={{0,3},{1,0},{2,1},{3,2},{4,7},{5,4},{6,5},{7,6},{8,11},{9,8},{10,9... | collective-permute-start | bytes 3342344 | tf_op jit(solution)/shard_map/ppermute | solution.py:718
  149.6 19.2 %collective-permute-start.17 = (bf16[256,2176]{1,0:T(8,128)(2,1)S(1)}, bf16[256,2176]{1,0:T(8,128)(2,1)S(1)}, u32[]{:S(2)}, u32[]{:S(2)}) collective-permute-start(bf16[256,2176]{1,0:T(8,128)(2,1)S(1)} %collective-permute-done.13.refs_2_), channel_id=1, source_target_pairs={{0,4},{4,0},{1,5},{5,1},{2,6},{6,2},{3,7},{7,3},{8,12},{12,8},{9,1... | collective-permute-start | bytes 3342344 | tf_op jit(solution)/shard_map/ppermute | solution.py:713
  149.6 28.9 %collective-permute-start.16 = (bf16[256,2176]{1,0:T(8,128)(2,1)S(1)}, bf16[256,2176]{1,0:T(8,128)(2,1)}, u32[]{:S(2)}, u32[]{:S(2)}) collective-permute-start(bf16[256,2176]{1,0:T(8,128)(2,1)S(1)} %collective-permute-done.13.refs_2_), channel_id=1, source_target_pairs={{0,3},{1,0},{2,1},{3,2},{4,7},{5,4},{6,5},{7,6},{8,11},{9,8},{10,9... | collective-permute-start | bytes 3342344 | tf_op jit(solution)/shard_map/ppermute | solution.py:718
  178.5 21.4 %collective-permute-start.18 = (bf16[256,2176]{1,0:T(8,128)(2,1)}, bf16[256,2176]{1,0:T(8,128)(2,1)S(1)}, u32[]{:S(2)}, u32[]{:S(2)}) collective-permute-start(bf16[256,2176]{1,0:T(8,128)(2,1)} %collective-permute-done.16.refs_3_), channel_id=1, source_target_pairs={{0,4},{4,0},{1,5},{5,1},{2,6},{6,2},{3,7},{7,3},{8,12},{12,8},{9,1... | collective-permute-start | bytes 3342344 | tf_op jit(solution)/shard_map/ppermute | solution.py:713
  178.5 21.4 %all-to-all-start.2 = ((bf16[32,64,128]{2,1,0:T(8,128)(2,1)}), bf16[32,64,128]{2,1,0:T(8,128)(2,1)S(1)}, u32[]{:S(2)}, u32[]{:S(2)}) async-start(bf16[32,64,128]{2,1,0:T(8,128)(2,1)} %get-tuple-element.243.refs_2_), calls=%async_computation.2 | async-start | bytes 1048576 | tf_op jit(solution)/shard_map/all_to_all | solution.py:901
  185.6 22.6 %collective-permute-start.19 = (bf16[128,2048]{1,0:T(8,128)(2,1)S(1)}, bf16[128,2048]{1,0:T(8,128)(2,1)}, u32[]{:S(2)}, u32[]{:S(2)}) collective-permute-start(bf16[128,2048]{1,0:T(8,128)(2,1)S(1)} %copy-done.34), channel_id=1, source_target_pairs={{0,3},{1,0},{2,1},{3,2},{4,7},{5,4},{6,5},{7,6},{8,11},{9,8},{10,9... | collective-permute-start | bytes 1572872 | tf_op jit(solution)/shard_map/ppermute | solution.py:718
  208.2 18.1 %collective-permute-start.20 = (bf16[128,2048]{1,0:T(8,128)(2,1)}, bf16[128,2048]{1,0:T(8,128)(2,1)S(1)}, u32[]{:S(2)}, u32[]{:S(2)}) collective-permute-start(bf16[128,2048]{1,0:T(8,128)(2,1)} %collective-permute-done.19.grad_own_ref), channel_id=1, source_target_pairs={{0,3},{1,0},{2,1},{3,2},{4,7},{5,4},{6,5},{7,6},{8,11},{9,8},{10,9... | collective-permute-start | bytes 1572872 | tf_op jit(solution)/shard_map/ppermute | solution.py:718
  226.3 9.2 %collective-permute-start.23 = (bf16[128,2048]{1,0:T(8,128)(2,1)S(1)}, bf16[128,2048]{1,0:T(8,128)(2,1)}, u32[]{:S(2)}, u32[]{:S(2)}) collective-permute-start(bf16[128,2048]{1,0:T(8,128)(2,1)S(1)} %copy-done.34), channel_id=1, source_target_pairs={{0,4},{4,0},{1,5},{5,1},{2,6},{6,2},{3,7},{7,3},{8,12},{12,8},{9,1... | collective-permute-start | bytes 1572872 | tf_op jit(solution)/shard_map/ppermute | solution.py:713
  227.7 20.1 %collective-permute-start.21 = (bf16[128,2048]{1,0:T(8,128)(2,1)S(1)}, bf16[128,2048]{1,0:T(8,128)(2,1)}, u32[]{:S(2)}, u32[]{:S(2)}) collective-permute-start(bf16[128,2048]{1,0:T(8,128)(2,1)S(1)} %get-tuple-element.257.own_ref), channel_id=1, source_target_pairs={{0,3},{1,0},{2,1},{3,2},{4,7},{5,4},{6,5},{7,6},{8,11},{9,8},{10,9... | collective-permute-start | bytes 1572872 | tf_op jit(solution)/shard_map/ppermute | solution.py:718
  231.9 15.9 %all-to-all-start.3 = ((bf16[4,8,64,128]{3,2,1,0:T(8,128)(2,1)}), bf16[4,8,64,128]{3,2,1,0:T(8,128)(2,1)S(1)}, u32[]{:S(2)}, u32[]{:S(2)}) async-start(bf16[4,8,64,128]{3,2,1,0:T(8,128)(2,1)} %bitcast.157), calls=%async_computation.3 | async-start | bytes 1048576 | tf_op jit(solution)/shard_map/all_to_all | solution.py:911
  235.3 176.4 %reduce-scatter.3.cloned.1.call-start = ((), (), s32[]{:S(2)}) async-start(), calls=%async_computation.12 | async-start | bytes 5242880 | tf_op jit(solution)/shard_map/reduce_scatter | solution.py:944
  235.4 19.7 %collective-permute-start.26 = (bf16[128,2048]{1,0:T(8,128)(2,1)}, bf16[128,2048]{1,0:T(8,128)(2,1)}, u32[]{:S(2)}, u32[]{:S(2)}) collective-permute-start(bf16[128,2048]{1,0:T(8,128)(2,1)} %copy-done.82), channel_id=1, source_target_pairs={{0,3},{1,0},{2,1},{3,2},{4,7},{5,4},{6,5},{7,6},{8,11},{9,8},{10,9... | collective-permute-start | bytes 1572872 | tf_op jit(solution)/shard_map/ppermute | solution.py:718
  255.6 17.6 %collective-permute-start.24 = (bf16[128,2048]{1,0:T(8,128)(2,1)}, bf16[128,2048]{1,0:T(8,128)(2,1)S(1)}, u32[]{:S(2)}, u32[]{:S(2)}) collective-permute-start(bf16[128,2048]{1,0:T(8,128)(2,1)} %collective-permute-done.21.own_ref), channel_id=1, source_target_pairs={{0,3},{1,0},{2,1},{3,2},{4,7},{5,4},{6,5},{7,6},{8,11},{9,8},{10,9... | collective-permute-start | bytes 1572872 | tf_op jit(solution)/shard_map/ppermute | solution.py:718
  273.9 18.8 %collective-permute-start.28 = (bf16[128,2048]{1,0:T(8,128)(2,1)S(1)}, bf16[128,2048]{1,0:T(8,128)(2,1)S(1)}, u32[]{:S(2)}, u32[]{:S(2)}) collective-permute-start(bf16[128,2048]{1,0:T(8,128)(2,1)S(1)} %collective-permute-done.24.own_ref), channel_id=1, source_target_pairs={{0,3},{1,0},{2,1},{3,2},{4,7},{5,4},{6,5},{7,6},{8,11},{9,8},{10,9... | collective-permute-start | bytes 1572872 | tf_op jit(solution)/shard_map/ppermute | solution.py:718
  277.6 21.8 %collective-permute-start.30 = (bf16[128,2048]{1,0:T(8,128)(2,1)S(1)}, bf16[128,2048]{1,0:T(8,128)(2,1)S(1)}, u32[]{:S(2)}, u32[]{:S(2)}) collective-permute-start(bf16[128,2048]{1,0:T(8,128)(2,1)S(1)} %add_convert_fusion.2), channel_id=1, source_target_pairs={{0,3},{1,0},{2,1},{3,2},{4,7},{5,4},{6,5},{7,6},{8,11},{9,8},{10,9... | collective-permute-start | bytes 1572872 | tf_op jit(solution)/shard_map/ppermute | solution.py:718
  302.9 17.5 %collective-permute-start.34 = (bf16[128,2048]{1,0:T(8,128)(2,1)S(1)}, bf16[128,2048]{1,0:T(8,128)(2,1)S(1)}, u32[]{:S(2)}, u32[]{:S(2)}) collective-permute-start(bf16[128,2048]{1,0:T(8,128)(2,1)S(1)} %add_convert_fusion.1), channel_id=1, source_target_pairs={{0,3},{1,0},{2,1},{3,2},{4,7},{5,4},{6,5},{7,6},{8,11},{9,8},{10,9... | collective-permute-start | bytes 1572872 | tf_op jit(solution)/shard_map/ppermute | solution.py:718
  324.9 14.6 %collective-permute-start.38 = (bf16[128,2048]{1,0:T(8,128)(2,1)}, bf16[128,2048]{1,0:T(8,128)(2,1)S(1)}, u32[]{:S(2)}, u32[]{:S(2)}) collective-permute-start(bf16[128,2048]{1,0:T(8,128)(2,1)} %add_add_fusion.1), channel_id=1, source_target_pairs={{0,3},{1,0},{2,1},{3,2},{4,7},{5,4},{6,5},{7,6},{8,11},{9,8},{10,9... | collective-permute-start | bytes 1572872 | tf_op jit(solution)/shard_map/ppermute | solution.py:718
  348.7 19.9 %collective-permute-start.40 = (bf16[4,128,2048]{2,1,0:T(8,128)(2,1)}, bf16[4,128,2048]{2,1,0:T(8,128)(2,1)}, u32[]{:S(2)}, u32[]{:S(2)}) collective-permute-start(bf16[4,128,2048]{2,1,0:T(8,128)(2,1)} %get-tuple-element.329), channel_id=1, source_target_pairs={{0,4},{4,0},{1,5},{5,1},{2,6},{6,2},{3,7},{7,3},{8,12},{12,8},{9,1... | collective-permute-start | bytes 6291464 | tf_op jit(solution)/shard_map/ppermute | solution.py:713
  348.9 19.7 %all-to-all-start.4 = ((bf16[32,64,128]{2,1,0:T(8,128)(2,1)}), bf16[32,64,128]{2,1,0:T(8,128)(2,1)}, u32[]{:S(2)}, u32[]{:S(2)}) async-start(bf16[32,64,128]{2,1,0:T(8,128)(2,1)} %get-tuple-element.325), calls=%async_computation.4 | async-start | bytes 1048576 | tf_op jit(solution)/shard_map/all_to_all | solution.py:953
  368.6 17.4 %collective-permute-start.42 = (bf16[128,2048]{1,0:T(8,128)(2,1)S(1)}, bf16[128,2048]{1,0:T(8,128)(2,1)S(1)}, u32[]{:S(2)}, u32[]{:S(2)}) collective-permute-start(bf16[128,2048]{1,0:T(8,128)(2,1)S(1)} %get-tuple-element.383.refs_0_), channel_id=1, source_target_pairs={{0,4},{4,0},{1,5},{5,1},{2,6},{6,2},{3,7},{7,3},{8,12},{12,8},{9,1... | collective-permute-start | bytes 1572872 | tf_op jit(solution)/shard_map/ppermute | solution.py:713
  369.9 16.1 %collective-permute-start.41 = (bf16[128,2048]{1,0:T(8,128)(2,1)S(1)}, bf16[128,2048]{1,0:T(8,128)(2,1)S(1)}, u32[]{:S(2)}, u32[]{:S(2)}) collective-permute-start(bf16[128,2048]{1,0:T(8,128)(2,1)S(1)} %get-tuple-element.383.refs_0_), channel_id=1, source_target_pairs={{0,3},{1,0},{2,1},{3,2},{4,7},{5,4},{6,5},{7,6},{8,11},{9,8},{10,9... | collective-permute-start | bytes 1572872 | tf_op jit(solution)/shard_map/ppermute | solution.py:718
  386.1 25.6 %collective-permute-start.45 = (bf16[128,2048]{1,0:T(8,128)(2,1)S(1)}, bf16[128,2048]{1,0:T(8,128)(2,1)S(1)}, u32[]{:S(2)}, u32[]{:S(2)}) collective-permute-start(bf16[128,2048]{1,0:T(8,128)(2,1)S(1)} %collective-permute-done.41.refs_2_), channel_id=1, source_target_pairs={{0,4},{4,0},{1,5},{5,1},{2,6},{6,2},{3,7},{7,3},{8,12},{12,8},{9,1... | collective-permute-start | bytes 1572872 | tf_op jit(solution)/shard_map/ppermute | solution.py:713
  386.4 25.3 %collective-permute-start.43 = (bf16[128,2048]{1,0:T(8,128)(2,1)S(1)}, bf16[128,2048]{1,0:T(8,128)(2,1)}, u32[]{:S(2)}, u32[]{:S(2)}) collective-permute-start(bf16[128,2048]{1,0:T(8,128)(2,1)S(1)} %collective-permute-done.41.refs_2_), channel_id=1, source_target_pairs={{0,3},{1,0},{2,1},{3,2},{4,7},{5,4},{6,5},{7,6},{8,11},{9,8},{10,9... | collective-permute-start | bytes 1572872 | tf_op jit(solution)/shard_map/ppermute | solution.py:718
  387.7 24.0 %collective-permute-start.44 = (bf16[128,2048]{1,0:T(8,128)(2,1)}, bf16[128,2048]{1,0:T(8,128)(2,1)S(1)}, u32[]{:S(2)}, u32[]{:S(2)}) collective-permute-start(bf16[128,2048]{1,0:T(8,128)(2,1)} %fusion.16), channel_id=1, source_target_pairs={{0,3},{1,0},{2,1},{3,2},{4,7},{5,4},{6,5},{7,6},{8,11},{9,8},{10,9... | collective-permute-start | bytes 1572872 | tf_op jit(solution)/shard_map/ppermute | solution.py:718
  411.7 30.4 %all-to-all-start.5 = ((bf16[4,8,3,64,128]{4,3,2,1,0:T(8,128)(2,1)}), bf16[4,8,3,64,128]{4,3,2,1,0:T(8,128)(2,1)}, u32[]{:S(2)}, u32[]{:S(2)}) async-start(bf16[4,8,3,64,128]{4,3,2,1,0:T(8,128)(2,1)} %bitcast.161), calls=%async_computation.6 | async-start | bytes 3145728 | tf_op jit(solution)/shard_map/all_to_all | solution.py:984
  416.1 89.5 %reduce-scatter.5.cloned.1.call-start = ((), (), s32[]{:S(2)}) async-start(), calls=%async_computation.13 | async-start | bytes 5242880 | tf_op jit(solution)/shard_map/reduce_scatter | solution.py:944
  416.9 32.9 %collective-permute-start.47 = (bf16[128,2048]{1,0:T(8,128)(2,1)}, bf16[128,2048]{1,0:T(8,128)(2,1)}, u32[]{:S(2)}, u32[]{:S(2)}) collective-permute-start(bf16[128,2048]{1,0:T(8,128)(2,1)} %collective-permute-done.43.refs_4_), channel_id=1, source_target_pairs={{0,3},{1,0},{2,1},{3,2},{4,7},{5,4},{6,5},{7,6},{8,11},{9,8},{10,9... | collective-permute-start | bytes 1572872 | tf_op jit(solution)/shard_map/ppermute | solution.py:718
  422.8 27.0 %collective-permute-start.48 = (bf16[128,2048]{1,0:T(8,128)(2,1)}, bf16[128,2048]{1,0:T(8,128)(2,1)}, u32[]{:S(2)}, u32[]{:S(2)}) collective-permute-start(bf16[128,2048]{1,0:T(8,128)(2,1)} %fusion.12), channel_id=1, source_target_pairs={{0,3},{1,0},{2,1},{3,2},{4,7},{5,4},{6,5},{7,6},{8,11},{9,8},{10,9... | collective-permute-start | bytes 1572872 | tf_op jit(solution)/shard_map/ppermute | solution.py:718
  449.8 25.3 %collective-permute-start.50 = (bf16[512,768]{1,0:T(8,128)(2,1)S(1)}, bf16[512,768]{1,0:T(8,128)(2,1)S(1)}, u32[]{:S(2)}, u32[]{:S(2)}) collective-permute-start(bf16[512,768]{1,0:T(8,128)(2,1)S(1)} %get-tuple-element.368), channel_id=1, source_target_pairs={{0,8},{8,0},{16,24},{24,16},{1,9},{9,1},{17,25},{25,17},{2,10},{10... | collective-permute-start | bytes 2359304 | tf_op jit(solution)/shard_map/ppermute | solution.py:722
  451.2 23.9 %collective-permute-start.51 = (bf16[512,768]{1,0:T(8,128)(2,1)S(1)}, bf16[512,768]{1,0:T(8,128)(2,1)S(1)}, u32[]{:S(2)}, u32[]{:S(2)}) collective-permute-start(bf16[512,768]{1,0:T(8,128)(2,1)S(1)} %get-tuple-element.369), channel_id=1, source_target_pairs={{0,16},{8,24},{16,0},{24,8},{1,17},{9,25},{17,1},{25,9},{2,18},{10... | collective-permute-start | bytes 2359304 | tf_op jit(solution)/shard_map/ppermute | solution.py:722
  453.1 12.2 %collective-permute-start.49 = (bf16[128,2048]{1,0:T(8,128)(2,1)S(1)}, bf16[128,2048]{1,0:T(8,128)(2,1)S(1)}, u32[]{:S(2)}, u32[]{:S(2)}) collective-permute-start(bf16[128,2048]{1,0:T(8,128)(2,1)S(1)} %fusion.11), channel_id=1, source_target_pairs={{0,3},{1,0},{2,1},{3,2},{4,7},{5,4},{6,5},{7,6},{8,11},{9,8},{10,9... | collective-permute-start | bytes 1572872 | tf_op jit(solution)/shard_map/ppermute | solution.py:718
  482.8 22.9 %collective-permute-start.53 = (bf16[128,2048]{1,0:T(8,128)(2,1)}, bf16[128,2048]{1,0:T(8,128)(2,1)}, u32[]{:S(2)}, u32[]{:S(2)}) collective-permute-start(bf16[128,2048]{1,0:T(8,128)(2,1)} %convert_add_fusion.3), channel_id=1, source_target_pairs={{0,3},{1,0},{2,1},{3,2},{4,7},{5,4},{6,5},{7,6},{8,11},{9,8},{10,9... | collective-permute-start | bytes 1572872 | tf_op jit(solution)/shard_map/ppermute | solution.py:718
  486.9 14.5 %collective-permute-start.56 = (bf16[128,2048]{1,0:T(8,128)(2,1)}, bf16[128,2048]{1,0:T(8,128)(2,1)S(1)}, u32[]{:S(2)}, u32[]{:S(2)}) collective-permute-start(bf16[128,2048]{1,0:T(8,128)(2,1)} %collective-permute-done.47.refs_6_), channel_id=1, source_target_pairs={{0,4},{4,0},{1,5},{5,1},{2,6},{6,2},{3,7},{7,3},{8,12},{12,8},{9,1... | collective-permute-start | bytes 1572872 | tf_op jit(solution)/shard_map/ppermute | solution.py:713
  487.2 11.6 %collective-permute-start.54 = (bf16[256,768]{1,0:T(8,128)(2,1)S(1)}, bf16[256,768]{1,0:T(8,128)(2,1)S(1)}, u32[]{:S(2)}, u32[]{:S(2)}) collective-permute-start(bf16[256,768]{1,0:T(8,128)(2,1)S(1)} %fusion.14), channel_id=1, source_target_pairs={{0,16},{8,24},{16,0},{24,8},{1,17},{9,25},{17,1},{25,9},{2,18},{10... | collective-permute-start | bytes 1179656 | tf_op jit(solution)/shard_map/ppermute | solution.py:722
  488.9 11.3 %collective-permute-start.55 = (bf16[256,768]{1,0:T(8,128)(2,1)S(1)}, bf16[256,768]{1,0:T(8,128)(2,1)S(1)}, u32[]{:S(2)}, u32[]{:S(2)}) collective-permute-start(bf16[256,768]{1,0:T(8,128)(2,1)S(1)} %fusion.13), channel_id=1, source_target_pairs={{0,8},{8,0},{16,24},{24,16},{1,9},{9,1},{17,25},{25,17},{2,10},{10... | collective-permute-start | bytes 1179656 | tf_op jit(solution)/shard_map/ppermute | solution.py:722
  508.3 15.2 %collective-permute-start.57 = (bf16[128,2048]{1,0:T(8,128)(2,1)}, bf16[128,2048]{1,0:T(8,128)(2,1)}, u32[]{:S(2)}, u32[]{:S(2)}) collective-permute-start(bf16[128,2048]{1,0:T(8,128)(2,1)} %fusion.8), channel_id=1, source_target_pairs={{0,3},{1,0},{2,1},{3,2},{4,7},{5,4},{6,5},{7,6},{8,11},{9,8},{10,9... | collective-permute-start | bytes 1572872 | tf_op jit(solution)/shard_map/ppermute | solution.py:718
  509.2 13.0 %collective-permute-start.58 = (bf16[512,384]{1,0:T(8,128)(2,1)}, bf16[512,384]{1,0:T(8,128)(2,1)}, u32[]{:S(2)}, u32[]{:S(2)}) collective-permute-start(bf16[512,384]{1,0:T(8,128)(2,1)} %pad_maximum_fusion.1), channel_id=1, source_target_pairs={{0,8},{8,0},{16,24},{24,16},{1,9},{9,1},{17,25},{25,17},{2,10},{10... | collective-permute-start | bytes 1179656 | tf_op jit(solution)/shard_map/ppermute | solution.py:722
  509.9 12.3 %collective-permute-start.59 = (bf16[512,384]{1,0:T(8,128)(2,1)S(1)}, bf16[512,384]{1,0:T(8,128)(2,1)S(1)}, u32[]{:S(2)}, u32[]{:S(2)}) collective-permute-start(bf16[512,384]{1,0:T(8,128)(2,1)S(1)} %pad_maximum_fusion.2), channel_id=1, source_target_pairs={{0,16},{8,24},{16,0},{24,8},{1,17},{9,25},{17,1},{25,9},{2,18},{10... | collective-permute-start | bytes 1179656 | tf_op jit(solution)/shard_map/ppermute | solution.py:722
  513.3 37.3 %all-to-all-start.6 = ((bf16[8,64,768]{2,1,0:T(8,128)(2,1)}), bf16[8,64,768]{2,1,0:T(8,128)(2,1)S(1)}, u32[]{:S(2)}, u32[]{:S(2)}) async-start(bf16[8,64,768]{2,1,0:T(8,128)(2,1)} %bitcast.88), calls=%async_computation.8 | async-start | bytes 1572864 | tf_op jit(solution)/shard_map/all_to_all | solution.py:806
  516.9 32.0 %collective-permute-start.61 = (bf16[256,2048]{1,0:T(8,128)(2,1)}, bf16[256,2048]{1,0:T(8,128)(2,1)S(1)}, u32[]{:S(2)}, u32[]{:S(2)}) collective-permute-start(bf16[256,2048]{1,0:T(8,128)(2,1)} %copy-done.33), channel_id=1, source_target_pairs={{0,8},{8,0},{16,24},{24,16},{1,9},{9,1},{17,25},{25,17},{2,10},{10... | collective-permute-start | bytes 3145736 | tf_op jit(solution)/shard_map/ppermute | solution.py:722
  518.4 32.2 %collective-permute-start.62 = (bf16[256,2048]{1,0:T(8,128)(2,1)}, bf16[256,2048]{1,0:T(8,128)(2,1)}, u32[]{:S(2)}, u32[]{:S(2)}) collective-permute-start(bf16[256,2048]{1,0:T(8,128)(2,1)} %copy-done.32), channel_id=1, source_target_pairs={{0,16},{8,24},{16,0},{24,8},{1,17},{9,25},{17,1},{25,9},{2,18},{10... | collective-permute-start | bytes 3145736 | tf_op jit(solution)/shard_map/ppermute | solution.py:722
  525.6 22.3 %collective-permute-start.63 = (bf16[256,384]{1,0:T(8,128)(2,1)S(1)}, bf16[256,384]{1,0:T(8,128)(2,1)S(1)}, u32[]{:S(2)}, u32[]{:S(2)}) collective-permute-start(bf16[256,384]{1,0:T(8,128)(2,1)S(1)} %get-tuple-element.427), channel_id=1, source_target_pairs={{0,16},{8,24},{16,0},{24,8},{1,17},{9,25},{17,1},{25,9},{2,18},{10... | collective-permute-start | bytes 589832 | tf_op jit(solution)/shard_map/ppermute | solution.py:722
  528.0 20.8 %collective-permute-start.60 = (bf16[128,2048]{1,0:T(8,128)(2,1)S(1)}, bf16[128,2048]{1,0:T(8,128)(2,1)S(1)}, u32[]{:S(2)}, u32[]{:S(2)}) collective-permute-start(bf16[128,2048]{1,0:T(8,128)(2,1)S(1)} %fusion.7), channel_id=1, source_target_pairs={{0,3},{1,0},{2,1},{3,2},{4,7},{5,4},{6,5},{7,6},{8,11},{9,8},{10,9... | collective-permute-start | bytes 1572872 | tf_op jit(solution)/shard_map/ppermute | solution.py:718
  531.5 16.5 %collective-permute-start.64 = (bf16[256,384]{1,0:T(8,128)(2,1)S(1)}, bf16[256,384]{1,0:T(8,128)(2,1)S(1)}, u32[]{:S(2)}, u32[]{:S(2)}) collective-permute-start(bf16[256,384]{1,0:T(8,128)(2,1)S(1)} %get-tuple-element.428), channel_id=1, source_target_pairs={{0,8},{8,0},{16,24},{24,16},{1,9},{9,1},{17,25},{25,17},{2,10},{10... | collective-permute-start | bytes 589832 | tf_op jit(solution)/shard_map/ppermute | solution.py:722
  552.2 28.8 %all-to-all-start.7 = ((bf16[8,64,384]{2,1,0:T(8,128)(2,1)}), bf16[8,64,384]{2,1,0:T(8,128)(2,1)S(1)}, u32[]{:S(2)}, u32[]{:S(2)}) async-start(bf16[8,64,384]{2,1,0:T(8,128)(2,1)} %bitcast.165), calls=%async_computation.9 | async-start | bytes 786432 | tf_op jit(solution)/shard_map/all_to_all | solution.py:806
  558.8 14.4 %collective-permute-start.65 = (bf16[128,2048]{1,0:T(8,128)(2,1)S(1)}, bf16[128,2048]{1,0:T(8,128)(2,1)S(1)}, u32[]{:S(2)}, u32[]{:S(2)}) collective-permute-start(bf16[128,2048]{1,0:T(8,128)(2,1)S(1)} %fusion.6), channel_id=1, source_target_pairs={{0,16},{8,24},{16,0},{24,8},{1,17},{9,25},{17,1},{25,9},{2,18},{10... | collective-permute-start | bytes 1572872 | tf_op jit(solution)/shard_map/ppermute | solution.py:722
  561.4 14.1 %collective-permute-start.66 = (bf16[128,2048]{1,0:T(8,128)(2,1)S(1)}, bf16[128,2048]{1,0:T(8,128)(2,1)S(1)}, u32[]{:S(2)}, u32[]{:S(2)}) collective-permute-start(bf16[128,2048]{1,0:T(8,128)(2,1)S(1)} %fusion.5), channel_id=1, source_target_pairs={{0,8},{8,0},{16,24},{24,16},{1,9},{9,1},{17,25},{25,17},{2,10},{10... | collective-permute-start | bytes 1572872 | tf_op jit(solution)/shard_map/ppermute | solution.py:722
  (107 other events, 835.6 us)
Sparse Core Ops, SparseCore 0:
  9.6 65.9 all-gather.2
  90.3 114.7 all-gather.4
  339.7 58.9 reduce-scatter.2
  419.9 67.3 reduce-scatter.4
